TPU v7x, 256 devices: a whole 4x4x8 slice. The times are simulated.
256 devices in a mesh: gx: 8 (over x, z_lo), gy: 4 (over y), gz: 8 (over z_hi, core).
Axes of the slice: x: 4, y: 4, z: 8 (z_hi: 4, z_lo: 2; z = z_hi * 2 + z_lo), core: 2. Of those that a mesh axis runs over, the one named last changes fastest.
Arguments:
- tokens: bfloat16 [65536, 768], P(('gx', 'gy', 'gz')), may hold values from -6 to 6
- norm_gain: float32 [768], replicated, may hold values from 0.5 to 1.5
- w_qkv: bfloat16 [768, 2304], replicated
- w_out: bfloat16 [768, 768], replicated, may hold values from -0.21875 to 0.21875
- send_rows: int32 [256, 7, 32], P(('gx', 'gy', 'gz')), may hold values from -1 to 255, as said below
- window_rows: int32 [256, 512], P(('gx', 'gy', 'gz')), may hold values from -1 to 479, as said below
- grad_out: bfloat16 [65536, 768], P(('gx', 'gy', 'gz')), may hold values from -6 to 6
Outputs:
- block_out: bfloat16 [65536, 768], P(('gx', 'gy', 'gz'))
- grad_tokens: bfloat16 [65536, 768], P(('gx', 'gy', 'gz'))
- grad_gain: float32 [768], P(('gx', 'gy', 'gz'))
- grad_w_qkv: float32 [768, 2304], P(('gx', 'gy', 'gz'))
- grad_w_out: float32 [768, 768], P(('gx', 'gy', 'gz'))
Inputs may be any that keep to these rules, and one draw needn't show every extreme that they name: `send_rows`: entries are rows of the tile (0 to 255) or -1 for empty; in each list the rows come first; a row stands in at most one list of its tile; a tile at the upper end of an axis has no rows in lists toward that axis; tile 0 fills all 7 lists. `window_rows`: entries index the owner's row list (256 own rows, then the 7 received lists of 32 in order k) or are -1 for padding; every own row that no list sends away and every non-empty received entry fills exactly one slot, nothing else does; a device's filled slots make whole windows but one.
All inputs are finite; a program needn't handle non-finite values.
Results may differ from a plain program's by a relative error of at most 0.018.
Values may be sent and summed in bfloat16 or wider, within the bound.
No kernel may reach another device: no remote copies, remote signals or barrier semaphores. Data moves between devices by JAX's collectives and lax.ppermute only.
A program may use at most 128 MiB of HBM per device.

v0:
```python
import jax
import jax.numpy as jnp
from jax import lax
from jax.sharding import PartitionSpec as P

HEADS = 12
WCAP = 128


epsilon = 1e-06
big_negative = -1e30


def passed_along(value, axis, steps):
    count = lax.axis_size(axis)
    initial, last = (max(0, -steps), min(count, count - steps))
    return lax.ppermute(value, axis, [(source, source + steps) for source in range(initial, last)])


def gather_rows(table, index):
    safe = jnp.maximum(index, 0)
    taken = jnp.take(table, safe, axis=0)
    return jnp.where((index >= 0)[..., None], taken, jnp.zeros((), table.dtype))


def spread_rows(values, index, length):
    target = jnp.where(index >= 0, index, length)
    empty = jnp.zeros((length, values.shape[-1]), values.dtype)
    return empty.at[target].set(values, mode="drop")


def carry_up(blocks):
    from_x = passed_along(blocks[3:7], "gx", 1)
    section_y = jnp.stack([blocks[1], blocks[2], from_x[2], from_x[3]])
    from_y = passed_along(section_y, "gy", 1)
    section_z = jnp.stack([blocks[0], from_y[1], from_x[1], from_y[3]])
    from_z = passed_along(section_z, "gz", 1)
    return jnp.concatenate(
        [from_z[0], from_y[0], from_z[1], from_x[0], from_z[2], from_y[2], from_z[3]], axis=0
    )


def carry_down(arrived, send, count):
    width = arrived.shape[-1]
    parts = arrived.reshape(7, send.shape[1], width)
    down_z = passed_along(jnp.stack([parts[0], parts[2], parts[4], parts[6]]), "gz", -1)
    down_y = passed_along(jnp.stack([parts[1], down_z[1], parts[5], down_z[3]]), "gy", -1)
    down_x = passed_along(jnp.stack([parts[3], down_z[2], down_y[2], down_y[3]]), "gx", -1)
    returned = jnp.stack(
        [down_z[0], down_y[0], down_y[1], down_x[0], down_x[1], down_x[2], down_x[3]]
    )
    return spread_rows(returned.reshape(-1, width), send.reshape(-1), count)


def split_heads(packed, heads):
    windows, length, triple = packed.shape
    head_dim = triple // 3 // heads
    split = packed.reshape(windows, length, 3, heads, head_dim)
    return (split[:, :, 0], split[:, :, 1], split[:, :, 2], head_dim)


def attend(packed, valid, heads):
    query, keys, values, head_dim = split_heads(packed, heads)
    scores = jnp.einsum(
        "wqhd,wkhd->whqk", query, keys, preferred_element_type=jnp.float32
    ) * head_dim ** (-0.5)
    scores = jnp.where(valid[:, None, None, :], scores, big_negative)
    top = jnp.max(scores, axis=-1, keepdims=True)
    expo = jnp.exp(scores - top)
    probs = expo / jnp.sum(expo, axis=-1, keepdims=True)
    weights = probs.astype(jnp.bfloat16)
    mixed = jnp.einsum(
        "whqk,wkhd->wqhd", weights, values, preferred_element_type=jnp.float32
    ).astype(jnp.bfloat16)
    return (mixed.reshape(packed.shape[0] * packed.shape[1], -1), probs, weights)


def attend_back(packed, probs, weights, delta_slots, heads):
    query, keys, values, head_dim = split_heads(packed, heads)
    windows, length = (packed.shape[0], packed.shape[1])
    grad_delta = delta_slots.reshape(windows, length, heads, head_dim)
    dweights = jnp.einsum("wqhd,wkhd->whqk", grad_delta, values, preferred_element_type=jnp.float32)
    dscores = probs * (dweights - jnp.sum(dweights * probs, axis=-1, keepdims=True))
    dscaled = (dscores * head_dim ** (-0.5)).astype(jnp.bfloat16)
    dquery = jnp.einsum("whqk,wkhd->wqhd", dscaled, keys, preferred_element_type=jnp.float32)
    dkeys = jnp.einsum("whqk,wqhd->wkhd", dscaled, query, preferred_element_type=jnp.float32)
    dvalues = jnp.einsum("whqk,wqhd->wkhd", weights, grad_delta, preferred_element_type=jnp.float32)
    joined = jnp.stack([dquery, dkeys, dvalues], axis=2)
    return joined.reshape(windows * length, -1).astype(jnp.bfloat16)


def on_device(tokens, norm_gain, w_qkv, w_out, send_rows, window_rows, grad_out):
    count = tokens.shape[0]
    send = send_rows[0]
    slot_index = window_rows[0]
    windows = slot_index.shape[0] // WCAP
    valid = (slot_index >= 0).reshape(windows, WCAP)
    span = count + send.shape[0] * send.shape[1]
    floats = tokens.astype(jnp.float32)
    centred = floats - jnp.mean(floats, axis=-1, keepdims=True)
    inv_std = lax.rsqrt(jnp.mean(centred * centred, axis=-1, keepdims=True) + epsilon)
    unit = centred * inv_std
    normed = (unit * norm_gain).astype(jnp.bfloat16)
    delta_own = jnp.einsum("te,de->td", grad_out, w_out, preferred_element_type=jnp.float32).astype(
        jnp.bfloat16
    )
    source = jnp.dot(normed, w_qkv, preferred_element_type=jnp.float32).astype(jnp.bfloat16)
    source_in = carry_up(gather_rows(source, send))
    local = jnp.concatenate([source, source_in], axis=0)
    packed = gather_rows(local, slot_index).reshape(windows, WCAP, -1)
    mixed, probs, weights = attend(packed, valid, HEADS)
    mixed_rows = spread_rows(mixed, slot_index, span)
    attended = mixed_rows[:count] + carry_down(mixed_rows[count:], send, count)
    block_out = (floats + jnp.dot(attended, w_out, preferred_element_type=jnp.float32)).astype(
        jnp.bfloat16
    )
    grad_proj = jnp.einsum("td,te->de", attended, grad_out, preferred_element_type=jnp.float32)
    delta_in = carry_up(gather_rows(delta_own, send))
    delta_slots = gather_rows(jnp.concatenate([delta_own, delta_in], axis=0), slot_index)
    dpacked = attend_back(packed, probs, weights, delta_slots, HEADS)
    dpacked_rows = spread_rows(dpacked, slot_index, span)
    dpacked_own = dpacked_rows[:count] + carry_down(dpacked_rows[count:], send, count)
    grad_qkv = jnp.einsum("td,te->de", normed, dpacked_own, preferred_element_type=jnp.float32)
    dnormed = jnp.einsum(
        "te,de->td", dpacked_own, w_qkv, preferred_element_type=jnp.float32
    ).astype(jnp.bfloat16)
    dnormed_f = dnormed.astype(jnp.float32)
    grad_gain = jnp.sum(dnormed_f * unit, axis=0)
    dunit = dnormed_f * norm_gain
    dcentre = inv_std * (
        dunit
        - jnp.mean(dunit, axis=-1, keepdims=True)
        - unit * jnp.mean(dunit * unit, axis=-1, keepdims=True)
    )
    grad_tokens = (grad_out.astype(jnp.float32) + dcentre).astype(jnp.bfloat16)
    totals = (
        lax.psum_scatter(grad_gain, ("gx", "gy", "gz"), scatter_dimension=0, tiled=True),
        lax.psum_scatter(grad_qkv, ("gx", "gy", "gz"), scatter_dimension=0, tiled=True),
        lax.psum_scatter(grad_proj, ("gx", "gy", "gz"), scatter_dimension=0, tiled=True),
    )
    return (block_out, grad_tokens, totals[0], totals[1], totals[2])


def solution(mesh):
    in_specs = (
        P(("gx", "gy", "gz"), None),
        P(),
        P(),
        P(),
        P(("gx", "gy", "gz"), None, None),
        P(("gx", "gy", "gz"), None),
        P(("gx", "gy", "gz"), None),
    )
    out_specs = (
        P(("gx", "gy", "gz"), None),
        P(("gx", "gy", "gz"), None),
        P(("gx", "gy", "gz")),
        P(("gx", "gy", "gz"), None),
        P(("gx", "gy", "gz"), None),
    )
    return jax.shard_map(
        on_device, mesh=mesh, in_specs=in_specs, out_specs=out_specs, check_vma=False
    )
```

profile of v0, /device:TPU:10, one launch (start us, length us, event | category | flops | bytes accessed | tf_op | source)
XLA Modules:
  0.0 548.1 jit_solution(1922771086085963004)
XLA Ops:
  8.1 1.5 maximum_reduce_fusion
  11.5 2.8 constant_dynamic-update-slice_fusion.1
  14.3 3.1 gather_fusion.2
  19.9 3.8 collective-permute-start.6
  26.1 3.6 constant_dynamic-update-slice_fusion
  29.7 4.7 gather_fusion
  36.0 2.9 collective-permute-start
  40.5 3.5 collective-permute-start.7
  45.4 3.1 collective-permute-done.7
  49.9 3.7 collective-permute-done
  53.6 3.5 collective-permute-start.1
  61.1 10.0 %collective-permute-done.1 = bf16[4,32,2304]{2,1,0:T(8,128)(2,1)S(1)} collective-permute-done((bf16[4,32,2304]{2,1,0:T(8,128)(2,1)S(1)}, bf16[4,32,2304]{2,1,0:T(8,128)(2,1)S(1)}, u32[]{:S(2)}, u32[]{:S(2)}) %collective-permute-start.1) | collective-permute-done | bytes 589856 | tf_op jit(solution)/shard_map/ppermute | solution.py:17
  72.9 2.7 collective-permute-start.2
  76.8 4.3 gather_fusion.3
  81.1 2.3 copy.46
  83.4 2.4 gather.25
  85.8 2.4 select_select_fusion.1
  88.2 1.6 fusion.69
  89.8 1.6 fusion.68
  91.4 1.6 fusion.67
  92.9 1.6 fusion.66
  94.5 1.6 fusion.65
  96.1 1.6 fusion.64
  97.7 1.6 fusion.63
  99.2 7.7 %gather_fusion.1 = bf16[512,2304]{1,0:T(8,128)(2,1)} fusion(bf16[480,2304]{1,0:T(8,128)(2,1)} %fusion.63, s32[1024]{0:T(1024)S(1)} %pad_clamp_fusion), kind=kCustom, calls=%fused_computation.1 | custom fusion | bytes 4720640 | tf_op jit(solution)/shard_map/jit(_take)/gather | solution.py:22
  106.9 4.3 copy.41
  111.2 5.3 gather.22
  116.5 2.1 fusion.6
  120.3 2.3 fusion.52
  122.6 1.5 fusion.92
  124.1 1.6 copy-done.18
  125.7 2.1 fusion.31
  127.9 6.8 %fusion.27 = bf16[4,128,1,12,64]{1,4,3,0,2:T(8,128)(2,1)} fusion(f32[4,12,128,128]{2,3,1,0:T(8,128)} %fusion.52, bf16[4,128,3,12,64]{1,4,3,0,2:T(8,128)(2,1)} %copy-done.1, f32[4,12,128,128]{2,3,1,0:T(8,128)} %copy-done.18, f32[4,12,128]{2,1,0:T(8,128)} %copy-done.19), kind=kOutput, calls=%fused_computation.34 | convolution fusion | flops 106567808 | bytes 14221312 | tf_op jit(solution)/shard_map/whqk,wkhd->wqhd/dot_general | solution.py:85
  134.7 6.8 %fusion.24 = bf16[4,128,1,12,64]{1,4,3,0,2:T(8,128)(2,1)} fusion(f32[4,12,128,128]{2,3,1,0:T(8,128)} %fusion.52, bf16[4,128,3,12,64]{1,4,3,0,2:T(8,128)(2,1)} %copy-done.1, f32[4,12,128,128]{2,3,1,0:T(8,128)} %copy-done.18, f32[4,12,128]{2,1,0:T(8,128)} %copy-done.19), kind=kOutput, calls=%fused_computation.33 | convolution fusion | flops 106567808 | bytes 14221312 | tf_op jit(solution)/shard_map/whqk,wqhd->wkhd/dot_general | solution.py:86
  141.6 2.6 fusion.30
  145.8 2.3 copy.45
  148.2 1.9 pad_maximum_fusion
  150.0 2.2 copy.52
  152.3 1.8 copy.73
  154.1 4.3 copy.53
  158.4 4.1 scatter_custom_fusion
  162.5 6.8 %scatter_custom_fusion.2 = bf16[480,2304]{1,0:T(8,128)(2,1)} fusion(s32[512]{0:T(512)} %bitcast.169, bf16[512,2304]{1,0:T(8,128)(2,1)} %copy.53, bf16[]{:T(256)} %constant.44.clone.1), kind=kCustom, calls=%fused_computation.45 | custom fusion | bytes 2212352 | tf_op jit(solution)/shard_map/scatter | solution.py:29
  169.3 2.0 slice_bitcast_fusion.9
  172.7 1.6 slice_bitcast_fusion.30
  175.6 5.4 collective-permute-done.3
  183.3 1.9 collective-permute-start.10
  186.0 1.9 collective-permute-start.4
  188.5 9.0 %collective-permute-done.4 = bf16[4,32,768]{2,1,0:T(8,128)(2,1)} collective-permute-done((bf16[4,32,768]{2,1,0:T(8,128)(2,1)}, bf16[4,32,768]{2,1,0:T(8,128)(2,1)}, u32[]{:S(2)}, u32[]{:S(2)}) %collective-permute-start.4) | collective-permute-done | bytes 196640 | tf_op jit(solution)/shard_map/ppermute | solution.py:17
  199.3 2.4 collective-permute-start.5
  201.7 1.8 fusion.87
  203.5 1.9 pad_maximum_fusion.6
  205.4 1.9 collective-permute-start.11
  208.6 2.7 scatter_custom_fusion.1
  211.3 3.2 fusion.70
  214.5 2.9 collective-permute-done.11
  217.5 2.2 pad_maximum_fusion.1
  219.6 3.9 scatter_custom_fusion.3
  223.5 6.0 %fusion.60 = f32[768,2304]{1,0:T(8,128)} fusion(bf16[256,2304]{1,0:T(8,128)(2,1)} %scatter_custom_fusion.3, bf16[480,2304]{1,0:T(8,128)(2,1)} %scatter_custom_fusion.2, bf16[256,768]{1,0:T(8,128)(2,1)} %param.7, f32[768]{0:T(1024)S(1)} %copy-done.11, f32[256]{0:T(256)S(1)} %add_rsqrt_fusion, f32[256]{0:T(256)S(1)} %broadcast_multiply_fusion.2), kind=kOutput, calls=%fused_computation.87 | convolution fusion | flops 907542528 | bytes 9835520 | tf_op jit(solution)/shard_map/td,te->de/dot_general | solution.py:123
  229.5 3.0 fusion.32
  232.5 4.0 fusion.48
  236.4 100.9 %all-reduce = f32[768]{0:T(1024)} all-reduce(f32[768]{0:T(1024)S(1)} %get-tuple-element.5), channel_id=2, replica_groups=mesh['gx'=8,'gy'=4,'gz'=8] {'gx','gy','gz'}, use_global_device_ids=true, to_apply=%region_12.13.clone | all-reduce | flops 768 | bytes 6144
  340.0 2.5 fusion.47
  342.4 195.6 %all-reduce.6.cloned.1.call-done = (f32[768,2304]{1,0:T(8,128)}, f32[768,768]{1,0:T(8,128)}) async-done(((f32[768,2304]{1,0:T(8,128)}, f32[768,768]{1,0:T(8,128)}), (f32[768,2304]{1,0:T(8,128)}, f32[768,768]{1,0:T(8,128)})) %all-reduce.6.cloned.1.call-update) | async-done | bytes 9437200
  538.1 1.5 constant_dynamic-slice_fusion.1
  (106 shorter events, 37.3 us)
Async XLA Ops:
  7.2 19.0 %copy-start = (bf16[768,2304]{1,0:T(8,128)(2,1)S(1)}, bf16[768,2304]{1,0:T(8,128)(2,1)}, u32[]{:S(2)}) copy-start(bf16[768,2304]{1,0:T(8,128)(2,1)} %param.9) | copy-start | bytes 10616836
  7.2 530.9 %all-reduce.6.cloned.1.call-start = ((), (), s32[]{:S(2)}) async-start(), calls=%async_computation | async-start | bytes 18874368
  11.5 5.9 %copy-start.13 = (pred[7,32]{1,0:T(8,128)(4,1)S(1)}, pred[7,32]{1,0:T(8,128)(4,1)}, u32[]{:S(2)}) copy-start(pred[7,32]{1,0:T(8,128)(4,1)} %get-tuple-element.55) | copy-start | bytes 676
  11.5 5.9 %copy-start.14 = (pred[7,32]{1,0:T(8,128)(4,1)S(1)}, pred[7,32]{1,0:T(8,128)(4,1)}, u32[]{:S(2)}) copy-start(pred[7,32]{1,0:T(8,128)(4,1)} %get-tuple-element.56) | copy-start | bytes 676
  14.3 11.8 %copy-start.11 = (f32[768]{0:T(1024)S(1)}, f32[768]{0:T(1024)}, u32[]{:S(2)}) copy-start(f32[768]{0:T(1024)} %param.8) | copy-start | bytes 9220
  18.5 0.7 copy-start.5
  19.9 19.7 %collective-permute-start.6 = (bf16[4,32,768]{2,1,0:T(8,128)(2,1)}, bf16[4,32,768]{2,1,0:T(8,128)(2,1)}, u32[]{:S(2)}, u32[]{:S(2)}) collective-permute-start(bf16[4,32,768]{2,1,0:T(8,128)(2,1)} %slice.378), channel_id=1, source_target_pairs={{0,32},{32,64},{64,96},{96,128},{128,160},{160,192},{192,224},{1,3... | collective-permute-start | bytes 589832 | tf_op jit(solution)/shard_map/ppermute | solution.py:17
  34.4 4.5 copy-start.15
  34.4 6.0 %slice-start.1 = ((bf16[7,32,768]{2,1,0:T(8,128)(2,1)}), bf16[2,32,768]{2,1,0:T(8,128)(2,1)S(1)}, s32[]{:S(2)}) async-start(bf16[7,32,768]{2,1,0:T(8,128)(2,1)} %copy-done.5), calls=%async_computation.2 | async-start | bytes 196608 | tf_op jit(solution)/shard_map/slice | solution.py:34
  34.4 14.1 %slice-start = ((bf16[7,32,768]{2,1,0:T(8,128)(2,1)}), bf16[1,32,768]{2,1,0:T(8,128)(2,1)S(1)}, s32[]{:S(2)}) async-start(bf16[7,32,768]{2,1,0:T(8,128)(2,1)} %copy-done.5), calls=%async_computation.1 | async-start | bytes 98304 | tf_op jit(solution)/shard_map/slice | solution.py:36
  36.0 17.6 %collective-permute-start = (bf16[4,32,2304]{2,1,0:T(8,128)(2,1)S(1)}, bf16[4,32,2304]{2,1,0:T(8,128)(2,1)S(1)}, u32[]{:S(2)}, u32[]{:S(2)}) collective-permute-start(bf16[4,32,2304]{2,1,0:T(8,128)(2,1)S(1)} %slice.347), channel_id=1, source_target_pairs={{0,32},{32,64},{64,96},{96,128},{128,160},{160,192},{192,224},{1,3... | collective-permute-start | bytes 1769480 | tf_op jit(solution)/shard_map/ppermute | solution.py:17
  40.5 8.0 %collective-permute-start.7 = (bf16[4,32,768]{2,1,0:T(8,128)(2,1)S(1)}, bf16[4,32,768]{2,1,0:T(8,128)(2,1)S(1)}, u32[]{:S(2)}, u32[]{:S(2)}) collective-permute-start(bf16[4,32,768]{2,1,0:T(8,128)(2,1)S(1)} %pad_maximum_fusion.11), channel_id=1, source_target_pairs={{0,8},{8,16},{16,24},{1,9},{9,17},{17,25},{2,10},{10,18},{18,26},{... | collective-permute-start | bytes 589832 | tf_op jit(solution)/shard_map/ppermute | solution.py:17
  48.6 8.6 %collective-permute-start.8 = (bf16[4,32,768]{2,1,0:T(8,128)(2,1)S(1)}, bf16[4,32,768]{2,1,0:T(8,128)(2,1)S(1)}, u32[]{:S(2)}, u32[]{:S(2)}) collective-permute-start(bf16[4,32,768]{2,1,0:T(8,128)(2,1)S(1)} %pad_maximum_fusion.12), channel_id=1, source_target_pairs={{0,1},{1,2},{2,3},{3,4},{4,5},{5,6},{6,7},{8,9},{9,10},{10,11},{11... | collective-permute-start | bytes 589832 | tf_op jit(solution)/shard_map/ppermute | solution.py:17
  53.6 19.3 %copy-start.8 = (bf16[4,32,2304]{2,1,0:T(8,128)(2,1)}, bf16[4,32,2304]{2,1,0:T(8,128)(2,1)S(1)}, u32[]{:S(2)}) copy-start(bf16[4,32,2304]{2,1,0:T(8,128)(2,1)S(1)} %collective-permute-done) | copy-start | bytes 1769476
  53.6 17.4 %collective-permute-start.1 = (bf16[4,32,2304]{2,1,0:T(8,128)(2,1)S(1)}, bf16[4,32,2304]{2,1,0:T(8,128)(2,1)S(1)}, u32[]{:S(2)}, u32[]{:S(2)}) collective-permute-start(bf16[4,32,2304]{2,1,0:T(8,128)(2,1)S(1)} %pad_maximum_fusion.2), channel_id=1, source_target_pairs={{0,8},{8,16},{16,24},{1,9},{9,17},{17,25},{2,10},{10,18},{18,26},{... | collective-permute-start | bytes 1769480 | tf_op jit(solution)/shard_map/ppermute | solution.py:17
  71.1 0.8 copy-start.9
  72.9 15.4 %collective-permute-start.2 = (bf16[4,32,2304]{2,1,0:T(8,128)(2,1)}, bf16[4,32,2304]{2,1,0:T(8,128)(2,1)}, u32[]{:S(2)}, u32[]{:S(2)}) collective-permute-start(bf16[4,32,2304]{2,1,0:T(8,128)(2,1)} %pad_maximum_fusion.3), channel_id=1, source_target_pairs={{0,1},{1,2},{2,3},{3,4},{4,5},{5,6},{6,7},{8,9},{9,10},{10,11},{11... | collective-permute-start | bytes 1769480 | tf_op jit(solution)/shard_map/ppermute | solution.py:17
  111.2 5.3 copy-start.16
  118.6 1.4 copy-start.1
  118.6 1.7 copy-start.4
  124.1 1.7 copy-start.18
  124.1 1.6 copy-start.19
  171.4 16.5 %copy-start.12 = (s32[7,32]{1,0:T(8,128)S(1)}, s32[7,32]{1,0:T(8,128)}, u32[]{:S(2)}) copy-start(s32[7,32]{1,0:T(8,128)} %get-tuple-element.9) | copy-start | bytes 2692
  171.4 10.3 %collective-permute-start.9 = (bf16[4,32,2304]{2,1,0:T(8,128)(2,1)S(1)}, bf16[4,32,2304]{2,1,0:T(8,128)(2,1)S(1)}, u32[]{:S(2)}, u32[]{:S(2)}) collective-permute-start(bf16[4,32,2304]{2,1,0:T(8,128)(2,1)S(1)} %pad_maximum_fusion.4), channel_id=1, source_target_pairs={{1,0},{2,1},{3,2},{4,3},{5,4},{6,5},{7,6},{9,8},{10,9},{11,10},{12... | collective-permute-start | bytes 1769480 | tf_op jit(solution)/shard_map/ppermute | solution.py:17
  174.3 6.7 %collective-permute-start.3 = (bf16[4,32,768]{2,1,0:T(8,128)(2,1)S(1)}, bf16[4,32,768]{2,1,0:T(8,128)(2,1)S(1)}, u32[]{:S(2)}, u32[]{:S(2)}) collective-permute-start(bf16[4,32,768]{2,1,0:T(8,128)(2,1)S(1)} %pad_maximum_fusion.8), channel_id=1, source_target_pairs={{1,0},{2,1},{3,2},{4,3},{5,4},{6,5},{7,6},{9,8},{10,9},{11,10},{12... | collective-permute-start | bytes 589832 | tf_op jit(solution)/shard_map/ppermute | solution.py:17
  183.3 18.4 %collective-permute-start.10 = (bf16[4,32,2304]{2,1,0:T(8,128)(2,1)}, bf16[4,32,2304]{2,1,0:T(8,128)(2,1)}, u32[]{:S(2)}, u32[]{:S(2)}) collective-permute-start(bf16[4,32,2304]{2,1,0:T(8,128)(2,1)} %pad_maximum_fusion.5), channel_id=1, source_target_pairs={{8,0},{16,8},{24,16},{9,1},{17,9},{25,17},{10,2},{18,10},{26,18},{... | collective-permute-start | bytes 1769480 | tf_op jit(solution)/shard_map/ppermute | solution.py:17
  186.0 11.6 %collective-permute-start.4 = (bf16[4,32,768]{2,1,0:T(8,128)(2,1)}, bf16[4,32,768]{2,1,0:T(8,128)(2,1)}, u32[]{:S(2)}, u32[]{:S(2)}) collective-permute-start(bf16[4,32,768]{2,1,0:T(8,128)(2,1)} %pad_maximum_fusion.9), channel_id=1, source_target_pairs={{8,0},{16,8},{24,16},{9,1},{17,9},{25,17},{10,2},{18,10},{26,18},{... | collective-permute-start | bytes 589832 | tf_op jit(solution)/shard_map/ppermute | solution.py:17
  188.5 18.8 %copy-start.17 = (s32[224,1]{0,1:T(1,128)S(1)}, s32[224,1]{0,1:T(1,128)}, u32[]{:S(2)}) copy-start(s32[224,1]{0,1:T(1,128)} %reshape_squeeze.4) | copy-start | bytes 2692
  188.5 19.3 %copy-start.10 = (bf16[1,32,768]{2,1,0:T(8,128)(2,1)S(1)}, bf16[1,32,768]{2,1,0:T(8,128)(2,1)}, u32[]{:S(2)}) copy-start(bf16[1,32,768]{2,1,0:T(8,128)(2,1)} %get-tuple-element.38) | copy-start | bytes 147460
  199.3 8.5 %collective-permute-start.5 = (bf16[4,32,768]{2,1,0:T(8,128)(2,1)S(1)}, bf16[4,32,768]{2,1,0:T(8,128)(2,1)S(1)}, u32[]{:S(2)}, u32[]{:S(2)}) collective-permute-start(bf16[4,32,768]{2,1,0:T(8,128)(2,1)S(1)} %pad_maximum_fusion.10), channel_id=1, source_target_pairs={{32,0},{64,32},{96,64},{128,96},{160,128},{192,160},{224,192},{33,... | collective-permute-start | bytes 589832 | tf_op jit(solution)/shard_map/ppermute | solution.py:17
  205.4 12.1 %collective-permute-start.11 = (bf16[4,32,2304]{2,1,0:T(8,128)(2,1)}, bf16[4,32,2304]{2,1,0:T(8,128)(2,1)}, u32[]{:S(2)}, u32[]{:S(2)}) collective-permute-start(bf16[4,32,2304]{2,1,0:T(8,128)(2,1)} %pad_maximum_fusion.6), channel_id=1, source_target_pairs={{32,0},{64,32},{96,64},{128,96},{160,128},{192,160},{224,192},{33,... | collective-permute-start | bytes 1769480 | tf_op jit(solution)/shard_map/ppermute | solution.py:17
  211.3 6.1 %copy-start.6 = (bf16[2,32,2304]{2,1,0:T(8,128)(2,1)S(1)}, bf16[2,32,2304]{2,1,0:T(8,128)(2,1)}, u32[]{:S(2)}) copy-start(bf16[2,32,2304]{2,1,0:T(8,128)(2,1)} %get-tuple-element.32) | copy-start | bytes 884740
  211.3 6.1 %copy-start.7 = (bf16[1,32,2304]{2,1,0:T(8,128)(2,1)S(1)}, bf16[1,32,2304]{2,1,0:T(8,128)(2,1)}, u32[]{:S(2)}) copy-start(bf16[1,32,2304]{2,1,0:T(8,128)(2,1)} %get-tuple-element.28) | copy-start | bytes 442372
  229.5 3.0 copy-start.2
  229.5 3.0 copy-start.3
Sparse Core Ops, SparseCore 0:
  229.6 308.4 all-reduce.5
where the time goes:
time: 555 us; the launch traced here: 548 us
  waiting for transfers between devices  230 us (41%)
  local copies, waits for them, and re-layouts  101 us (18%)
  blocking collectives  101 us (18%)
  matrix products  43.8 us (8%)
  other arithmetic  29.7 us (5%)
  starting transfers between devices  28.4 us (5%)
  between operations  14.7 us (3%)
    unnamed x2, waiting for transfers between devices  196 us
    unnamed x1, blocking collectives  101 us
    ppermute x12, waiting for transfers between devices, passed_along(): lax.ppermute(value, axis, [(source, source + steps) for source in range(i...  34.2 us
    gather x8, local copies, waits for them, and re-layouts, gather_rows(): taken = jnp.take(table, safe, axis=0)  34.1 us
    ppermute x12, starting transfers between devices, passed_along(): lax.ppermute(value, axis, [(source, source + steps) for source in range(i...  28.4 us
    unnamed x58, local copies, waits for them, and re-layouts  25.9 us
    scatter x4, local copies, waits for them, and re-layouts, spread_rows(): return empty.at[target].set(values, mode='drop')  17.4 us
  transfers between devices with their start and end apart: 13, of which 7 were waited for; matrix products, arithmetic and copies ran while one was open for 11% of the time, Pallas kernels for 0%

commit v1 on v0

v1 whole, which is shorter than its diff:
```python
import functools
import itertools

import jax
import jax.numpy as jnp
from jax import lax
from jax.experimental import pallas as pl
from jax.experimental.pallas import tpu as pltpu
from jax.sharding import PartitionSpec as P

D = 768
WCAP = 128
SLOTS = 512
ROWS = 256
WIDE = 2 * D
COLS_A = 2 * D
COLS_B = 2 * D + 128
COLS = COLS_A + COLS_B
AXES = ("gx", "gy", "gz")
EPSILON = 1e-06
BIG_NEGATIVE = -1e30
BF = jnp.bfloat16
F32 = jnp.float32
NT = (((1,), (1,)), ((), ()))
TN = (((0,), (0,)), ((), ()))
PARAMS = pltpu.CompilerParams(vmem_limit_bytes=56 * 1024 * 1024)
VMEM = pl.BlockSpec(memory_space=pltpu.VMEM)


def dot(a, b):
    return jnp.dot(a, b, preferred_element_type=F32)


def iota(shape, dim):
    return lax.broadcasted_iota(jnp.int32, shape, dim)


def column(row):
    n = row.shape[1]
    spread = jnp.broadcast_to(row.astype(F32), (n, n))
    return jnp.sum(jnp.where(iota((n, n), 0) == iota((n, n), 1), spread, 0.0), axis=1, keepdims=True)


def one_hot(condition):
    return jnp.where(condition, 1.0, 0.0).astype(BF)


def passed_along(value, axis, steps):
    count = lax.axis_size(axis)
    initial, last = (max(0, -steps), min(count, count - steps))
    return lax.ppermute(value, axis, [(source, source + steps) for source in range(initial, last)])


def crossed(value, axis, mask):
    count = lax.axis_size(axis)
    return lax.ppermute(value, axis, [(source, source ^ mask) for source in range(count)])


def pack_body(tok_ref, go_ref, send_ref, out_ref):
    chosen = [
        one_hot(iota((32, ROWS), 1).astype(F32) == column(send_ref[0, k : k + 1, :])) for k in range(7)
    ]
    chosen = jnp.concatenate(chosen, axis=0)
    for part, ref in enumerate((tok_ref, go_ref)):
        taken = dot(chosen, ref[...]).astype(BF)
        out_ref[:, :, part * D : (part + 1) * D] = taken.reshape(7, 32, D)


def normalised(x):
    centred = x - jnp.mean(x, axis=-1, keepdims=True)
    inv_std = lax.rsqrt(jnp.mean(centred * centred, axis=-1, keepdims=True) + EPSILON)
    return centred * inv_std, inv_std


def order(me_ref, piece):
    j = iota((D, 1), 0)
    core = j // 384
    rest = j % 384
    if piece == 0:
        gx, gy = rest // 48, rest % 48 // 12
    else:
        gy, gx = rest // 96, rest % 96 // 12
    z_hi, r = rest % 12 // 3, rest % 3
    gx = gx ^ me_ref[0]
    gy = gy ^ me_ref[1]
    gz = (z_hi * 2 + core) ^ me_ref[2]
    return ((gx * 4 + gy) * 8 + gz) * 3 + r


def main_body(
    me_ref, tok_ref, go_ref, fx_ref, fy_ref, fz_ref, win_ref, gain_ref, wqkv_ref, wout_ref,
    own_ref, snd_ref, xs_ref, gos_ref, mixed_ref, dn_ref,
    rows_ref, normed_ref, unit_ref, packed_ref, delta_ref, dpacked_ref,
):
    rows_ref[:ROWS, :D] = tok_ref[...]
    rows_ref[:ROWS, D:] = go_ref[...]
    arrived = (
        fz_ref[0], fy_ref[0], fz_ref[1], fx_ref[0], fz_ref[2], fy_ref[2], fz_ref[3],
    )
    for k, block in enumerate(arrived):
        rows_ref[ROWS + 32 * k : ROWS + 32 * (k + 1), :] = block
    rows_ref[480:, :] = jnp.zeros((32, WIDE), BF)
    gain = gain_ref[...]

    def gather_window(w, carry):
        at = pl.ds(pl.multiple_of(w * WCAP, WCAP), WCAP)
        picks = one_hot(iota((WCAP, SLOTS), 1).astype(F32) == column(win_ref[:, at]))
        taken = dot(picks, rows_ref[...])
        x = taken[:, :D]
        xs_ref[at, :] = x.astype(BF)
        gos_ref[at, :] = taken[:, D:].astype(BF)
        unit, _ = normalised(x)
        unit_ref[at, :] = unit
        normed_ref[at, :] = (unit * gain).astype(BF)
        return carry

    lax.fori_loop(0, SLOTS // WCAP, gather_window, 0)

    def project(c, carry):
        at = pl.ds(pl.multiple_of(c * D, D), D)
        packed_ref[:, at] = dot(normed_ref[...], wqkv_ref[:, at]).astype(BF)
        return carry

    lax.fori_loop(0, 3, project, 0)
    delta_ref[...] = lax.dot_general(
        gos_ref[...], wout_ref[...], NT, preferred_element_type=F32
    ).astype(BF)

    low = iota((WCAP, 128), 1) < 64
    zero = jnp.zeros((), BF)

    def both(value):
        return jnp.concatenate([jnp.where(low, value, zero), jnp.where(low, zero, value)], axis=0)

    def attend(w, carry):
        at = pl.ds(pl.multiple_of(w * WCAP, WCAP), WCAP)
        filled = jnp.broadcast_to(column(win_ref[:, at]) >= 0, (WCAP, WCAP))[None]
        for p in range(6):
            q_at = pl.ds(p * 128, 128)
            k_at = pl.ds(D + p * 128, 128)
            v_at = pl.ds(2 * D + p * 128, 128)
            q = packed_ref[at, q_at]
            k_both = both(packed_ref[at, k_at])
            v_both = both(packed_ref[at, v_at])
            d = delta_ref[at, q_at]
            scores = lax.dot_general(k_both, q, NT, preferred_element_type=F32) * 0.125
            scores = jnp.where(filled, scores.reshape(2, WCAP, WCAP), BIG_NEGATIVE)
            expo = jnp.exp(scores - jnp.max(scores, axis=1, keepdims=True))
            probs = expo * (1.0 / jnp.sum(expo, axis=1, keepdims=True))
            weights = probs.astype(BF)
            mixed = lax.dot_general(
                weights.reshape(2 * WCAP, WCAP), v_both, TN, preferred_element_type=F32
            )
            mixed_ref[at, q_at] = mixed.astype(BF)
            dweights = lax.dot_general(v_both, d, NT, preferred_element_type=F32)
            dweights = dweights.reshape(2, WCAP, WCAP)
            inner = jnp.sum(dweights * probs, axis=1, keepdims=True)
            dscaled = (probs * (dweights - inner) * 0.125).astype(BF)
            dq = lax.dot_general(
                dscaled.reshape(2 * WCAP, WCAP), k_both, TN, preferred_element_type=F32
            )
            dpacked_ref[at, q_at] = dq.astype(BF)
            beside = jnp.concatenate([dscaled[0], dscaled[1]], axis=1)
            dpacked_ref[at, k_at] = dot(beside, both(q)).astype(BF)
            beside = jnp.concatenate([weights[0], weights[1]], axis=1)
            dpacked_ref[at, v_at] = dot(beside, both(d)).astype(BF)
        return carry

    lax.fori_loop(0, SLOTS // WCAP, attend, 0)

    dn = lax.dot_general(
        dpacked_ref[...], wqkv_ref[...], NT, preferred_element_type=F32
    ).astype(BF)
    dn_ref[...] = dn
    gain_row = jnp.sum(dn.astype(F32) * unit_ref[...], axis=0, keepdims=True)

    def halves(value, start):
        own_ref[:, pl.ds(start, value.shape[1])] = value[:384].astype(BF)
        snd_ref[:, pl.ds(start, value.shape[1])] = value[384:].astype(BF)

    place = iota((D, D), 1) == order(me_ref, 0)
    turned = lax.dot_general(
        one_hot(place), normed_ref[...], NT, preferred_element_type=F32
    ).astype(BF)
    for c in range(2):
        halves(dot(turned, dpacked_ref[:, c * D : (c + 1) * D]), c * D)
    place = iota((D, D), 1) == order(me_ref, 1)
    hot = one_hot(place)
    turned = lax.dot_general(hot, normed_ref[...], NT, preferred_element_type=F32).astype(BF)
    halves(dot(turned, dpacked_ref[:, 2 * D :]), 2 * D)
    turned = lax.dot_general(hot, mixed_ref[...], NT, preferred_element_type=F32).astype(BF)
    halves(dot(turned, gos_ref[...]), 3 * D)
    gain_col = jnp.sum(jnp.where(place, gain_row, 0.0), axis=1, keepdims=True)
    halves(jnp.broadcast_to(gain_col, (D, 128)), 4 * D)


def back_body(xs_ref, gos_ref, mixed_ref, dn_ref, win_ref, gain_ref, wout_ref, own_ref, ret_ref, cat_ref):
    gain = gain_ref[...]
    projected = dot(mixed_ref[...], wout_ref[...])
    cat_ref[:, :D] = (xs_ref[...].astype(F32) + projected).astype(BF)
    for w in range(4):
        at = slice(w * WCAP, (w + 1) * WCAP)
        unit, inv_std = normalised(xs_ref[at, :].astype(F32))
        dunit = dn_ref[at, :].astype(F32) * gain
        dcentre = inv_std * (
            dunit
            - jnp.mean(dunit, axis=-1, keepdims=True)
            - unit * jnp.mean(dunit * unit, axis=-1, keepdims=True)
        )
        cat_ref[at, D:] = (gos_ref[at, :].astype(F32) + dcentre).astype(BF)
    back = one_hot(iota((480, SLOTS), 0) == win_ref[...])
    own_ref[...] = dot(back[:ROWS], cat_ref[...]).astype(BF)
    ret_ref[...] = dot(back[ROWS:], cat_ref[...]).astype(BF).reshape(7, 32, WIDE)


def join_body(own_ref, dx_ref, dy_ref, dz_ref, send_ref, out_ref, grad_ref):
    arrived = (
        dz_ref[0], dy_ref[0], dy_ref[1], dx_ref[0], dx_ref[1], dx_ref[2], dx_ref[3],
    )
    total = own_ref[...].astype(F32)
    for k, block in enumerate(arrived):
        total += dot(one_hot(iota((ROWS, 32), 0) == send_ref[0, k : k + 1, :]), block)
    out_ref[...] = total[:, :D].astype(BF)
    grad_ref[...] = total[:, D:].astype(BF)


def sum1_body(own_ref, got_ref, *outs):
    for i in range(8):
        at = slice(48 * i, 48 * (i + 1))
        outs[i][...] = (
            own_ref[at, :COLS_A].astype(F32) + got_ref[at, :COLS_A].astype(F32)
        ).astype(BF)
    for i in range(4):
        at = slice(96 * i, 96 * (i + 1))
        outs[8 + i][...] = (
            own_ref[at, COLS_A:].astype(F32) + got_ref[at, COLS_A:].astype(F32)
        ).astype(BF)


def added(refs):
    total = refs[0][...].astype(F32)
    for ref in refs[1:]:
        total += ref[...].astype(F32)
    return total.astype(BF)


def cut(total, parts, rows, padded):
    shape = (parts * padded, total.shape[0])
    j = iota(shape, 0)
    wanted = jnp.where(j % padded < rows, j // padded * rows + j % padded, -1)
    return dot(one_hot(iota(shape, 1) == wanted), total)


def sum2_body(*refs):
    ins, outs = refs[:12], refs[12:]
    a = cut(added(ins[:8]), 4, 12, 16)
    for i in range(4):
        outs[i][...] = a[16 * i : 16 * (i + 1)].astype(BF)
    b = cut(added(ins[8:]), 8, 12, 16)
    for i in range(8):
        outs[4 + i][...] = b[16 * i : 16 * (i + 1)].astype(BF)


def sum3_body(*refs):
    ins, outs = refs[:12], refs[12:]
    a = cut(added(ins[:4]), 4, 3, 8)
    b = cut(added(ins[4:]), 4, 3, 8)
    for i in range(4):
        outs[i][:, :COLS_A] = a[8 * i : 8 * (i + 1)].astype(BF)
        outs[i][:, COLS_A:] = b[8 * i : 8 * (i + 1)].astype(BF)


def sum4_body(*refs):
    ins, (qkv_ref, out_ref, gain_ref) = refs[:4], refs[4:]
    total = ins[0][...].astype(F32)
    for ref in ins[1:]:
        total += ref[...].astype(F32)
    qkv_ref[...] = total[:3, : 3 * D]
    out_ref[...] = total[:3, 3 * D : 4 * D]
    gain_ref[...] = total[:3, 4 * D :]


def call(body, shapes, *args, scratch=(), smem=()):
    return pl.pallas_call(
        body,
        out_shape=[jax.ShapeDtypeStruct(shape, dtype) for shape, dtype in shapes],
        in_specs=[
            pl.BlockSpec(memory_space=pltpu.SMEM) if i in smem else VMEM for i in range(len(args))
        ],
        out_specs=[VMEM] * len(shapes),
        scratch_shapes=list(scratch),
        compiler_params=PARAMS,
    )(*args)


def on_device(tokens, norm_gain, w_qkv, w_out, send_rows, window_rows, grad_out):
    gain = norm_gain.reshape(1, D)
    me = jnp.stack([lax.axis_index(a) for a in AXES]).astype(jnp.int32)
    (blocks,) = call(pack_body, [((7, 32, WIDE), BF)], tokens, grad_out, send_rows)
    from_x = passed_along(blocks[3:7], "gx", 1)
    from_y = passed_along(jnp.stack([blocks[1], blocks[2], from_x[2], from_x[3]]), "gy", 1)
    from_z = passed_along(jnp.stack([blocks[0], from_y[1], from_x[1], from_y[3]]), "gz", 1)

    half = (384, COLS)
    slot = (SLOTS, D)
    own, sent, xs, gos, mixed, dn = call(
        main_body,
        [(half, BF), (half, BF), (slot, BF), (slot, BF), (slot, BF), (slot, BF)],
        me, tokens, grad_out, from_x, from_y, from_z, window_rows, gain, w_qkv, w_out,
        scratch=[
            pltpu.VMEM((SLOTS, WIDE), BF),
            pltpu.VMEM(slot, BF),
            pltpu.VMEM(slot, F32),
            pltpu.VMEM((SLOTS, 3 * D), BF),
            pltpu.VMEM(slot, BF),
            pltpu.VMEM((SLOTS, 3 * D), BF),
        ],
        smem=(0,),
    )

    got = crossed(sent, "gz", 1)
    parts = call(sum1_body, [((48, COLS_A), BF)] * 8 + [((96, COLS_B), BF)] * 4, own, got)
    a = [parts[0]] + [crossed(parts[i], "gx", i) for i in range(1, 8)]
    b = [parts[8]] + [crossed(parts[8 + i], "gy", i) for i in range(1, 4)]
    parts = call(sum2_body, [((16, COLS_A), BF)] * 4 + [((16, COLS_B), BF)] * 8, *a, *b)
    a = [parts[0]] + [crossed(parts[i], "gy", i) for i in range(1, 4)]
    b = [parts[4]] + [crossed(parts[4 + i], "gx", i) for i in range(1, 8)]
    parts = call(sum3_body, [((8, COLS), BF)] * 4, *a, *b)
    c = [parts[0]] + [crossed(parts[i], "gz", 2 * i) for i in range(1, 4)]
    grad_qkv, grad_proj, gain_rows = call(
        sum4_body, [((3, 3 * D), F32), ((3, D), F32), ((3, 128), F32)], *c
    )

    kept, back = call(
        back_body, [((ROWS, WIDE), BF), ((7, 32, WIDE), BF)],
        xs, gos, mixed, dn, window_rows, gain, w_out,
        scratch=[pltpu.VMEM((SLOTS, WIDE), BF)],
    )
    down_z = passed_along(jnp.stack([back[0], back[2], back[4], back[6]]), "gz", -1)
    down_y = passed_along(jnp.stack([back[1], down_z[1], back[5], down_z[3]]), "gy", -1)
    down_x = passed_along(jnp.stack([back[3], down_z[2], down_y[2], down_y[3]]), "gx", -1)
    block_out, grad_tokens = call(
        join_body, [((ROWS, D), BF), ((ROWS, D), BF)], kept, down_x, down_y, down_z, send_rows
    )
    return (block_out, grad_tokens, gain_rows[:, 0], grad_qkv, grad_proj)


def solution(mesh):
    spread = P(AXES, None)
    in_specs = (spread, P(), P(), P(), P(AXES, None, None), spread, spread)
    out_specs = (spread, spread, P(AXES), spread, spread)
    return jax.shard_map(
        on_device, mesh=mesh, in_specs=in_specs, out_specs=out_specs, check_vma=False
    )
```

time: 555 us -> 186 us (0.34)
  waiting for transfers between devices: 230 us -> 37.6 us
  blocking collectives: 101 us -> 0 us
  local copies, waits for them, and re-layouts: 101 us -> 11.5 us
  starting transfers between devices: 28.4 us -> 83 us
  Pallas kernels: 0 us -> 49.5 us
  matrix products: 43.8 us -> 0 us
  other arithmetic: 29.7 us -> 0.84 us
  between operations: 14.7 us -> 1.04 us
    unnamed x2 -> x0, waiting for transfers between devices: 196 us -> none
    unnamed x1 -> x0, blocking collectives: 101 us -> none
    ppermute x0 -> x24, starting transfers between devices: none -> 66.8 us  [crossed(): lax.ppermute(value, axis, [(source, source ^ mask) for source in range(co...]
    pallas_call x0 -> x8, Pallas kernels: none -> 49.5 us  [call(): pl.pallas_call(body, out_shape=[jax.ShapeDtypeStruct(shape, dtype) for sh...]
    dot_general x12 -> x0, matrix products: 43.8 us -> none  [the longest x1 6.85 us: attend_back(): jnp.einsum('whqk,wkhd->wqhd', dscaled, keys, preferred_element_type=jnp.f...]
    gather x8 -> x0, local copies, waits for them, and re-layouts: 34.1 us -> none  [gather_rows(): taken = jnp.take(table, safe, axis=0)]
    unnamed x58 -> x63, local copies, waits for them, and re-layouts: 25.9 us -> 6.36 us
    ppermute x0 -> x24, waiting for transfers between devices: none -> 17.9 us  [crossed(): lax.ppermute(value, axis, [(source, source ^ mask) for source in range(co...]
  transfers between devices with their start and end apart: 13 -> 30, of which waited for: 7 -> 10; matrix products, arithmetic and copies ran while one was open for 11% -> 2% of each run, Pallas kernels for 0% -> 10%
where the time goes in v1:
time: 186 us; the launch traced here: 183 us
  starting transfers between devices  83 us (45%)
  Pallas kernels  49.5 us (27%)
  waiting for transfers between devices  37.6 us (20%)
  local copies, waits for them, and re-layouts  11.5 us (6%)
    ppermute x24, starting transfers between devices, crossed(): lax.ppermute(value, axis, [(source, source ^ mask) for source in range(co...  66.8 us
    pallas_call x8, Pallas kernels, call(): pl.pallas_call(body, out_shape=[jax.ShapeDtypeStruct(shape, dtype) for sh...  49.5 us
    ppermute x6, waiting for transfers between devices, passed_along(): lax.ppermute(value, axis, [(source, source + steps) for source in range(i...  19.7 us
    ppermute x24, waiting for transfers between devices, crossed(): lax.ppermute(value, axis, [(source, source ^ mask) for source in range(co...  17.9 us
    ppermute x6, starting transfers between devices, passed_along(): lax.ppermute(value, axis, [(source, source + steps) for source in range(i...  16.2 us
    unnamed x63, local copies, waits for them, and re-layouts  6.36 us
  transfers between devices with their start and end apart: 30, of which 10 were waited for; matrix products, arithmetic and copies ran while one was open for 2% of the time, Pallas kernels for 10%

profile of v1, /device:TPU:10, one launch (start us, length us, event | category | flops | bytes accessed | tf_op | source)
XLA Modules:
  0.0 183.5 jit_solution(1193467297333795665)
XLA Ops:
  0.6 1.3 copy.14.send_ref
  1.9 2.4 %shard_map.110 = bf16[7,32,1536]{2,1,0:T(8,128)(2,1)} custom-call(bf16[256,768]{1,0:T(8,128)(2,1)} %tok_ref.3, bf16[256,768]{1,0:T(8,128)(2,1)} %go_ref.3, s32[1,7,32]{2,1,0:T(8,128)} %copy.14.send_ref), custom_call_target="tpu_custom_call" | custom-call | tf_op jit(solution)/shard_map/pallas_call | solution.py:284
  4.3 1.1 slice.82
  5.4 3.8 %collective-permute-start = (bf16[4,32,1536]{2,1,0:T(8,128)(2,1)S(1)}, bf16[4,32,1536]{2,1,0:T(8,128)(2,1)S(1)}, u32[]{:S(2)}, u32[]{:S(2)}) collective-permute-start(bf16[4,32,1536]{2,1,0:T(8,128)(2,1)S(1)} %slice.82), channel_id=1, source_target_pairs={{0,32},{32,64},{64,96},{96,128},{128,160},{160,192},{192,224},{1,3... | collective-permute-start | bytes 1179656 | tf_op jit(solution)/shard_map/ppermute | solution.py:51
  9.2 0.9 slice.83
  10.2 8.9 %collective-permute-done.fx_ref = bf16[4,32,1536]{2,1,0:T(8,128)(2,1)S(1)} collective-permute-done((bf16[4,32,1536]{2,1,0:T(8,128)(2,1)S(1)}, bf16[4,32,1536]{2,1,0:T(8,128)(2,1)S(1)}, u32[]{:S(2)}, u32[]{:S(2)}) %collective-permute-start) | collective-permute-done | bytes 393248 | tf_op jit(solution)/shard_map/ppermute | solution.py:51
  19.1 3.5 %collective-permute-start.1 = (bf16[4,32,1536]{2,1,0:T(8,128)(2,1)S(1)}, bf16[4,32,1536]{2,1,0:T(8,128)(2,1)S(1)}, u32[]{:S(2)}, u32[]{:S(2)}) collective-permute-start(bf16[4,32,1536]{2,1,0:T(8,128)(2,1)S(1)} %pad_maximum_fusion), channel_id=1, source_target_pairs={{0,8},{8,16},{16,24},{1,9},{9,17},{17,25},{2,10},{10,18},{18,26},{... | collective-permute-start | bytes 1179656 | tf_op jit(solution)/shard_map/ppermute | solution.py:51
  22.6 8.4 %collective-permute-done.1.fy_ref = bf16[4,32,1536]{2,1,0:T(8,128)(2,1)S(1)} collective-permute-done((bf16[4,32,1536]{2,1,0:T(8,128)(2,1)S(1)}, bf16[4,32,1536]{2,1,0:T(8,128)(2,1)S(1)}, u32[]{:S(2)}, u32[]{:S(2)}) %collective-permute-start.1) | collective-permute-done | bytes 393248 | tf_op jit(solution)/shard_map/ppermute | solution.py:51
  31.0 0.1 pad_maximum_fusion.1
  31.1 1.3 collective-permute-start.2
  32.4 0.6 reshape.13.gain_ref
  33.0 0.6 pad_add_fusion.me_ref
  33.6 0.1 collective-permute-done.2.fz_ref
  33.7 0.8 copy-done.5
  34.5 27.2 %shard_map.111 = (bf16[384,3200]{1,0:T(8,128)(2,1)}, bf16[384,3200]{1,0:T(8,128)(2,1)}, bf16[512,768]{1,0:T(8,128)(2,1)}, bf16[512,768]{1,0:T(8,128)(2,1)}, bf16...) custom-call(s32[3]{0:T(128)} %pad_add_fusion.me_ref, bf16[256,768]{1,0:T(8,128)(2,1)} %tok_ref.3, bf16[256,768]{1,0:T(8,128)(2,1)} %go_ref.3, ...), custom_call_target="tpu_custom_call" | custom-call | tf_op jit(solution)/shard_map/pallas_call | solution.py:284
  61.7 7.4 %collective-permute-start.6 = (bf16[384,3200]{1,0:T(8,128)(2,1)}, bf16[384,3200]{1,0:T(8,128)(2,1)S(1)}, u32[]{:S(2)}, u32[]{:S(2)}) collective-permute-start(bf16[384,3200]{1,0:T(8,128)(2,1)} %get-tuple-element.55), channel_id=1, source_target_pairs={{0,1},{1,0},{2,3},{3,2},{4,5},{5,4},{6,7},{7,6},{8,9},{9,8},{10,11... | collective-permute-start | bytes 7372808 | tf_op jit(solution)/shard_map/ppermute | solution.py:56
  69.1 5.7 %shard_map.112 = (bf16[256,1536]{1,0:T(8,128)(2,1)}, bf16[7,32,1536]{2,1,0:T(8,128)(2,1)}) custom-call(bf16[512,768]{1,0:T(8,128)(2,1)} %get-tuple-element.46.xs_ref, bf16[512,768]{1,0:T(8,128)(2,1)} %get-tuple-element.47.gos_ref, bf16[512,768]{1,0:T(8,128)(2,1)} %get-tuple-element.48.mixed_ref, bf16[512,768]{1,0:T(8,128)(2,1)} %get-tuple-element.49.dn_ref, ...), custom_call_target="tpu_custom_call" | custom-call | tf_op jit(solution)/shard_map/pallas_call | solution.py:284
  74.7 1.2 fusion
  76.0 0.1 pad_maximum_fusion.2
  76.0 1.3 collective-permute-start.3
  77.3 2.3 %collective-permute-done.3.dz_ref = bf16[4,32,1536]{2,1,0:T(8,128)(2,1)S(1)} collective-permute-done((bf16[4,32,1536]{2,1,0:T(8,128)(2,1)S(1)}, bf16[4,32,1536]{2,1,0:T(8,128)(2,1)S(1)}, u32[]{:S(2)}, u32[]{:S(2)}) %collective-permute-start.3) | collective-permute-done | bytes 393248 | tf_op jit(solution)/shard_map/ppermute | solution.py:51
  79.7 0.1 pad_maximum_fusion.3
  79.7 1.9 %collective-permute-start.4 = (bf16[4,32,1536]{2,1,0:T(8,128)(2,1)S(1)}, bf16[4,32,1536]{2,1,0:T(8,128)(2,1)S(1)}, u32[]{:S(2)}, u32[]{:S(2)}) collective-permute-start(bf16[4,32,1536]{2,1,0:T(8,128)(2,1)S(1)} %pad_maximum_fusion.3), channel_id=1, source_target_pairs={{8,0},{16,8},{24,16},{9,1},{17,9},{25,17},{10,2},{18,10},{26,18},{... | collective-permute-start | bytes 1179656 | tf_op jit(solution)/shard_map/ppermute | solution.py:51
  81.7 1.4 copy-done
  83.1 3.9 %shard_map.114 = (bf16[48,1536]{1,0:T(8,128)(2,1)}, bf16[48,1536]{1,0:T(8,128)(2,1)}, bf16[48,1536]{1,0:T(8,128)(2,1)}, bf16[48,1536]{1,0:T(8,128)(2,1)}, bf16[4...) custom-call(bf16[384,3200]{1,0:T(8,128)(2,1)} %get-tuple-element.54., ...), custom_call_target="tpu_custom_call" | custom-call | tf_op jit(solution)/shard_map/pallas_call | solution.py:284
  87.0 5.3 %collective-permute-start.7 = (bf16[48,1536]{1,0:T(8,128)(2,1)}, bf16[48,1536]{1,0:T(8,128)(2,1)S(1)}, u32[]{:S(2)}, u32[]{:S(2)}) collective-permute-start(bf16[48,1536]{1,0:T(8,128)(2,1)} %get-tuple-element.57), channel_id=1, source_target_pairs={{0,32},{32,0},{64,96},{96,64},{128,160},{160,128},{192,224},{224,1... | collective-permute-start | bytes 442376 | tf_op jit(solution)/shard_map/ppermute | solution.py:56
  92.3 1.6 collective-permute-start.9
  93.9 2.1 %collective-permute-start.10 = (bf16[48,1536]{1,0:T(8,128)(2,1)}, bf16[48,1536]{1,0:T(8,128)(2,1)S(1)}, u32[]{:S(2)}, u32[]{:S(2)}) collective-permute-start(bf16[48,1536]{1,0:T(8,128)(2,1)} %get-tuple-element.60), channel_id=1, source_target_pairs={{0,128},{32,160},{64,192},{96,224},{128,0},{160,32},{192,64},{224,... | collective-permute-start | bytes 442376 | tf_op jit(solution)/shard_map/ppermute | solution.py:56
  96.0 2.9 %collective-permute-start.11 = (bf16[48,1536]{1,0:T(8,128)(2,1)}, bf16[48,1536]{1,0:T(8,128)(2,1)S(1)}, u32[]{:S(2)}, u32[]{:S(2)}) collective-permute-start(bf16[48,1536]{1,0:T(8,128)(2,1)} %get-tuple-element.61), channel_id=1, source_target_pairs={{0,160},{32,128},{64,224},{96,192},{128,32},{160,0},{192,96},{224,... | collective-permute-start | bytes 442376 | tf_op jit(solution)/shard_map/ppermute | solution.py:56
  98.9 1.5 collective-permute-start.12
  100.4 0.0 collective-permute-done.8.refs_2_
  100.4 3.5 %collective-permute-start.15 = (bf16[96,1664]{1,0:T(8,128)(2,1)}, bf16[96,1664]{1,0:T(8,128)(2,1)S(1)}, u32[]{:S(2)}, u32[]{:S(2)}) collective-permute-start(bf16[96,1664]{1,0:T(8,128)(2,1)} %get-tuple-element.66), channel_id=1, source_target_pairs={{0,16},{8,24},{16,0},{24,8},{1,17},{9,25},{17,1},{25,9},{2,18},{10... | collective-permute-start | bytes 958472 | tf_op jit(solution)/shard_map/ppermute | solution.py:56
  103.8 0.4 collective-permute-start.16
  104.3 4.3 %collective-permute-start.5 = (bf16[4,32,1536]{2,1,0:T(8,128)(2,1)S(1)}, bf16[4,32,1536]{2,1,0:T(8,128)(2,1)S(1)}, u32[]{:S(2)}, u32[]{:S(2)}) collective-permute-start(bf16[4,32,1536]{2,1,0:T(8,128)(2,1)S(1)} %pad_maximum_fusion.4), channel_id=1, source_target_pairs={{32,0},{64,32},{96,64},{128,96},{160,128},{192,160},{224,192},{33,... | collective-permute-start | bytes 1179656 | tf_op jit(solution)/shard_map/ppermute | solution.py:51
  108.7 0.7 collective-permute-start.13
  109.4 8.8 %collective-permute-done.13.refs_7_ = bf16[48,1536]{1,0:T(8,128)(2,1)S(1)} collective-permute-done((bf16[48,1536]{1,0:T(8,128)(2,1)}, bf16[48,1536]{1,0:T(8,128)(2,1)S(1)}, u32[]{:S(2)}, u32[]{:S(2)}) %collective-permute-start.13) | collective-permute-done | bytes 147488 | tf_op jit(solution)/shard_map/ppermute | solution.py:56
  118.3 0.6 copy-done.16
  118.9 0.1 copy-done.7
  119.0 0.1 copy-done.8
  119.1 0.1 copy-done.9
  119.2 3.0 %shard_map.115 = (bf16[16,1536]{1,0:T(8,128)(2,1)}, bf16[16,1536]{1,0:T(8,128)(2,1)}, bf16[16,1536]{1,0:T(8,128)(2,1)}, bf16[16,1536]{1,0:T(8,128)(2,1)}, bf16[1...) custom-call(bf16[48,1536]{1,0:T(8,128)(2,1)} %get-tuple-element.56.r, ...), custom_call_target="tpu_custom_call" | custom-call | tf_op jit(solution)/shard_map/pallas_call | solution.py:284
  122.2 0.7 collective-permute-start.17
  122.9 2.3 %collective-permute-start.18 = (bf16[16,1536]{1,0:T(8,128)(2,1)}, bf16[16,1536]{1,0:T(8,128)(2,1)S(1)}, u32[]{:S(2)}, u32[]{:S(2)}) collective-permute-start(bf16[16,1536]{1,0:T(8,128)(2,1)} %get-tuple-element.70), channel_id=1, source_target_pairs={{0,16},{8,24},{16,0},{24,8},{1,17},{9,25},{17,1},{25,9},{2,18},{10... | collective-permute-start | bytes 147464 | tf_op jit(solution)/shard_map/ppermute | solution.py:56
  125.1 4.0 %collective-permute-start.20 = (bf16[16,1664]{1,0:T(8,128)(2,1)}, bf16[16,1664]{1,0:T(8,128)(2,1)S(1)}, u32[]{:S(2)}, u32[]{:S(2)}) collective-permute-start(bf16[16,1664]{1,0:T(8,128)(2,1)} %get-tuple-element.73), channel_id=1, source_target_pairs={{0,32},{32,0},{64,96},{96,64},{128,160},{160,128},{192,224},{224,1... | collective-permute-start | bytes 159752 | tf_op jit(solution)/shard_map/ppermute | solution.py:56
  129.1 1.5 collective-permute-start.22
  130.6 0.8 collective-permute-start.19
  131.4 3.5 %collective-permute-done.19.refs_3_ = bf16[16,1536]{1,0:T(8,128)(2,1)S(1)} collective-permute-done((bf16[16,1536]{1,0:T(8,128)(2,1)}, bf16[16,1536]{1,0:T(8,128)(2,1)S(1)}, u32[]{:S(2)}, u32[]{:S(2)}) %collective-permute-start.19) | collective-permute-done | bytes 49184 | tf_op jit(solution)/shard_map/ppermute | solution.py:56
  134.9 1.3 collective-permute-start.23
  136.1 4.1 %collective-permute-start.24 = (bf16[16,1664]{1,0:T(8,128)(2,1)}, bf16[16,1664]{1,0:T(8,128)(2,1)S(1)}, u32[]{:S(2)}, u32[]{:S(2)}) collective-permute-start(bf16[16,1664]{1,0:T(8,128)(2,1)} %get-tuple-element.77), channel_id=1, source_target_pairs={{0,160},{32,128},{64,224},{96,192},{128,32},{160,0},{192,96},{224,... | collective-permute-start | bytes 159752 | tf_op jit(solution)/shard_map/ppermute | solution.py:56
  140.3 1.0 collective-permute-start.26
  141.3 1.5 collective-permute-done.24.refs_9_
  142.9 1.7 collective-permute-done.25.refs_10_
  144.6 1.0 collective-permute-done.26.refs_11_
  145.7 0.6 copy-done.23
  146.3 2.0 %shard_map.116 = (bf16[8,3200]{1,0:T(8,128)(2,1)}, bf16[8,3200]{1,0:T(8,128)(2,1)}, bf16[8,3200]{1,0:T(8,128)(2,1)}, bf16[8,3200]{1,0:T(8,128)(2,1)}) custom-call(bf16[16,1536]{1,0:T(8,128)(2,1)} %get-tuple-element.68.refs_0_, bf16[16,1536]{1,0:T(8,128)(2,1)} %copy-done.27, bf16[16,1536]{1,0:T(8,128)(2,1)} %copy-done.28, bf16[16,1536]{1,0:T(8,128)(2,1)} %copy-done.29, ...), custom_call_target="tpu_custom_call" | custom-call | tf_op jit(solution)/shard_map/pallas_call | solution.py:284
  148.3 19.7 %collective-permute-start.27 = (bf16[8,3200]{1,0:T(8,128)(2,1)}, bf16[8,3200]{1,0:T(8,128)(2,1)S(1)}, u32[]{:S(2)}, u32[]{:S(2)}) collective-permute-start(bf16[8,3200]{1,0:T(8,128)(2,1)} %get-tuple-element.81), channel_id=1, source_target_pairs={{0,2},{1,3},{2,0},{3,1},{4,6},{5,7},{6,4},{7,5},{8,10},{9,11},{10,... | collective-permute-start | bytes 153608 | tf_op jit(solution)/shard_map/ppermute | solution.py:56
  168.0 5.6 %collective-permute-start.28 = (bf16[8,3200]{1,0:T(8,128)(2,1)}, bf16[8,3200]{1,0:T(8,128)(2,1)S(1)}, u32[]{:S(2)}, u32[]{:S(2)}) collective-permute-start(bf16[8,3200]{1,0:T(8,128)(2,1)} %get-tuple-element.82), channel_id=1, source_target_pairs={{0,4},{1,5},{2,6},{3,7},{4,0},{5,1},{6,2},{7,3},{8,12},{9,13},{10,... | collective-permute-start | bytes 153608 | tf_op jit(solution)/shard_map/ppermute | solution.py:56
  173.6 0.5 collective-permute-start.29
  174.1 0.7 copy-done.6
  174.8 3.8 %shard_map.113 = (bf16[256,768]{1,0:T(8,128)(2,1)}, bf16[256,768]{1,0:T(8,128)(2,1)}) custom-call(bf16[256,1536]{1,0:T(8,128)(2,1)} %get-tuple-element.50.own_ref, bf16[4,32,1536]{2,1,0:T(8,128)(2,1)} %copy-done.6, bf16[4,32,1536]{2,1,0:T(8,128)(2,1)} %copy-done.4, bf16[4,32,1536]{2,1,0:T(8,128)(2,1)} %copy-done.2, s32[1,7,32]{2,1,0:T(8,128)} %copy.14.send_ref), custom_call_target="tpu_custom_call" | custom-call | tf_op jit(solution)/shard_map/pallas_call | solution.py:284
  178.7 1.4 collective-permute-done.29.refs_3_
  180.1 0.6 copy-done.26
  180.7 1.5 shard_map.117
  182.2 1.3 slice_reduce_fusion
  (85 shorter events, 0.3 us)
Async XLA Ops:
  1.9 30.5 %copy-start.30 = (f32[768]{0:T(1024)S(1)}, f32[768]{0:T(1024)}, u32[]{:S(2)}) copy-start(f32[768]{0:T(1024)} %param.8) | copy-start | bytes 9220
  4.3 26.7 %slice-start = ((bf16[7,32,1536]{2,1,0:T(8,128)(2,1)}), bf16[1,32,1536]{2,1,0:T(8,128)(2,1)S(1)}, s32[]{:S(2)}) async-start(bf16[7,32,1536]{2,1,0:T(8,128)(2,1)} %shard_map.110), calls=%async_computation | async-start | bytes 196608 | tf_op jit(solution)/shard_map/slice | solution.py:302
  5.4 13.6 %collective-permute-start = (bf16[4,32,1536]{2,1,0:T(8,128)(2,1)S(1)}, bf16[4,32,1536]{2,1,0:T(8,128)(2,1)S(1)}, u32[]{:S(2)}, u32[]{:S(2)}) collective-permute-start(bf16[4,32,1536]{2,1,0:T(8,128)(2,1)S(1)} %slice.82), channel_id=1, source_target_pairs={{0,32},{32,64},{64,96},{96,128},{128,160},{160,192},{192,224},{1,3... | collective-permute-start | bytes 1179656 | tf_op jit(solution)/shard_map/ppermute | solution.py:51
  19.0 14.7 %copy-start.1 = (bf16[4,32,1536]{2,1,0:T(8,128)(2,1)}, bf16[4,32,1536]{2,1,0:T(8,128)(2,1)S(1)}, u32[]{:S(2)}) copy-start(bf16[4,32,1536]{2,1,0:T(8,128)(2,1)S(1)} %collective-permute-done.fx_ref) | copy-start | bytes 1179652
  19.1 11.9 %collective-permute-start.1 = (bf16[4,32,1536]{2,1,0:T(8,128)(2,1)S(1)}, bf16[4,32,1536]{2,1,0:T(8,128)(2,1)S(1)}, u32[]{:S(2)}, u32[]{:S(2)}) collective-permute-start(bf16[4,32,1536]{2,1,0:T(8,128)(2,1)S(1)} %pad_maximum_fusion), channel_id=1, source_target_pairs={{0,8},{8,16},{16,24},{1,9},{9,17},{17,25},{2,10},{10,18},{18,26},{... | collective-permute-start | bytes 1179656 | tf_op jit(solution)/shard_map/ppermute | solution.py:51
  31.0 2.7 %copy-start.3 = (bf16[4,32,1536]{2,1,0:T(8,128)(2,1)}, bf16[4,32,1536]{2,1,0:T(8,128)(2,1)S(1)}, u32[]{:S(2)}) copy-start(bf16[4,32,1536]{2,1,0:T(8,128)(2,1)S(1)} %collective-permute-done.1.fy_ref) | copy-start | bytes 1179652
  31.1 2.6 %collective-permute-start.2 = (bf16[4,32,1536]{2,1,0:T(8,128)(2,1)S(1)}, bf16[4,32,1536]{2,1,0:T(8,128)(2,1)S(1)}, u32[]{:S(2)}, u32[]{:S(2)}) collective-permute-start(bf16[4,32,1536]{2,1,0:T(8,128)(2,1)S(1)} %pad_maximum_fusion.1), channel_id=1, source_target_pairs={{0,1},{1,2},{2,3},{3,4},{4,5},{5,6},{6,7},{8,9},{9,10},{10,11},{11... | collective-permute-start | bytes 1179656 | tf_op jit(solution)/shard_map/ppermute | solution.py:51
  33.7 0.8 copy-start.5
  61.7 20.0 %collective-permute-start.6 = (bf16[384,3200]{1,0:T(8,128)(2,1)}, bf16[384,3200]{1,0:T(8,128)(2,1)S(1)}, u32[]{:S(2)}, u32[]{:S(2)}) collective-permute-start(bf16[384,3200]{1,0:T(8,128)(2,1)} %get-tuple-element.55), channel_id=1, source_target_pairs={{0,1},{1,0},{2,3},{3,2},{4,5},{5,4},{6,7},{7,6},{8,9},{9,8},{10,11... | collective-permute-start | bytes 7372808 | tf_op jit(solution)/shard_map/ppermute | solution.py:56
  76.0 3.6 %collective-permute-start.3 = (bf16[4,32,1536]{2,1,0:T(8,128)(2,1)S(1)}, bf16[4,32,1536]{2,1,0:T(8,128)(2,1)S(1)}, u32[]{:S(2)}, u32[]{:S(2)}) collective-permute-start(bf16[4,32,1536]{2,1,0:T(8,128)(2,1)S(1)} %pad_maximum_fusion.2), channel_id=1, source_target_pairs={{1,0},{2,1},{3,2},{4,3},{5,4},{6,5},{7,6},{9,8},{10,9},{11,10},{12... | collective-permute-start | bytes 1179656 | tf_op jit(solution)/shard_map/ppermute | solution.py:51
  79.6 7.4 %copy-start.2 = (bf16[4,32,1536]{2,1,0:T(8,128)(2,1)}, bf16[4,32,1536]{2,1,0:T(8,128)(2,1)S(1)}, u32[]{:S(2)}) copy-start(bf16[4,32,1536]{2,1,0:T(8,128)(2,1)S(1)} %collective-permute-done.3.dz_ref) | copy-start | bytes 1179652
  79.7 16.3 %collective-permute-start.4 = (bf16[4,32,1536]{2,1,0:T(8,128)(2,1)S(1)}, bf16[4,32,1536]{2,1,0:T(8,128)(2,1)S(1)}, u32[]{:S(2)}, u32[]{:S(2)}) collective-permute-start(bf16[4,32,1536]{2,1,0:T(8,128)(2,1)S(1)} %pad_maximum_fusion.3), channel_id=1, source_target_pairs={{8,0},{16,8},{24,16},{9,1},{17,9},{25,17},{10,2},{18,10},{26,18},{... | collective-permute-start | bytes 1179656 | tf_op jit(solution)/shard_map/ppermute | solution.py:51
  81.7 1.5 copy-start
  87.0 11.8 %collective-permute-start.7 = (bf16[48,1536]{1,0:T(8,128)(2,1)}, bf16[48,1536]{1,0:T(8,128)(2,1)S(1)}, u32[]{:S(2)}, u32[]{:S(2)}) collective-permute-start(bf16[48,1536]{1,0:T(8,128)(2,1)} %get-tuple-element.57), channel_id=1, source_target_pairs={{0,32},{32,0},{64,96},{96,64},{128,160},{160,128},{192,224},{224,1... | collective-permute-start | bytes 442376 | tf_op jit(solution)/shard_map/ppermute | solution.py:56
  92.3 8.1 %collective-permute-start.8 = (bf16[48,1536]{1,0:T(8,128)(2,1)}, bf16[48,1536]{1,0:T(8,128)(2,1)S(1)}, u32[]{:S(2)}, u32[]{:S(2)}) collective-permute-start(bf16[48,1536]{1,0:T(8,128)(2,1)} %get-tuple-element.58), channel_id=1, source_target_pairs={{0,64},{32,96},{64,0},{96,32},{128,192},{160,224},{192,128},{224,1... | collective-permute-start | bytes 442376 | tf_op jit(solution)/shard_map/ppermute | solution.py:56
  92.3 8.1 %collective-permute-start.9 = (bf16[48,1536]{1,0:T(8,128)(2,1)}, bf16[48,1536]{1,0:T(8,128)(2,1)S(1)}, u32[]{:S(2)}, u32[]{:S(2)}) collective-permute-start(bf16[48,1536]{1,0:T(8,128)(2,1)} %get-tuple-element.59), channel_id=1, source_target_pairs={{0,96},{32,64},{64,32},{96,0},{128,224},{160,192},{192,160},{224,1... | collective-permute-start | bytes 442376 | tf_op jit(solution)/shard_map/ppermute | solution.py:56
  93.9 10.0 %collective-permute-start.10 = (bf16[48,1536]{1,0:T(8,128)(2,1)}, bf16[48,1536]{1,0:T(8,128)(2,1)S(1)}, u32[]{:S(2)}, u32[]{:S(2)}) collective-permute-start(bf16[48,1536]{1,0:T(8,128)(2,1)} %get-tuple-element.60), channel_id=1, source_target_pairs={{0,128},{32,160},{64,192},{96,224},{128,0},{160,32},{192,64},{224,... | collective-permute-start | bytes 442376 | tf_op jit(solution)/shard_map/ppermute | solution.py:56
  96.0 78.1 %copy-start.4 = (bf16[4,32,1536]{2,1,0:T(8,128)(2,1)}, bf16[4,32,1536]{2,1,0:T(8,128)(2,1)S(1)}, u32[]{:S(2)}) copy-start(bf16[4,32,1536]{2,1,0:T(8,128)(2,1)S(1)} %collective-permute-done.4.dy_ref) | copy-start | bytes 1179652
  96.0 8.3 %collective-permute-start.11 = (bf16[48,1536]{1,0:T(8,128)(2,1)}, bf16[48,1536]{1,0:T(8,128)(2,1)S(1)}, u32[]{:S(2)}, u32[]{:S(2)}) collective-permute-start(bf16[48,1536]{1,0:T(8,128)(2,1)} %get-tuple-element.61), channel_id=1, source_target_pairs={{0,160},{32,128},{64,224},{96,192},{128,32},{160,0},{192,96},{224,... | collective-permute-start | bytes 442376 | tf_op jit(solution)/shard_map/ppermute | solution.py:56
  98.9 19.4 %copy-start.10 = (bf16[48,1536]{1,0:T(8,128)(2,1)}, bf16[48,1536]{1,0:T(8,128)(2,1)S(1)}, u32[]{:S(2)}) copy-start(bf16[48,1536]{1,0:T(8,128)(2,1)S(1)} %collective-permute-done.7.refs_1_) | copy-start | bytes 442372
  98.9 9.8 %collective-permute-start.12 = (bf16[48,1536]{1,0:T(8,128)(2,1)}, bf16[48,1536]{1,0:T(8,128)(2,1)S(1)}, u32[]{:S(2)}, u32[]{:S(2)}) collective-permute-start(bf16[48,1536]{1,0:T(8,128)(2,1)} %get-tuple-element.62), channel_id=1, source_target_pairs={{0,192},{32,224},{64,128},{96,160},{128,64},{160,96},{192,0},{224,... | collective-permute-start | bytes 442376 | tf_op jit(solution)/shard_map/ppermute | solution.py:56
  100.4 17.9 %copy-start.11 = (bf16[48,1536]{1,0:T(8,128)(2,1)}, bf16[48,1536]{1,0:T(8,128)(2,1)S(1)}, u32[]{:S(2)}) copy-start(bf16[48,1536]{1,0:T(8,128)(2,1)S(1)} %collective-permute-done.8.refs_2_) | copy-start | bytes 442372
  100.4 17.8 %collective-permute-start.14 = (bf16[96,1664]{1,0:T(8,128)(2,1)}, bf16[96,1664]{1,0:T(8,128)(2,1)S(1)}, u32[]{:S(2)}, u32[]{:S(2)}) collective-permute-start(bf16[96,1664]{1,0:T(8,128)(2,1)} %get-tuple-element.65), channel_id=1, source_target_pairs={{0,8},{8,0},{16,24},{24,16},{1,9},{9,1},{17,25},{25,17},{2,10},{10... | collective-permute-start | bytes 958472 | tf_op jit(solution)/shard_map/ppermute | solution.py:56
  100.4 17.9 %copy-start.12 = (bf16[48,1536]{1,0:T(8,128)(2,1)}, bf16[48,1536]{1,0:T(8,128)(2,1)S(1)}, u32[]{:S(2)}) copy-start(bf16[48,1536]{1,0:T(8,128)(2,1)S(1)} %collective-permute-done.9.refs_3_) | copy-start | bytes 442372
  100.4 17.8 %collective-permute-start.15 = (bf16[96,1664]{1,0:T(8,128)(2,1)}, bf16[96,1664]{1,0:T(8,128)(2,1)S(1)}, u32[]{:S(2)}, u32[]{:S(2)}) collective-permute-start(bf16[96,1664]{1,0:T(8,128)(2,1)} %get-tuple-element.66), channel_id=1, source_target_pairs={{0,16},{8,24},{16,0},{24,8},{1,17},{9,25},{17,1},{25,9},{2,18},{10... | collective-permute-start | bytes 958472 | tf_op jit(solution)/shard_map/ppermute | solution.py:56
  103.8 14.4 %copy-start.13 = (bf16[48,1536]{1,0:T(8,128)(2,1)}, bf16[48,1536]{1,0:T(8,128)(2,1)S(1)}, u32[]{:S(2)}) copy-start(bf16[48,1536]{1,0:T(8,128)(2,1)S(1)} %collective-permute-done.10.refs_4_) | copy-start | bytes 442372
  103.8 14.4 %collective-permute-start.16 = (bf16[96,1664]{1,0:T(8,128)(2,1)}, bf16[96,1664]{1,0:T(8,128)(2,1)S(1)}, u32[]{:S(2)}, u32[]{:S(2)}) collective-permute-start(bf16[96,1664]{1,0:T(8,128)(2,1)} %get-tuple-element.67), channel_id=1, source_target_pairs={{0,24},{8,16},{16,8},{24,0},{1,25},{9,17},{17,9},{25,1},{2,26},{10... | collective-permute-start | bytes 958472 | tf_op jit(solution)/shard_map/ppermute | solution.py:56
  104.3 14.0 %copy-start.14 = (bf16[48,1536]{1,0:T(8,128)(2,1)}, bf16[48,1536]{1,0:T(8,128)(2,1)S(1)}, u32[]{:S(2)}) copy-start(bf16[48,1536]{1,0:T(8,128)(2,1)S(1)} %collective-permute-done.11.refs_5_) | copy-start | bytes 442372
  104.3 69.8 %collective-permute-start.5 = (bf16[4,32,1536]{2,1,0:T(8,128)(2,1)S(1)}, bf16[4,32,1536]{2,1,0:T(8,128)(2,1)S(1)}, u32[]{:S(2)}, u32[]{:S(2)}) collective-permute-start(bf16[4,32,1536]{2,1,0:T(8,128)(2,1)S(1)} %pad_maximum_fusion.4), channel_id=1, source_target_pairs={{32,0},{64,32},{96,64},{128,96},{160,128},{192,160},{224,192},{33,... | collective-permute-start | bytes 1179656 | tf_op jit(solution)/shard_map/ppermute | solution.py:51
  108.7 9.6 %copy-start.15 = (bf16[48,1536]{1,0:T(8,128)(2,1)}, bf16[48,1536]{1,0:T(8,128)(2,1)S(1)}, u32[]{:S(2)}) copy-start(bf16[48,1536]{1,0:T(8,128)(2,1)S(1)} %collective-permute-done.12.refs_6_) | copy-start | bytes 442372
  108.7 9.5 %collective-permute-start.13 = (bf16[48,1536]{1,0:T(8,128)(2,1)}, bf16[48,1536]{1,0:T(8,128)(2,1)S(1)}, u32[]{:S(2)}, u32[]{:S(2)}) collective-permute-start(bf16[48,1536]{1,0:T(8,128)(2,1)} %get-tuple-element.63), channel_id=1, source_target_pairs={{0,224},{32,192},{64,160},{96,128},{128,96},{160,64},{192,32},{224... | collective-permute-start | bytes 442376 | tf_op jit(solution)/shard_map/ppermute | solution.py:56
  118.2 0.7 copy-start.16
  118.2 0.8 copy-start.7
  118.2 0.9 copy-start.8
  118.2 1.0 copy-start.9
  122.2 6.9 %collective-permute-start.17 = (bf16[16,1536]{1,0:T(8,128)(2,1)}, bf16[16,1536]{1,0:T(8,128)(2,1)S(1)}, u32[]{:S(2)}, u32[]{:S(2)}) collective-permute-start(bf16[16,1536]{1,0:T(8,128)(2,1)} %get-tuple-element.69), channel_id=1, source_target_pairs={{0,8},{8,0},{16,24},{24,16},{1,9},{9,1},{17,25},{25,17},{2,10},{10... | collective-permute-start | bytes 147464 | tf_op jit(solution)/shard_map/ppermute | solution.py:56
  122.9 7.7 %collective-permute-start.18 = (bf16[16,1536]{1,0:T(8,128)(2,1)}, bf16[16,1536]{1,0:T(8,128)(2,1)S(1)}, u32[]{:S(2)}, u32[]{:S(2)}) collective-permute-start(bf16[16,1536]{1,0:T(8,128)(2,1)} %get-tuple-element.70), channel_id=1, source_target_pairs={{0,16},{8,24},{16,0},{24,8},{1,17},{9,25},{17,1},{25,9},{2,18},{10... | collective-permute-start | bytes 147464 | tf_op jit(solution)/shard_map/ppermute | solution.py:56
  125.1 11.0 %collective-permute-start.20 = (bf16[16,1664]{1,0:T(8,128)(2,1)}, bf16[16,1664]{1,0:T(8,128)(2,1)S(1)}, u32[]{:S(2)}, u32[]{:S(2)}) collective-permute-start(bf16[16,1664]{1,0:T(8,128)(2,1)} %get-tuple-element.73), channel_id=1, source_target_pairs={{0,32},{32,0},{64,96},{96,64},{128,160},{160,128},{192,224},{224,1... | collective-permute-start | bytes 159752 | tf_op jit(solution)/shard_map/ppermute | solution.py:56
  129.1 11.2 %collective-permute-start.21 = (bf16[16,1664]{1,0:T(8,128)(2,1)}, bf16[16,1664]{1,0:T(8,128)(2,1)S(1)}, u32[]{:S(2)}, u32[]{:S(2)}) collective-permute-start(bf16[16,1664]{1,0:T(8,128)(2,1)} %get-tuple-element.74), channel_id=1, source_target_pairs={{0,64},{32,96},{64,0},{96,32},{128,192},{160,224},{192,128},{224,1... | collective-permute-start | bytes 159752 | tf_op jit(solution)/shard_map/ppermute | solution.py:56
  129.1 16.6 %copy-start.27 = (bf16[16,1536]{1,0:T(8,128)(2,1)}, bf16[16,1536]{1,0:T(8,128)(2,1)S(1)}, u32[]{:S(2)}) copy-start(bf16[16,1536]{1,0:T(8,128)(2,1)S(1)} %collective-permute-done.17.refs_1_) | copy-start | bytes 147460
  129.1 11.2 %collective-permute-start.22 = (bf16[16,1664]{1,0:T(8,128)(2,1)}, bf16[16,1664]{1,0:T(8,128)(2,1)S(1)}, u32[]{:S(2)}, u32[]{:S(2)}) collective-permute-start(bf16[16,1664]{1,0:T(8,128)(2,1)} %get-tuple-element.75), channel_id=1, source_target_pairs={{0,96},{32,64},{64,32},{96,0},{128,224},{160,192},{192,160},{224,1... | collective-permute-start | bytes 159752 | tf_op jit(solution)/shard_map/ppermute | solution.py:56
  130.6 15.1 %copy-start.28 = (bf16[16,1536]{1,0:T(8,128)(2,1)}, bf16[16,1536]{1,0:T(8,128)(2,1)S(1)}, u32[]{:S(2)}) copy-start(bf16[16,1536]{1,0:T(8,128)(2,1)S(1)} %collective-permute-done.18.refs_2_) | copy-start | bytes 147460
  130.6 4.3 %collective-permute-start.19 = (bf16[16,1536]{1,0:T(8,128)(2,1)}, bf16[16,1536]{1,0:T(8,128)(2,1)S(1)}, u32[]{:S(2)}, u32[]{:S(2)}) collective-permute-start(bf16[16,1536]{1,0:T(8,128)(2,1)} %get-tuple-element.71), channel_id=1, source_target_pairs={{0,24},{8,16},{16,8},{24,0},{1,25},{9,17},{17,9},{25,1},{2,26},{10... | collective-permute-start | bytes 147464 | tf_op jit(solution)/shard_map/ppermute | solution.py:56
  134.9 10.8 %copy-start.29 = (bf16[16,1536]{1,0:T(8,128)(2,1)}, bf16[16,1536]{1,0:T(8,128)(2,1)S(1)}, u32[]{:S(2)}) copy-start(bf16[16,1536]{1,0:T(8,128)(2,1)S(1)} %collective-permute-done.19.refs_3_) | copy-start | bytes 147460
  134.9 6.5 %collective-permute-start.23 = (bf16[16,1664]{1,0:T(8,128)(2,1)}, bf16[16,1664]{1,0:T(8,128)(2,1)S(1)}, u32[]{:S(2)}, u32[]{:S(2)}) collective-permute-start(bf16[16,1664]{1,0:T(8,128)(2,1)} %get-tuple-element.76), channel_id=1, source_target_pairs={{0,128},{32,160},{64,192},{96,224},{128,0},{160,32},{192,64},{224,... | collective-permute-start | bytes 159752 | tf_op jit(solution)/shard_map/ppermute | solution.py:56
  136.1 9.5 %copy-start.17 = (bf16[16,1664]{1,0:T(8,128)(2,1)}, bf16[16,1664]{1,0:T(8,128)(2,1)S(1)}, u32[]{:S(2)}) copy-start(bf16[16,1664]{1,0:T(8,128)(2,1)S(1)} %collective-permute-done.20.refs_5_) | copy-start | bytes 159748
  136.1 6.7 %collective-permute-start.24 = (bf16[16,1664]{1,0:T(8,128)(2,1)}, bf16[16,1664]{1,0:T(8,128)(2,1)S(1)}, u32[]{:S(2)}, u32[]{:S(2)}) collective-permute-start(bf16[16,1664]{1,0:T(8,128)(2,1)} %get-tuple-element.77), channel_id=1, source_target_pairs={{0,160},{32,128},{64,224},{96,192},{128,32},{160,0},{192,96},{224,... | collective-permute-start | bytes 159752 | tf_op jit(solution)/shard_map/ppermute | solution.py:56
  140.3 5.4 %copy-start.18 = (bf16[16,1664]{1,0:T(8,128)(2,1)}, bf16[16,1664]{1,0:T(8,128)(2,1)S(1)}, u32[]{:S(2)}) copy-start(bf16[16,1664]{1,0:T(8,128)(2,1)S(1)} %collective-permute-done.21.refs_6_) | copy-start | bytes 159748
  140.3 4.3 %collective-permute-start.25 = (bf16[16,1664]{1,0:T(8,128)(2,1)}, bf16[16,1664]{1,0:T(8,128)(2,1)S(1)}, u32[]{:S(2)}, u32[]{:S(2)}) collective-permute-start(bf16[16,1664]{1,0:T(8,128)(2,1)} %get-tuple-element.78), channel_id=1, source_target_pairs={{0,192},{32,224},{64,128},{96,160},{128,64},{160,96},{192,0},{224,... | collective-permute-start | bytes 159752 | tf_op jit(solution)/shard_map/ppermute | solution.py:56
  140.3 5.4 %copy-start.19 = (bf16[16,1664]{1,0:T(8,128)(2,1)}, bf16[16,1664]{1,0:T(8,128)(2,1)S(1)}, u32[]{:S(2)}) copy-start(bf16[16,1664]{1,0:T(8,128)(2,1)S(1)} %collective-permute-done.22.refs_7_) | copy-start | bytes 159748
  140.3 5.3 %collective-permute-start.26 = (bf16[16,1664]{1,0:T(8,128)(2,1)}, bf16[16,1664]{1,0:T(8,128)(2,1)S(1)}, u32[]{:S(2)}, u32[]{:S(2)}) collective-permute-start(bf16[16,1664]{1,0:T(8,128)(2,1)} %get-tuple-element.79), channel_id=1, source_target_pairs={{0,224},{32,192},{64,160},{96,128},{128,96},{160,64},{192,32},{224... | collective-permute-start | bytes 159752 | tf_op jit(solution)/shard_map/ppermute | solution.py:56
  141.3 4.3 %copy-start.20 = (bf16[16,1664]{1,0:T(8,128)(2,1)}, bf16[16,1664]{1,0:T(8,128)(2,1)S(1)}, u32[]{:S(2)}) copy-start(bf16[16,1664]{1,0:T(8,128)(2,1)S(1)} %collective-permute-done.23.refs_8_) | copy-start | bytes 159748
  142.9 2.8 %copy-start.21 = (bf16[16,1664]{1,0:T(8,128)(2,1)}, bf16[16,1664]{1,0:T(8,128)(2,1)S(1)}, u32[]{:S(2)}) copy-start(bf16[16,1664]{1,0:T(8,128)(2,1)S(1)} %collective-permute-done.24.refs_9_) | copy-start | bytes 159748
  144.6 1.1 copy-start.22
  145.6 0.6 copy-start.23
  148.3 30.4 %collective-permute-start.27 = (bf16[8,3200]{1,0:T(8,128)(2,1)}, bf16[8,3200]{1,0:T(8,128)(2,1)S(1)}, u32[]{:S(2)}, u32[]{:S(2)}) collective-permute-start(bf16[8,3200]{1,0:T(8,128)(2,1)} %get-tuple-element.81), channel_id=1, source_target_pairs={{0,2},{1,3},{2,0},{3,1},{4,6},{5,7},{6,4},{7,5},{8,10},{9,11},{10,... | collective-permute-start | bytes 153608 | tf_op jit(solution)/shard_map/ppermute | solution.py:56
  168.0 10.7 %collective-permute-start.28 = (bf16[8,3200]{1,0:T(8,128)(2,1)}, bf16[8,3200]{1,0:T(8,128)(2,1)S(1)}, u32[]{:S(2)}, u32[]{:S(2)}) collective-permute-start(bf16[8,3200]{1,0:T(8,128)(2,1)} %get-tuple-element.82), channel_id=1, source_target_pairs={{0,4},{1,5},{2,6},{3,7},{4,0},{5,1},{6,2},{7,3},{8,12},{9,13},{10,... | collective-permute-start | bytes 153608 | tf_op jit(solution)/shard_map/ppermute | solution.py:56
  173.6 6.4 %collective-permute-start.29 = (bf16[8,3200]{1,0:T(8,128)(2,1)}, bf16[8,3200]{1,0:T(8,128)(2,1)S(1)}, u32[]{:S(2)}, u32[]{:S(2)}) collective-permute-start(bf16[8,3200]{1,0:T(8,128)(2,1)} %get-tuple-element.83), channel_id=1, source_target_pairs={{0,6},{1,7},{2,4},{3,5},{4,2},{5,3},{6,0},{7,1},{8,14},{9,15},{10,... | collective-permute-start | bytes 153608 | tf_op jit(solution)/shard_map/ppermute | solution.py:56
  174.1 0.7 copy-start.6
  178.7 1.4 copy-start.24
  178.7 1.4 copy-start.25
  180.0 0.6 copy-start.26

commit v2 on v1

v2 whole, which is shorter than its diff:
```python
import jax
import jax.numpy as jnp
from jax import lax
from jax.experimental import pallas as pl
from jax.experimental.pallas import tpu as pltpu
from jax.sharding import PartitionSpec as P

D = 768
WCAP = 128
SLOTS = 512
ROWS = 256
WIDE = 2 * D
HALF = 512
COLS = 3 * D + 128
AXES = ("gx", "gy", "gz")
FIRST = ("gx", "gy", "gz")
SECOND = ("gy", "gz", "gx")
EPSILON = 1e-06
BIG_NEGATIVE = -1e30
BF = jnp.bfloat16
F32 = jnp.float32
NT = (((1,), (1,)), ((), ()))
TN = (((0,), (0,)), ((), ()))
VMEM = pl.BlockSpec(memory_space=pltpu.VMEM)


def dot(a, b):
    return jnp.dot(a, b, preferred_element_type=F32)


def iota(shape, dim):
    return lax.broadcasted_iota(jnp.int32, shape, dim)


def column(row):
    n = row.shape[1]
    spread = jnp.broadcast_to(row.astype(F32), (n, n))
    return jnp.sum(jnp.where(iota((n, n), 0) == iota((n, n), 1), spread, 0.0), axis=1, keepdims=True)


def one_hot(condition):
    return jnp.where(condition, 1.0, 0.0).astype(BF)


def passed_along(value, axis, steps):
    count = lax.axis_size(axis)
    initial, last = (max(0, -steps), min(count, count - steps))
    return lax.ppermute(value, axis, [(source, source + steps) for source in range(initial, last)])


def bit(k, axis):
    return k // (4, 2, 1)[AXES.index(axis)] % 2


def carried(blocks, axes, steps):
    at = {k: blocks[k - 1 : k] for k in range(1, 8)}
    stages = []
    for axis in axes:
        moving = [k for k in range(1, 8) if bit(k, axis)]
        moved = passed_along(jnp.concatenate([at[k] for k in moving]), axis, steps)
        for i, k in enumerate(moving):
            at[k] = moved[i : i + 1]
        stages.append(moved)
    return stages


def arrival(axes):
    for k in range(1, 8):
        stage = max(s for s, axis in enumerate(axes) if bit(k, axis))
        moving = [m for m in range(1, 8) if bit(m, axes[stage])]
        yield stage, moving.index(k)


def crossed(value, axis, mask):
    count = lax.axis_size(axis)
    return lax.ppermute(value, axis, [(source, source ^ mask) for source in range(count)])


def pack_body(tok_ref, go_ref, send_ref, *outs):
    chosen = [
        one_hot(iota((32, ROWS), 1).astype(F32) == column(send_ref[0, k : k + 1, :])) for k in range(7)
    ]
    chosen = jnp.concatenate(chosen, axis=0)
    for part, ref in enumerate((tok_ref, go_ref)):
        outs[part][...] = dot(chosen, ref[...]).astype(BF).reshape(7, 32, D)


def normalised(x):
    centred = x - jnp.mean(x, axis=-1, keepdims=True)
    inv_std = lax.rsqrt(jnp.mean(centred * centred, axis=-1, keepdims=True) + EPSILON)
    return centred * inv_std, inv_std


def first_row(gz, core, block):
    gx, gy, z_hi = block // 16, block % 16 // 4, block % 4
    return ((gx * 4 + gy) * 8 + ((z_hi * 2 + core) ^ gz)) * 3


def half_place(gz, core):
    j = iota((HALF, 1), 0)
    row = jnp.where(j % 4 < 3, first_row(gz, core, j // 4) + j % 4, -1)
    return iota((HALF, D), 1) == row


def half_sums(gz, core, normed, mixed, gos, dpacked_ref, out_ref):
    place = half_place(gz, core)
    turned = lax.dot_general(one_hot(place), normed, NT, preferred_element_type=F32).astype(BF)
    i = iota((384, 1), 0)
    picks = one_hot(iota((384, D), 1) == first_row(gz, core, i % 128) + i // 128)
    picks = lax.dot_general(picks, mixed, NT, preferred_element_type=F32).astype(BF)
    proj = dot(picks, gos).astype(BF)
    j = iota((HALF, 1), 0)
    widen = one_hot(iota((HALF, 128), 1) == jnp.where(j % 4 == 3, j // 4, -1))
    for g in range(3):
        at = slice(g * D, (g + 1) * D)
        total = dot(turned, dpacked_ref[:, at]) + dot(widen, proj[g * 128 : (g + 1) * 128])
        out_ref[:, at] = total.astype(BF)
    return place


def main_body(
    me_ref, tok_ref, go_ref, t_refs, g_refs, win_ref, gain_ref, wqkv_ref, wout_ref,
    snd_ref, xs_ref, gos_ref, normed_ref, mixed_ref, dpacked_ref,
    rows_ref, packed_ref, delta_ref,
):
    rows_ref[:ROWS, :D] = tok_ref[...]
    rows_ref[:ROWS, D:] = go_ref[...]
    for part, (refs, axes) in enumerate(((t_refs, FIRST), (g_refs, SECOND))):
        for k, (stage, i) in enumerate(arrival(axes)):
            rows_ref[ROWS + 32 * k : ROWS + 32 * (k + 1), part * D : (part + 1) * D] = refs[stage][i]
    rows_ref[480:, :] = jnp.zeros((32, WIDE), BF)
    gain = gain_ref[...]

    def gather_window(w, carry):
        at = pl.ds(pl.multiple_of(w * WCAP, WCAP), WCAP)
        picks = one_hot(iota((WCAP, SLOTS), 1).astype(F32) == column(win_ref[:, at]))
        taken = dot(picks, rows_ref[...])
        x = taken[:, :D]
        xs_ref[at, :] = x.astype(BF)
        gos_ref[at, :] = taken[:, D:].astype(BF)
        unit, _ = normalised(x)
        normed_ref[at, :] = (unit * gain).astype(BF)
        return carry

    lax.fori_loop(0, SLOTS // WCAP, gather_window, 0)

    def project(c, carry):
        at = pl.ds(pl.multiple_of(c * D, D), D)
        packed_ref[:, at] = dot(normed_ref[...], wqkv_ref[:, at]).astype(BF)
        return carry

    lax.fori_loop(0, 3, project, 0)
    delta_ref[...] = lax.dot_general(
        gos_ref[...], wout_ref[...], NT, preferred_element_type=F32
    ).astype(BF)

    low = iota((WCAP, 128), 1) < 64
    zero = jnp.zeros((), BF)

    def both(value):
        return jnp.concatenate([jnp.where(low, value, zero), jnp.where(low, zero, value)], axis=0)

    def attend(w, carry):
        at = pl.ds(pl.multiple_of(w * WCAP, WCAP), WCAP)
        filled = jnp.broadcast_to(column(win_ref[:, at]) >= 0, (WCAP, WCAP))[None]
        for p in range(6):
            q_at = pl.ds(p * 128, 128)
            k_at = pl.ds(D + p * 128, 128)
            v_at = pl.ds(2 * D + p * 128, 128)
            q = packed_ref[at, q_at]
            k_both = both(packed_ref[at, k_at])
            v_both = both(packed_ref[at, v_at])
            d = delta_ref[at, q_at]
            scores = lax.dot_general(k_both, q, NT, preferred_element_type=F32) * 0.125
            scores = jnp.where(filled, scores.reshape(2, WCAP, WCAP), BIG_NEGATIVE)
            expo = jnp.exp(scores - jnp.max(scores, axis=1, keepdims=True))
            probs = expo * (1.0 / jnp.sum(expo, axis=1, keepdims=True))
            weights = probs.astype(BF)
            mixed = lax.dot_general(
                weights.reshape(2 * WCAP, WCAP), v_both, TN, preferred_element_type=F32
            )
            mixed_ref[at, q_at] = mixed.astype(BF)
            dweights = lax.dot_general(v_both, d, NT, preferred_element_type=F32)
            dweights = dweights.reshape(2, WCAP, WCAP)
            inner = jnp.sum(dweights * probs, axis=1, keepdims=True)
            dscaled = (probs * (dweights - inner) * 0.125).astype(BF)
            dq = lax.dot_general(
                dscaled.reshape(2 * WCAP, WCAP), k_both, TN, preferred_element_type=F32
            )
            dpacked_ref[at, q_at] = dq.astype(BF)
            beside = jnp.concatenate([dscaled[0], dscaled[1]], axis=1)
            dpacked_ref[at, k_at] = dot(beside, both(q)).astype(BF)
            beside = jnp.concatenate([weights[0], weights[1]], axis=1)
            dpacked_ref[at, v_at] = dot(beside, both(d)).astype(BF)
        return carry

    lax.fori_loop(0, SLOTS // WCAP, attend, 0)

    half_sums(
        me_ref[0], 1, normed_ref[...], mixed_ref[...], gos_ref[...], dpacked_ref, snd_ref
    )


def back_body(
    me_ref, xs_ref, gos_ref, normed_ref, mixed_ref, dpacked_ref, win_ref, gain_ref, wqkv_ref, wout_ref,
    own_ref, gain_own_ref, gain_snd_ref, kept_ref, *rest,
):
    ret_refs, cat_ref, dn_ref = rest[:-2], rest[-2], rest[-1]
    gain = gain_ref[...]
    place = half_sums(
        me_ref[0], 0, normed_ref[...], mixed_ref[...], gos_ref[...], dpacked_ref, own_ref
    )
    dn_ref[...] = lax.dot_general(
        dpacked_ref[...], wqkv_ref[...], NT, preferred_element_type=F32
    ).astype(BF)
    gain_row = jnp.zeros((1, D), F32)
    projected = dot(mixed_ref[...], wout_ref[...])
    cat_ref[:, :D] = (xs_ref[...].astype(F32) + projected).astype(BF)
    for w in range(4):
        at = slice(w * WCAP, (w + 1) * WCAP)
        unit, inv_std = normalised(xs_ref[at, :].astype(F32))
        dnormed = dn_ref[at, :].astype(F32)
        gain_row += jnp.sum(dnormed * unit, axis=0, keepdims=True)
        dunit = dnormed * gain
        dcentre = inv_std * (
            dunit
            - jnp.mean(dunit, axis=-1, keepdims=True)
            - unit * jnp.mean(dunit * unit, axis=-1, keepdims=True)
        )
        cat_ref[at, D:] = (gos_ref[at, :].astype(F32) + dcentre).astype(BF)
    back = one_hot(iota((480, SLOTS), 0) == win_ref[...])
    kept_ref[...] = dot(back[:ROWS], cat_ref[...]).astype(BF)
    sent = dot(back[ROWS:], cat_ref[...]).astype(BF).reshape(7, 32, WIDE)
    for part, ref in enumerate(ret_refs):
        ref[...] = sent[:, :, part * D : (part + 1) * D]
    own = jnp.where(place, gain_row, 0.0)
    gain_own_ref[...] = jnp.broadcast_to(jnp.sum(own, axis=1, keepdims=True), (HALF, 128))
    other = half_place(me_ref[0], 1)
    own = jnp.where(other, gain_row, 0.0)
    gain_snd_ref[...] = jnp.broadcast_to(jnp.sum(own, axis=1, keepdims=True), (HALF, 128))


def join_body(kept_ref, t_refs, g_refs, send_ref, out_ref, grad_ref):
    for part, (refs, axes, out) in enumerate(
        ((t_refs, FIRST, out_ref), (g_refs, SECOND, grad_ref))
    ):
        total = kept_ref[:, part * D : (part + 1) * D].astype(F32)
        for k, (stage, i) in enumerate(arrival(axes[::-1])):
            total += dot(one_hot(iota((ROWS, 32), 0) == send_ref[0, k : k + 1, :]), refs[stage][i])
        out[...] = total.astype(BF)


def sum1_body(own_ref, got_ref, gain_own_ref, gain_got_ref, out_ref):
    out_ref[:, : 3 * D] = (own_ref[...].astype(F32) + got_ref[...].astype(F32)).astype(BF)
    out_ref[:, 3 * D :] = (gain_own_ref[...] + gain_got_ref[...]).astype(BF)


def sum2_body(got_ref, *outs):
    total = jnp.sum(got_ref[...].astype(F32), axis=0)
    for i in range(4):
        outs[i][...] = total[4 * i : 4 * (i + 1)].astype(BF)


def sum3_body(a_ref, b_ref, c_ref, d_ref, qkv_ref, out_ref, gain_ref):
    total = a_ref[...].astype(F32) + b_ref[...].astype(F32)
    total += c_ref[...].astype(F32) + d_ref[...].astype(F32)
    qkv_ref[...] = total[:3, : 3 * D]
    for g in range(3):
        out_ref[g : g + 1, :] = total[3:4, g * D : (g + 1) * D]
    gain_ref[...] = total[:3, 3 * D :]


def call(body, shapes, *args, scratch=(), smem=(), mib=16):
    tree = jax.tree.structure(args)
    count = tree.num_leaves

    def flat(*refs):
        body(*jax.tree.unflatten(tree, refs[:count]), *refs[count:])

    return pl.pallas_call(
        flat,
        out_shape=[jax.ShapeDtypeStruct(shape, dtype) for shape, dtype in shapes],
        in_specs=[pl.BlockSpec(memory_space=pltpu.SMEM) if i in smem else VMEM for i in range(count)],
        out_specs=[VMEM] * len(shapes),
        scratch_shapes=list(scratch),
        compiler_params=pltpu.CompilerParams(vmem_limit_bytes=mib * 1024 * 1024),
    )(*jax.tree.leaves(args))


def on_device(tokens, norm_gain, w_qkv, w_out, send_rows, window_rows, grad_out):
    gain = norm_gain.reshape(1, D)
    me = lax.axis_index("gz").astype(jnp.int32).reshape(1)
    lists = ((7, 32, D), BF)
    blocks = call(pack_body, [lists, lists], tokens, grad_out, send_rows)
    arrived_t = carried(blocks[0], FIRST, 1)
    arrived_g = carried(blocks[1], SECOND, 1)

    slot, wide, half = ((SLOTS, D), BF), ((SLOTS, 3 * D), BF), ((HALF, 3 * D), BF)
    gains = ((HALF, 128), F32)
    sent, xs, gos, normed, mixed, dpacked = call(
        main_body,
        [half, slot, slot, slot, slot, wide],
        me, tokens, grad_out, arrived_t, arrived_g, window_rows, gain, w_qkv, w_out,
        scratch=[pltpu.VMEM((SLOTS, WIDE), BF), pltpu.VMEM(*wide), pltpu.VMEM(*slot)],
        smem=(0,),
        mib=34,
    )
    got = crossed(sent, "gz", 1)
    own, gain_own, gain_sent, kept, *back = call(
        back_body,
        [half, gains, gains, ((ROWS, WIDE), BF), lists, lists],
        me, xs, gos, normed, mixed, dpacked, window_rows, gain, w_qkv, w_out,
        scratch=[pltpu.VMEM((SLOTS, WIDE), BF), pltpu.VMEM(*slot)],
        smem=(0,),
        mib=34,
    )
    gain_got = crossed(gain_sent, "gz", 1)

    (paired,) = call(sum1_body, [((HALF, COLS), BF)], own, got, gain_own, gain_got)
    spread = lax.all_to_all(paired, ("gx", "gy"), split_axis=0, concat_axis=0, tiled=True)
    parts = call(sum2_body, [((4, COLS), BF)] * 4, spread.reshape(32, 16, COLS))
    last = [parts[0]] + [crossed(parts[i], "gz", 2 * i) for i in range(1, 4)]
    grad_qkv, grad_proj, gain_rows = call(
        sum3_body, [((3, 3 * D), F32), ((3, D), F32), ((3, 128), F32)], *last
    )

    block_out, grad_tokens = call(
        join_body,
        [((ROWS, D), BF), ((ROWS, D), BF)],
        kept,
        carried(back[0], FIRST[::-1], -1),
        carried(back[1], SECOND[::-1], -1),
        send_rows,
    )
    return (block_out, grad_tokens, gain_rows[:, 0], grad_qkv, grad_proj)


def solution(mesh):
    spread = P(AXES, None)
    in_specs = (spread, P(), P(), P(), P(AXES, None, None), spread, spread)
    out_specs = (spread, spread, P(AXES), spread, spread)
    return jax.shard_map(
        on_device, mesh=mesh, in_specs=in_specs, out_specs=out_specs, check_vma=False
    )
```

time: 186 us -> 157 us (0.84)
  Pallas kernels: 49.5 us -> 30.8 us
  starting transfers between devices: 83 us -> 66.7 us
  local copies, waits for them, and re-layouts: 11.5 us -> 14 us
  other arithmetic: 0.84 us -> 3.04 us
    ppermute x24 -> x5, starting transfers between devices: 66.8 us -> 25.2 us  [crossed(): lax.ppermute(value, axis, [(source, source ^ mask) for source in range(co...]
    pallas_call x8 -> x7, Pallas kernels: 49.5 us -> 30.8 us  [call(): pl.pallas_call(flat, out_shape=[jax.ShapeDtypeStruct(shape, dtype) for sh...]
    ppermute x6 -> x12, starting transfers between devices: 16.2 us -> 32.3 us  [passed_along(): lax.ppermute(value, axis, [(source, source + steps) for source in range(i...]
    ppermute x6 -> x12, waiting for transfers between devices: 19.7 us -> 35 us  [passed_along(): lax.ppermute(value, axis, [(source, source + steps) for source in range(i...]
    ppermute x24 -> x5, waiting for transfers between devices: 17.9 us -> 3.44 us  [crossed(): lax.ppermute(value, axis, [(source, source ^ mask) for source in range(co...]
    all_to_all x0 -> x1, starting transfers between devices: none -> 9.18 us  [on_device(): lax.all_to_all(paired, ('gx', 'gy'), split_axis=0, concat_axis=0, tiled=T...]
    unnamed x63 -> x59, local copies, waits for them, and re-layouts: 6.36 us -> 13.2 us
    slice x10 -> x16, local copies, waits for them, and re-layouts: 3.3 us -> 0.19 us  [the longest x7 0.11 us: carried(): at = {k: blocks[k - 1:k] for k in range(1, 8)}]
  transfers between devices with their start and end apart: 30 -> 18, of which waited for: 10 -> 7; matrix products, arithmetic and copies ran while one was open for 2% -> 2% of each run, Pallas kernels for 10% -> 7%
where the time goes in v2:
time: 157 us; the launch traced here: 154 us
  starting transfers between devices  66.7 us (42%)
  waiting for transfers between devices  38.5 us (25%)
  Pallas kernels  30.8 us (20%)
  local copies, waits for them, and re-layouts  14 us (9%)
  other arithmetic  3.04 us (2%)
    ppermute x12, waiting for transfers between devices, passed_along(): lax.ppermute(value, axis, [(source, source + steps) for source in range(i...  35 us
    ppermute x12, starting transfers between devices, passed_along(): lax.ppermute(value, axis, [(source, source + steps) for source in range(i...  32.3 us
    pallas_call x7, Pallas kernels, call(): pl.pallas_call(flat, out_shape=[jax.ShapeDtypeStruct(shape, dtype) for sh...  30.8 us
    ppermute x5, starting transfers between devices, crossed(): lax.ppermute(value, axis, [(source, source ^ mask) for source in range(co...  25.2 us
    unnamed x59, local copies, waits for them, and re-layouts  13.2 us
    all_to_all x1, starting transfers between devices, on_device(): lax.all_to_all(paired, ('gx', 'gy'), split_axis=0, concat_axis=0, tiled=T...  9.18 us
    ppermute x5, waiting for transfers between devices, crossed(): lax.ppermute(value, axis, [(source, source ^ mask) for source in range(co...  3.44 us
  transfers between devices with their start and end apart: 18, of which 7 were waited for; matrix products, arithmetic and copies ran while one was open for 2% of the time, Pallas kernels for 7%

profile of v2, /device:TPU:10, one launch (start us, length us, event | category | flops | bytes accessed | tf_op | source)
XLA Modules:
  0.0 154.2 jit_solution(11016333379741010126)
XLA Ops:
  0.6 0.7 copy.14.refs_2_.refs_7_
  1.3 1.0 copy-done.3
  2.3 1.0 copy-done.5
  3.3 0.4 shard_map.110
  3.7 0.0 copy-start.28
  3.7 0.0 copy-start
  3.7 0.0 copy-start.27
  3.8 3.7 %collective-permute-start.3 = (bf16[4,32,768]{2,1,0:T(8,128)(2,1)S(1)}, bf16[4,32,768]{2,1,0:T(8,128)(2,1)S(1)}, u32[]{:S(2)}, u32[]{:S(2)}) collective-permute-start(bf16[4,32,768]{2,1,0:T(8,128)(2,1)S(1)} %pad_maximum_fusion.2), channel_id=1, source_target_pairs={{0,8},{8,16},{16,24},{1,9},{9,17},{17,25},{2,10},{10,18},{18,26},{... | collective-permute-start | bytes 589832 | tf_op jit(solution)/shard_map/ppermute | solution.py:48
  7.6 3.8 %collective-permute-start = (bf16[4,32,768]{2,1,0:T(8,128)(2,1)S(1)}, bf16[4,32,768]{2,1,0:T(8,128)(2,1)S(1)}, u32[]{:S(2)}, u32[]{:S(2)}) collective-permute-start(bf16[4,32,768]{2,1,0:T(8,128)(2,1)S(1)} %slice.132), channel_id=1, source_target_pairs={{0,32},{32,64},{64,96},{96,128},{128,160},{160,192},{192,224},{1,3... | collective-permute-start | bytes 589832 | tf_op jit(solution)/shard_map/ppermute | solution.py:48
  11.4 1.2 collective-permute-done.3.refs_6_
  12.6 0.7 copy-done.9
  13.3 1.3 collective-permute-start.4
  14.7 2.1 %collective-permute-done.refs_3_ = bf16[4,32,768]{2,1,0:T(8,128)(2,1)S(1)} collective-permute-done((bf16[4,32,768]{2,1,0:T(8,128)(2,1)S(1)}, bf16[4,32,768]{2,1,0:T(8,128)(2,1)S(1)}, u32[]{:S(2)}, u32[]{:S(2)}) %collective-permute-start) | collective-permute-done | bytes 196640 | tf_op jit(solution)/shard_map/ppermute | solution.py:48
  16.8 3.2 %collective-permute-start.1 = (bf16[4,32,768]{2,1,0:T(8,128)(2,1)S(1)}, bf16[4,32,768]{2,1,0:T(8,128)(2,1)S(1)}, u32[]{:S(2)}, u32[]{:S(2)}) collective-permute-start(bf16[4,32,768]{2,1,0:T(8,128)(2,1)S(1)} %pad_maximum_fusion), channel_id=1, source_target_pairs={{0,8},{8,16},{16,24},{1,9},{9,17},{17,25},{2,10},{10,18},{18,26},{... | collective-permute-start | bytes 589832 | tf_op jit(solution)/shard_map/ppermute | solution.py:48
  20.0 0.7 copy-done.15
  20.7 0.7 pad_maximum_fusion.4
  21.4 2.9 %collective-permute-start.5 = (bf16[4,32,768]{2,1,0:T(8,128)(2,1)}, bf16[4,32,768]{2,1,0:T(8,128)(2,1)}, u32[]{:S(2)}, u32[]{:S(2)}) collective-permute-start(bf16[4,32,768]{2,1,0:T(8,128)(2,1)} %pad_maximum_fusion.4), channel_id=1, source_target_pairs={{0,32},{32,64},{64,96},{96,128},{128,160},{160,192},{192,224},{1,3... | collective-permute-start | bytes 589832 | tf_op jit(solution)/shard_map/ppermute | solution.py:48
  24.3 1.1 collective-permute-done.1.refs_4_
  25.5 0.0 copy-start.17
  25.5 0.7 copy-done.17
  26.2 0.7 pad_maximum_fusion.1
  26.9 5.0 %collective-permute-start.2 = (bf16[4,32,768]{2,1,0:T(8,128)(2,1)}, bf16[4,32,768]{2,1,0:T(8,128)(2,1)}, u32[]{:S(2)}, u32[]{:S(2)}) collective-permute-start(bf16[4,32,768]{2,1,0:T(8,128)(2,1)} %pad_maximum_fusion.1), channel_id=1, source_target_pairs={{0,1},{1,2},{2,3},{3,4},{4,5},{5,6},{6,7},{8,9},{9,10},{10,11},{11... | collective-permute-start | bytes 589832 | tf_op jit(solution)/shard_map/ppermute | solution.py:48
  31.8 0.7 collective-permute-done.2.refs_5_
  32.6 1.3 copy-done.2
  33.8 1.0 copy-done.4
  34.8 1.0 copy-done.6
  35.8 0.9 copy-done.10
  36.7 0.9 copy-done.12
  37.7 0.9 copy-done.16
  38.6 0.9 copy-done.18
  39.5 18.1 %shard_map.111 = (bf16[512,2304]{1,0:T(8,128)(2,1)S(1)}, bf16[512,768]{1,0:T(8,128)(2,1)S(1)}, bf16[512,768]{1,0:T(8,128)(2,1)S(1)}, bf16[512,768]{1,0:T(8,128)(...) custom-call(s32[1]{0:T(128)} %bitcast.refs_0_, bf16[256,768]{1,0:T(8,128)(2,1)S(1)} %copy-done.4, ...), custom_call_target="tpu_custom_call" | custom-call | tf_op jit(solution)/shard_map/pallas_call | solution.py:280
  57.6 5.5 %collective-permute-start.12 = (bf16[512,2304]{1,0:T(8,128)(2,1)S(1)}, bf16[512,2304]{1,0:T(8,128)(2,1)S(1)}, u32[]{:S(2)}, u32[]{:S(2)}) collective-permute-start(bf16[512,2304]{1,0:T(8,128)(2,1)S(1)} %get-tuple-element.41), channel_id=1, source_target_pairs={{0,1},{1,0},{2,3},{3,2},{4,5},{5,4},{6,7},{7,6},{8,9},{9,8},{10,11... | collective-permute-start | bytes 7077896 | tf_op jit(solution)/shard_map/ppermute | solution.py:76
  63.2 7.3 %shard_map.112 = (bf16[512,2304]{1,0:T(8,128)(2,1)S(1)}, f32[512,128]{1,0:T(8,128)S(1)}, f32[512,128]{1,0:T(8,128)S(1)}, bf16[256,1536]{1,0:T(8,128)(2,1)S(1)}, ...) custom-call(s32[1]{0:T(128)} %bitcast.refs_0_, bf16[512,768]{1,0:T(8,128)(2,1)S(1)} %get-tuple-element.30.refs_1_, ...), custom_call_target="tpu_custom_call" | custom-call | tf_op jit(solution)/shard_map/pallas_call | solution.py:280
  70.5 0.0 copy-start.23
  70.5 0.0 copy-start.25
  70.5 0.1 collective-permute-start.13
  70.6 1.5 collective-permute-done.13.refs_3_
  72.1 0.6 shard_map.114
  72.7 1.4 copy-done.1
  74.2 9.2 %all-to-all-start = ((bf16[32,16,2432]{2,1,0:T(8,128)(2,1)}), bf16[32,16,2432]{2,1,0:T(8,128)(2,1)S(1)}, u32[]{:S(2)}, u32[]{:S(2)}) async-start(bf16[32,16,2432]{2,1,0:T(8,128)(2,1)} %bitcast.2), calls=%async_computation | async-start | bytes 4980736 | tf_op jit(solution)/shard_map/all_to_all | solution.py:320
  83.5 1.3 collective-permute-start.6
  84.8 3.4 %collective-permute-start.9 = (bf16[4,32,768]{2,1,0:T(8,128)(2,1)S(1)}, bf16[4,32,768]{2,1,0:T(8,128)(2,1)S(1)}, u32[]{:S(2)}, u32[]{:S(2)}) collective-permute-start(bf16[4,32,768]{2,1,0:T(8,128)(2,1)S(1)} %slice.160), channel_id=1, source_target_pairs={{32,0},{64,32},{96,64},{128,96},{160,128},{192,160},{224,192},{33,... | collective-permute-start | bytes 589832 | tf_op jit(solution)/shard_map/ppermute | solution.py:48
  88.2 0.0 collective-permute-done.6.refs_1_
  88.3 2.6 %collective-permute-start.7 = (bf16[4,32,768]{2,1,0:T(8,128)(2,1)S(1)}, bf16[4,32,768]{2,1,0:T(8,128)(2,1)S(1)}, u32[]{:S(2)}, u32[]{:S(2)}) collective-permute-start(bf16[4,32,768]{2,1,0:T(8,128)(2,1)S(1)} %pad_maximum_fusion.6), channel_id=1, source_target_pairs={{8,0},{16,8},{24,16},{9,1},{17,9},{25,17},{10,2},{18,10},{26,18},{... | collective-permute-start | bytes 589832 | tf_op jit(solution)/shard_map/ppermute | solution.py:48
  90.9 29.9 %collective-permute-done.9.refs_4_ = bf16[4,32,768]{2,1,0:T(8,128)(2,1)S(1)} collective-permute-done((bf16[4,32,768]{2,1,0:T(8,128)(2,1)S(1)}, bf16[4,32,768]{2,1,0:T(8,128)(2,1)S(1)}, u32[]{:S(2)}, u32[]{:S(2)}) %collective-permute-start.9) | collective-permute-done | bytes 196640 | tf_op jit(solution)/shard_map/ppermute | solution.py:48
  120.9 1.3 collective-permute-start.10
  122.2 0.0 collective-permute-done.7.refs_2_
  122.2 0.0 copy-start.19
  122.2 0.7 pad_maximum_fusion.7
  122.9 1.9 %collective-permute-start.8 = (bf16[4,32,768]{2,1,0:T(8,128)(2,1)}, bf16[4,32,768]{2,1,0:T(8,128)(2,1)}, u32[]{:S(2)}, u32[]{:S(2)}) collective-permute-start(bf16[4,32,768]{2,1,0:T(8,128)(2,1)} %pad_maximum_fusion.7), channel_id=1, source_target_pairs={{32,0},{64,32},{96,64},{128,96},{160,128},{192,160},{224,192},{33,... | collective-permute-start | bytes 589832 | tf_op jit(solution)/shard_map/ppermute | solution.py:48
  124.8 0.0 collective-permute-done.10.refs_5_
  124.9 0.8 pad_maximum_fusion.9
  125.6 1.9 %collective-permute-start.11 = (bf16[4,32,768]{2,1,0:T(8,128)(2,1)}, bf16[4,32,768]{2,1,0:T(8,128)(2,1)}, u32[]{:S(2)}, u32[]{:S(2)}) collective-permute-start(bf16[4,32,768]{2,1,0:T(8,128)(2,1)} %pad_maximum_fusion.9), channel_id=1, source_target_pairs={{8,0},{16,8},{24,16},{9,1},{17,9},{25,17},{10,2},{18,10},{26,18},{... | collective-permute-start | bytes 589832 | tf_op jit(solution)/shard_map/ppermute | solution.py:48
  127.6 0.0 all-to-all-done.refs_0_
  127.6 0.0 copy-start.20
  127.6 0.4 shard_map.115
  128.0 12.3 %collective-permute-start.14 = (bf16[4,2432]{1,0:T(4,128)(2,1)S(1)}, bf16[4,2432]{1,0:T(4,128)(2,1)S(1)}, u32[]{:S(2)}, u32[]{:S(2)}) collective-permute-start(bf16[4,2432]{1,0:T(4,128)(2,1)S(1)} %get-tuple-element.45), channel_id=1, source_target_pairs={{0,2},{1,3},{2,0},{3,1},{4,6},{5,7},{6,4},{7,5},{8,10},{9,11},{10,... | collective-permute-start | bytes 58376 | tf_op jit(solution)/shard_map/ppermute | solution.py:76
  140.3 6.7 %collective-permute-start.15 = (bf16[4,2432]{1,0:T(4,128)(2,1)S(1)}, bf16[4,2432]{1,0:T(4,128)(2,1)S(1)}, u32[]{:S(2)}, u32[]{:S(2)}) collective-permute-start(bf16[4,2432]{1,0:T(4,128)(2,1)S(1)} %get-tuple-element.46), channel_id=1, source_target_pairs={{0,4},{1,5},{2,6},{3,7},{4,0},{5,1},{6,2},{7,3},{8,12},{9,13},{10,... | collective-permute-start | bytes 58376 | tf_op jit(solution)/shard_map/ppermute | solution.py:76
  147.1 0.5 collective-permute-start.16
  147.6 3.5 %shard_map.113 = (bf16[256,768]{1,0:T(8,128)(2,1)}, bf16[256,768]{1,0:T(8,128)(2,1)}) custom-call(bf16[256,1536]{1,0:T(8,128)(2,1)S(1)} %copy-done.8, bf16[4,32,768]{2,1,0:T(8,128)(2,1)S(1)} %collective-permute-done.6.refs_1_, bf16[4,32,768]{2,1,0:T(8,128)(2,1)S(1)} %copy-done.20, bf16[4,32,768]{2,1,0:T(8,128)(2,1)} %collective-permute-done.8.refs_3_, ...), custom_call_target="tpu_custom_call" | custom-call | tf_op jit(solution)/shard_map/pallas_call | solution.py:280
  151.0 0.0 collective-permute-done.14.refs_1_
  151.0 1.9 %collective-permute-done.16.refs_3_ = bf16[4,2432]{1,0:T(4,128)(2,1)S(1)} collective-permute-done((bf16[4,2432]{1,0:T(4,128)(2,1)S(1)}, bf16[4,2432]{1,0:T(4,128)(2,1)S(1)}, u32[]{:S(2)}, u32[]{:S(2)}) %collective-permute-start.16) | collective-permute-done | bytes 19488 | tf_op jit(solution)/shard_map/ppermute | solution.py:76
  152.9 0.6 shard_map.116
  153.6 0.6 slice_reduce_fusion
  (66 shorter events, 0.4 us)
Async XLA Ops:
  1.3 1.0 copy-start.3
  2.3 1.0 copy-start.5
  3.7 28.1 %copy-start.28 = (f32[768]{0:T(1024)S(1)}, f32[768]{0:T(1024)}, u32[]{:S(2)}) copy-start(f32[768]{0:T(1024)} %param.8) | copy-start | bytes 9220
  3.7 28.8 %copy-start = (bf16[768,2304]{1,0:T(8,128)(2,1)S(1)}, bf16[768,2304]{1,0:T(8,128)(2,1)}, u32[]{:S(2)}) copy-start(bf16[768,2304]{1,0:T(8,128)(2,1)} %refs_8_.1) | copy-start | bytes 10616836
  3.7 28.8 %copy-start.27 = (s32[1,512]{1,0:T(1,128)S(1)}, s32[1,512]{1,0:T(1,128)}, u32[]{:S(2)}) copy-start(s32[1,512]{1,0:T(1,128)} %refs_6_.1) | copy-start | bytes 6148
  3.8 8.8 %collective-permute-start.3 = (bf16[4,32,768]{2,1,0:T(8,128)(2,1)S(1)}, bf16[4,32,768]{2,1,0:T(8,128)(2,1)S(1)}, u32[]{:S(2)}, u32[]{:S(2)}) collective-permute-start(bf16[4,32,768]{2,1,0:T(8,128)(2,1)S(1)} %pad_maximum_fusion.2), channel_id=1, source_target_pairs={{0,8},{8,16},{16,24},{1,9},{9,17},{17,25},{2,10},{10,18},{18,26},{... | collective-permute-start | bytes 589832 | tf_op jit(solution)/shard_map/ppermute | solution.py:48
  7.6 9.2 %collective-permute-start = (bf16[4,32,768]{2,1,0:T(8,128)(2,1)S(1)}, bf16[4,32,768]{2,1,0:T(8,128)(2,1)S(1)}, u32[]{:S(2)}, u32[]{:S(2)}) collective-permute-start(bf16[4,32,768]{2,1,0:T(8,128)(2,1)S(1)} %slice.132), channel_id=1, source_target_pairs={{0,32},{32,64},{64,96},{96,128},{128,160},{160,192},{192,224},{1,3... | collective-permute-start | bytes 589832 | tf_op jit(solution)/shard_map/ppermute | solution.py:48
  12.6 0.7 copy-start.9
  13.3 6.7 %collective-permute-start.4 = (bf16[4,32,768]{2,1,0:T(8,128)(2,1)S(1)}, bf16[4,32,768]{2,1,0:T(8,128)(2,1)S(1)}, u32[]{:S(2)}, u32[]{:S(2)}) collective-permute-start(bf16[4,32,768]{2,1,0:T(8,128)(2,1)S(1)} %pad_maximum_fusion.3), channel_id=1, source_target_pairs={{0,1},{1,2},{2,3},{3,4},{4,5},{5,6},{6,7},{8,9},{9,10},{10,11},{11... | collective-permute-start | bytes 589832 | tf_op jit(solution)/shard_map/ppermute | solution.py:48
  16.7 3.2 %copy-start.11 = (bf16[4,32,768]{2,1,0:T(8,128)(2,1)}, bf16[4,32,768]{2,1,0:T(8,128)(2,1)S(1)}, u32[]{:S(2)}) copy-start(bf16[4,32,768]{2,1,0:T(8,128)(2,1)S(1)} %collective-permute-done.refs_3_) | copy-start | bytes 589828
  16.8 8.7 %collective-permute-start.1 = (bf16[4,32,768]{2,1,0:T(8,128)(2,1)S(1)}, bf16[4,32,768]{2,1,0:T(8,128)(2,1)S(1)}, u32[]{:S(2)}, u32[]{:S(2)}) collective-permute-start(bf16[4,32,768]{2,1,0:T(8,128)(2,1)S(1)} %pad_maximum_fusion), channel_id=1, source_target_pairs={{0,8},{8,16},{16,24},{1,9},{9,17},{17,25},{2,10},{10,18},{18,26},{... | collective-permute-start | bytes 589832 | tf_op jit(solution)/shard_map/ppermute | solution.py:48
  20.0 0.7 copy-start.15
  21.4 10.4 %collective-permute-start.5 = (bf16[4,32,768]{2,1,0:T(8,128)(2,1)}, bf16[4,32,768]{2,1,0:T(8,128)(2,1)}, u32[]{:S(2)}, u32[]{:S(2)}) collective-permute-start(bf16[4,32,768]{2,1,0:T(8,128)(2,1)} %pad_maximum_fusion.4), channel_id=1, source_target_pairs={{0,32},{32,64},{64,96},{96,128},{128,160},{160,192},{192,224},{1,3... | collective-permute-start | bytes 589832 | tf_op jit(solution)/shard_map/ppermute | solution.py:48
  25.5 0.7 copy-start.17
  26.9 5.7 %collective-permute-start.2 = (bf16[4,32,768]{2,1,0:T(8,128)(2,1)}, bf16[4,32,768]{2,1,0:T(8,128)(2,1)}, u32[]{:S(2)}, u32[]{:S(2)}) collective-permute-start(bf16[4,32,768]{2,1,0:T(8,128)(2,1)} %pad_maximum_fusion.1), channel_id=1, source_target_pairs={{0,1},{1,2},{2,3},{3,4},{4,5},{5,6},{6,7},{8,9},{9,10},{10,11},{11... | collective-permute-start | bytes 589832 | tf_op jit(solution)/shard_map/ppermute | solution.py:48
  32.6 1.3 copy-start.2
  33.8 1.0 copy-start.4
  34.8 1.0 copy-start.6
  35.8 0.9 copy-start.10
  36.7 0.9 copy-start.12
  37.7 0.9 copy-start.16
  38.6 0.9 copy-start.18
  57.6 14.5 %collective-permute-start.12 = (bf16[512,2304]{1,0:T(8,128)(2,1)S(1)}, bf16[512,2304]{1,0:T(8,128)(2,1)S(1)}, u32[]{:S(2)}, u32[]{:S(2)}) collective-permute-start(bf16[512,2304]{1,0:T(8,128)(2,1)S(1)} %get-tuple-element.41), channel_id=1, source_target_pairs={{0,1},{1,0},{2,3},{3,2},{4,5},{5,4},{6,7},{7,6},{8,9},{9,8},{10,11... | collective-permute-start | bytes 7077896 | tf_op jit(solution)/shard_map/ppermute | solution.py:76
  70.5 2.2 %copy-start.7 = (bf16[256,1536]{1,0:T(8,128)(2,1)}, bf16[256,1536]{1,0:T(8,128)(2,1)S(1)}, u32[]{:S(2)}) copy-start(bf16[256,1536]{1,0:T(8,128)(2,1)S(1)} %get-tuple-element.35.refs_0_) | copy-start | bytes 2359300
  70.5 2.2 %copy-start.23 = (bf16[7,32,768]{2,1,0:T(8,128)(2,1)}, bf16[7,32,768]{2,1,0:T(8,128)(2,1)S(1)}, u32[]{:S(2)}) copy-start(bf16[7,32,768]{2,1,0:T(8,128)(2,1)S(1)} %get-tuple-element.37) | copy-start | bytes 1032196
  70.5 2.2 %copy-start.25 = (bf16[7,32,768]{2,1,0:T(8,128)(2,1)}, bf16[7,32,768]{2,1,0:T(8,128)(2,1)S(1)}, u32[]{:S(2)}) copy-start(bf16[7,32,768]{2,1,0:T(8,128)(2,1)S(1)} %get-tuple-element.36) | copy-start | bytes 1032196
  70.5 1.6 %collective-permute-start.13 = (f32[512,128]{1,0:T(8,128)S(1)}, f32[512,128]{1,0:T(8,128)S(1)}, u32[]{:S(2)}, u32[]{:S(2)}) collective-permute-start(f32[512,128]{1,0:T(8,128)S(1)} %get-tuple-element.43), channel_id=1, source_target_pairs={{0,1},{1,0},{2,3},{3,2},{4,5},{5,4},{6,7},{7,6},{8,9},{9,8},{10,11... | collective-permute-start | bytes 786440 | tf_op jit(solution)/shard_map/ppermute | solution.py:76
  72.7 1.5 copy-start.1
  74.2 9.2 %copy-start.24 = (bf16[7,32,768]{2,1,0:T(8,128)(2,1)S(1)}, bf16[7,32,768]{2,1,0:T(8,128)(2,1)}, u32[]{:S(2)}) copy-start(bf16[7,32,768]{2,1,0:T(8,128)(2,1)} %copy-done.23) | copy-start | bytes 1032196
  74.2 9.2 %copy-start.26 = (bf16[7,32,768]{2,1,0:T(8,128)(2,1)S(1)}, bf16[7,32,768]{2,1,0:T(8,128)(2,1)}, u32[]{:S(2)}) copy-start(bf16[7,32,768]{2,1,0:T(8,128)(2,1)} %copy-done.25) | copy-start | bytes 1032196
  74.2 53.4 %all-to-all-start = ((bf16[32,16,2432]{2,1,0:T(8,128)(2,1)}), bf16[32,16,2432]{2,1,0:T(8,128)(2,1)S(1)}, u32[]{:S(2)}, u32[]{:S(2)}) async-start(bf16[32,16,2432]{2,1,0:T(8,128)(2,1)} %bitcast.2), calls=%async_computation | async-start | bytes 4980736 | tf_op jit(solution)/shard_map/all_to_all | solution.py:320
  83.5 4.7 %collective-permute-start.6 = (bf16[4,32,768]{2,1,0:T(8,128)(2,1)S(1)}, bf16[4,32,768]{2,1,0:T(8,128)(2,1)S(1)}, u32[]{:S(2)}, u32[]{:S(2)}) collective-permute-start(bf16[4,32,768]{2,1,0:T(8,128)(2,1)S(1)} %pad_maximum_fusion.5), channel_id=1, source_target_pairs={{1,0},{2,1},{3,2},{4,3},{5,4},{6,5},{7,6},{9,8},{10,9},{11,10},{12... | collective-permute-start | bytes 589832 | tf_op jit(solution)/shard_map/ppermute | solution.py:48
  84.8 36.0 %collective-permute-start.9 = (bf16[4,32,768]{2,1,0:T(8,128)(2,1)S(1)}, bf16[4,32,768]{2,1,0:T(8,128)(2,1)S(1)}, u32[]{:S(2)}, u32[]{:S(2)}) collective-permute-start(bf16[4,32,768]{2,1,0:T(8,128)(2,1)S(1)} %slice.160), channel_id=1, source_target_pairs={{32,0},{64,32},{96,64},{128,96},{160,128},{192,160},{224,192},{33,... | collective-permute-start | bytes 589832 | tf_op jit(solution)/shard_map/ppermute | solution.py:48
  88.2 59.3 %copy-start.8 = (bf16[256,1536]{1,0:T(8,128)(2,1)S(1)}, bf16[256,1536]{1,0:T(8,128)(2,1)}, u32[]{:S(2)}) copy-start(bf16[256,1536]{1,0:T(8,128)(2,1)} %copy-done.7) | copy-start | bytes 2359300
  88.3 33.9 %collective-permute-start.7 = (bf16[4,32,768]{2,1,0:T(8,128)(2,1)S(1)}, bf16[4,32,768]{2,1,0:T(8,128)(2,1)S(1)}, u32[]{:S(2)}, u32[]{:S(2)}) collective-permute-start(bf16[4,32,768]{2,1,0:T(8,128)(2,1)S(1)} %pad_maximum_fusion.6), channel_id=1, source_target_pairs={{8,0},{16,8},{24,16},{9,1},{17,9},{25,17},{10,2},{18,10},{26,18},{... | collective-permute-start | bytes 589832 | tf_op jit(solution)/shard_map/ppermute | solution.py:48
  120.8 4.8 %copy-start.13 = (bf16[4,32,768]{2,1,0:T(8,128)(2,1)}, bf16[4,32,768]{2,1,0:T(8,128)(2,1)S(1)}, u32[]{:S(2)}) copy-start(bf16[4,32,768]{2,1,0:T(8,128)(2,1)S(1)} %collective-permute-done.9.refs_4_) | copy-start | bytes 589828
  120.9 4.0 %collective-permute-start.10 = (bf16[4,32,768]{2,1,0:T(8,128)(2,1)S(1)}, bf16[4,32,768]{2,1,0:T(8,128)(2,1)S(1)}, u32[]{:S(2)}, u32[]{:S(2)}) collective-permute-start(bf16[4,32,768]{2,1,0:T(8,128)(2,1)S(1)} %pad_maximum_fusion.8), channel_id=1, source_target_pairs={{1,0},{2,1},{3,2},{4,3},{5,4},{6,5},{7,6},{9,8},{10,9},{11,10},{12... | collective-permute-start | bytes 589832 | tf_op jit(solution)/shard_map/ppermute | solution.py:48
  122.2 3.5 %copy-start.19 = (bf16[4,32,768]{2,1,0:T(8,128)(2,1)}, bf16[4,32,768]{2,1,0:T(8,128)(2,1)S(1)}, u32[]{:S(2)}) copy-start(bf16[4,32,768]{2,1,0:T(8,128)(2,1)S(1)} %collective-permute-done.7.refs_2_) | copy-start | bytes 589828
  122.9 24.6 %collective-permute-start.8 = (bf16[4,32,768]{2,1,0:T(8,128)(2,1)}, bf16[4,32,768]{2,1,0:T(8,128)(2,1)}, u32[]{:S(2)}, u32[]{:S(2)}) collective-permute-start(bf16[4,32,768]{2,1,0:T(8,128)(2,1)} %pad_maximum_fusion.7), channel_id=1, source_target_pairs={{32,0},{64,32},{96,64},{128,96},{160,128},{192,160},{224,192},{33,... | collective-permute-start | bytes 589832 | tf_op jit(solution)/shard_map/ppermute | solution.py:48
  124.8 0.8 copy-start.21
  125.6 21.9 %collective-permute-start.11 = (bf16[4,32,768]{2,1,0:T(8,128)(2,1)}, bf16[4,32,768]{2,1,0:T(8,128)(2,1)}, u32[]{:S(2)}, u32[]{:S(2)}) collective-permute-start(bf16[4,32,768]{2,1,0:T(8,128)(2,1)} %pad_maximum_fusion.9), channel_id=1, source_target_pairs={{8,0},{16,8},{24,16},{9,1},{17,9},{25,17},{10,2},{18,10},{26,18},{... | collective-permute-start | bytes 589832 | tf_op jit(solution)/shard_map/ppermute | solution.py:48
  127.6 20.0 %copy-start.14 = (bf16[4,32,768]{2,1,0:T(8,128)(2,1)S(1)}, bf16[4,32,768]{2,1,0:T(8,128)(2,1)}, u32[]{:S(2)}) copy-start(bf16[4,32,768]{2,1,0:T(8,128)(2,1)} %copy-done.13) | copy-start | bytes 589828
  127.6 20.0 %copy-start.20 = (bf16[4,32,768]{2,1,0:T(8,128)(2,1)S(1)}, bf16[4,32,768]{2,1,0:T(8,128)(2,1)}, u32[]{:S(2)}) copy-start(bf16[4,32,768]{2,1,0:T(8,128)(2,1)} %copy-done.19) | copy-start | bytes 589828
  127.6 20.0 %copy-start.22 = (bf16[4,32,768]{2,1,0:T(8,128)(2,1)S(1)}, bf16[4,32,768]{2,1,0:T(8,128)(2,1)}, u32[]{:S(2)}) copy-start(bf16[4,32,768]{2,1,0:T(8,128)(2,1)} %copy-done.21) | copy-start | bytes 589828
  128.0 23.0 %collective-permute-start.14 = (bf16[4,2432]{1,0:T(4,128)(2,1)S(1)}, bf16[4,2432]{1,0:T(4,128)(2,1)S(1)}, u32[]{:S(2)}, u32[]{:S(2)}) collective-permute-start(bf16[4,2432]{1,0:T(4,128)(2,1)S(1)} %get-tuple-element.45), channel_id=1, source_target_pairs={{0,2},{1,3},{2,0},{3,1},{4,6},{5,7},{6,4},{7,5},{8,10},{9,11},{10,... | collective-permute-start | bytes 58376 | tf_op jit(solution)/shard_map/ppermute | solution.py:76
  140.3 10.7 %collective-permute-start.15 = (bf16[4,2432]{1,0:T(4,128)(2,1)S(1)}, bf16[4,2432]{1,0:T(4,128)(2,1)S(1)}, u32[]{:S(2)}, u32[]{:S(2)}) collective-permute-start(bf16[4,2432]{1,0:T(4,128)(2,1)S(1)} %get-tuple-element.46), channel_id=1, source_target_pairs={{0,4},{1,5},{2,6},{3,7},{4,0},{5,1},{6,2},{7,3},{8,12},{9,13},{10,... | collective-permute-start | bytes 58376 | tf_op jit(solution)/shard_map/ppermute | solution.py:76
  147.1 5.9 %collective-permute-start.16 = (bf16[4,2432]{1,0:T(4,128)(2,1)S(1)}, bf16[4,2432]{1,0:T(4,128)(2,1)S(1)}, u32[]{:S(2)}, u32[]{:S(2)}) collective-permute-start(bf16[4,2432]{1,0:T(4,128)(2,1)S(1)} %get-tuple-element.47), channel_id=1, source_target_pairs={{0,6},{1,7},{2,4},{3,5},{4,2},{5,3},{6,0},{7,1},{8,14},{9,15},{10,... | collective-permute-start | bytes 58376 | tf_op jit(solution)/shard_map/ppermute | solution.py:76

commit v3 on v2

--- a/solution.py
+++ b/solution.py
@@ -1,3 +1,5 @@
+import functools
+
 import jax
 import jax.numpy as jnp
 from jax import lax
@@ -11,6 +13,7 @@
 ROWS = 256
 WIDE = 2 * D
 HALF = 512
+MAIN, BACK, SUMS, SMALL = 18, 16, 12, 6
 COLS = 3 * D + 128
 AXES = ("gx", "gy", "gz")
 FIRST = ("gx", "gy", "gz")
@@ -22,6 +25,8 @@
 NT = (((1,), (1,)), ((), ()))
 TN = (((0,), (0,)), ((), ()))
 VMEM = pl.BlockSpec(memory_space=pltpu.VMEM)
+SMEM = pl.BlockSpec(memory_space=pltpu.SMEM)
+ANY = pl.BlockSpec(memory_space=pl.ANY)
 
 
 def dot(a, b):
@@ -52,16 +57,22 @@
     return k // (4, 2, 1)[AXES.index(axis)] % 2
 
 
-def carried(blocks, axes, steps):
-    at = {k: blocks[k - 1 : k] for k in range(1, 8)}
-    stages = []
-    for axis in axes:
-        moving = [k for k in range(1, 8) if bit(k, axis)]
-        moved = passed_along(jnp.concatenate([at[k] for k in moving]), axis, steps)
-        for i, k in enumerate(moving):
-            at[k] = moved[i : i + 1]
-        stages.append(moved)
-    return stages
+def stage(at, axis, steps):
+    moving = [k for k in range(1, 8) if bit(k, axis)]
+    moved = passed_along(jnp.concatenate([at[k] for k in moving]), axis, steps)
+    return at | {k: moved[i : i + 1] for i, k in enumerate(moving)}, moved
+
+
+def numbered(blocks):
+    return {k: blocks[k - 1 : k] for k in range(1, 8)}
+
+
+def carried(t, g, steps, ways):
+    t, g = numbered(t), numbered(g)
+    for axis_t, axis_g in zip(*ways):
+        t, moved_t = stage(t, axis_t, steps)
+        g, moved_g = stage(g, axis_g, steps)
+        yield moved_t, moved_g
 
 
 def arrival(axes):
@@ -76,11 +87,22 @@
     return lax.ppermute(value, axis, [(source, source ^ mask) for source in range(count)])
 
 
+def named(send_ref):
+    rows = [one_hot(iota((32, ROWS), 1).astype(F32) == column(send_ref[0, k : k + 1, :])) for k in range(7)]
+    return jnp.concatenate(rows, axis=0)
+
+
+def fetches(t_refs, g_refs, axes, to_ref, start, sems):
+    copies = []
+    for part, (refs, way) in enumerate(((t_refs, axes[0]), (g_refs, axes[1]))):
+        for k, (stage, i) in enumerate(arrival(way)):
+            at = to_ref.at[pl.ds(start + 32 * k, 32), pl.ds(part * D, D)]
+            copies.append(pltpu.make_async_copy(refs[stage].at[i], at, sems.at[part, k]))
+    return copies
+
+
 def pack_body(tok_ref, go_ref, send_ref, *outs):
-    chosen = [
-        one_hot(iota((32, ROWS), 1).astype(F32) == column(send_ref[0, k : k + 1, :])) for k in range(7)
-    ]
-    chosen = jnp.concatenate(chosen, axis=0)
+    chosen = named(send_ref)
     for part, ref in enumerate((tok_ref, go_ref)):
         outs[part][...] = dot(chosen, ref[...]).astype(BF).reshape(7, 32, D)
 
@@ -102,34 +124,41 @@
     return iota((HALF, D), 1) == row
 
 
-def half_sums(gz, core, normed, mixed, gos, dpacked_ref, out_ref):
+def half_sums(core, me_ref, normed_ref, mixed_ref, gos_ref, dpacked_ref, gain_ref, out_ref):
+    gz = me_ref[0]
     place = half_place(gz, core)
-    turned = lax.dot_general(one_hot(place), normed, NT, preferred_element_type=F32).astype(BF)
+    turned = lax.dot_general(one_hot(place), normed_ref[...], NT, preferred_element_type=F32).astype(BF)
     i = iota((384, 1), 0)
     picks = one_hot(iota((384, D), 1) == first_row(gz, core, i % 128) + i // 128)
-    picks = lax.dot_general(picks, mixed, NT, preferred_element_type=F32).astype(BF)
-    proj = dot(picks, gos).astype(BF)
+    picks = lax.dot_general(picks, mixed_ref[...], NT, preferred_element_type=F32).astype(BF)
+    proj = dot(picks, gos_ref[...]).astype(BF)
     j = iota((HALF, 1), 0)
     widen = one_hot(iota((HALF, 128), 1) == jnp.where(j % 4 == 3, j // 4, -1))
     for g in range(3):
         at = slice(g * D, (g + 1) * D)
         total = dot(turned, dpacked_ref[:, at]) + dot(widen, proj[g * 128 : (g + 1) * 128])
         out_ref[:, at] = total.astype(BF)
-    return place
+    gains = jnp.sum(jnp.where(place, gain_ref[...], 0.0), axis=1, keepdims=True)
+    out_ref[:, 3 * D :] = jnp.broadcast_to(gains, (HALF, 128)).astype(BF)
 
 
 def main_body(
-    me_ref, tok_ref, go_ref, t_refs, g_refs, win_ref, gain_ref, wqkv_ref, wout_ref,
-    snd_ref, xs_ref, gos_ref, normed_ref, mixed_ref, dpacked_ref,
-    rows_ref, packed_ref, delta_ref,
+    tok_ref, go_ref, t_refs, g_refs, win_ref, gain_ref, wqkv_ref, wout_ref,
+    xs_ref, gos_ref, normed_ref, mixed_ref, dpacked_ref,
+    rows_ref, packed_ref, delta_ref, held_ref, sems,
 ):
-    rows_ref[:ROWS, :D] = tok_ref[...]
-    rows_ref[:ROWS, D:] = go_ref[...]
-    for part, (refs, axes) in enumerate(((t_refs, FIRST), (g_refs, SECOND))):
-        for k, (stage, i) in enumerate(arrival(axes)):
-            rows_ref[ROWS + 32 * k : ROWS + 32 * (k + 1), part * D : (part + 1) * D] = refs[stage][i]
+    copies = fetches(t_refs, g_refs, (FIRST, SECOND), rows_ref, ROWS, sems)
+    own = rows_ref.at[pl.ds(0, ROWS), :]
+    copies.append(pltpu.make_async_copy(tok_ref, own.at[:, pl.ds(0, D)], sems.at[0, 7]))
+    copies.append(pltpu.make_async_copy(go_ref, own.at[:, pl.ds(D, D)], sems.at[1, 7]))
+    weights_copy = pltpu.make_async_copy(wout_ref, held_ref, sems.at[2, 0])
+    for copy in copies:
+        copy.start()
+    weights_copy.start()
     rows_ref[480:, :] = jnp.zeros((32, WIDE), BF)
     gain = gain_ref[...]
+    for copy in copies:
+        copy.wait()
 
     def gather_window(w, carry):
         at = pl.ds(pl.multiple_of(w * WCAP, WCAP), WCAP)
@@ -150,8 +179,9 @@
         return carry
 
     lax.fori_loop(0, 3, project, 0)
+    weights_copy.wait()
     delta_ref[...] = lax.dot_general(
-        gos_ref[...], wout_ref[...], NT, preferred_element_type=F32
+        gos_ref[...], held_ref[...], NT, preferred_element_type=F32
     ).astype(BF)
 
     low = iota((WCAP, 128), 1) < 64
@@ -196,20 +226,12 @@
 
     lax.fori_loop(0, SLOTS // WCAP, attend, 0)
 
-    half_sums(
-        me_ref[0], 1, normed_ref[...], mixed_ref[...], gos_ref[...], dpacked_ref, snd_ref
-    )
-
 
 def back_body(
-    me_ref, xs_ref, gos_ref, normed_ref, mixed_ref, dpacked_ref, win_ref, gain_ref, wqkv_ref, wout_ref,
-    own_ref, gain_own_ref, gain_snd_ref, kept_ref, *rest,
+    xs_ref, gos_ref, mixed_ref, dpacked_ref, win_ref, gain_ref, wqkv_ref, wout_ref,
+    t_ref, g_ref, kept_ref, gain_sum_ref, cat_ref, dn_ref,
 ):
-    ret_refs, cat_ref, dn_ref = rest[:-2], rest[-2], rest[-1]
     gain = gain_ref[...]
-    place = half_sums(
-        me_ref[0], 0, normed_ref[...], mixed_ref[...], gos_ref[...], dpacked_ref, own_ref
-    )
     dn_ref[...] = lax.dot_general(
         dpacked_ref[...], wqkv_ref[...], NT, preferred_element_type=F32
     ).astype(BF)
@@ -231,28 +253,27 @@
     back = one_hot(iota((480, SLOTS), 0) == win_ref[...])
     kept_ref[...] = dot(back[:ROWS], cat_ref[...]).astype(BF)
     sent = dot(back[ROWS:], cat_ref[...]).astype(BF).reshape(7, 32, WIDE)
-    for part, ref in enumerate(ret_refs):
-        ref[...] = sent[:, :, part * D : (part + 1) * D]
-    own = jnp.where(place, gain_row, 0.0)
-    gain_own_ref[...] = jnp.broadcast_to(jnp.sum(own, axis=1, keepdims=True), (HALF, 128))
-    other = half_place(me_ref[0], 1)
-    own = jnp.where(other, gain_row, 0.0)
-    gain_snd_ref[...] = jnp.broadcast_to(jnp.sum(own, axis=1, keepdims=True), (HALF, 128))
-
-
-def join_body(kept_ref, t_refs, g_refs, send_ref, out_ref, grad_ref):
-    for part, (refs, axes, out) in enumerate(
-        ((t_refs, FIRST, out_ref), (g_refs, SECOND, grad_ref))
-    ):
-        total = kept_ref[:, part * D : (part + 1) * D].astype(F32)
-        for k, (stage, i) in enumerate(arrival(axes[::-1])):
-            total += dot(one_hot(iota((ROWS, 32), 0) == send_ref[0, k : k + 1, :]), refs[stage][i])
-        out[...] = total.astype(BF)
-
-
-def sum1_body(own_ref, got_ref, gain_own_ref, gain_got_ref, out_ref):
-    out_ref[:, : 3 * D] = (own_ref[...].astype(F32) + got_ref[...].astype(F32)).astype(BF)
-    out_ref[:, 3 * D :] = (gain_own_ref[...] + gain_got_ref[...]).astype(BF)
+    t_ref[...] = sent[:, :, :D]
+    g_ref[...] = sent[:, :, D:]
+    gain_sum_ref[...] = gain_row
+
+
+def join_body(kept_ref, t_refs, g_refs, send_ref, out_ref, grad_ref, own_ref, rows_ref, sems):
+    copies = fetches(t_refs, g_refs, (FIRST[::-1], SECOND[::-1]), rows_ref, 0, sems)
+    copies.append(pltpu.make_async_copy(kept_ref, own_ref, sems.at[2, 0]))
+    for copy in copies:
+        copy.start()
+    chosen = named(send_ref)
+    for copy in copies:
+        copy.wait()
+    for part, out in enumerate((out_ref, grad_ref)):
+        at = slice(part * D, (part + 1) * D)
+        back = lax.dot_general(chosen, rows_ref[:, at], TN, preferred_element_type=F32)
+        out[...] = (own_ref[:, at].astype(F32) + back).astype(BF)
+
+
+def sum1_body(own_ref, got_ref, out_ref):
+    out_ref[...] = (own_ref[...].astype(F32) + got_ref[...].astype(F32)).astype(BF)
 
 
 def sum2_body(got_ref, *outs):
@@ -270,7 +291,7 @@
     gain_ref[...] = total[:3, 3 * D :]
 
 
-def call(body, shapes, *args, scratch=(), smem=(), mib=16):
+def call(body, shapes, *args, scratch=(), smem=(), outside=(), mib=SMALL):
     tree = jax.tree.structure(args)
     count = tree.num_leaves
 
@@ -280,7 +301,7 @@
     return pl.pallas_call(
         flat,
         out_shape=[jax.ShapeDtypeStruct(shape, dtype) for shape, dtype in shapes],
-        in_specs=[pl.BlockSpec(memory_space=pltpu.SMEM) if i in smem else VMEM for i in range(count)],
+        in_specs=[ANY if i in outside else SMEM if i in smem else VMEM for i in range(count)],
         out_specs=[VMEM] * len(shapes),
         scratch_shapes=list(scratch),
         compiler_params=pltpu.CompilerParams(vmem_limit_bytes=mib * 1024 * 1024),
@@ -290,33 +311,45 @@
 def on_device(tokens, norm_gain, w_qkv, w_out, send_rows, window_rows, grad_out):
     gain = norm_gain.reshape(1, D)
     me = lax.axis_index("gz").astype(jnp.int32).reshape(1)
+    me, tokens, grad_out = lax.optimization_barrier((me, tokens, grad_out))
     lists = ((7, 32, D), BF)
     blocks = call(pack_body, [lists, lists], tokens, grad_out, send_rows)
-    arrived_t = carried(blocks[0], FIRST, 1)
-    arrived_g = carried(blocks[1], SECOND, 1)
-
-    slot, wide, half = ((SLOTS, D), BF), ((SLOTS, 3 * D), BF), ((HALF, 3 * D), BF)
-    gains = ((HALF, 128), F32)
-    sent, xs, gos, normed, mixed, dpacked = call(
+    arrived_t, arrived_g = zip(*carried(*blocks, 1, (FIRST, SECOND)))
+
+    slot, wide, half = ((SLOTS, D), BF), ((SLOTS, 3 * D), BF), ((HALF, COLS), BF)
+    xs, gos, normed, mixed, dpacked = call(
         main_body,
-        [half, slot, slot, slot, slot, wide],
-        me, tokens, grad_out, arrived_t, arrived_g, window_rows, gain, w_qkv, w_out,
-        scratch=[pltpu.VMEM((SLOTS, WIDE), BF), pltpu.VMEM(*wide), pltpu.VMEM(*slot)],
-        smem=(0,),
-        mib=34,
-    )
+        [slot, slot, slot, slot, wide],
+        tokens, grad_out, arrived_t, arrived_g, window_rows, gain, w_qkv, w_out,
+        scratch=[
+            pltpu.VMEM((SLOTS, WIDE), BF),
+            pltpu.VMEM(*wide),
+            pltpu.VMEM(*slot),
+            pltpu.VMEM((D, D), BF),
+            pltpu.SemaphoreType.DMA((3, 8)),
+        ],
+        outside=(0, 1, 2, 3, 4, 5, 6, 7, 11),
+        mib=MAIN,
+    )
+    back_t, back_g, kept, gain_sum = call(
+        back_body,
+        [lists, lists, ((ROWS, WIDE), BF), ((1, D), F32)],
+        xs, gos, mixed, dpacked, window_rows, gain, w_qkv, w_out,
+        scratch=[pltpu.VMEM((SLOTS, WIDE), BF), pltpu.VMEM(*slot)],
+        mib=BACK,
+    )
+    way = carried(back_t, back_g, -1, (FIRST[::-1], SECOND[::-1]))
+    first = next(way)
+    operands = (me, normed, mixed, gos, dpacked, gain_sum)
+    (sent,) = call(functools.partial(half_sums, 1), [half], *operands, smem=(0,), mib=SUMS)
     got = crossed(sent, "gz", 1)
-    own, gain_own, gain_sent, kept, *back = call(
-        back_body,
-        [half, gains, gains, ((ROWS, WIDE), BF), lists, lists],
-        me, xs, gos, normed, mixed, dpacked, window_rows, gain, w_qkv, w_out,
-        scratch=[pltpu.VMEM((SLOTS, WIDE), BF), pltpu.VMEM(*slot)],
-        smem=(0,),
-        mib=34,
-    )
-    gain_got = crossed(gain_sent, "gz", 1)
-
-    (paired,) = call(sum1_body, [((HALF, COLS), BF)], own, got, gain_own, gain_got)
+    operands, first = lax.optimization_barrier((operands, first))
+    (own,) = call(functools.partial(half_sums, 0), [half], *operands, smem=(0,), mib=SUMS)
+
+    (paired,) = call(sum1_body, [half], own, got)
+    second = next(way)
+    paired, second = lax.optimization_barrier((paired, second))
+    third = next(way)
     spread = lax.all_to_all(paired, ("gx", "gy"), split_axis=0, concat_axis=0, tiled=True)
     parts = call(sum2_body, [((4, COLS), BF)] * 4, spread.reshape(32, 16, COLS))
     last = [parts[0]] + [crossed(parts[i], "gz", 2 * i) for i in range(1, 4)]
@@ -327,10 +360,13 @@
     block_out, grad_tokens = call(
         join_body,
         [((ROWS, D), BF), ((ROWS, D), BF)],
-        kept,
-        carried(back[0], FIRST[::-1], -1),
-        carried(back[1], SECOND[::-1], -1),
-        send_rows,
+        kept, *zip(first, second, third), send_rows,
+        scratch=[
+            pltpu.VMEM((ROWS, WIDE), BF),
+            pltpu.VMEM((224, WIDE), BF),
+            pltpu.SemaphoreType.DMA((3, 8)),
+        ],
+        outside=range(7),
     )
     return (block_out, grad_tokens, gain_rows[:, 0], grad_qkv, grad_proj)
 

time: 157 us -> 142 us (0.904)
  the two profiles are of different devices: /device:TPU:10 before, /device:TPU:42 now
where the time goes in v3:
time: 142 us; the launch traced here: 141 us
  starting transfers between devices  61.5 us (43%)
  waiting for transfers between devices  36.3 us (26%)
  Pallas kernels  31.5 us (22%)
  local copies, waits for them, and re-layouts  7.53 us (5%)
  other arithmetic  3.24 us (2%)
    ppermute x12, starting transfers between devices, passed_along(): lax.ppermute(value, axis, [(source, source + steps) for source in range(i...  32.1 us
    pallas_call x9, Pallas kernels, call(): pl.pallas_call(flat, out_shape=[jax.ShapeDtypeStruct(shape, dtype) for sh...  31.5 us
    ppermute x4, starting transfers between devices, crossed(): lax.ppermute(value, axis, [(source, source ^ mask) for source in range(co...  20.2 us
    all_to_all x1, waiting for transfers between devices, on_device(): lax.all_to_all(paired, ('gx', 'gy'), split_axis=0, concat_axis=0, tiled=T...  18.7 us
    ppermute x12, waiting for transfers between devices, passed_along(): lax.ppermute(value, axis, [(source, source + steps) for source in range(i...  14.3 us
    all_to_all x1, starting transfers between devices, on_device(): lax.all_to_all(paired, ('gx', 'gy'), split_axis=0, concat_axis=0, tiled=T...  9.17 us
    unnamed x21, local copies, waits for them, and re-layouts  3.7 us
    ppermute x4, waiting for transfers between devices, crossed(): lax.ppermute(value, axis, [(source, source ^ mask) for source in range(co...  3.28 us
  transfers between devices with their start and end apart: 17, of which 6 were waited for; matrix products, arithmetic and copies ran while one was open for 5% of the time, Pallas kernels for 6%

profile of v3, /device:TPU:42, one launch (start us, length us, event | category | flops | bytes accessed | tf_op | source)
XLA Modules:
  0.0 141.1 jit_solution(8505496810445044285)
XLA Ops:
  0.6 0.7 copy.14.refs_2_.refs_7_
  1.3 0.0 copy-start.2
  1.3 1.0 copy-done.2
  2.3 1.0 copy-done.4
  3.3 0.0 copy-start.8
  3.3 0.4 shard_map.110
  3.8 3.2 %collective-permute-start = (bf16[4,32,768]{2,1,0:T(8,128)(2,1)S(1)}, bf16[4,32,768]{2,1,0:T(8,128)(2,1)S(1)}, u32[]{:S(2)}, u32[]{:S(2)}) collective-permute-start(bf16[4,32,768]{2,1,0:T(8,128)(2,1)S(1)} %slice.132), channel_id=1, source_target_pairs={{0,32},{32,64},{64,96},{96,128},{128,160},{160,192},{192,224},{1,3... | collective-permute-start | bytes 589832 | tf_op jit(solution)/shard_map/ppermute | solution.py:53
  7.0 3.5 %collective-permute-start.3 = (bf16[4,32,768]{2,1,0:T(8,128)(2,1)S(1)}, bf16[4,32,768]{2,1,0:T(8,128)(2,1)S(1)}, u32[]{:S(2)}, u32[]{:S(2)}) collective-permute-start(bf16[4,32,768]{2,1,0:T(8,128)(2,1)S(1)} %pad_maximum_fusion.2), channel_id=1, source_target_pairs={{0,8},{8,16},{16,24},{1,9},{9,17},{17,25},{2,10},{10,18},{18,26},{... | collective-permute-start | bytes 589832 | tf_op jit(solution)/shard_map/ppermute | solution.py:53
  10.6 2.0 %collective-permute-done.refs_2_ = bf16[4,32,768]{2,1,0:T(8,128)(2,1)S(1)} collective-permute-done((bf16[4,32,768]{2,1,0:T(8,128)(2,1)S(1)}, bf16[4,32,768]{2,1,0:T(8,128)(2,1)S(1)}, u32[]{:S(2)}, u32[]{:S(2)}) %collective-permute-start) | collective-permute-done | bytes 196640 | tf_op jit(solution)/shard_map/ppermute | solution.py:53
  12.6 3.5 %collective-permute-start.1 = (bf16[4,32,768]{2,1,0:T(8,128)(2,1)S(1)}, bf16[4,32,768]{2,1,0:T(8,128)(2,1)S(1)}, u32[]{:S(2)}, u32[]{:S(2)}) collective-permute-start(bf16[4,32,768]{2,1,0:T(8,128)(2,1)S(1)} %pad_maximum_fusion), channel_id=1, source_target_pairs={{0,8},{8,16},{16,24},{1,9},{9,17},{17,25},{2,10},{10,18},{18,26},{... | collective-permute-start | bytes 589832 | tf_op jit(solution)/shard_map/ppermute | solution.py:53
  16.1 0.0 collective-permute-done.3.refs_5_
  16.2 1.3 collective-permute-start.4
  17.5 2.8 %collective-permute-done.1.refs_3_ = bf16[4,32,768]{2,1,0:T(8,128)(2,1)S(1)} collective-permute-done((bf16[4,32,768]{2,1,0:T(8,128)(2,1)S(1)}, bf16[4,32,768]{2,1,0:T(8,128)(2,1)S(1)}, u32[]{:S(2)}, u32[]{:S(2)}) %collective-permute-start.1) | collective-permute-done | bytes 196640 | tf_op jit(solution)/shard_map/ppermute | solution.py:53
  20.3 3.1 %collective-permute-start.2 = (bf16[4,32,768]{2,1,0:T(8,128)(2,1)S(1)}, bf16[4,32,768]{2,1,0:T(8,128)(2,1)S(1)}, u32[]{:S(2)}, u32[]{:S(2)}) collective-permute-start(bf16[4,32,768]{2,1,0:T(8,128)(2,1)S(1)} %pad_maximum_fusion.1), channel_id=1, source_target_pairs={{0,1},{1,2},{2,3},{3,4},{4,5},{5,6},{6,7},{8,9},{9,10},{10,11},{11... | collective-permute-start | bytes 589832 | tf_op jit(solution)/shard_map/ppermute | solution.py:53
  23.5 0.0 collective-permute-done.4.refs_6_
  23.5 3.8 %collective-permute-start.5 = (bf16[4,32,768]{2,1,0:T(8,128)(2,1)S(1)}, bf16[4,32,768]{2,1,0:T(8,128)(2,1)S(1)}, u32[]{:S(2)}, u32[]{:S(2)}) collective-permute-start(bf16[4,32,768]{2,1,0:T(8,128)(2,1)S(1)} %pad_maximum_fusion.4), channel_id=1, source_target_pairs={{0,32},{32,64},{64,96},{96,128},{128,160},{160,192},{192,224},{1,3... | collective-permute-start | bytes 589832 | tf_op jit(solution)/shard_map/ppermute | solution.py:53
  27.4 0.0 copy-done.9
  27.4 0.0 collective-permute-done.2.refs_4_
  27.4 5.2 %collective-permute-done.5.refs_7_ = bf16[4,32,768]{2,1,0:T(8,128)(2,1)S(1)} collective-permute-done((bf16[4,32,768]{2,1,0:T(8,128)(2,1)S(1)}, bf16[4,32,768]{2,1,0:T(8,128)(2,1)S(1)}, u32[]{:S(2)}, u32[]{:S(2)}) %collective-permute-start.5) | collective-permute-done | bytes 196640 | tf_op jit(solution)/shard_map/ppermute | solution.py:53
  32.6 0.0 copy-done
  32.6 0.0 copy-done.1
  32.6 0.0 copy-done.3
  32.6 0.0 copy-done.8
  32.6 0.0 copy-start.5
  32.6 1.0 copy-done.5
  33.6 14.4 %shard_map.111 = (bf16[512,768]{1,0:T(8,128)(2,1)S(1)}, bf16[512,768]{1,0:T(8,128)(2,1)S(1)}, bf16[512,768]{1,0:T(8,128)(2,1)S(1)}, bf16[512,768]{1,0:T(8,128)(2,1)S(1)}, bf16[512,2304]{1,0:T(8,128)(2,1)S(1)}) custom-call(bf16[256,768]{1,0:T(8,128)(2,1)S(1)} %copy-done.3, bf16[256,768]{1,0:T(8,128)(2,1)S(1)} %copy-done.5, ...), custom_call_target="tpu_custom_call" | custom-call | tf_op jit(solution)/shard_map/pallas_call | solution.py:301
  48.1 4.3 %shard_map.112 = (bf16[7,32,768]{2,1,0:T(8,128)(2,1)S(1)}, bf16[7,32,768]{2,1,0:T(8,128)(2,1)S(1)}, bf16[256,1536]{1,0:T(8,128)(2,1)S(1)}, f32[1,768]{1,0:T(1,128)S(1)}) custom-call(bf16[512,768]{1,0:T(8,128)(2,1)S(1)} %get-tuple-element.43.refs_0_, bf16[512,768]{1,0:T(8,128)(2,1)S(1)} %get-tuple-element.57.refs_1_.refs_3_, ...), custom_call_target="tpu_custom_call" | custom-call | tf_op jit(solution)/shard_map/pallas_call | solution.py:301
  52.3 3.5 %shard_map.114 = bf16[512,2432]{1,0:T(8,128)(2,1)S(1)} custom-call(s32[1]{0:T(128)} %bitcast.refs_0_, bf16[512,768]{1,0:T(8,128)(2,1)S(1)} %get-tuple-element.55.refs_1_, bf16[512,768]{1,0:T(8,128)(2,1)S(1)} %get-tuple-element.56.refs_2_, bf16[512,768]{1,0:T(8,128)(2,1)S(1)} %get-tuple-element.57.refs_1_.refs_3_, ...), custom_call_target="tpu_custom_call" | custom-call | tf_op jit(solution)/shard_map/pallas_call | solution.py:301
  55.8 1.1 collective-permute-start.8
  56.9 0.7 fusion
  57.6 1.3 collective-permute-start.6
  58.9 3.3 %collective-permute-start.7 = (bf16[4,32,768]{2,1,0:T(8,128)(2,1)S(1)}, bf16[4,32,768]{2,1,0:T(8,128)(2,1)S(1)}, u32[]{:S(2)}, u32[]{:S(2)}) collective-permute-start(bf16[4,32,768]{2,1,0:T(8,128)(2,1)S(1)} %slice.153), channel_id=1, source_target_pairs={{32,0},{64,32},{96,64},{128,96},{160,128},{192,160},{224,192},{33,... | collective-permute-start | bytes 589832 | tf_op jit(solution)/shard_map/ppermute | solution.py:53
  62.2 0.0 collective-permute-done.6.refs_1_
  62.3 2.7 %collective-permute-start.9 = (bf16[4,32,768]{2,1,0:T(8,128)(2,1)S(1)}, bf16[4,32,768]{2,1,0:T(8,128)(2,1)}, u32[]{:S(2)}, u32[]{:S(2)}) collective-permute-start(bf16[4,32,768]{2,1,0:T(8,128)(2,1)S(1)} %pad_maximum_fusion.6), channel_id=1, source_target_pairs={{8,0},{16,8},{24,16},{9,1},{17,9},{25,17},{10,2},{18,10},{26,18},{... | collective-permute-start | bytes 589832 | tf_op jit(solution)/shard_map/ppermute | solution.py:53
  65.0 4.4 %collective-permute-done.7.refs_4_ = bf16[4,32,768]{2,1,0:T(8,128)(2,1)S(1)} collective-permute-done((bf16[4,32,768]{2,1,0:T(8,128)(2,1)S(1)}, bf16[4,32,768]{2,1,0:T(8,128)(2,1)S(1)}, u32[]{:S(2)}, u32[]{:S(2)}) %collective-permute-start.7) | collective-permute-done | bytes 196640 | tf_op jit(solution)/shard_map/ppermute | solution.py:53
  69.3 0.7 fusion.5
  70.0 1.5 %collective-permute-start.10 = (bf16[4,32,768]{2,1,0:T(8,128)(2,1)S(1)}, bf16[4,32,768]{2,1,0:T(8,128)(2,1)}, u32[]{:S(2)}, u32[]{:S(2)}) collective-permute-start(bf16[4,32,768]{2,1,0:T(8,128)(2,1)S(1)} %pad_maximum_fusion.7), channel_id=1, source_target_pairs={{1,0},{2,1},{3,2},{4,3},{5,4},{6,5},{7,6},{9,8},{10,9},{11,10},{12... | collective-permute-start | bytes 589832 | tf_op jit(solution)/shard_map/ppermute | solution.py:53
  71.5 3.5 %shard_map.113.refs_0_ = bf16[512,2432]{1,0:T(8,128)(2,1)S(1)} custom-call(s32[1]{0:T(128)} %bitcast.refs_0_, bf16[512,768]{1,0:T(8,128)(2,1)S(1)} %get-tuple-element.55.refs_1_, bf16[512,768]{1,0:T(8,128)(2,1)S(1)} %get-tuple-element.56.refs_2_, bf16[512,768]{1,0:T(8,128)(2,1)S(1)} %get-tuple-element.57.refs_1_.refs_3_, ...), custom_call_target="tpu_custom_call" | custom-call | tf_op jit(solution)/shard_map/pallas_call | solution.py:301
  75.0 0.0 copy-done.6
  75.0 0.0 collective-permute-done.8.refs_1_
  75.0 2.0 %shard_map.115 = bf16[512,2432]{1,0:T(8,128)(2,1)} custom-call(bf16[512,2432]{1,0:T(8,128)(2,1)S(1)} %shard_map.113.refs_0_, bf16[512,2432]{1,0:T(8,128)(2,1)S(1)} %collective-permute-done.8.refs_1_), custom_call_target="tpu_custom_call" | custom-call | tf_op jit(solution)/shard_map/pallas_call | solution.py:301
  77.0 0.0 collective-permute-done.9.refs_2_
  77.0 0.0 collective-permute-done.10.refs_5_
  77.0 9.2 %all-to-all-start = ((bf16[32,16,2432]{2,1,0:T(8,128)(2,1)}), bf16[32,16,2432]{2,1,0:T(8,128)(2,1)S(1)}, u32[]{:S(2)}, u32[]{:S(2)}) async-start(bf16[32,16,2432]{2,1,0:T(8,128)(2,1)} %bitcast.1), calls=%async_computation | async-start | bytes 4980736 | tf_op jit(solution)/shard_map/all_to_all | solution.py:353
  86.2 0.9 slice.184
  87.1 1.5 %pad_maximum_fusion.8 = bf16[4,32,768]{2,1,0:T(8,128)(2,1)} fusion(bf16[2,32,768]{2,1,0:T(8,128)(2,1)S(1)} %slice.184, bf16[1,32,768]{2,1,0:T(8,128)(2,1)S(1)} %get-tuple-element.93, bf16[1,32,768]{2,1,0:T(8,128)(2,1)} %get-tuple-element.109), kind=kLoop, calls=%fused_computation.8 | loop fusion | flops 196608 | bytes 393216 | tf_op jit(solution)/shard_map/concatenate | solution.py:62
  88.6 2.5 %collective-permute-start.11 = (bf16[4,32,768]{2,1,0:T(8,128)(2,1)}, bf16[4,32,768]{2,1,0:T(8,128)(2,1)}, u32[]{:S(2)}, u32[]{:S(2)}) collective-permute-start(bf16[4,32,768]{2,1,0:T(8,128)(2,1)} %pad_maximum_fusion.8), channel_id=1, source_target_pairs={{32,0},{64,32},{96,64},{128,96},{160,128},{192,160},{224,192},{33,... | collective-permute-start | bytes 589832 | tf_op jit(solution)/shard_map/ppermute | solution.py:53
  91.1 0.8 fusion.4
  91.9 1.5 %pad_maximum_fusion.9 = bf16[4,32,768]{2,1,0:T(8,128)(2,1)} fusion(bf16[1,32,768]{2,1,0:T(8,128)(2,1)S(1)} %get-tuple-element.89, bf16[1,32,768]{2,1,0:T(8,128)(2,1)} %get-tuple-element.90, bf16[1,32,768]{2,1,0:T(8,128)(2,1)S(1)} %get-tuple-element.88, bf16[1,32,768]{2,1,0:T(8,128)(2,1)} %get-tuple-element.73), kind=kLoop, calls=%fused_computation.9 | loop fusion | flops 294912 | bytes 393216 | tf_op jit(solution)/shard_map/concatenate | solution.py:62
  93.4 2.5 %collective-permute-start.12 = (bf16[4,32,768]{2,1,0:T(8,128)(2,1)}, bf16[4,32,768]{2,1,0:T(8,128)(2,1)}, u32[]{:S(2)}, u32[]{:S(2)}) collective-permute-start(bf16[4,32,768]{2,1,0:T(8,128)(2,1)} %pad_maximum_fusion.9), channel_id=1, source_target_pairs={{8,0},{16,8},{24,16},{9,1},{17,9},{25,17},{10,2},{18,10},{26,18},{... | collective-permute-start | bytes 589832 | tf_op jit(solution)/shard_map/ppermute | solution.py:53
  95.9 18.7 %all-to-all-done.refs_0_ = bf16[32,16,2432]{2,1,0:T(8,128)(2,1)S(1)} async-done(((bf16[32,16,2432]{2,1,0:T(8,128)(2,1)}), bf16[32,16,2432]{2,1,0:T(8,128)(2,1)S(1)}, u32[]{:S(2)}, u32[]{:S(2)}) %all-to-all-start) | async-done | bytes 2490400 | tf_op jit(solution)/shard_map/all_to_all | solution.py:353
  114.6 0.4 shard_map.117
  115.0 8.2 %collective-permute-start.13 = (bf16[4,2432]{1,0:T(4,128)(2,1)S(1)}, bf16[4,2432]{1,0:T(4,128)(2,1)S(1)}, u32[]{:S(2)}, u32[]{:S(2)}) collective-permute-start(bf16[4,2432]{1,0:T(4,128)(2,1)S(1)} %get-tuple-element.67), channel_id=1, source_target_pairs={{0,2},{1,3},{2,0},{3,1},{4,6},{5,7},{6,4},{7,5},{8,10},{9,11},{10,... | collective-permute-start | bytes 58376 | tf_op jit(solution)/shard_map/ppermute | solution.py:87
  123.2 10.8 %collective-permute-start.14 = (bf16[4,2432]{1,0:T(4,128)(2,1)S(1)}, bf16[4,2432]{1,0:T(4,128)(2,1)S(1)}, u32[]{:S(2)}, u32[]{:S(2)}) collective-permute-start(bf16[4,2432]{1,0:T(4,128)(2,1)S(1)} %get-tuple-element.68), channel_id=1, source_target_pairs={{0,4},{1,5},{2,6},{3,7},{4,0},{5,1},{6,2},{7,3},{8,12},{9,13},{10,... | collective-permute-start | bytes 58376 | tf_op jit(solution)/shard_map/ppermute | solution.py:87
  134.0 0.1 collective-permute-start.15
  134.1 0.0 collective-permute-done.11.refs_3_
  134.1 0.0 collective-permute-done.12.refs_6_
  134.1 0.0 copy-done.7
  134.1 2.5 %shard_map.116 = (bf16[256,768]{1,0:T(8,128)(2,1)}, bf16[256,768]{1,0:T(8,128)(2,1)}) custom-call(bf16[256,1536]{1,0:T(8,128)(2,1)S(1)} %get-tuple-element.47.refs_0_, bf16[4,32,768]{2,1,0:T(8,128)(2,1)S(1)} %collective-permute-done.6.refs_1_, bf16[4,32,768]{2,1,0:T(8,128)(2,1)} %collective-permute-done.9.refs_2_, ...), custom_call_target="tpu_custom_call" | custom-call | tf_op jit(solution)/shard_map/pallas_call | solution.py:301
  136.6 0.0 collective-permute-done.13.refs_1_
  136.6 0.0 collective-permute-done.14.refs_2_
  136.6 3.3 %collective-permute-done.15.refs_3_ = bf16[4,2432]{1,0:T(4,128)(2,1)S(1)} collective-permute-done((bf16[4,2432]{1,0:T(4,128)(2,1)S(1)}, bf16[4,2432]{1,0:T(4,128)(2,1)S(1)}, u32[]{:S(2)}, u32[]{:S(2)}) %collective-permute-start.15) | collective-permute-done | bytes 19488 | tf_op jit(solution)/shard_map/ppermute | solution.py:87
  139.9 0.6 shard_map.118
  140.5 0.6 slice_reduce_fusion
  (28 shorter events, 0.4 us)
Async XLA Ops:
  1.3 1.0 copy-start.2
  2.3 1.0 copy-start.4
  3.3 24.1 %copy-start.9 = (f32[768]{0:T(1024)S(1)}, f32[768]{0:T(1024)}, u32[]{:S(2)}) copy-start(f32[768]{0:T(1024)} %param.8) | copy-start | bytes 9220
  3.3 29.3 %copy-start = (bf16[768,2304]{1,0:T(8,128)(2,1)S(1)}, bf16[768,2304]{1,0:T(8,128)(2,1)}, u32[]{:S(2)}) copy-start(bf16[768,2304]{1,0:T(8,128)(2,1)} %refs_6_.1) | copy-start | bytes 10616836
  3.3 29.3 %copy-start.1 = (bf16[768,768]{1,0:T(8,128)(2,1)S(1)}, bf16[768,768]{1,0:T(8,128)(2,1)}, u32[]{:S(2)}) copy-start(bf16[768,768]{1,0:T(8,128)(2,1)} %refs_7_.2) | copy-start | bytes 3538948
  3.3 29.3 %copy-start.3 = (bf16[256,768]{1,0:T(8,128)(2,1)S(1)}, bf16[256,768]{1,0:T(8,128)(2,1)}, u32[]{:S(2)}) copy-start(bf16[256,768]{1,0:T(8,128)(2,1)} %refs_0_.1) | copy-start | bytes 1179652
  3.3 29.3 %copy-start.8 = (s32[1,512]{1,0:T(1,128)S(1)}, s32[1,512]{1,0:T(1,128)}, u32[]{:S(2)}) copy-start(s32[1,512]{1,0:T(1,128)} %refs_4_.1) | copy-start | bytes 6148
  3.8 8.8 %collective-permute-start = (bf16[4,32,768]{2,1,0:T(8,128)(2,1)S(1)}, bf16[4,32,768]{2,1,0:T(8,128)(2,1)S(1)}, u32[]{:S(2)}, u32[]{:S(2)}) collective-permute-start(bf16[4,32,768]{2,1,0:T(8,128)(2,1)S(1)} %slice.132), channel_id=1, source_target_pairs={{0,32},{32,64},{64,96},{96,128},{128,160},{160,192},{192,224},{1,3... | collective-permute-start | bytes 589832 | tf_op jit(solution)/shard_map/ppermute | solution.py:53
  7.0 9.1 %collective-permute-start.3 = (bf16[4,32,768]{2,1,0:T(8,128)(2,1)S(1)}, bf16[4,32,768]{2,1,0:T(8,128)(2,1)S(1)}, u32[]{:S(2)}, u32[]{:S(2)}) collective-permute-start(bf16[4,32,768]{2,1,0:T(8,128)(2,1)S(1)} %pad_maximum_fusion.2), channel_id=1, source_target_pairs={{0,8},{8,16},{16,24},{1,9},{9,17},{17,25},{2,10},{10,18},{18,26},{... | collective-permute-start | bytes 589832 | tf_op jit(solution)/shard_map/ppermute | solution.py:53
  12.6 7.7 %collective-permute-start.1 = (bf16[4,32,768]{2,1,0:T(8,128)(2,1)S(1)}, bf16[4,32,768]{2,1,0:T(8,128)(2,1)S(1)}, u32[]{:S(2)}, u32[]{:S(2)}) collective-permute-start(bf16[4,32,768]{2,1,0:T(8,128)(2,1)S(1)} %pad_maximum_fusion), channel_id=1, source_target_pairs={{0,8},{8,16},{16,24},{1,9},{9,17},{17,25},{2,10},{10,18},{18,26},{... | collective-permute-start | bytes 589832 | tf_op jit(solution)/shard_map/ppermute | solution.py:53
  16.2 7.3 %collective-permute-start.4 = (bf16[4,32,768]{2,1,0:T(8,128)(2,1)S(1)}, bf16[4,32,768]{2,1,0:T(8,128)(2,1)S(1)}, u32[]{:S(2)}, u32[]{:S(2)}) collective-permute-start(bf16[4,32,768]{2,1,0:T(8,128)(2,1)S(1)} %pad_maximum_fusion.3), channel_id=1, source_target_pairs={{0,1},{1,2},{2,3},{3,4},{4,5},{5,6},{6,7},{8,9},{9,10},{10,11},{11... | collective-permute-start | bytes 589832 | tf_op jit(solution)/shard_map/ppermute | solution.py:53
  20.3 7.1 %collective-permute-start.2 = (bf16[4,32,768]{2,1,0:T(8,128)(2,1)S(1)}, bf16[4,32,768]{2,1,0:T(8,128)(2,1)S(1)}, u32[]{:S(2)}, u32[]{:S(2)}) collective-permute-start(bf16[4,32,768]{2,1,0:T(8,128)(2,1)S(1)} %pad_maximum_fusion.1), channel_id=1, source_target_pairs={{0,1},{1,2},{2,3},{3,4},{4,5},{5,6},{6,7},{8,9},{9,10},{10,11},{11... | collective-permute-start | bytes 589832 | tf_op jit(solution)/shard_map/ppermute | solution.py:53
  23.5 9.1 %collective-permute-start.5 = (bf16[4,32,768]{2,1,0:T(8,128)(2,1)S(1)}, bf16[4,32,768]{2,1,0:T(8,128)(2,1)S(1)}, u32[]{:S(2)}, u32[]{:S(2)}) collective-permute-start(bf16[4,32,768]{2,1,0:T(8,128)(2,1)S(1)} %pad_maximum_fusion.4), channel_id=1, source_target_pairs={{0,32},{32,64},{64,96},{96,128},{128,160},{160,192},{192,224},{1,3... | collective-permute-start | bytes 589832 | tf_op jit(solution)/shard_map/ppermute | solution.py:53
  32.6 1.0 copy-start.5
  55.8 19.2 %collective-permute-start.8 = (bf16[512,2432]{1,0:T(8,128)(2,1)S(1)}, bf16[512,2432]{1,0:T(8,128)(2,1)S(1)}, u32[]{:S(2)}, u32[]{:S(2)}) collective-permute-start(bf16[512,2432]{1,0:T(8,128)(2,1)S(1)} %shard_map.114), channel_id=1, source_target_pairs={{0,1},{1,0},{2,3},{3,2},{4,5},{5,4},{6,7},{7,6},{8,9},{9,8},{10,11... | collective-permute-start | bytes 7471112 | tf_op jit(solution)/shard_map/ppermute | solution.py:87
  57.6 4.6 %collective-permute-start.6 = (bf16[4,32,768]{2,1,0:T(8,128)(2,1)S(1)}, bf16[4,32,768]{2,1,0:T(8,128)(2,1)S(1)}, u32[]{:S(2)}, u32[]{:S(2)}) collective-permute-start(bf16[4,32,768]{2,1,0:T(8,128)(2,1)S(1)} %pad_maximum_fusion.5), channel_id=1, source_target_pairs={{1,0},{2,1},{3,2},{4,3},{5,4},{6,5},{7,6},{9,8},{10,9},{11,10},{12... | collective-permute-start | bytes 589832 | tf_op jit(solution)/shard_map/ppermute | solution.py:53
  58.9 10.4 %collective-permute-start.7 = (bf16[4,32,768]{2,1,0:T(8,128)(2,1)S(1)}, bf16[4,32,768]{2,1,0:T(8,128)(2,1)S(1)}, u32[]{:S(2)}, u32[]{:S(2)}) collective-permute-start(bf16[4,32,768]{2,1,0:T(8,128)(2,1)S(1)} %slice.153), channel_id=1, source_target_pairs={{32,0},{64,32},{96,64},{128,96},{160,128},{192,160},{224,192},{33,... | collective-permute-start | bytes 589832 | tf_op jit(solution)/shard_map/ppermute | solution.py:53
  62.3 14.7 %collective-permute-start.9 = (bf16[4,32,768]{2,1,0:T(8,128)(2,1)S(1)}, bf16[4,32,768]{2,1,0:T(8,128)(2,1)}, u32[]{:S(2)}, u32[]{:S(2)}) collective-permute-start(bf16[4,32,768]{2,1,0:T(8,128)(2,1)S(1)} %pad_maximum_fusion.6), channel_id=1, source_target_pairs={{8,0},{16,8},{24,16},{9,1},{17,9},{25,17},{10,2},{18,10},{26,18},{... | collective-permute-start | bytes 589832 | tf_op jit(solution)/shard_map/ppermute | solution.py:53
  69.3 5.7 %copy-start.6 = (bf16[4,32,768]{2,1,0:T(8,128)(2,1)}, bf16[4,32,768]{2,1,0:T(8,128)(2,1)S(1)}, u32[]{:S(2)}) copy-start(bf16[4,32,768]{2,1,0:T(8,128)(2,1)S(1)} %collective-permute-done.7.refs_4_) | copy-start | bytes 589828
  70.0 7.0 %collective-permute-start.10 = (bf16[4,32,768]{2,1,0:T(8,128)(2,1)S(1)}, bf16[4,32,768]{2,1,0:T(8,128)(2,1)}, u32[]{:S(2)}, u32[]{:S(2)}) collective-permute-start(bf16[4,32,768]{2,1,0:T(8,128)(2,1)S(1)} %pad_maximum_fusion.7), channel_id=1, source_target_pairs={{1,0},{2,1},{3,2},{4,3},{5,4},{6,5},{7,6},{9,8},{10,9},{11,10},{12... | collective-permute-start | bytes 589832 | tf_op jit(solution)/shard_map/ppermute | solution.py:53
  77.0 37.6 %all-to-all-start = ((bf16[32,16,2432]{2,1,0:T(8,128)(2,1)}), bf16[32,16,2432]{2,1,0:T(8,128)(2,1)S(1)}, u32[]{:S(2)}, u32[]{:S(2)}) async-start(bf16[32,16,2432]{2,1,0:T(8,128)(2,1)} %bitcast.1), calls=%async_computation | async-start | bytes 4980736 | tf_op jit(solution)/shard_map/all_to_all | solution.py:353
  88.6 45.5 %collective-permute-start.11 = (bf16[4,32,768]{2,1,0:T(8,128)(2,1)}, bf16[4,32,768]{2,1,0:T(8,128)(2,1)}, u32[]{:S(2)}, u32[]{:S(2)}) collective-permute-start(bf16[4,32,768]{2,1,0:T(8,128)(2,1)} %pad_maximum_fusion.8), channel_id=1, source_target_pairs={{32,0},{64,32},{96,64},{128,96},{160,128},{192,160},{224,192},{33,... | collective-permute-start | bytes 589832 | tf_op jit(solution)/shard_map/ppermute | solution.py:53
  93.4 40.7 %collective-permute-start.12 = (bf16[4,32,768]{2,1,0:T(8,128)(2,1)}, bf16[4,32,768]{2,1,0:T(8,128)(2,1)}, u32[]{:S(2)}, u32[]{:S(2)}) collective-permute-start(bf16[4,32,768]{2,1,0:T(8,128)(2,1)} %pad_maximum_fusion.9), channel_id=1, source_target_pairs={{8,0},{16,8},{24,16},{9,1},{17,9},{25,17},{10,2},{18,10},{26,18},{... | collective-permute-start | bytes 589832 | tf_op jit(solution)/shard_map/ppermute | solution.py:53
  114.6 19.5 %copy-start.7 = (bf16[4,32,768]{2,1,0:T(8,128)(2,1)S(1)}, bf16[4,32,768]{2,1,0:T(8,128)(2,1)}, u32[]{:S(2)}) copy-start(bf16[4,32,768]{2,1,0:T(8,128)(2,1)} %copy-done.6) | copy-start | bytes 589828
  115.0 21.6 %collective-permute-start.13 = (bf16[4,2432]{1,0:T(4,128)(2,1)S(1)}, bf16[4,2432]{1,0:T(4,128)(2,1)S(1)}, u32[]{:S(2)}, u32[]{:S(2)}) collective-permute-start(bf16[4,2432]{1,0:T(4,128)(2,1)S(1)} %get-tuple-element.67), channel_id=1, source_target_pairs={{0,2},{1,3},{2,0},{3,1},{4,6},{5,7},{6,4},{7,5},{8,10},{9,11},{10,... | collective-permute-start | bytes 58376 | tf_op jit(solution)/shard_map/ppermute | solution.py:87
  123.2 13.4 %collective-permute-start.14 = (bf16[4,2432]{1,0:T(4,128)(2,1)S(1)}, bf16[4,2432]{1,0:T(4,128)(2,1)S(1)}, u32[]{:S(2)}, u32[]{:S(2)}) collective-permute-start(bf16[4,2432]{1,0:T(4,128)(2,1)S(1)} %get-tuple-element.68), channel_id=1, source_target_pairs={{0,4},{1,5},{2,6},{3,7},{4,0},{5,1},{6,2},{7,3},{8,12},{9,13},{10,... | collective-permute-start | bytes 58376 | tf_op jit(solution)/shard_map/ppermute | solution.py:87
  134.0 5.9 %collective-permute-start.15 = (bf16[4,2432]{1,0:T(4,128)(2,1)S(1)}, bf16[4,2432]{1,0:T(4,128)(2,1)S(1)}, u32[]{:S(2)}, u32[]{:S(2)}) collective-permute-start(bf16[4,2432]{1,0:T(4,128)(2,1)S(1)} %get-tuple-element.69), channel_id=1, source_target_pairs={{0,6},{1,7},{2,4},{3,5},{4,2},{5,3},{6,0},{7,1},{8,14},{9,15},{10,... | collective-permute-start | bytes 58376 | tf_op jit(solution)/shard_map/ppermute | solution.py:87

commit v4 on v3

--- a/solution.py
+++ b/solution.py
@@ -57,22 +57,22 @@
     return k // (4, 2, 1)[AXES.index(axis)] % 2
 
 
-def stage(at, axis, steps):
+def stage(arrays, place, axis, steps):
     moving = [k for k in range(1, 8) if bit(k, axis)]
-    moved = passed_along(jnp.concatenate([at[k] for k in moving]), axis, steps)
-    return at | {k: moved[i : i + 1] for i, k in enumerate(moving)}, moved
-
-
-def numbered(blocks):
-    return {k: blocks[k - 1 : k] for k in range(1, 8)}
-
-
-def carried(t, g, steps, ways):
-    t, g = numbered(t), numbered(g)
-    for axis_t, axis_g in zip(*ways):
-        t, moved_t = stage(t, axis_t, steps)
-        g, moved_g = stage(g, axis_g, steps)
-        yield moved_t, moved_g
+    blocks = [lax.slice_in_dim(arrays[place[k][0]], place[k][1], place[k][1] + 1) for k in moving]
+    for i, k in enumerate(moving):
+        place[k] = (len(arrays), i)
+    return [*arrays, passed_along(jnp.concatenate(blocks), axis, steps)]
+
+
+def starts():
+    return [{k: (0, k - 1) for k in range(1, 8)} for _ in range(2)]
+
+
+def step(pair, places, ways, number, steps):
+    return [
+        stage(arrays, place, way[number], steps) for arrays, place, way in zip(pair, places, ways)
+    ]
 
 
 def arrival(axes):
@@ -314,7 +314,11 @@
     me, tokens, grad_out = lax.optimization_barrier((me, tokens, grad_out))
     lists = ((7, 32, D), BF)
     blocks = call(pack_body, [lists, lists], tokens, grad_out, send_rows)
-    arrived_t, arrived_g = zip(*carried(*blocks, 1, (FIRST, SECOND)))
+    up = [[blocks[0]], [blocks[1]]]
+    places = starts()
+    for number in range(3):
+        up = step(up, places, (FIRST, SECOND), number, 1)
+    arrived_t, arrived_g = up[0][1:], up[1][1:]
 
     slot, wide, half = ((SLOTS, D), BF), ((SLOTS, 3 * D), BF), ((HALF, COLS), BF)
     xs, gos, normed, mixed, dpacked = call(
@@ -338,21 +342,22 @@
         scratch=[pltpu.VMEM((SLOTS, WIDE), BF), pltpu.VMEM(*slot)],
         mib=BACK,
     )
-    way = carried(back_t, back_g, -1, (FIRST[::-1], SECOND[::-1]))
-    first = next(way)
+    ways, places = (FIRST[::-1], SECOND[::-1]), starts()
+    down = step([[back_t], [back_g]], places, ways, 0, -1)
     operands = (me, normed, mixed, gos, dpacked, gain_sum)
     (sent,) = call(functools.partial(half_sums, 1), [half], *operands, smem=(0,), mib=SUMS)
     got = crossed(sent, "gz", 1)
-    operands, first = lax.optimization_barrier((operands, first))
     (own,) = call(functools.partial(half_sums, 0), [half], *operands, smem=(0,), mib=SUMS)
 
     (paired,) = call(sum1_body, [half], own, got)
-    second = next(way)
-    paired, second = lax.optimization_barrier((paired, second))
-    third = next(way)
+    paired, down = lax.optimization_barrier((paired, down))
     spread = lax.all_to_all(paired, ("gx", "gy"), split_axis=0, concat_axis=0, tiled=True)
     parts = call(sum2_body, [((4, COLS), BF)] * 4, spread.reshape(32, 16, COLS))
+    parts, down = lax.optimization_barrier((parts, down))
+    down = step(down, places, ways, 1, -1)
     last = [parts[0]] + [crossed(parts[i], "gz", 2 * i) for i in range(1, 4)]
+    last, down = lax.optimization_barrier((last, down))
+    down = step(down, places, ways, 2, -1)
     grad_qkv, grad_proj, gain_rows = call(
         sum3_body, [((3, 3 * D), F32), ((3, D), F32), ((3, 128), F32)], *last
     )
@@ -360,7 +365,7 @@
     block_out, grad_tokens = call(
         join_body,
         [((ROWS, D), BF), ((ROWS, D), BF)],
-        kept, *zip(first, second, third), send_rows,
+        kept, down[0][1:], down[1][1:], send_rows,
         scratch=[
             pltpu.VMEM((ROWS, WIDE), BF),
             pltpu.VMEM((224, WIDE), BF),

time: 142 us -> 145 us (1.021)
  the two profiles are of different devices: /device:TPU:42 before, /device:TPU:10 now
where the time goes in v4:
time: 145 us; the launch traced here: 144 us
  starting transfers between devices  46.6 us (32%)
  blocking collectives  40.6 us (28%)
  Pallas kernels  29.3 us (20%)
  waiting for transfers between devices  21.8 us (15%)
  local copies, waits for them, and re-layouts  4.51 us (3%)
    all_to_all x1, blocking collectives, on_device(): lax.all_to_all(paired, ('gx', 'gy'), split_axis=0, concat_axis=0, tiled=T...  40.6 us
    ppermute x12, starting transfers between devices, passed_along(): lax.ppermute(value, axis, [(source, source + steps) for source in range(i...  33.9 us
    pallas_call x9, Pallas kernels, call(): pl.pallas_call(flat, out_shape=[jax.ShapeDtypeStruct(shape, dtype) for sh...  29.3 us
    ppermute x12, waiting for transfers between devices, passed_along(): lax.ppermute(value, axis, [(source, source + steps) for source in range(i...  16.4 us
    ppermute x4, starting transfers between devices, crossed(): lax.ppermute(value, axis, [(source, source ^ mask) for source in range(co...  12.7 us
    ppermute x4, waiting for transfers between devices, crossed(): lax.ppermute(value, axis, [(source, source ^ mask) for source in range(co...  5.42 us
    unnamed x17, local copies, waits for them, and re-layouts  3.69 us
  transfers between devices with their start and end apart: 16, of which 9 were waited for; matrix products, arithmetic and copies ran while one was open for 1% of the time, Pallas kernels for 3%

profile of v4, /device:TPU:10, one launch (start us, length us, event | category | flops | bytes accessed | tf_op | source)
XLA Modules:
  0.0 144.4 jit_solution(9762493389092861125)
XLA Ops:
  0.6 0.7 copy.14.refs_2_.refs_7_
  1.3 0.0 copy-start.2
  1.3 1.0 copy-done.2
  2.3 0.0 copy-start.4
  2.3 1.0 copy-done.4
  3.3 0.0 copy-start.7
  3.3 0.0 copy-start
  3.3 0.0 copy-start.1
  3.3 0.0 copy-start.3
  3.3 0.0 copy-start.6
  3.3 0.4 shard_map.110
  3.8 4.1 %collective-permute-start = (bf16[4,32,768]{2,1,0:T(8,128)(2,1)S(1)}, bf16[4,32,768]{2,1,0:T(8,128)(2,1)S(1)}, u32[]{:S(2)}, u32[]{:S(2)}) collective-permute-start(bf16[4,32,768]{2,1,0:T(8,128)(2,1)S(1)} %slice.132), channel_id=1, source_target_pairs={{0,32},{32,64},{64,96},{96,128},{128,160},{160,192},{192,224},{1,3... | collective-permute-start | bytes 589832 | tf_op jit(solution)/shard_map/ppermute | solution.py:53
  7.9 3.5 %collective-permute-start.3 = (bf16[4,32,768]{2,1,0:T(8,128)(2,1)S(1)}, bf16[4,32,768]{2,1,0:T(8,128)(2,1)S(1)}, u32[]{:S(2)}, u32[]{:S(2)}) collective-permute-start(bf16[4,32,768]{2,1,0:T(8,128)(2,1)S(1)} %pad_maximum_fusion.2), channel_id=1, source_target_pairs={{0,8},{8,16},{16,24},{1,9},{9,17},{17,25},{2,10},{10,18},{18,26},{... | collective-permute-start | bytes 589832 | tf_op jit(solution)/shard_map/ppermute | solution.py:53
  11.4 2.0 %collective-permute-done.refs_2_ = bf16[4,32,768]{2,1,0:T(8,128)(2,1)S(1)} collective-permute-done((bf16[4,32,768]{2,1,0:T(8,128)(2,1)S(1)}, bf16[4,32,768]{2,1,0:T(8,128)(2,1)S(1)}, u32[]{:S(2)}, u32[]{:S(2)}) %collective-permute-start) | collective-permute-done | bytes 196640 | tf_op jit(solution)/shard_map/ppermute | solution.py:53
  13.5 3.5 %collective-permute-start.1 = (bf16[4,32,768]{2,1,0:T(8,128)(2,1)S(1)}, bf16[4,32,768]{2,1,0:T(8,128)(2,1)S(1)}, u32[]{:S(2)}, u32[]{:S(2)}) collective-permute-start(bf16[4,32,768]{2,1,0:T(8,128)(2,1)S(1)} %pad_maximum_fusion), channel_id=1, source_target_pairs={{0,8},{8,16},{16,24},{1,9},{9,17},{17,25},{2,10},{10,18},{18,26},{... | collective-permute-start | bytes 589832 | tf_op jit(solution)/shard_map/ppermute | solution.py:53
  17.0 0.0 collective-permute-done.3.refs_5_
  17.1 1.3 collective-permute-start.4
  18.4 2.8 %collective-permute-done.1.refs_3_ = bf16[4,32,768]{2,1,0:T(8,128)(2,1)S(1)} collective-permute-done((bf16[4,32,768]{2,1,0:T(8,128)(2,1)S(1)}, bf16[4,32,768]{2,1,0:T(8,128)(2,1)S(1)}, u32[]{:S(2)}, u32[]{:S(2)}) %collective-permute-start.1) | collective-permute-done | bytes 196640 | tf_op jit(solution)/shard_map/ppermute | solution.py:53
  21.2 3.2 %collective-permute-start.2 = (bf16[4,32,768]{2,1,0:T(8,128)(2,1)S(1)}, bf16[4,32,768]{2,1,0:T(8,128)(2,1)S(1)}, u32[]{:S(2)}, u32[]{:S(2)}) collective-permute-start(bf16[4,32,768]{2,1,0:T(8,128)(2,1)S(1)} %pad_maximum_fusion.1), channel_id=1, source_target_pairs={{0,1},{1,2},{2,3},{3,4},{4,5},{5,6},{6,7},{8,9},{9,10},{10,11},{11... | collective-permute-start | bytes 589832 | tf_op jit(solution)/shard_map/ppermute | solution.py:53
  24.4 0.0 collective-permute-done.4.refs_6_
  24.4 2.9 %collective-permute-start.5 = (bf16[4,32,768]{2,1,0:T(8,128)(2,1)S(1)}, bf16[4,32,768]{2,1,0:T(8,128)(2,1)S(1)}, u32[]{:S(2)}, u32[]{:S(2)}) collective-permute-start(bf16[4,32,768]{2,1,0:T(8,128)(2,1)S(1)} %pad_maximum_fusion.4), channel_id=1, source_target_pairs={{0,32},{32,64},{64,96},{96,128},{128,160},{160,192},{192,224},{1,3... | collective-permute-start | bytes 589832 | tf_op jit(solution)/shard_map/ppermute | solution.py:53
  27.4 0.0 copy-done.7
  27.4 0.0 collective-permute-done.2.refs_4_
  27.4 5.5 %collective-permute-done.5.refs_7_ = bf16[4,32,768]{2,1,0:T(8,128)(2,1)S(1)} collective-permute-done((bf16[4,32,768]{2,1,0:T(8,128)(2,1)S(1)}, bf16[4,32,768]{2,1,0:T(8,128)(2,1)S(1)}, u32[]{:S(2)}, u32[]{:S(2)}) %collective-permute-start.5) | collective-permute-done | bytes 196640 | tf_op jit(solution)/shard_map/ppermute | solution.py:53
  32.9 0.0 copy-done
  32.9 0.0 copy-done.1
  32.9 0.0 copy-done.3
  32.9 0.0 copy-done.6
  32.9 0.0 copy-start.5
  32.9 1.0 copy-done.5
  33.9 14.4 %shard_map.111 = (bf16[512,768]{1,0:T(8,128)(2,1)S(1)}, bf16[512,768]{1,0:T(8,128)(2,1)S(1)}, bf16[512,768]{1,0:T(8,128)(2,1)S(1)}, bf16[512,768]{1,0:T(8,128)(2,1)S(1)}, bf16[512,2304]{1,0:T(8,128)(2,1)S(1)}) custom-call(bf16[256,768]{1,0:T(8,128)(2,1)S(1)} %copy-done.3, bf16[256,768]{1,0:T(8,128)(2,1)S(1)} %copy-done.5, ...), custom_call_target="tpu_custom_call" | custom-call | tf_op jit(solution)/shard_map/pallas_call | solution.py:301
  48.3 4.2 %shard_map.112 = (bf16[7,32,768]{2,1,0:T(8,128)(2,1)S(1)}, bf16[7,32,768]{2,1,0:T(8,128)(2,1)S(1)}, bf16[256,1536]{1,0:T(8,128)(2,1)S(1)}, f32[1,768]{1,0:T(1,128)S(1)}) custom-call(bf16[512,768]{1,0:T(8,128)(2,1)S(1)} %get-tuple-element.55.refs_0_, bf16[512,768]{1,0:T(8,128)(2,1)S(1)} %get-tuple-element.56.refs_1_.refs_3_, ...), custom_call_target="tpu_custom_call" | custom-call | tf_op jit(solution)/shard_map/pallas_call | solution.py:301
  52.5 3.5 %shard_map.114 = bf16[512,2432]{1,0:T(8,128)(2,1)S(1)} custom-call(s32[1]{0:T(128)} %bitcast.refs_0_, bf16[512,768]{1,0:T(8,128)(2,1)S(1)} %get-tuple-element.61.refs_1_, bf16[512,768]{1,0:T(8,128)(2,1)S(1)} %get-tuple-element.57.refs_2_, bf16[512,768]{1,0:T(8,128)(2,1)S(1)} %get-tuple-element.56.refs_1_.refs_3_, ...), custom_call_target="tpu_custom_call" | custom-call | tf_op jit(solution)/shard_map/pallas_call | solution.py:301
  56.0 2.1 %collective-permute-start.6 = (bf16[512,2432]{1,0:T(8,128)(2,1)S(1)}, bf16[512,2432]{1,0:T(8,128)(2,1)S(1)}, u32[]{:S(2)}, u32[]{:S(2)}) collective-permute-start(bf16[512,2432]{1,0:T(8,128)(2,1)S(1)} %shard_map.114), channel_id=1, source_target_pairs={{0,1},{1,0},{2,3},{3,2},{4,5},{5,4},{6,7},{7,6},{8,9},{9,8},{10,11... | collective-permute-start | bytes 7471112 | tf_op jit(solution)/shard_map/ppermute | solution.py:87
  58.1 1.3 collective-permute-start.7
  59.5 3.8 %collective-permute-start.8 = (bf16[4,32,768]{2,1,0:T(8,128)(2,1)S(1)}, bf16[4,32,768]{2,1,0:T(8,128)(2,1)S(1)}, u32[]{:S(2)}, u32[]{:S(2)}) collective-permute-start(bf16[4,32,768]{2,1,0:T(8,128)(2,1)S(1)} %slice.153), channel_id=1, source_target_pairs={{32,0},{64,32},{96,64},{128,96},{160,128},{192,160},{224,192},{33,... | collective-permute-start | bytes 589832 | tf_op jit(solution)/shard_map/ppermute | solution.py:53
  63.3 3.5 %shard_map.113.refs_0_ = bf16[512,2432]{1,0:T(8,128)(2,1)S(1)} custom-call(s32[1]{0:T(128)} %bitcast.refs_0_, bf16[512,768]{1,0:T(8,128)(2,1)S(1)} %get-tuple-element.61.refs_1_, bf16[512,768]{1,0:T(8,128)(2,1)S(1)} %get-tuple-element.57.refs_2_, bf16[512,768]{1,0:T(8,128)(2,1)S(1)} %get-tuple-element.56.refs_1_.refs_3_, ...), custom_call_target="tpu_custom_call" | custom-call | tf_op jit(solution)/shard_map/pallas_call | solution.py:301
  66.8 0.0 collective-permute-done.6.refs_1_
  66.8 0.6 shard_map.115
  67.3 0.0 collective-permute-done.7.refs_1_
  67.4 1.7 %collective-permute-done.8.refs_4_ = bf16[4,32,768]{2,1,0:T(8,128)(2,1)S(1)} collective-permute-done((bf16[4,32,768]{2,1,0:T(8,128)(2,1)S(1)}, bf16[4,32,768]{2,1,0:T(8,128)(2,1)S(1)}, u32[]{:S(2)}, u32[]{:S(2)}) %collective-permute-start.8) | collective-permute-done | bytes 196640 | tf_op jit(solution)/shard_map/ppermute | solution.py:53
  69.1 40.6 %all_to_all.9.refs_0_ = bf16[32,16,2432]{2,1,0:T(8,128)(2,1)S(1)} all-to-all(bf16[32,16,2432]{2,1,0:T(8,128)(2,1)S(1)} %bitcast.2), channel_id=1, replica_groups=mesh['gx'=8,'gy'=4,'gz'=8] {'gx','gy'}, dimensions={0} | all-to-all | bytes 4980736 | tf_op jit(solution)/shard_map/all_to_all | solution.py:354
  109.7 0.4 shard_map.116
  110.2 2.9 %collective-permute-start.12 = (bf16[4,32,768]{2,1,0:T(8,128)(2,1)S(1)}, bf16[4,32,768]{2,1,0:T(8,128)(2,1)S(1)}, u32[]{:S(2)}, u32[]{:S(2)}) collective-permute-start(bf16[4,32,768]{2,1,0:T(8,128)(2,1)S(1)} %pad_maximum_fusion.6), channel_id=1, source_target_pairs={{8,0},{16,8},{24,16},{9,1},{17,9},{25,17},{10,2},{18,10},{26,18},{... | collective-permute-start | bytes 589832 | tf_op jit(solution)/shard_map/ppermute | solution.py:53
  113.1 1.3 collective-permute-start.13
  114.4 6.0 %collective-permute-start.9 = (bf16[4,2432]{1,0:T(4,128)(2,1)S(1)}, bf16[4,2432]{1,0:T(4,128)(2,1)S(1)}, u32[]{:S(2)}, u32[]{:S(2)}) collective-permute-start(bf16[4,2432]{1,0:T(4,128)(2,1)S(1)} %get-tuple-element.75), channel_id=1, source_target_pairs={{0,2},{1,3},{2,0},{3,1},{4,6},{5,7},{6,4},{7,5},{8,10},{9,11},{10,... | collective-permute-start | bytes 58376 | tf_op jit(solution)/shard_map/ppermute | solution.py:87
  120.4 4.1 %collective-permute-start.10 = (bf16[4,2432]{1,0:T(4,128)(2,1)S(1)}, bf16[4,2432]{1,0:T(4,128)(2,1)S(1)}, u32[]{:S(2)}, u32[]{:S(2)}) collective-permute-start(bf16[4,2432]{1,0:T(4,128)(2,1)S(1)} %get-tuple-element.76), channel_id=1, source_target_pairs={{0,4},{1,5},{2,6},{3,7},{4,0},{5,1},{6,2},{7,3},{8,12},{9,13},{10,... | collective-permute-start | bytes 58376 | tf_op jit(solution)/shard_map/ppermute | solution.py:87
  124.5 0.5 collective-permute-start.11
  125.0 1.9 %collective-permute-done.9.refs_1_ = bf16[4,2432]{1,0:T(4,128)(2,1)S(1)} collective-permute-done((bf16[4,2432]{1,0:T(4,128)(2,1)S(1)}, bf16[4,2432]{1,0:T(4,128)(2,1)S(1)}, u32[]{:S(2)}, u32[]{:S(2)}) %collective-permute-start.9) | collective-permute-done | bytes 19488 | tf_op jit(solution)/shard_map/ppermute | solution.py:87
  126.9 1.2 collective-permute-done.10.refs_2_
  128.1 2.3 %collective-permute-done.11.refs_3_ = bf16[4,2432]{1,0:T(4,128)(2,1)S(1)} collective-permute-done((bf16[4,2432]{1,0:T(4,128)(2,1)S(1)}, bf16[4,2432]{1,0:T(4,128)(2,1)S(1)}, u32[]{:S(2)}, u32[]{:S(2)}) %collective-permute-start.11) | collective-permute-done | bytes 19488 | tf_op jit(solution)/shard_map/ppermute | solution.py:87
  130.4 0.0 collective-permute-done.12.refs_2_
  130.4 0.0 collective-permute-done.13.refs_5_
  130.5 4.2 %collective-permute-start.14 = (bf16[4,32,768]{2,1,0:T(8,128)(2,1)S(1)}, bf16[4,32,768]{2,1,0:T(8,128)(2,1)S(1)}, u32[]{:S(2)}, u32[]{:S(2)}) collective-permute-start(bf16[4,32,768]{2,1,0:T(8,128)(2,1)S(1)} %pad_maximum_fusion.8), channel_id=1, source_target_pairs={{32,0},{64,32},{96,64},{128,96},{160,128},{192,160},{224,192},{33,... | collective-permute-start | bytes 589832 | tf_op jit(solution)/shard_map/ppermute | solution.py:53
  134.8 1.9 %collective-permute-start.15 = (bf16[4,32,768]{2,1,0:T(8,128)(2,1)S(1)}, bf16[4,32,768]{2,1,0:T(8,128)(2,1)S(1)}, u32[]{:S(2)}, u32[]{:S(2)}) collective-permute-start(bf16[4,32,768]{2,1,0:T(8,128)(2,1)S(1)} %pad_maximum_fusion.9), channel_id=1, source_target_pairs={{8,0},{16,8},{24,16},{9,1},{17,9},{25,17},{10,2},{18,10},{26,18},{... | collective-permute-start | bytes 589832 | tf_op jit(solution)/shard_map/ppermute | solution.py:53
  136.8 0.6 shard_map.118
  137.4 0.6 slice_reduce_fusion
  138.0 0.2 collective-permute-done.14.refs_3_
  138.3 4.1 %collective-permute-done.15.refs_6_ = bf16[4,32,768]{2,1,0:T(8,128)(2,1)S(1)} collective-permute-done((bf16[4,32,768]{2,1,0:T(8,128)(2,1)S(1)}, bf16[4,32,768]{2,1,0:T(8,128)(2,1)S(1)}, u32[]{:S(2)}, u32[]{:S(2)}) %collective-permute-start.15) | collective-permute-done | bytes 196640 | tf_op jit(solution)/shard_map/ppermute | solution.py:53
  142.4 1.8 %shard_map.117 = (bf16[256,768]{1,0:T(8,128)(2,1)}, bf16[256,768]{1,0:T(8,128)(2,1)}) custom-call(bf16[256,1536]{1,0:T(8,128)(2,1)S(1)} %get-tuple-element.59.refs_0_, bf16[4,32,768]{2,1,0:T(8,128)(2,1)S(1)} %collective-permute-done.7.refs_1_, bf16[4,32,768]{2,1,0:T(8,128)(2,1)S(1)} %collective-permute-done.12.refs_2_, ...), custom_call_target="tpu_custom_call" | custom-call | tf_op jit(solution)/shard_map/pallas_call | solution.py:301
  (31 shorter events, 0.5 us)
Async XLA Ops:
  1.3 1.0 copy-start.2
  2.3 1.0 copy-start.4
  3.3 24.0 %copy-start.7 = (f32[768]{0:T(1024)S(1)}, f32[768]{0:T(1024)}, u32[]{:S(2)}) copy-start(f32[768]{0:T(1024)} %param.8) | copy-start | bytes 9220
  3.3 29.6 %copy-start = (bf16[768,2304]{1,0:T(8,128)(2,1)S(1)}, bf16[768,2304]{1,0:T(8,128)(2,1)}, u32[]{:S(2)}) copy-start(bf16[768,2304]{1,0:T(8,128)(2,1)} %refs_6_.1) | copy-start | bytes 10616836
  3.3 29.6 %copy-start.1 = (bf16[768,768]{1,0:T(8,128)(2,1)S(1)}, bf16[768,768]{1,0:T(8,128)(2,1)}, u32[]{:S(2)}) copy-start(bf16[768,768]{1,0:T(8,128)(2,1)} %refs_7_.2) | copy-start | bytes 3538948
  3.3 29.6 %copy-start.3 = (bf16[256,768]{1,0:T(8,128)(2,1)S(1)}, bf16[256,768]{1,0:T(8,128)(2,1)}, u32[]{:S(2)}) copy-start(bf16[256,768]{1,0:T(8,128)(2,1)} %refs_0_.1) | copy-start | bytes 1179652
  3.3 29.6 %copy-start.6 = (s32[1,512]{1,0:T(1,128)S(1)}, s32[1,512]{1,0:T(1,128)}, u32[]{:S(2)}) copy-start(s32[1,512]{1,0:T(1,128)} %refs_4_.1) | copy-start | bytes 6148
  3.8 9.7 %collective-permute-start = (bf16[4,32,768]{2,1,0:T(8,128)(2,1)S(1)}, bf16[4,32,768]{2,1,0:T(8,128)(2,1)S(1)}, u32[]{:S(2)}, u32[]{:S(2)}) collective-permute-start(bf16[4,32,768]{2,1,0:T(8,128)(2,1)S(1)} %slice.132), channel_id=1, source_target_pairs={{0,32},{32,64},{64,96},{96,128},{128,160},{160,192},{192,224},{1,3... | collective-permute-start | bytes 589832 | tf_op jit(solution)/shard_map/ppermute | solution.py:53
  7.9 9.1 %collective-permute-start.3 = (bf16[4,32,768]{2,1,0:T(8,128)(2,1)S(1)}, bf16[4,32,768]{2,1,0:T(8,128)(2,1)S(1)}, u32[]{:S(2)}, u32[]{:S(2)}) collective-permute-start(bf16[4,32,768]{2,1,0:T(8,128)(2,1)S(1)} %pad_maximum_fusion.2), channel_id=1, source_target_pairs={{0,8},{8,16},{16,24},{1,9},{9,17},{17,25},{2,10},{10,18},{18,26},{... | collective-permute-start | bytes 589832 | tf_op jit(solution)/shard_map/ppermute | solution.py:53
  13.5 7.7 %collective-permute-start.1 = (bf16[4,32,768]{2,1,0:T(8,128)(2,1)S(1)}, bf16[4,32,768]{2,1,0:T(8,128)(2,1)S(1)}, u32[]{:S(2)}, u32[]{:S(2)}) collective-permute-start(bf16[4,32,768]{2,1,0:T(8,128)(2,1)S(1)} %pad_maximum_fusion), channel_id=1, source_target_pairs={{0,8},{8,16},{16,24},{1,9},{9,17},{17,25},{2,10},{10,18},{18,26},{... | collective-permute-start | bytes 589832 | tf_op jit(solution)/shard_map/ppermute | solution.py:53
  17.1 7.3 %collective-permute-start.4 = (bf16[4,32,768]{2,1,0:T(8,128)(2,1)S(1)}, bf16[4,32,768]{2,1,0:T(8,128)(2,1)S(1)}, u32[]{:S(2)}, u32[]{:S(2)}) collective-permute-start(bf16[4,32,768]{2,1,0:T(8,128)(2,1)S(1)} %pad_maximum_fusion.3), channel_id=1, source_target_pairs={{0,1},{1,2},{2,3},{3,4},{4,5},{5,6},{6,7},{8,9},{9,10},{10,11},{11... | collective-permute-start | bytes 589832 | tf_op jit(solution)/shard_map/ppermute | solution.py:53
  21.2 6.2 %collective-permute-start.2 = (bf16[4,32,768]{2,1,0:T(8,128)(2,1)S(1)}, bf16[4,32,768]{2,1,0:T(8,128)(2,1)S(1)}, u32[]{:S(2)}, u32[]{:S(2)}) collective-permute-start(bf16[4,32,768]{2,1,0:T(8,128)(2,1)S(1)} %pad_maximum_fusion.1), channel_id=1, source_target_pairs={{0,1},{1,2},{2,3},{3,4},{4,5},{5,6},{6,7},{8,9},{9,10},{10,11},{11... | collective-permute-start | bytes 589832 | tf_op jit(solution)/shard_map/ppermute | solution.py:53
  24.4 8.5 %collective-permute-start.5 = (bf16[4,32,768]{2,1,0:T(8,128)(2,1)S(1)}, bf16[4,32,768]{2,1,0:T(8,128)(2,1)S(1)}, u32[]{:S(2)}, u32[]{:S(2)}) collective-permute-start(bf16[4,32,768]{2,1,0:T(8,128)(2,1)S(1)} %pad_maximum_fusion.4), channel_id=1, source_target_pairs={{0,32},{32,64},{64,96},{96,128},{128,160},{160,192},{192,224},{1,3... | collective-permute-start | bytes 589832 | tf_op jit(solution)/shard_map/ppermute | solution.py:53
  32.9 1.0 copy-start.5
  56.0 10.8 %collective-permute-start.6 = (bf16[512,2432]{1,0:T(8,128)(2,1)S(1)}, bf16[512,2432]{1,0:T(8,128)(2,1)S(1)}, u32[]{:S(2)}, u32[]{:S(2)}) collective-permute-start(bf16[512,2432]{1,0:T(8,128)(2,1)S(1)} %shard_map.114), channel_id=1, source_target_pairs={{0,1},{1,0},{2,3},{3,2},{4,5},{5,4},{6,7},{7,6},{8,9},{9,8},{10,11... | collective-permute-start | bytes 7471112 | tf_op jit(solution)/shard_map/ppermute | solution.py:87
  58.1 9.2 %collective-permute-start.7 = (bf16[4,32,768]{2,1,0:T(8,128)(2,1)S(1)}, bf16[4,32,768]{2,1,0:T(8,128)(2,1)S(1)}, u32[]{:S(2)}, u32[]{:S(2)}) collective-permute-start(bf16[4,32,768]{2,1,0:T(8,128)(2,1)S(1)} %pad_maximum_fusion.5), channel_id=1, source_target_pairs={{1,0},{2,1},{3,2},{4,3},{5,4},{6,5},{7,6},{9,8},{10,9},{11,10},{12... | collective-permute-start | bytes 589832 | tf_op jit(solution)/shard_map/ppermute | solution.py:53
  59.5 9.6 %collective-permute-start.8 = (bf16[4,32,768]{2,1,0:T(8,128)(2,1)S(1)}, bf16[4,32,768]{2,1,0:T(8,128)(2,1)S(1)}, u32[]{:S(2)}, u32[]{:S(2)}) collective-permute-start(bf16[4,32,768]{2,1,0:T(8,128)(2,1)S(1)} %slice.153), channel_id=1, source_target_pairs={{32,0},{64,32},{96,64},{128,96},{160,128},{192,160},{224,192},{33,... | collective-permute-start | bytes 589832 | tf_op jit(solution)/shard_map/ppermute | solution.py:53
  110.2 20.3 %collective-permute-start.12 = (bf16[4,32,768]{2,1,0:T(8,128)(2,1)S(1)}, bf16[4,32,768]{2,1,0:T(8,128)(2,1)S(1)}, u32[]{:S(2)}, u32[]{:S(2)}) collective-permute-start(bf16[4,32,768]{2,1,0:T(8,128)(2,1)S(1)} %pad_maximum_fusion.6), channel_id=1, source_target_pairs={{8,0},{16,8},{24,16},{9,1},{17,9},{25,17},{10,2},{18,10},{26,18},{... | collective-permute-start | bytes 589832 | tf_op jit(solution)/shard_map/ppermute | solution.py:53
  113.1 17.3 %collective-permute-start.13 = (bf16[4,32,768]{2,1,0:T(8,128)(2,1)S(1)}, bf16[4,32,768]{2,1,0:T(8,128)(2,1)S(1)}, u32[]{:S(2)}, u32[]{:S(2)}) collective-permute-start(bf16[4,32,768]{2,1,0:T(8,128)(2,1)S(1)} %pad_maximum_fusion.7), channel_id=1, source_target_pairs={{1,0},{2,1},{3,2},{4,3},{5,4},{6,5},{7,6},{9,8},{10,9},{11,10},{12... | collective-permute-start | bytes 589832 | tf_op jit(solution)/shard_map/ppermute | solution.py:53
  114.4 12.4 %collective-permute-start.9 = (bf16[4,2432]{1,0:T(4,128)(2,1)S(1)}, bf16[4,2432]{1,0:T(4,128)(2,1)S(1)}, u32[]{:S(2)}, u32[]{:S(2)}) collective-permute-start(bf16[4,2432]{1,0:T(4,128)(2,1)S(1)} %get-tuple-element.75), channel_id=1, source_target_pairs={{0,2},{1,3},{2,0},{3,1},{4,6},{5,7},{6,4},{7,5},{8,10},{9,11},{10,... | collective-permute-start | bytes 58376 | tf_op jit(solution)/shard_map/ppermute | solution.py:87
  120.4 7.7 %collective-permute-start.10 = (bf16[4,2432]{1,0:T(4,128)(2,1)S(1)}, bf16[4,2432]{1,0:T(4,128)(2,1)S(1)}, u32[]{:S(2)}, u32[]{:S(2)}) collective-permute-start(bf16[4,2432]{1,0:T(4,128)(2,1)S(1)} %get-tuple-element.76), channel_id=1, source_target_pairs={{0,4},{1,5},{2,6},{3,7},{4,0},{5,1},{6,2},{7,3},{8,12},{9,13},{10,... | collective-permute-start | bytes 58376 | tf_op jit(solution)/shard_map/ppermute | solution.py:87
  124.5 5.9 %collective-permute-start.11 = (bf16[4,2432]{1,0:T(4,128)(2,1)S(1)}, bf16[4,2432]{1,0:T(4,128)(2,1)S(1)}, u32[]{:S(2)}, u32[]{:S(2)}) collective-permute-start(bf16[4,2432]{1,0:T(4,128)(2,1)S(1)} %get-tuple-element.77), channel_id=1, source_target_pairs={{0,6},{1,7},{2,4},{3,5},{4,2},{5,3},{6,0},{7,1},{8,14},{9,15},{10,... | collective-permute-start | bytes 58376 | tf_op jit(solution)/shard_map/ppermute | solution.py:87
  130.5 7.8 %collective-permute-start.14 = (bf16[4,32,768]{2,1,0:T(8,128)(2,1)S(1)}, bf16[4,32,768]{2,1,0:T(8,128)(2,1)S(1)}, u32[]{:S(2)}, u32[]{:S(2)}) collective-permute-start(bf16[4,32,768]{2,1,0:T(8,128)(2,1)S(1)} %pad_maximum_fusion.8), channel_id=1, source_target_pairs={{32,0},{64,32},{96,64},{128,96},{160,128},{192,160},{224,192},{33,... | collective-permute-start | bytes 589832 | tf_op jit(solution)/shard_map/ppermute | solution.py:53
  134.8 7.6 %collective-permute-start.15 = (bf16[4,32,768]{2,1,0:T(8,128)(2,1)S(1)}, bf16[4,32,768]{2,1,0:T(8,128)(2,1)S(1)}, u32[]{:S(2)}, u32[]{:S(2)}) collective-permute-start(bf16[4,32,768]{2,1,0:T(8,128)(2,1)S(1)} %pad_maximum_fusion.9), channel_id=1, source_target_pairs={{8,0},{16,8},{24,16},{9,1},{17,9},{25,17},{10,2},{18,10},{26,18},{... | collective-permute-start | bytes 589832 | tf_op jit(solution)/shard_map/ppermute | solution.py:53

commit v5 on v4

--- a/solution.py
+++ b/solution.py
@@ -144,7 +144,7 @@
 
 def main_body(
     tok_ref, go_ref, t_refs, g_refs, win_ref, gain_ref, wqkv_ref, wout_ref,
-    xs_ref, gos_ref, normed_ref, mixed_ref, dpacked_ref,
+    xs_ref, gos_ref, normed_ref, mixed_ref, dpacked_ref, dn_ref, gain_sum_ref,
     rows_ref, packed_ref, delta_ref, held_ref, sems,
 ):
     copies = fetches(t_refs, g_refs, (FIRST, SECOND), rows_ref, ROWS, sems)
@@ -225,24 +225,24 @@
         return carry
 
     lax.fori_loop(0, SLOTS // WCAP, attend, 0)
+    dnormed = lax.dot_general(
+        dpacked_ref[...], wqkv_ref[...], NT, preferred_element_type=F32
+    ).astype(BF)
+    dn_ref[...] = dnormed
+    unit, _ = normalised(xs_ref[...].astype(F32))
+    gain_sum_ref[...] = jnp.sum(dnormed.astype(F32) * unit, axis=0, keepdims=True)
 
 
 def back_body(
-    xs_ref, gos_ref, mixed_ref, dpacked_ref, win_ref, gain_ref, wqkv_ref, wout_ref,
-    t_ref, g_ref, kept_ref, gain_sum_ref, cat_ref, dn_ref,
+    xs_ref, gos_ref, mixed_ref, dn_ref, win_ref, gain_ref, wout_ref, t_ref, g_ref, kept_ref, cat_ref,
 ):
     gain = gain_ref[...]
-    dn_ref[...] = lax.dot_general(
-        dpacked_ref[...], wqkv_ref[...], NT, preferred_element_type=F32
-    ).astype(BF)
-    gain_row = jnp.zeros((1, D), F32)
     projected = dot(mixed_ref[...], wout_ref[...])
     cat_ref[:, :D] = (xs_ref[...].astype(F32) + projected).astype(BF)
     for w in range(4):
         at = slice(w * WCAP, (w + 1) * WCAP)
         unit, inv_std = normalised(xs_ref[at, :].astype(F32))
         dnormed = dn_ref[at, :].astype(F32)
-        gain_row += jnp.sum(dnormed * unit, axis=0, keepdims=True)
         dunit = dnormed * gain
         dcentre = inv_std * (
             dunit
@@ -255,7 +255,6 @@
     sent = dot(back[ROWS:], cat_ref[...]).astype(BF).reshape(7, 32, WIDE)
     t_ref[...] = sent[:, :, :D]
     g_ref[...] = sent[:, :, D:]
-    gain_sum_ref[...] = gain_row
 
 
 def join_body(kept_ref, t_refs, g_refs, send_ref, out_ref, grad_ref, own_ref, rows_ref, sems):
@@ -321,9 +320,9 @@
     arrived_t, arrived_g = up[0][1:], up[1][1:]
 
     slot, wide, half = ((SLOTS, D), BF), ((SLOTS, 3 * D), BF), ((HALF, COLS), BF)
-    xs, gos, normed, mixed, dpacked = call(
+    xs, gos, normed, mixed, dpacked, dn, gain_sum = call(
         main_body,
-        [slot, slot, slot, slot, wide],
+        [slot, slot, slot, slot, wide, slot, ((1, D), F32)],
         tokens, grad_out, arrived_t, arrived_g, window_rows, gain, w_qkv, w_out,
         scratch=[
             pltpu.VMEM((SLOTS, WIDE), BF),
@@ -335,29 +334,29 @@
         outside=(0, 1, 2, 3, 4, 5, 6, 7, 11),
         mib=MAIN,
     )
-    back_t, back_g, kept, gain_sum = call(
-        back_body,
-        [lists, lists, ((ROWS, WIDE), BF), ((1, D), F32)],
-        xs, gos, mixed, dpacked, window_rows, gain, w_qkv, w_out,
-        scratch=[pltpu.VMEM((SLOTS, WIDE), BF), pltpu.VMEM(*slot)],
-        mib=BACK,
-    )
-    ways, places = (FIRST[::-1], SECOND[::-1]), starts()
-    down = step([[back_t], [back_g]], places, ways, 0, -1)
     operands = (me, normed, mixed, gos, dpacked, gain_sum)
     (sent,) = call(functools.partial(half_sums, 1), [half], *operands, smem=(0,), mib=SUMS)
     got = crossed(sent, "gz", 1)
+    sent, xs = lax.optimization_barrier((sent, xs))
+    back_t, back_g, kept = call(
+        back_body,
+        [lists, lists, ((ROWS, WIDE), BF)],
+        xs, gos, mixed, dn, window_rows, gain, w_out,
+        scratch=[pltpu.VMEM((SLOTS, WIDE), BF)],
+        mib=BACK,
+    )
+    ways, places = (FIRST[::-1], SECOND[::-1]), starts()
+    down = step([[back_t], [back_g]], places, ways, 0, -1)
     (own,) = call(functools.partial(half_sums, 0), [half], *operands, smem=(0,), mib=SUMS)
 
     (paired,) = call(sum1_body, [half], own, got)
     paired, down = lax.optimization_barrier((paired, down))
+    down = step(down, places, ways, 1, -1)
     spread = lax.all_to_all(paired, ("gx", "gy"), split_axis=0, concat_axis=0, tiled=True)
     parts = call(sum2_body, [((4, COLS), BF)] * 4, spread.reshape(32, 16, COLS))
     parts, down = lax.optimization_barrier((parts, down))
-    down = step(down, places, ways, 1, -1)
+    down = step(down, places, ways, 2, -1)
     last = [parts[0]] + [crossed(parts[i], "gz", 2 * i) for i in range(1, 4)]
-    last, down = lax.optimization_barrier((last, down))
-    down = step(down, places, ways, 2, -1)
     grad_qkv, grad_proj, gain_rows = call(
         sum3_body, [((3, 3 * D), F32), ((3, D), F32), ((3, 128), F32)], *last
     )

time: 145 us -> 144 us (level)
  blocking collectives: 40.6 us -> 0 us
  waiting for transfers between devices: 21.8 us -> 44.5 us
  starting transfers between devices: 46.6 us -> 52.8 us
  local copies, waits for them, and re-layouts: 4.51 us -> 10.3 us
  Pallas kernels: 29.3 us -> 31.9 us
    all_to_all x1 -> x0, blocking collectives: 40.6 us -> none  [on_device(): lax.all_to_all(paired, ('gx', 'gy'), split_axis=0, concat_axis=0, tiled=T...]
    all_to_all x0 -> x1, waiting for transfers between devices: none -> 28.3 us  [on_device(): lax.all_to_all(paired, ('gx', 'gy'), split_axis=0, concat_axis=0, tiled=T...]
    all_to_all x0 -> x1, starting transfers between devices: none -> 9.12 us  [on_device(): lax.all_to_all(paired, ('gx', 'gy'), split_axis=0, concat_axis=0, tiled=T...]
    slice x20, local copies, waits for them, and re-layouts: 0.19 us -> 6 us  [stage(): lax.slice_in_dim(arrays[place[k][0]], place[k][1], place[k][1] + 1)]
    ppermute x12, waiting for transfers between devices: 16.4 us -> 10.7 us  [passed_along(): lax.ppermute(value, axis, [(source, source + steps) for source in range(i...]
    ppermute x12, starting transfers between devices: 33.9 us -> 31.1 us  [passed_along(): lax.ppermute(value, axis, [(source, source + steps) for source in range(i...]
    pallas_call x9, Pallas kernels: 29.3 us -> 31.9 us  [call(): pl.pallas_call(flat, out_shape=[jax.ShapeDtypeStruct(shape, dtype) for sh...]
    unnamed x17 -> x21, local copies, waits for them, and re-layouts: 3.69 us -> 3.7 us
  transfers between devices with their start and end apart: 16 -> 17, of which waited for: 9 -> 7; matrix products, arithmetic and copies ran while one was open for 1% -> 5% of each run, Pallas kernels for 3% -> 6%
where the time goes in v5:
time: 144 us; the launch traced here: 142 us
  starting transfers between devices  52.8 us (37%)
  waiting for transfers between devices  44.5 us (31%)
  Pallas kernels  31.9 us (22%)
  local copies, waits for them, and re-layouts  10.3 us (7%)
  other arithmetic  1.63 us (1%)
    pallas_call x9, Pallas kernels, call(): pl.pallas_call(flat, out_shape=[jax.ShapeDtypeStruct(shape, dtype) for sh...  31.9 us
    ppermute x12, starting transfers between devices, passed_along(): lax.ppermute(value, axis, [(source, source + steps) for source in range(i...  31.1 us
    all_to_all x1, waiting for transfers between devices, on_device(): lax.all_to_all(paired, ('gx', 'gy'), split_axis=0, concat_axis=0, tiled=T...  28.3 us
    ppermute x4, starting transfers between devices, crossed(): lax.ppermute(value, axis, [(source, source ^ mask) for source in range(co...  12.6 us
    ppermute x12, waiting for transfers between devices, passed_along(): lax.ppermute(value, axis, [(source, source + steps) for source in range(i...  10.7 us
    all_to_all x1, starting transfers between devices, on_device(): lax.all_to_all(paired, ('gx', 'gy'), split_axis=0, concat_axis=0, tiled=T...  9.12 us
    slice x20, local copies, waits for them, and re-layouts, stage(): lax.slice_in_dim(arrays[place[k][0]], place[k][1], place[k][1] + 1)  6 us
    ppermute x4, waiting for transfers between devices, crossed(): lax.ppermute(value, axis, [(source, source ^ mask) for source in range(co...  5.42 us
  transfers between devices with their start and end apart: 17, of which 7 were waited for; matrix products, arithmetic and copies ran while one was open for 5% of the time, Pallas kernels for 6%

profile of v5, /device:TPU:10, one launch (start us, length us, event | category | flops | bytes accessed | tf_op | source)
XLA Modules:
  0.0 142.4 jit_solution(12217591596827355983)
XLA Ops:
  0.6 0.7 copy.14.refs_2_.refs_7_
  1.3 1.0 copy-done.2
  2.3 1.0 copy-done.4
  3.3 0.0 copy-start.8
  3.3 0.4 shard_map.110
  3.8 4.1 %collective-permute-start = (bf16[4,32,768]{2,1,0:T(8,128)(2,1)S(1)}, bf16[4,32,768]{2,1,0:T(8,128)(2,1)S(1)}, u32[]{:S(2)}, u32[]{:S(2)}) collective-permute-start(bf16[4,32,768]{2,1,0:T(8,128)(2,1)S(1)} %slice.132), channel_id=1, source_target_pairs={{0,32},{32,64},{64,96},{96,128},{128,160},{160,192},{192,224},{1,3... | collective-permute-start | bytes 589832 | tf_op jit(solution)/shard_map/ppermute | solution.py:53
  7.9 3.5 %collective-permute-start.3 = (bf16[4,32,768]{2,1,0:T(8,128)(2,1)S(1)}, bf16[4,32,768]{2,1,0:T(8,128)(2,1)S(1)}, u32[]{:S(2)}, u32[]{:S(2)}) collective-permute-start(bf16[4,32,768]{2,1,0:T(8,128)(2,1)S(1)} %pad_maximum_fusion.2), channel_id=1, source_target_pairs={{0,8},{8,16},{16,24},{1,9},{9,17},{17,25},{2,10},{10,18},{18,26},{... | collective-permute-start | bytes 589832 | tf_op jit(solution)/shard_map/ppermute | solution.py:53
  11.4 2.0 %collective-permute-done.refs_2_ = bf16[4,32,768]{2,1,0:T(8,128)(2,1)S(1)} collective-permute-done((bf16[4,32,768]{2,1,0:T(8,128)(2,1)S(1)}, bf16[4,32,768]{2,1,0:T(8,128)(2,1)S(1)}, u32[]{:S(2)}, u32[]{:S(2)}) %collective-permute-start) | collective-permute-done | bytes 196640 | tf_op jit(solution)/shard_map/ppermute | solution.py:53
  13.5 3.5 %collective-permute-start.1 = (bf16[4,32,768]{2,1,0:T(8,128)(2,1)S(1)}, bf16[4,32,768]{2,1,0:T(8,128)(2,1)S(1)}, u32[]{:S(2)}, u32[]{:S(2)}) collective-permute-start(bf16[4,32,768]{2,1,0:T(8,128)(2,1)S(1)} %pad_maximum_fusion), channel_id=1, source_target_pairs={{0,8},{8,16},{16,24},{1,9},{9,17},{17,25},{2,10},{10,18},{18,26},{... | collective-permute-start | bytes 589832 | tf_op jit(solution)/shard_map/ppermute | solution.py:53
  17.0 0.0 collective-permute-done.3.refs_5_
  17.1 1.3 collective-permute-start.4
  18.4 2.8 %collective-permute-done.1.refs_3_ = bf16[4,32,768]{2,1,0:T(8,128)(2,1)S(1)} collective-permute-done((bf16[4,32,768]{2,1,0:T(8,128)(2,1)S(1)}, bf16[4,32,768]{2,1,0:T(8,128)(2,1)S(1)}, u32[]{:S(2)}, u32[]{:S(2)}) %collective-permute-start.1) | collective-permute-done | bytes 196640 | tf_op jit(solution)/shard_map/ppermute | solution.py:53
  21.2 3.2 %collective-permute-start.2 = (bf16[4,32,768]{2,1,0:T(8,128)(2,1)S(1)}, bf16[4,32,768]{2,1,0:T(8,128)(2,1)S(1)}, u32[]{:S(2)}, u32[]{:S(2)}) collective-permute-start(bf16[4,32,768]{2,1,0:T(8,128)(2,1)S(1)} %pad_maximum_fusion.1), channel_id=1, source_target_pairs={{0,1},{1,2},{2,3},{3,4},{4,5},{5,6},{6,7},{8,9},{9,10},{10,11},{11... | collective-permute-start | bytes 589832 | tf_op jit(solution)/shard_map/ppermute | solution.py:53
  24.4 0.0 collective-permute-done.4.refs_6_
  24.4 2.9 %collective-permute-start.5 = (bf16[4,32,768]{2,1,0:T(8,128)(2,1)S(1)}, bf16[4,32,768]{2,1,0:T(8,128)(2,1)S(1)}, u32[]{:S(2)}, u32[]{:S(2)}) collective-permute-start(bf16[4,32,768]{2,1,0:T(8,128)(2,1)S(1)} %pad_maximum_fusion.4), channel_id=1, source_target_pairs={{0,32},{32,64},{64,96},{96,128},{128,160},{160,192},{192,224},{1,3... | collective-permute-start | bytes 589832 | tf_op jit(solution)/shard_map/ppermute | solution.py:53
  27.4 0.0 copy-done.9
  27.4 0.0 collective-permute-done.2.refs_4_
  27.4 5.5 %collective-permute-done.5.refs_7_ = bf16[4,32,768]{2,1,0:T(8,128)(2,1)S(1)} collective-permute-done((bf16[4,32,768]{2,1,0:T(8,128)(2,1)S(1)}, bf16[4,32,768]{2,1,0:T(8,128)(2,1)S(1)}, u32[]{:S(2)}, u32[]{:S(2)}) %collective-permute-start.5) | collective-permute-done | bytes 196640 | tf_op jit(solution)/shard_map/ppermute | solution.py:53
  32.9 0.0 copy-done
  32.9 0.0 copy-start.5
  32.9 1.0 copy-done.5
  33.9 16.6 %shard_map.111 = (bf16[512,768]{1,0:T(8,128)(2,1)S(1)}, bf16[512,768]{1,0:T(8,128)(2,1)S(1)}, bf16[512,768]{1,0:T(8,128)(2,1)S(1)}, bf16[512,768]{1,0:T(8,128)(2...) custom-call(bf16[256,768]{1,0:T(8,128)(2,1)S(1)} %copy-done.3, ...), custom_call_target="tpu_custom_call" | custom-call | tf_op jit(solution)/shard_map/pallas_call | solution.py:300
  50.5 3.5 %shard_map.112 = bf16[512,2432]{1,0:T(8,128)(2,1)S(1)} custom-call(s32[1]{0:T(128)} %bitcast.refs_0_, bf16[512,768]{1,0:T(8,128)(2,1)S(1)} %get-tuple-element.50.refs_1_, bf16[512,768]{1,0:T(8,128)(2,1)S(1)} %get-tuple-element.51.refs_2_, bf16[512,768]{1,0:T(8,128)(2,1)S(1)} %get-tuple-element.52.refs_3_.refs_1_, ...), custom_call_target="tpu_custom_call" | custom-call | tf_op jit(solution)/shard_map/pallas_call | solution.py:300
  54.0 2.1 %collective-permute-start.6 = (bf16[512,2432]{1,0:T(8,128)(2,1)S(1)}, bf16[512,2432]{1,0:T(8,128)(2,1)S(1)}, u32[]{:S(2)}, u32[]{:S(2)}) collective-permute-start(bf16[512,2432]{1,0:T(8,128)(2,1)S(1)} %shard_map.112), channel_id=1, source_target_pairs={{0,1},{1,0},{2,3},{3,2},{4,5},{5,4},{6,7},{7,6},{8,9},{9,8},{10,11... | collective-permute-start | bytes 7471112 | tf_op jit(solution)/shard_map/ppermute | solution.py:87
  56.1 2.6 %shard_map.113 = (bf16[7,32,768]{2,1,0:T(8,128)(2,1)S(1)}, bf16[7,32,768]{2,1,0:T(8,128)(2,1)S(1)}, bf16[256,1536]{1,0:T(8,128)(2,1)S(1)}) custom-call(bf16[512,768]{1,0:T(8,128)(2,1)S(1)} %get-tuple-element.56.refs_0_, bf16[512,768]{1,0:T(8,128)(2,1)S(1)} %get-tuple-element.52.refs_3_.refs_1_, bf16[512,768]{1,0:T(8,128)(2,1)S(1)} %get-tuple-element.51.refs_2_, ...), custom_call_target="tpu_custom_call" | custom-call | tf_op jit(solution)/shard_map/pallas_call | solution.py:300
  58.8 0.0 copy-start.6
  58.8 0.0 copy-start.7
  58.8 1.3 collective-permute-start.7
  60.2 3.8 %collective-permute-start.8 = (bf16[4,32,768]{2,1,0:T(8,128)(2,1)S(1)}, bf16[4,32,768]{2,1,0:T(8,128)(2,1)}, u32[]{:S(2)}, u32[]{:S(2)}) collective-permute-start(bf16[4,32,768]{2,1,0:T(8,128)(2,1)S(1)} %slice.153), channel_id=1, source_target_pairs={{32,0},{64,32},{96,64},{128,96},{160,128},{192,160},{224,192},{33,... | collective-permute-start | bytes 589832 | tf_op jit(solution)/shard_map/ppermute | solution.py:53
  64.0 3.5 %shard_map.114.refs_0_ = bf16[512,2432]{1,0:T(8,128)(2,1)S(1)} custom-call(s32[1]{0:T(128)} %bitcast.refs_0_, bf16[512,768]{1,0:T(8,128)(2,1)S(1)} %get-tuple-element.50.refs_1_, bf16[512,768]{1,0:T(8,128)(2,1)S(1)} %get-tuple-element.51.refs_2_, bf16[512,768]{1,0:T(8,128)(2,1)S(1)} %get-tuple-element.52.refs_3_.refs_1_, ...), custom_call_target="tpu_custom_call" | custom-call | tf_op jit(solution)/shard_map/pallas_call | solution.py:300
  67.4 0.0 collective-permute-done.6.refs_1_
  67.4 2.0 %shard_map.115 = bf16[512,2432]{1,0:T(8,128)(2,1)} custom-call(bf16[512,2432]{1,0:T(8,128)(2,1)S(1)} %shard_map.114.refs_0_, bf16[512,2432]{1,0:T(8,128)(2,1)S(1)} %collective-permute-done.6.refs_1_), custom_call_target="tpu_custom_call" | custom-call | tf_op jit(solution)/shard_map/pallas_call | solution.py:300
  69.5 0.0 copy-done.7
  69.5 0.0 collective-permute-done.7.refs_1_
  69.5 0.4 collective-permute-done.8.refs_4_
  69.9 9.1 %all-to-all-start = ((bf16[32,16,2432]{2,1,0:T(8,128)(2,1)}), bf16[32,16,2432]{2,1,0:T(8,128)(2,1)S(1)}, u32[]{:S(2)}, u32[]{:S(2)}) async-start(bf16[32,16,2432]{2,1,0:T(8,128)(2,1)} %bitcast.1), calls=%async_computation | async-start | bytes 4980736 | tf_op jit(solution)/shard_map/all_to_all | solution.py:355
  79.0 0.8 fusion.6
  79.8 0.9 fusion
  80.7 0.7 pad_maximum_fusion.6
  81.4 2.5 %collective-permute-start.9 = (bf16[4,32,768]{2,1,0:T(8,128)(2,1)}, bf16[4,32,768]{2,1,0:T(8,128)(2,1)}, u32[]{:S(2)}, u32[]{:S(2)}) collective-permute-start(bf16[4,32,768]{2,1,0:T(8,128)(2,1)} %pad_maximum_fusion.6), channel_id=1, source_target_pairs={{8,0},{16,8},{24,16},{9,1},{17,9},{25,17},{10,2},{18,10},{26,18},{... | collective-permute-start | bytes 589832 | tf_op jit(solution)/shard_map/ppermute | solution.py:53
  83.9 0.7 pad_maximum_fusion.7
  84.6 1.3 collective-permute-start.10
  85.9 28.3 %all-to-all-done.refs_0_ = bf16[32,16,2432]{2,1,0:T(8,128)(2,1)S(1)} async-done(((bf16[32,16,2432]{2,1,0:T(8,128)(2,1)}), bf16[32,16,2432]{2,1,0:T(8,128)(2,1)S(1)}, u32[]{:S(2)}, u32[]{:S(2)}) %all-to-all-start) | async-done | bytes 2490400 | tf_op jit(solution)/shard_map/all_to_all | solution.py:355
  114.3 0.4 shard_map.116
  114.6 0.0 collective-permute-done.9.refs_2_
  114.6 0.0 collective-permute-done.10.refs_5_
  114.6 0.9 slice.164
  115.6 0.8 slice.162
  116.4 1.9 %collective-permute-start.11 = (bf16[4,32,768]{2,1,0:T(8,128)(2,1)S(1)}, bf16[4,32,768]{2,1,0:T(8,128)(2,1)S(1)}, u32[]{:S(2)}, u32[]{:S(2)}) collective-permute-start(bf16[4,32,768]{2,1,0:T(8,128)(2,1)S(1)} %pad_maximum_fusion.8), channel_id=1, source_target_pairs={{32,0},{64,32},{96,64},{128,96},{160,128},{192,160},{224,192},{33,... | collective-permute-start | bytes 589832 | tf_op jit(solution)/shard_map/ppermute | solution.py:53
  118.3 0.8 fusion.5
  119.2 0.8 slice.167
  120.0 0.8 slice.165
  120.8 1.9 %collective-permute-start.12 = (bf16[4,32,768]{2,1,0:T(8,128)(2,1)S(1)}, bf16[4,32,768]{2,1,0:T(8,128)(2,1)S(1)}, u32[]{:S(2)}, u32[]{:S(2)}) collective-permute-start(bf16[4,32,768]{2,1,0:T(8,128)(2,1)S(1)} %pad_maximum_fusion.9), channel_id=1, source_target_pairs={{8,0},{16,8},{24,16},{9,1},{17,9},{25,17},{10,2},{18,10},{26,18},{... | collective-permute-start | bytes 589832 | tf_op jit(solution)/shard_map/ppermute | solution.py:53
  122.7 5.3 %collective-permute-start.13 = (bf16[4,2432]{1,0:T(4,128)(2,1)S(1)}, bf16[4,2432]{1,0:T(4,128)(2,1)S(1)}, u32[]{:S(2)}, u32[]{:S(2)}) collective-permute-start(bf16[4,2432]{1,0:T(4,128)(2,1)S(1)} %get-tuple-element.79), channel_id=1, source_target_pairs={{0,2},{1,3},{2,0},{3,1},{4,6},{5,7},{6,4},{7,5},{8,10},{9,11},{10,... | collective-permute-start | bytes 58376 | tf_op jit(solution)/shard_map/ppermute | solution.py:87
  128.0 4.7 %collective-permute-start.14 = (bf16[4,2432]{1,0:T(4,128)(2,1)S(1)}, bf16[4,2432]{1,0:T(4,128)(2,1)S(1)}, u32[]{:S(2)}, u32[]{:S(2)}) collective-permute-start(bf16[4,2432]{1,0:T(4,128)(2,1)S(1)} %get-tuple-element.80), channel_id=1, source_target_pairs={{0,4},{1,5},{2,6},{3,7},{4,0},{5,1},{6,2},{7,3},{8,12},{9,13},{10,... | collective-permute-start | bytes 58376 | tf_op jit(solution)/shard_map/ppermute | solution.py:87
  132.7 0.5 collective-permute-start.15
  133.2 0.0 collective-permute-done.13.refs_1_
  133.2 2.5 %collective-permute-done.14.refs_2_ = bf16[4,2432]{1,0:T(4,128)(2,1)S(1)} collective-permute-done((bf16[4,2432]{1,0:T(4,128)(2,1)S(1)}, bf16[4,2432]{1,0:T(4,128)(2,1)S(1)}, u32[]{:S(2)}, u32[]{:S(2)}) %collective-permute-start.14) | collective-permute-done | bytes 19488 | tf_op jit(solution)/shard_map/ppermute | solution.py:87
  135.7 2.9 %collective-permute-done.15.refs_3_ = bf16[4,2432]{1,0:T(4,128)(2,1)S(1)} collective-permute-done((bf16[4,2432]{1,0:T(4,128)(2,1)S(1)}, bf16[4,2432]{1,0:T(4,128)(2,1)S(1)}, u32[]{:S(2)}, u32[]{:S(2)}) %collective-permute-start.15) | collective-permute-done | bytes 19488 | tf_op jit(solution)/shard_map/ppermute | solution.py:87
  138.6 0.6 shard_map.118
  139.2 0.6 slice_reduce_fusion
  139.8 0.0 collective-permute-done.11.refs_3_
  139.8 0.0 collective-permute-done.12.refs_6_
  139.8 2.4 %shard_map.117 = (bf16[256,768]{1,0:T(8,128)(2,1)}, bf16[256,768]{1,0:T(8,128)(2,1)}) custom-call(bf16[256,1536]{1,0:T(8,128)(2,1)S(1)} %get-tuple-element.58.refs_0_, bf16[4,32,768]{2,1,0:T(8,128)(2,1)S(1)} %collective-permute-done.7.refs_1_, bf16[4,32,768]{2,1,0:T(8,128)(2,1)} %collective-permute-done.9.refs_2_, ...), custom_call_target="tpu_custom_call" | custom-call | tf_op jit(solution)/shard_map/pallas_call | solution.py:300
  (32 shorter events, 0.4 us)
Async XLA Ops:
  1.3 1.0 copy-start.2
  2.3 1.0 copy-start.4
  3.3 24.0 %copy-start.9 = (f32[768]{0:T(1024)S(1)}, f32[768]{0:T(1024)}, u32[]{:S(2)}) copy-start(f32[768]{0:T(1024)} %param.8) | copy-start | bytes 9220
  3.3 29.6 %copy-start = (bf16[768,768]{1,0:T(8,128)(2,1)S(1)}, bf16[768,768]{1,0:T(8,128)(2,1)}, u32[]{:S(2)}) copy-start(bf16[768,768]{1,0:T(8,128)(2,1)} %refs_6_.1) | copy-start | bytes 3538948
  3.3 29.6 %copy-start.1 = (bf16[768,2304]{1,0:T(8,128)(2,1)S(1)}, bf16[768,2304]{1,0:T(8,128)(2,1)}, u32[]{:S(2)}) copy-start(bf16[768,2304]{1,0:T(8,128)(2,1)} %refs_10_.1) | copy-start | bytes 10616836
  3.3 29.6 %copy-start.3 = (bf16[256,768]{1,0:T(8,128)(2,1)S(1)}, bf16[256,768]{1,0:T(8,128)(2,1)}, u32[]{:S(2)}) copy-start(bf16[256,768]{1,0:T(8,128)(2,1)} %refs_0_.1) | copy-start | bytes 1179652
  3.3 29.6 %copy-start.8 = (s32[1,512]{1,0:T(1,128)S(1)}, s32[1,512]{1,0:T(1,128)}, u32[]{:S(2)}) copy-start(s32[1,512]{1,0:T(1,128)} %refs_4_.1) | copy-start | bytes 6148
  3.8 9.7 %collective-permute-start = (bf16[4,32,768]{2,1,0:T(8,128)(2,1)S(1)}, bf16[4,32,768]{2,1,0:T(8,128)(2,1)S(1)}, u32[]{:S(2)}, u32[]{:S(2)}) collective-permute-start(bf16[4,32,768]{2,1,0:T(8,128)(2,1)S(1)} %slice.132), channel_id=1, source_target_pairs={{0,32},{32,64},{64,96},{96,128},{128,160},{160,192},{192,224},{1,3... | collective-permute-start | bytes 589832 | tf_op jit(solution)/shard_map/ppermute | solution.py:53
  7.9 9.1 %collective-permute-start.3 = (bf16[4,32,768]{2,1,0:T(8,128)(2,1)S(1)}, bf16[4,32,768]{2,1,0:T(8,128)(2,1)S(1)}, u32[]{:S(2)}, u32[]{:S(2)}) collective-permute-start(bf16[4,32,768]{2,1,0:T(8,128)(2,1)S(1)} %pad_maximum_fusion.2), channel_id=1, source_target_pairs={{0,8},{8,16},{16,24},{1,9},{9,17},{17,25},{2,10},{10,18},{18,26},{... | collective-permute-start | bytes 589832 | tf_op jit(solution)/shard_map/ppermute | solution.py:53
  13.5 7.7 %collective-permute-start.1 = (bf16[4,32,768]{2,1,0:T(8,128)(2,1)S(1)}, bf16[4,32,768]{2,1,0:T(8,128)(2,1)S(1)}, u32[]{:S(2)}, u32[]{:S(2)}) collective-permute-start(bf16[4,32,768]{2,1,0:T(8,128)(2,1)S(1)} %pad_maximum_fusion), channel_id=1, source_target_pairs={{0,8},{8,16},{16,24},{1,9},{9,17},{17,25},{2,10},{10,18},{18,26},{... | collective-permute-start | bytes 589832 | tf_op jit(solution)/shard_map/ppermute | solution.py:53
  17.1 7.3 %collective-permute-start.4 = (bf16[4,32,768]{2,1,0:T(8,128)(2,1)S(1)}, bf16[4,32,768]{2,1,0:T(8,128)(2,1)S(1)}, u32[]{:S(2)}, u32[]{:S(2)}) collective-permute-start(bf16[4,32,768]{2,1,0:T(8,128)(2,1)S(1)} %pad_maximum_fusion.3), channel_id=1, source_target_pairs={{0,1},{1,2},{2,3},{3,4},{4,5},{5,6},{6,7},{8,9},{9,10},{10,11},{11... | collective-permute-start | bytes 589832 | tf_op jit(solution)/shard_map/ppermute | solution.py:53
  21.2 6.2 %collective-permute-start.2 = (bf16[4,32,768]{2,1,0:T(8,128)(2,1)S(1)}, bf16[4,32,768]{2,1,0:T(8,128)(2,1)S(1)}, u32[]{:S(2)}, u32[]{:S(2)}) collective-permute-start(bf16[4,32,768]{2,1,0:T(8,128)(2,1)S(1)} %pad_maximum_fusion.1), channel_id=1, source_target_pairs={{0,1},{1,2},{2,3},{3,4},{4,5},{5,6},{6,7},{8,9},{9,10},{10,11},{11... | collective-permute-start | bytes 589832 | tf_op jit(solution)/shard_map/ppermute | solution.py:53
  24.4 8.5 %collective-permute-start.5 = (bf16[4,32,768]{2,1,0:T(8,128)(2,1)S(1)}, bf16[4,32,768]{2,1,0:T(8,128)(2,1)S(1)}, u32[]{:S(2)}, u32[]{:S(2)}) collective-permute-start(bf16[4,32,768]{2,1,0:T(8,128)(2,1)S(1)} %pad_maximum_fusion.4), channel_id=1, source_target_pairs={{0,32},{32,64},{64,96},{96,128},{128,160},{160,192},{192,224},{1,3... | collective-permute-start | bytes 589832 | tf_op jit(solution)/shard_map/ppermute | solution.py:53
  32.9 1.0 copy-start.5
  54.0 13.5 %collective-permute-start.6 = (bf16[512,2432]{1,0:T(8,128)(2,1)S(1)}, bf16[512,2432]{1,0:T(8,128)(2,1)S(1)}, u32[]{:S(2)}, u32[]{:S(2)}) collective-permute-start(bf16[512,2432]{1,0:T(8,128)(2,1)S(1)} %shard_map.112), channel_id=1, source_target_pairs={{0,1},{1,0},{2,3},{3,2},{4,5},{5,4},{6,7},{7,6},{8,9},{9,8},{10,11... | collective-permute-start | bytes 7471112 | tf_op jit(solution)/shard_map/ppermute | solution.py:87
  58.8 10.7 %copy-start.6 = (bf16[7,32,768]{2,1,0:T(8,128)(2,1)}, bf16[7,32,768]{2,1,0:T(8,128)(2,1)S(1)}, u32[]{:S(2)}) copy-start(bf16[7,32,768]{2,1,0:T(8,128)(2,1)S(1)} %get-tuple-element.75) | copy-start | bytes 1032196
  58.8 10.7 %copy-start.7 = (bf16[7,32,768]{2,1,0:T(8,128)(2,1)}, bf16[7,32,768]{2,1,0:T(8,128)(2,1)S(1)}, u32[]{:S(2)}) copy-start(bf16[7,32,768]{2,1,0:T(8,128)(2,1)S(1)} %get-tuple-element.72) | copy-start | bytes 1032196
  58.8 10.6 %collective-permute-start.7 = (bf16[4,32,768]{2,1,0:T(8,128)(2,1)S(1)}, bf16[4,32,768]{2,1,0:T(8,128)(2,1)S(1)}, u32[]{:S(2)}, u32[]{:S(2)}) collective-permute-start(bf16[4,32,768]{2,1,0:T(8,128)(2,1)S(1)} %pad_maximum_fusion.5), channel_id=1, source_target_pairs={{1,0},{2,1},{3,2},{4,3},{5,4},{6,5},{7,6},{9,8},{10,9},{11,10},{12... | collective-permute-start | bytes 589832 | tf_op jit(solution)/shard_map/ppermute | solution.py:53
  60.2 9.7 %collective-permute-start.8 = (bf16[4,32,768]{2,1,0:T(8,128)(2,1)S(1)}, bf16[4,32,768]{2,1,0:T(8,128)(2,1)}, u32[]{:S(2)}, u32[]{:S(2)}) collective-permute-start(bf16[4,32,768]{2,1,0:T(8,128)(2,1)S(1)} %slice.153), channel_id=1, source_target_pairs={{32,0},{64,32},{96,64},{128,96},{160,128},{192,160},{224,192},{33,... | collective-permute-start | bytes 589832 | tf_op jit(solution)/shard_map/ppermute | solution.py:53
  69.9 44.4 %all-to-all-start = ((bf16[32,16,2432]{2,1,0:T(8,128)(2,1)}), bf16[32,16,2432]{2,1,0:T(8,128)(2,1)S(1)}, u32[]{:S(2)}, u32[]{:S(2)}) async-start(bf16[32,16,2432]{2,1,0:T(8,128)(2,1)} %bitcast.1), calls=%async_computation | async-start | bytes 4980736 | tf_op jit(solution)/shard_map/all_to_all | solution.py:355
  81.4 33.2 %collective-permute-start.9 = (bf16[4,32,768]{2,1,0:T(8,128)(2,1)}, bf16[4,32,768]{2,1,0:T(8,128)(2,1)}, u32[]{:S(2)}, u32[]{:S(2)}) collective-permute-start(bf16[4,32,768]{2,1,0:T(8,128)(2,1)} %pad_maximum_fusion.6), channel_id=1, source_target_pairs={{8,0},{16,8},{24,16},{9,1},{17,9},{25,17},{10,2},{18,10},{26,18},{... | collective-permute-start | bytes 589832 | tf_op jit(solution)/shard_map/ppermute | solution.py:53
  84.6 30.0 %collective-permute-start.10 = (bf16[4,32,768]{2,1,0:T(8,128)(2,1)}, bf16[4,32,768]{2,1,0:T(8,128)(2,1)}, u32[]{:S(2)}, u32[]{:S(2)}) collective-permute-start(bf16[4,32,768]{2,1,0:T(8,128)(2,1)} %pad_maximum_fusion.7), channel_id=1, source_target_pairs={{1,0},{2,1},{3,2},{4,3},{5,4},{6,5},{7,6},{9,8},{10,9},{11,10},{12... | collective-permute-start | bytes 589832 | tf_op jit(solution)/shard_map/ppermute | solution.py:53
  116.4 23.5 %collective-permute-start.11 = (bf16[4,32,768]{2,1,0:T(8,128)(2,1)S(1)}, bf16[4,32,768]{2,1,0:T(8,128)(2,1)S(1)}, u32[]{:S(2)}, u32[]{:S(2)}) collective-permute-start(bf16[4,32,768]{2,1,0:T(8,128)(2,1)S(1)} %pad_maximum_fusion.8), channel_id=1, source_target_pairs={{32,0},{64,32},{96,64},{128,96},{160,128},{192,160},{224,192},{33,... | collective-permute-start | bytes 589832 | tf_op jit(solution)/shard_map/ppermute | solution.py:53
  120.8 19.1 %collective-permute-start.12 = (bf16[4,32,768]{2,1,0:T(8,128)(2,1)S(1)}, bf16[4,32,768]{2,1,0:T(8,128)(2,1)S(1)}, u32[]{:S(2)}, u32[]{:S(2)}) collective-permute-start(bf16[4,32,768]{2,1,0:T(8,128)(2,1)S(1)} %pad_maximum_fusion.9), channel_id=1, source_target_pairs={{8,0},{16,8},{24,16},{9,1},{17,9},{25,17},{10,2},{18,10},{26,18},{... | collective-permute-start | bytes 589832 | tf_op jit(solution)/shard_map/ppermute | solution.py:53
  122.7 10.4 %collective-permute-start.13 = (bf16[4,2432]{1,0:T(4,128)(2,1)S(1)}, bf16[4,2432]{1,0:T(4,128)(2,1)S(1)}, u32[]{:S(2)}, u32[]{:S(2)}) collective-permute-start(bf16[4,2432]{1,0:T(4,128)(2,1)S(1)} %get-tuple-element.79), channel_id=1, source_target_pairs={{0,2},{1,3},{2,0},{3,1},{4,6},{5,7},{6,4},{7,5},{8,10},{9,11},{10,... | collective-permute-start | bytes 58376 | tf_op jit(solution)/shard_map/ppermute | solution.py:87
  128.0 7.7 %collective-permute-start.14 = (bf16[4,2432]{1,0:T(4,128)(2,1)S(1)}, bf16[4,2432]{1,0:T(4,128)(2,1)S(1)}, u32[]{:S(2)}, u32[]{:S(2)}) collective-permute-start(bf16[4,2432]{1,0:T(4,128)(2,1)S(1)} %get-tuple-element.80), channel_id=1, source_target_pairs={{0,4},{1,5},{2,6},{3,7},{4,0},{5,1},{6,2},{7,3},{8,12},{9,13},{10,... | collective-permute-start | bytes 58376 | tf_op jit(solution)/shard_map/ppermute | solution.py:87
  132.7 5.9 %collective-permute-start.15 = (bf16[4,2432]{1,0:T(4,128)(2,1)S(1)}, bf16[4,2432]{1,0:T(4,128)(2,1)S(1)}, u32[]{:S(2)}, u32[]{:S(2)}) collective-permute-start(bf16[4,2432]{1,0:T(4,128)(2,1)S(1)} %get-tuple-element.81), channel_id=1, source_target_pairs={{0,6},{1,7},{2,4},{3,5},{4,2},{5,3},{6,0},{7,1},{8,14},{9,15},{10,... | collective-permute-start | bytes 58376 | tf_op jit(solution)/shard_map/ppermute | solution.py:87

commit v6 on v5

--- a/solution.py
+++ b/solution.py
@@ -16,8 +16,8 @@
 MAIN, BACK, SUMS, SMALL = 18, 16, 12, 6
 COLS = 3 * D + 128
 AXES = ("gx", "gy", "gz")
-FIRST = ("gx", "gy", "gz")
-SECOND = ("gy", "gz", "gx")
+UP = (("gx", "gy", "gz"), ("gz", "gx", "gy"))
+DOWN = (("gz", "gy", "gx"), ("gx", "gz", "gy"))
 EPSILON = 1e-06
 BIG_NEGATIVE = -1e30
 BF = jnp.bfloat16
@@ -147,7 +147,7 @@
     xs_ref, gos_ref, normed_ref, mixed_ref, dpacked_ref, dn_ref, gain_sum_ref,
     rows_ref, packed_ref, delta_ref, held_ref, sems,
 ):
-    copies = fetches(t_refs, g_refs, (FIRST, SECOND), rows_ref, ROWS, sems)
+    copies = fetches(t_refs, g_refs, UP, rows_ref, ROWS, sems)
     own = rows_ref.at[pl.ds(0, ROWS), :]
     copies.append(pltpu.make_async_copy(tok_ref, own.at[:, pl.ds(0, D)], sems.at[0, 7]))
     copies.append(pltpu.make_async_copy(go_ref, own.at[:, pl.ds(D, D)], sems.at[1, 7]))
@@ -258,7 +258,7 @@
 
 
 def join_body(kept_ref, t_refs, g_refs, send_ref, out_ref, grad_ref, own_ref, rows_ref, sems):
-    copies = fetches(t_refs, g_refs, (FIRST[::-1], SECOND[::-1]), rows_ref, 0, sems)
+    copies = fetches(t_refs, g_refs, DOWN, rows_ref, 0, sems)
     copies.append(pltpu.make_async_copy(kept_ref, own_ref, sems.at[2, 0]))
     for copy in copies:
         copy.start()
@@ -275,15 +275,15 @@
     out_ref[...] = (own_ref[...].astype(F32) + got_ref[...].astype(F32)).astype(BF)
 
 
-def sum2_body(got_ref, *outs):
+def sum2_body(me_ref, got_ref, out_ref):
     total = jnp.sum(got_ref[...].astype(F32), axis=0)
     for i in range(4):
-        outs[i][...] = total[4 * i : 4 * (i + 1)].astype(BF)
-
-
-def sum3_body(a_ref, b_ref, c_ref, d_ref, qkv_ref, out_ref, gain_ref):
-    total = a_ref[...].astype(F32) + b_ref[...].astype(F32)
-    total += c_ref[...].astype(F32) + d_ref[...].astype(F32)
+        rows = jnp.concatenate([total[4 * i : 4 * (i + 1)], jnp.zeros((4, COLS), F32)])
+        out_ref[(me_ref[0] // 2) ^ i] = rows.astype(BF)
+
+
+def sum3_body(got_ref, qkv_ref, out_ref, gain_ref):
+    total = jnp.sum(got_ref[...].astype(F32), axis=0)
     qkv_ref[...] = total[:3, : 3 * D]
     for g in range(3):
         out_ref[g : g + 1, :] = total[3:4, g * D : (g + 1) * D]
@@ -316,7 +316,7 @@
     up = [[blocks[0]], [blocks[1]]]
     places = starts()
     for number in range(3):
-        up = step(up, places, (FIRST, SECOND), number, 1)
+        up = step(up, places, UP, number, 1)
     arrived_t, arrived_g = up[0][1:], up[1][1:]
 
     slot, wide, half = ((SLOTS, D), BF), ((SLOTS, 3 * D), BF), ((HALF, COLS), BF)
@@ -345,20 +345,23 @@
         scratch=[pltpu.VMEM((SLOTS, WIDE), BF)],
         mib=BACK,
     )
-    ways, places = (FIRST[::-1], SECOND[::-1]), starts()
-    down = step([[back_t], [back_g]], places, ways, 0, -1)
+    places = starts()
+    down = step([[back_t], [back_g]], places, DOWN, 0, -1)
     (own,) = call(functools.partial(half_sums, 0), [half], *operands, smem=(0,), mib=SUMS)
 
     (paired,) = call(sum1_body, [half], own, got)
     paired, down = lax.optimization_barrier((paired, down))
-    down = step(down, places, ways, 1, -1)
+    down = step(down, places, DOWN, 1, -1)
     spread = lax.all_to_all(paired, ("gx", "gy"), split_axis=0, concat_axis=0, tiled=True)
-    parts = call(sum2_body, [((4, COLS), BF)] * 4, spread.reshape(32, 16, COLS))
-    parts, down = lax.optimization_barrier((parts, down))
-    down = step(down, places, ways, 2, -1)
-    last = [parts[0]] + [crossed(parts[i], "gz", 2 * i) for i in range(1, 4)]
+    (part,) = call(sum2_body, [((4, 8, COLS), BF)], me, spread.reshape(32, 16, COLS), smem=(0,))
+    part, down = lax.optimization_barrier((part, down))
+    down = step(down, places, DOWN, 2, -1)
+    groups = [[2 * i + core for i in range(4)] for core in range(2)]
+    last = lax.all_to_all(
+        part, "gz", split_axis=0, concat_axis=0, tiled=True, axis_index_groups=groups
+    )
     grad_qkv, grad_proj, gain_rows = call(
-        sum3_body, [((3, 3 * D), F32), ((3, D), F32), ((3, 128), F32)], *last
+        sum3_body, [((3, 3 * D), F32), ((3, D), F32), ((3, 128), F32)], last
     )
 
     block_out, grad_tokens = call(

time: 144 us -> 142 us (0.986)
  starting transfers between devices: 52.8 us -> 43.8 us
  waiting for transfers between devices: 44.5 us -> 51.4 us
    ppermute x12, waiting for transfers between devices: 10.7 us -> 23.9 us  [passed_along(): lax.ppermute(value, axis, [(source, source + steps) for source in range(i...]
    ppermute x4 -> x1, starting transfers between devices: 12.6 us -> 0.39 us  [crossed(): lax.ppermute(value, axis, [(source, source ^ mask) for source in range(co...]
    all_to_all x0 -> x1, starting transfers between devices: none -> 6.63 us  [on_device(): lax.all_to_all(part, 'gz', split_axis=0, concat_axis=0, tiled=True, axis_...]
    ppermute x4 -> x1, waiting for transfers between devices: 5.42 us -> 0.01 us  [crossed(): lax.ppermute(value, axis, [(source, source ^ mask) for source in range(co...]
    all_to_all x1, starting transfers between devices: 9.12 us -> 7.31 us  [on_device(): lax.all_to_all(paired, ('gx', 'gy'), split_axis=0, concat_axis=0, tiled=T...]
    ppermute x12, starting transfers between devices: 31.1 us -> 29.5 us  [passed_along(): lax.ppermute(value, axis, [(source, source + steps) for source in range(i...]
    slice x20 -> x19, local copies, waits for them, and re-layouts: 6 us -> 6 us  [stage(): lax.slice_in_dim(arrays[place[k][0]], place[k][1], place[k][1] + 1)]
  transfers between devices with their start and end apart: 17 -> 15, of which waited for: 7 -> 7; matrix products, arithmetic and copies ran while one was open for 5% -> 4% of each run, Pallas kernels for 6% -> 8%
where the time goes in v6:
time: 142 us; the launch traced here: 141 us
  waiting for transfers between devices  51.4 us (36%)
  starting transfers between devices  43.8 us (31%)
  Pallas kernels  32.6 us (23%)
  local copies, waits for them, and re-layouts  10.3 us (7%)
  other arithmetic  1.61 us (1%)
    pallas_call x9, Pallas kernels, call(): pl.pallas_call(flat, out_shape=[jax.ShapeDtypeStruct(shape, dtype) for sh...  32.6 us
    ppermute x12, starting transfers between devices, passed_along(): lax.ppermute(value, axis, [(source, source + steps) for source in range(i...  29.5 us
    all_to_all x1, waiting for transfers between devices, on_device(): lax.all_to_all(paired, ('gx', 'gy'), split_axis=0, concat_axis=0, tiled=T...  27.4 us
    ppermute x12, waiting for transfers between devices, passed_along(): lax.ppermute(value, axis, [(source, source + steps) for source in range(i...  23.9 us
    all_to_all x1, starting transfers between devices, on_device(): lax.all_to_all(paired, ('gx', 'gy'), split_axis=0, concat_axis=0, tiled=T...  7.31 us
    all_to_all x1, starting transfers between devices, on_device(): lax.all_to_all(part, 'gz', split_axis=0, concat_axis=0, tiled=True, axis_...  6.63 us
    slice x19, local copies, waits for them, and re-layouts, stage(): lax.slice_in_dim(arrays[place[k][0]], place[k][1], place[k][1] + 1)  6 us
    unnamed x21, local copies, waits for them, and re-layouts  3.7 us
  transfers between devices with their start and end apart: 15, of which 7 were waited for; matrix products, arithmetic and copies ran while one was open for 4% of the time, Pallas kernels for 8%

profile of v6, /device:TPU:10, one launch (start us, length us, event | category | flops | bytes accessed | tf_op | source)
XLA Modules:
  0.0 140.7 jit_solution(4836282250932914727)
XLA Ops:
  0.6 0.7 copy.14.refs_2_.refs_7_
  1.3 1.0 copy-done.2
  2.3 1.0 copy-done.4
  3.3 0.0 copy-start.8
  3.3 0.4 shard_map.110
  3.8 4.1 %collective-permute-start = (bf16[4,32,768]{2,1,0:T(8,128)(2,1)S(1)}, bf16[4,32,768]{2,1,0:T(8,128)(2,1)S(1)}, u32[]{:S(2)}, u32[]{:S(2)}) collective-permute-start(bf16[4,32,768]{2,1,0:T(8,128)(2,1)S(1)} %slice.133), channel_id=1, source_target_pairs={{0,32},{32,64},{64,96},{96,128},{128,160},{160,192},{192,224},{1,3... | collective-permute-start | bytes 589832 | tf_op jit(solution)/shard_map/ppermute | solution.py:53
  7.9 1.5 %collective-permute-start.3 = (bf16[4,32,768]{2,1,0:T(8,128)(2,1)S(1)}, bf16[4,32,768]{2,1,0:T(8,128)(2,1)S(1)}, u32[]{:S(2)}, u32[]{:S(2)}) collective-permute-start(bf16[4,32,768]{2,1,0:T(8,128)(2,1)S(1)} %pad_maximum_fusion.2), channel_id=1, source_target_pairs={{0,1},{1,2},{2,3},{3,4},{4,5},{5,6},{6,7},{8,9},{9,10},{10,11},{11... | collective-permute-start | bytes 589832 | tf_op jit(solution)/shard_map/ppermute | solution.py:53
  9.4 4.0 %collective-permute-done.refs_2_ = bf16[4,32,768]{2,1,0:T(8,128)(2,1)S(1)} collective-permute-done((bf16[4,32,768]{2,1,0:T(8,128)(2,1)S(1)}, bf16[4,32,768]{2,1,0:T(8,128)(2,1)S(1)}, u32[]{:S(2)}, u32[]{:S(2)}) %collective-permute-start) | collective-permute-done | bytes 196640 | tf_op jit(solution)/shard_map/ppermute | solution.py:53
  13.5 3.5 %collective-permute-start.1 = (bf16[4,32,768]{2,1,0:T(8,128)(2,1)S(1)}, bf16[4,32,768]{2,1,0:T(8,128)(2,1)S(1)}, u32[]{:S(2)}, u32[]{:S(2)}) collective-permute-start(bf16[4,32,768]{2,1,0:T(8,128)(2,1)S(1)} %pad_maximum_fusion), channel_id=1, source_target_pairs={{0,8},{8,16},{16,24},{1,9},{9,17},{17,25},{2,10},{10,18},{18,26},{... | collective-permute-start | bytes 589832 | tf_op jit(solution)/shard_map/ppermute | solution.py:53
  17.0 0.0 collective-permute-done.3.refs_5_
  17.1 2.9 %collective-permute-start.4 = (bf16[4,32,768]{2,1,0:T(8,128)(2,1)S(1)}, bf16[4,32,768]{2,1,0:T(8,128)(2,1)S(1)}, u32[]{:S(2)}, u32[]{:S(2)}) collective-permute-start(bf16[4,32,768]{2,1,0:T(8,128)(2,1)S(1)} %pad_maximum_fusion.3), channel_id=1, source_target_pairs={{0,32},{32,64},{64,96},{96,128},{128,160},{160,192},{192,224},{1,3... | collective-permute-start | bytes 589832 | tf_op jit(solution)/shard_map/ppermute | solution.py:53
  20.0 2.0 %collective-permute-done.1.refs_3_ = bf16[4,32,768]{2,1,0:T(8,128)(2,1)S(1)} collective-permute-done((bf16[4,32,768]{2,1,0:T(8,128)(2,1)S(1)}, bf16[4,32,768]{2,1,0:T(8,128)(2,1)S(1)}, u32[]{:S(2)}, u32[]{:S(2)}) %collective-permute-start.1) | collective-permute-done | bytes 196640 | tf_op jit(solution)/shard_map/ppermute | solution.py:53
  22.1 1.3 collective-permute-start.2
  23.4 2.8 %collective-permute-done.4.refs_6_ = bf16[4,32,768]{2,1,0:T(8,128)(2,1)S(1)} collective-permute-done((bf16[4,32,768]{2,1,0:T(8,128)(2,1)S(1)}, bf16[4,32,768]{2,1,0:T(8,128)(2,1)S(1)}, u32[]{:S(2)}, u32[]{:S(2)}) %collective-permute-start.4) | collective-permute-done | bytes 196640 | tf_op jit(solution)/shard_map/ppermute | solution.py:53
  26.2 3.3 %collective-permute-start.5 = (bf16[4,32,768]{2,1,0:T(8,128)(2,1)S(1)}, bf16[4,32,768]{2,1,0:T(8,128)(2,1)S(1)}, u32[]{:S(2)}, u32[]{:S(2)}) collective-permute-start(bf16[4,32,768]{2,1,0:T(8,128)(2,1)S(1)} %pad_maximum_fusion.4), channel_id=1, source_target_pairs={{0,8},{8,16},{16,24},{1,9},{9,17},{17,25},{2,10},{10,18},{18,26},{... | collective-permute-start | bytes 589832 | tf_op jit(solution)/shard_map/ppermute | solution.py:53
  29.5 0.0 copy-done.9
  29.6 0.0 collective-permute-done.2.refs_4_
  29.6 5.9 %collective-permute-done.5.refs_7_ = bf16[4,32,768]{2,1,0:T(8,128)(2,1)S(1)} collective-permute-done((bf16[4,32,768]{2,1,0:T(8,128)(2,1)S(1)}, bf16[4,32,768]{2,1,0:T(8,128)(2,1)S(1)}, u32[]{:S(2)}, u32[]{:S(2)}) %collective-permute-start.5) | collective-permute-done | bytes 196640 | tf_op jit(solution)/shard_map/ppermute | solution.py:53
  35.4 0.0 copy-done
  35.4 0.0 copy-done.1
  35.4 0.0 copy-done.3
  35.5 0.0 copy-done.8
  35.5 0.0 copy-start.5
  35.5 1.0 copy-done.5
  36.5 16.6 %shard_map.111 = (bf16[512,768]{1,0:T(8,128)(2,1)S(1)}, bf16[512,768]{1,0:T(8,128)(2,1)S(1)}, bf16[512,768]{1,0:T(8,128)(2,1)S(1)}, bf16[512,768]{1,0:T(8,128)(2...) custom-call(bf16[256,768]{1,0:T(8,128)(2,1)S(1)} %copy-done.3, ...), custom_call_target="tpu_custom_call" | custom-call | tf_op jit(solution)/shard_map/pallas_call | solution.py:300
  53.1 3.5 %shard_map.112 = bf16[512,2432]{1,0:T(8,128)(2,1)S(1)} custom-call(s32[1]{0:T(128)} %bitcast.refs_0_, bf16[512,768]{1,0:T(8,128)(2,1)S(1)} %get-tuple-element.43.refs_1_, bf16[512,768]{1,0:T(8,128)(2,1)S(1)} %get-tuple-element.44.refs_2_, bf16[512,768]{1,0:T(8,128)(2,1)S(1)} %get-tuple-element.45.refs_3_.refs_1_, ...), custom_call_target="tpu_custom_call" | custom-call | tf_op jit(solution)/shard_map/pallas_call | solution.py:300
  56.5 0.4 collective-permute-start.6
  56.9 2.6 %shard_map.113 = (bf16[7,32,768]{2,1,0:T(8,128)(2,1)S(1)}, bf16[7,32,768]{2,1,0:T(8,128)(2,1)S(1)}, bf16[256,1536]{1,0:T(8,128)(2,1)S(1)}) custom-call(bf16[512,768]{1,0:T(8,128)(2,1)S(1)} %get-tuple-element.49.refs_0_, bf16[512,768]{1,0:T(8,128)(2,1)S(1)} %get-tuple-element.45.refs_3_.refs_1_, bf16[512,768]{1,0:T(8,128)(2,1)S(1)} %get-tuple-element.44.refs_2_, ...), custom_call_target="tpu_custom_call" | custom-call | tf_op jit(solution)/shard_map/pallas_call | solution.py:300
  59.6 0.0 copy-start.6
  59.6 0.0 copy-start.7
  59.6 1.3 collective-permute-start.7
  61.0 3.6 %collective-permute-start.8 = (bf16[4,32,768]{2,1,0:T(8,128)(2,1)S(1)}, bf16[4,32,768]{2,1,0:T(8,128)(2,1)}, u32[]{:S(2)}, u32[]{:S(2)}) collective-permute-start(bf16[4,32,768]{2,1,0:T(8,128)(2,1)S(1)} %slice.155), channel_id=1, source_target_pairs={{32,0},{64,32},{96,64},{128,96},{160,128},{192,160},{224,192},{33,... | collective-permute-start | bytes 589832 | tf_op jit(solution)/shard_map/ppermute | solution.py:53
  64.6 3.5 %shard_map.114.refs_0_ = bf16[512,2432]{1,0:T(8,128)(2,1)S(1)} custom-call(s32[1]{0:T(128)} %bitcast.refs_0_, bf16[512,768]{1,0:T(8,128)(2,1)S(1)} %get-tuple-element.43.refs_1_, bf16[512,768]{1,0:T(8,128)(2,1)S(1)} %get-tuple-element.44.refs_2_, bf16[512,768]{1,0:T(8,128)(2,1)S(1)} %get-tuple-element.45.refs_3_.refs_1_, ...), custom_call_target="tpu_custom_call" | custom-call | tf_op jit(solution)/shard_map/pallas_call | solution.py:300
  68.0 0.0 collective-permute-done.6.refs_1_
  68.0 2.0 %shard_map.115 = bf16[512,2432]{1,0:T(8,128)(2,1)} custom-call(bf16[512,2432]{1,0:T(8,128)(2,1)S(1)} %shard_map.114.refs_0_, bf16[512,2432]{1,0:T(8,128)(2,1)S(1)} %collective-permute-done.6.refs_1_), custom_call_target="tpu_custom_call" | custom-call | tf_op jit(solution)/shard_map/pallas_call | solution.py:300
  70.1 0.0 copy-done.6
  70.1 0.0 copy-done.7
  70.1 0.0 collective-permute-done.7.refs_1_
  70.1 2.6 %collective-permute-done.8.refs_4_ = bf16[4,32,768]{2,1,0:T(8,128)(2,1)} collective-permute-done((bf16[4,32,768]{2,1,0:T(8,128)(2,1)S(1)}, bf16[4,32,768]{2,1,0:T(8,128)(2,1)}, u32[]{:S(2)}, u32[]{:S(2)}) %collective-permute-start.8) | collective-permute-done | bytes 196640 | tf_op jit(solution)/shard_map/ppermute | solution.py:53
  72.7 7.3 %all-to-all-start = ((bf16[32,16,2432]{2,1,0:T(8,128)(2,1)}), bf16[32,16,2432]{2,1,0:T(8,128)(2,1)S(1)}, u32[]{:S(2)}, u32[]{:S(2)}) async-start(bf16[32,16,2432]{2,1,0:T(8,128)(2,1)} %bitcast.1), calls=%async_computation | async-start | bytes 4980736 | tf_op jit(solution)/shard_map/all_to_all | solution.py:355
  80.0 0.8 fusion.5
  80.8 0.9 fusion
  81.7 0.7 pad_maximum_fusion.6
  82.4 2.5 %collective-permute-start.9 = (bf16[4,32,768]{2,1,0:T(8,128)(2,1)}, bf16[4,32,768]{2,1,0:T(8,128)(2,1)}, u32[]{:S(2)}, u32[]{:S(2)}) collective-permute-start(bf16[4,32,768]{2,1,0:T(8,128)(2,1)} %pad_maximum_fusion.6), channel_id=1, source_target_pairs={{8,0},{16,8},{24,16},{9,1},{17,9},{25,17},{10,2},{18,10},{26,18},{... | collective-permute-start | bytes 589832 | tf_op jit(solution)/shard_map/ppermute | solution.py:53
  84.9 0.7 pad_maximum_fusion.7
  85.6 1.3 collective-permute-start.10
  86.9 27.4 %all-to-all-done.refs_1_ = bf16[32,16,2432]{2,1,0:T(8,128)(2,1)S(1)} async-done(((bf16[32,16,2432]{2,1,0:T(8,128)(2,1)}), bf16[32,16,2432]{2,1,0:T(8,128)(2,1)S(1)}, u32[]{:S(2)}, u32[]{:S(2)}) %all-to-all-start) | async-done | bytes 2490400 | tf_op jit(solution)/shard_map/all_to_all | solution.py:355
  114.3 1.0 shard_map.116
  115.3 0.0 collective-permute-done.9.refs_2_
  115.3 0.0 collective-permute-done.10.refs_5_
  115.3 0.9 slice.166
  116.2 0.8 slice.164
  117.1 1.9 %collective-permute-start.11 = (bf16[4,32,768]{2,1,0:T(8,128)(2,1)S(1)}, bf16[4,32,768]{2,1,0:T(8,128)(2,1)S(1)}, u32[]{:S(2)}, u32[]{:S(2)}) collective-permute-start(bf16[4,32,768]{2,1,0:T(8,128)(2,1)S(1)} %pad_maximum_fusion.8), channel_id=1, source_target_pairs={{32,0},{64,32},{96,64},{128,96},{160,128},{192,160},{224,192},{33,... | collective-permute-start | bytes 589832 | tf_op jit(solution)/shard_map/ppermute | solution.py:53
  119.0 0.8 fusion.4
  119.8 0.8 slice.169
  120.6 0.8 slice.167
  121.4 6.6 %all-to-all-start.1 = ((bf16[4,8,2432]{2,1,0:T(8,128)(2,1)}), bf16[4,8,2432]{2,1,0:T(8,128)(2,1)S(1)}, u32[]{:S(2)}, u32[]{:S(2)}) async-start(bf16[4,8,2432]{2,1,0:T(8,128)(2,1)} %shard_map.116), calls=%async_computation.1 | async-start | bytes 311296 | tf_op jit(solution)/shard_map/all_to_all | solution.py:360
  128.1 2.4 %collective-permute-start.12 = (bf16[4,32,768]{2,1,0:T(8,128)(2,1)S(1)}, bf16[4,32,768]{2,1,0:T(8,128)(2,1)S(1)}, u32[]{:S(2)}, u32[]{:S(2)}) collective-permute-start(bf16[4,32,768]{2,1,0:T(8,128)(2,1)S(1)} %pad_maximum_fusion.9), channel_id=1, source_target_pairs={{8,0},{16,8},{24,16},{9,1},{17,9},{25,17},{10,2},{18,10},{26,18},{... | collective-permute-start | bytes 589832 | tf_op jit(solution)/shard_map/ppermute | solution.py:53
  130.5 0.0 collective-permute-done.11.refs_3_
  130.5 6.6 %collective-permute-done.12.refs_6_ = bf16[4,32,768]{2,1,0:T(8,128)(2,1)S(1)} collective-permute-done((bf16[4,32,768]{2,1,0:T(8,128)(2,1)S(1)}, bf16[4,32,768]{2,1,0:T(8,128)(2,1)S(1)}, u32[]{:S(2)}, u32[]{:S(2)}) %collective-permute-start.12) | collective-permute-done | bytes 196640 | tf_op jit(solution)/shard_map/ppermute | solution.py:53
  137.1 2.4 %shard_map.117 = (bf16[256,768]{1,0:T(8,128)(2,1)}, bf16[256,768]{1,0:T(8,128)(2,1)}) custom-call(bf16[256,1536]{1,0:T(8,128)(2,1)S(1)} %get-tuple-element.51.refs_0_, bf16[4,32,768]{2,1,0:T(8,128)(2,1)S(1)} %collective-permute-done.7.refs_1_, bf16[4,32,768]{2,1,0:T(8,128)(2,1)} %collective-permute-done.9.refs_2_, ...), custom_call_target="tpu_custom_call" | custom-call | tf_op jit(solution)/shard_map/pallas_call | solution.py:300
  139.4 0.0 all-to-all-done.1.refs_0_
  139.4 0.6 shard_map.118
  140.1 0.6 slice_reduce_fusion
  (27 shorter events, 0.4 us)
Async XLA Ops:
  1.3 1.0 copy-start.2
  2.3 1.0 copy-start.4
  3.3 26.2 %copy-start.9 = (f32[768]{0:T(1024)S(1)}, f32[768]{0:T(1024)}, u32[]{:S(2)}) copy-start(f32[768]{0:T(1024)} %param.8) | copy-start | bytes 9220
  3.3 32.1 %copy-start = (bf16[768,768]{1,0:T(8,128)(2,1)S(1)}, bf16[768,768]{1,0:T(8,128)(2,1)}, u32[]{:S(2)}) copy-start(bf16[768,768]{1,0:T(8,128)(2,1)} %refs_6_.1) | copy-start | bytes 3538948
  3.3 32.1 %copy-start.1 = (bf16[768,2304]{1,0:T(8,128)(2,1)S(1)}, bf16[768,2304]{1,0:T(8,128)(2,1)}, u32[]{:S(2)}) copy-start(bf16[768,2304]{1,0:T(8,128)(2,1)} %refs_10_.1) | copy-start | bytes 10616836
  3.3 32.1 %copy-start.3 = (bf16[256,768]{1,0:T(8,128)(2,1)S(1)}, bf16[256,768]{1,0:T(8,128)(2,1)}, u32[]{:S(2)}) copy-start(bf16[256,768]{1,0:T(8,128)(2,1)} %refs_0_.1) | copy-start | bytes 1179652
  3.3 32.1 %copy-start.8 = (s32[1,512]{1,0:T(1,128)S(1)}, s32[1,512]{1,0:T(1,128)}, u32[]{:S(2)}) copy-start(s32[1,512]{1,0:T(1,128)} %refs_4_.1) | copy-start | bytes 6148
  3.8 9.7 %collective-permute-start = (bf16[4,32,768]{2,1,0:T(8,128)(2,1)S(1)}, bf16[4,32,768]{2,1,0:T(8,128)(2,1)S(1)}, u32[]{:S(2)}, u32[]{:S(2)}) collective-permute-start(bf16[4,32,768]{2,1,0:T(8,128)(2,1)S(1)} %slice.133), channel_id=1, source_target_pairs={{0,32},{32,64},{64,96},{96,128},{128,160},{160,192},{192,224},{1,3... | collective-permute-start | bytes 589832 | tf_op jit(solution)/shard_map/ppermute | solution.py:53
  7.9 9.1 %collective-permute-start.3 = (bf16[4,32,768]{2,1,0:T(8,128)(2,1)S(1)}, bf16[4,32,768]{2,1,0:T(8,128)(2,1)S(1)}, u32[]{:S(2)}, u32[]{:S(2)}) collective-permute-start(bf16[4,32,768]{2,1,0:T(8,128)(2,1)S(1)} %pad_maximum_fusion.2), channel_id=1, source_target_pairs={{0,1},{1,2},{2,3},{3,4},{4,5},{5,6},{6,7},{8,9},{9,10},{10,11},{11... | collective-permute-start | bytes 589832 | tf_op jit(solution)/shard_map/ppermute | solution.py:53
  13.5 8.5 %collective-permute-start.1 = (bf16[4,32,768]{2,1,0:T(8,128)(2,1)S(1)}, bf16[4,32,768]{2,1,0:T(8,128)(2,1)S(1)}, u32[]{:S(2)}, u32[]{:S(2)}) collective-permute-start(bf16[4,32,768]{2,1,0:T(8,128)(2,1)S(1)} %pad_maximum_fusion), channel_id=1, source_target_pairs={{0,8},{8,16},{16,24},{1,9},{9,17},{17,25},{2,10},{10,18},{18,26},{... | collective-permute-start | bytes 589832 | tf_op jit(solution)/shard_map/ppermute | solution.py:53
  17.1 9.1 %collective-permute-start.4 = (bf16[4,32,768]{2,1,0:T(8,128)(2,1)S(1)}, bf16[4,32,768]{2,1,0:T(8,128)(2,1)S(1)}, u32[]{:S(2)}, u32[]{:S(2)}) collective-permute-start(bf16[4,32,768]{2,1,0:T(8,128)(2,1)S(1)} %pad_maximum_fusion.3), channel_id=1, source_target_pairs={{0,32},{32,64},{64,96},{96,128},{128,160},{160,192},{192,224},{1,3... | collective-permute-start | bytes 589832 | tf_op jit(solution)/shard_map/ppermute | solution.py:53
  22.1 7.5 %collective-permute-start.2 = (bf16[4,32,768]{2,1,0:T(8,128)(2,1)S(1)}, bf16[4,32,768]{2,1,0:T(8,128)(2,1)S(1)}, u32[]{:S(2)}, u32[]{:S(2)}) collective-permute-start(bf16[4,32,768]{2,1,0:T(8,128)(2,1)S(1)} %pad_maximum_fusion.1), channel_id=1, source_target_pairs={{0,1},{1,2},{2,3},{3,4},{4,5},{5,6},{6,7},{8,9},{9,10},{10,11},{11... | collective-permute-start | bytes 589832 | tf_op jit(solution)/shard_map/ppermute | solution.py:53
  26.2 9.2 %collective-permute-start.5 = (bf16[4,32,768]{2,1,0:T(8,128)(2,1)S(1)}, bf16[4,32,768]{2,1,0:T(8,128)(2,1)S(1)}, u32[]{:S(2)}, u32[]{:S(2)}) collective-permute-start(bf16[4,32,768]{2,1,0:T(8,128)(2,1)S(1)} %pad_maximum_fusion.4), channel_id=1, source_target_pairs={{0,8},{8,16},{16,24},{1,9},{9,17},{17,25},{2,10},{10,18},{18,26},{... | collective-permute-start | bytes 589832 | tf_op jit(solution)/shard_map/ppermute | solution.py:53
  35.5 1.0 copy-start.5
  56.5 11.5 %collective-permute-start.6 = (bf16[512,2432]{1,0:T(8,128)(2,1)S(1)}, bf16[512,2432]{1,0:T(8,128)(2,1)S(1)}, u32[]{:S(2)}, u32[]{:S(2)}) collective-permute-start(bf16[512,2432]{1,0:T(8,128)(2,1)S(1)} %shard_map.112), channel_id=1, source_target_pairs={{0,1},{1,0},{2,3},{3,2},{4,5},{5,4},{6,7},{7,6},{8,9},{9,8},{10,11... | collective-permute-start | bytes 7471112 | tf_op jit(solution)/shard_map/ppermute | solution.py:87
  59.6 10.5 %copy-start.6 = (bf16[7,32,768]{2,1,0:T(8,128)(2,1)}, bf16[7,32,768]{2,1,0:T(8,128)(2,1)S(1)}, u32[]{:S(2)}) copy-start(bf16[7,32,768]{2,1,0:T(8,128)(2,1)S(1)} %get-tuple-element.64) | copy-start | bytes 1032196
  59.6 10.5 %copy-start.7 = (bf16[7,32,768]{2,1,0:T(8,128)(2,1)}, bf16[7,32,768]{2,1,0:T(8,128)(2,1)S(1)}, u32[]{:S(2)}) copy-start(bf16[7,32,768]{2,1,0:T(8,128)(2,1)S(1)} %get-tuple-element.61) | copy-start | bytes 1032196
  59.6 10.4 %collective-permute-start.7 = (bf16[4,32,768]{2,1,0:T(8,128)(2,1)S(1)}, bf16[4,32,768]{2,1,0:T(8,128)(2,1)S(1)}, u32[]{:S(2)}, u32[]{:S(2)}) collective-permute-start(bf16[4,32,768]{2,1,0:T(8,128)(2,1)S(1)} %pad_maximum_fusion.5), channel_id=1, source_target_pairs={{1,0},{2,1},{3,2},{4,3},{5,4},{6,5},{7,6},{9,8},{10,9},{11,10},{12... | collective-permute-start | bytes 589832 | tf_op jit(solution)/shard_map/ppermute | solution.py:53
  61.0 11.7 %collective-permute-start.8 = (bf16[4,32,768]{2,1,0:T(8,128)(2,1)S(1)}, bf16[4,32,768]{2,1,0:T(8,128)(2,1)}, u32[]{:S(2)}, u32[]{:S(2)}) collective-permute-start(bf16[4,32,768]{2,1,0:T(8,128)(2,1)S(1)} %slice.155), channel_id=1, source_target_pairs={{32,0},{64,32},{96,64},{128,96},{160,128},{192,160},{224,192},{33,... | collective-permute-start | bytes 589832 | tf_op jit(solution)/shard_map/ppermute | solution.py:53
  72.7 41.6 %all-to-all-start = ((bf16[32,16,2432]{2,1,0:T(8,128)(2,1)}), bf16[32,16,2432]{2,1,0:T(8,128)(2,1)S(1)}, u32[]{:S(2)}, u32[]{:S(2)}) async-start(bf16[32,16,2432]{2,1,0:T(8,128)(2,1)} %bitcast.1), calls=%async_computation | async-start | bytes 4980736 | tf_op jit(solution)/shard_map/all_to_all | solution.py:355
  82.4 32.9 %collective-permute-start.9 = (bf16[4,32,768]{2,1,0:T(8,128)(2,1)}, bf16[4,32,768]{2,1,0:T(8,128)(2,1)}, u32[]{:S(2)}, u32[]{:S(2)}) collective-permute-start(bf16[4,32,768]{2,1,0:T(8,128)(2,1)} %pad_maximum_fusion.6), channel_id=1, source_target_pairs={{8,0},{16,8},{24,16},{9,1},{17,9},{25,17},{10,2},{18,10},{26,18},{... | collective-permute-start | bytes 589832 | tf_op jit(solution)/shard_map/ppermute | solution.py:53
  85.6 29.7 %collective-permute-start.10 = (bf16[4,32,768]{2,1,0:T(8,128)(2,1)}, bf16[4,32,768]{2,1,0:T(8,128)(2,1)}, u32[]{:S(2)}, u32[]{:S(2)}) collective-permute-start(bf16[4,32,768]{2,1,0:T(8,128)(2,1)} %pad_maximum_fusion.7), channel_id=1, source_target_pairs={{1,0},{2,1},{3,2},{4,3},{5,4},{6,5},{7,6},{9,8},{10,9},{11,10},{12... | collective-permute-start | bytes 589832 | tf_op jit(solution)/shard_map/ppermute | solution.py:53
  117.1 13.4 %collective-permute-start.11 = (bf16[4,32,768]{2,1,0:T(8,128)(2,1)S(1)}, bf16[4,32,768]{2,1,0:T(8,128)(2,1)S(1)}, u32[]{:S(2)}, u32[]{:S(2)}) collective-permute-start(bf16[4,32,768]{2,1,0:T(8,128)(2,1)S(1)} %pad_maximum_fusion.8), channel_id=1, source_target_pairs={{32,0},{64,32},{96,64},{128,96},{160,128},{192,160},{224,192},{33,... | collective-permute-start | bytes 589832 | tf_op jit(solution)/shard_map/ppermute | solution.py:53
  121.4 18.0 %all-to-all-start.1 = ((bf16[4,8,2432]{2,1,0:T(8,128)(2,1)}), bf16[4,8,2432]{2,1,0:T(8,128)(2,1)S(1)}, u32[]{:S(2)}, u32[]{:S(2)}) async-start(bf16[4,8,2432]{2,1,0:T(8,128)(2,1)} %shard_map.116), calls=%async_computation.1 | async-start | bytes 311296 | tf_op jit(solution)/shard_map/all_to_all | solution.py:360
  128.1 9.0 %collective-permute-start.12 = (bf16[4,32,768]{2,1,0:T(8,128)(2,1)S(1)}, bf16[4,32,768]{2,1,0:T(8,128)(2,1)S(1)}, u32[]{:S(2)}, u32[]{:S(2)}) collective-permute-start(bf16[4,32,768]{2,1,0:T(8,128)(2,1)S(1)} %pad_maximum_fusion.9), channel_id=1, source_target_pairs={{8,0},{16,8},{24,16},{9,1},{17,9},{25,17},{10,2},{18,10},{26,18},{... | collective-permute-start | bytes 589832 | tf_op jit(solution)/shard_map/ppermute | solution.py:53

commit v7 on v6

--- a/solution.py
+++ b/solution.py
@@ -124,7 +124,12 @@
     return iota((HALF, D), 1) == row
 
 
-def half_sums(core, me_ref, normed_ref, mixed_ref, gos_ref, dpacked_ref, gain_ref, out_ref):
+def with_other(total, at, rest):
+    return total + rest[0][:, at].astype(F32) if len(rest) == 2 else total
+
+
+def half_sums(core, me_ref, normed_ref, mixed_ref, gos_ref, dpacked_ref, gain_ref, *rest):
+    out_ref = rest[-1]
     gz = me_ref[0]
     place = half_place(gz, core)
     turned = lax.dot_general(one_hot(place), normed_ref[...], NT, preferred_element_type=F32).astype(BF)
@@ -137,9 +142,11 @@
     for g in range(3):
         at = slice(g * D, (g + 1) * D)
         total = dot(turned, dpacked_ref[:, at]) + dot(widen, proj[g * 128 : (g + 1) * 128])
-        out_ref[:, at] = total.astype(BF)
+        out_ref[:, at] = with_other(total, at, rest).astype(BF)
     gains = jnp.sum(jnp.where(place, gain_ref[...], 0.0), axis=1, keepdims=True)
-    out_ref[:, 3 * D :] = jnp.broadcast_to(gains, (HALF, 128)).astype(BF)
+    gains = jnp.broadcast_to(gains, (HALF, 128))
+    at = slice(3 * D, COLS)
+    out_ref[:, at] = with_other(gains, at, rest).astype(BF)
 
 
 def main_body(
@@ -171,7 +178,7 @@
         normed_ref[at, :] = (unit * gain).astype(BF)
         return carry
 
-    lax.fori_loop(0, SLOTS // WCAP, gather_window, 0)
+    lax.fori_loop(0, SLOTS // WCAP, gather_window, 0, unroll=True)
 
     def project(c, carry):
         at = pl.ds(pl.multiple_of(c * D, D), D)
@@ -201,7 +208,8 @@
             k_both = both(packed_ref[at, k_at])
             v_both = both(packed_ref[at, v_at])
             d = delta_ref[at, q_at]
-            scores = lax.dot_general(k_both, q, NT, preferred_element_type=F32) * 0.125
+            scaled = q * jnp.asarray(0.125, BF)
+            scores = lax.dot_general(k_both, scaled, NT, preferred_element_type=F32)
             scores = jnp.where(filled, scores.reshape(2, WCAP, WCAP), BIG_NEGATIVE)
             expo = jnp.exp(scores - jnp.max(scores, axis=1, keepdims=True))
             probs = expo * (1.0 / jnp.sum(expo, axis=1, keepdims=True))
@@ -224,7 +232,7 @@
             dpacked_ref[at, v_at] = dot(beside, both(d)).astype(BF)
         return carry
 
-    lax.fori_loop(0, SLOTS // WCAP, attend, 0)
+    lax.fori_loop(0, SLOTS // WCAP, attend, 0, unroll=True)
     dnormed = lax.dot_general(
         dpacked_ref[...], wqkv_ref[...], NT, preferred_element_type=F32
     ).astype(BF)
@@ -271,10 +279,6 @@
         out[...] = (own_ref[:, at].astype(F32) + back).astype(BF)
 
 
-def sum1_body(own_ref, got_ref, out_ref):
-    out_ref[...] = (own_ref[...].astype(F32) + got_ref[...].astype(F32)).astype(BF)
-
-
 def sum2_body(me_ref, got_ref, out_ref):
     total = jnp.sum(got_ref[...].astype(F32), axis=0)
     for i in range(4):
@@ -347,9 +351,7 @@
     )
     places = starts()
     down = step([[back_t], [back_g]], places, DOWN, 0, -1)
-    (own,) = call(functools.partial(half_sums, 0), [half], *operands, smem=(0,), mib=SUMS)
-
-    (paired,) = call(sum1_body, [half], own, got)
+    (paired,) = call(functools.partial(half_sums, 0), [half], *operands, got, smem=(0,), mib=SUMS)
     paired, down = lax.optimization_barrier((paired, down))
     down = step(down, places, DOWN, 1, -1)
     spread = lax.all_to_all(paired, ("gx", "gy"), split_axis=0, concat_axis=0, tiled=True)

time: 142 us -> 139 us (0.979)
  Pallas kernels: 32.6 us -> 29.3 us
    pallas_call x9 -> x8, Pallas kernels: 32.6 us -> 29.3 us  [call(): pl.pallas_call(flat, out_shape=[jax.ShapeDtypeStruct(shape, dtype) for sh...]
where the time goes in v7:
time: 139 us; the launch traced here: 138 us
  waiting for transfers between devices  52 us (37%)
  starting transfers between devices  43.9 us (32%)
  Pallas kernels  29.3 us (21%)
  local copies, waits for them, and re-layouts  10.3 us (7%)
  other arithmetic  1.61 us (1%)
    pallas_call x8, Pallas kernels, call(): pl.pallas_call(flat, out_shape=[jax.ShapeDtypeStruct(shape, dtype) for sh...  29.3 us
    ppermute x12, starting transfers between devices, passed_along(): lax.ppermute(value, axis, [(source, source + steps) for source in range(i...  29.1 us
    all_to_all x1, waiting for transfers between devices, on_device(): lax.all_to_all(paired, ('gx', 'gy'), split_axis=0, concat_axis=0, tiled=T...  27.4 us
    ppermute x12, waiting for transfers between devices, passed_along(): lax.ppermute(value, axis, [(source, source + steps) for source in range(i...  24.6 us
    all_to_all x1, starting transfers between devices, on_device(): lax.all_to_all(paired, ('gx', 'gy'), split_axis=0, concat_axis=0, tiled=T...  7.31 us
    all_to_all x1, starting transfers between devices, on_device(): lax.all_to_all(part, 'gz', split_axis=0, concat_axis=0, tiled=True, axis_...  6.9 us
    slice x19, local copies, waits for them, and re-layouts, stage(): lax.slice_in_dim(arrays[place[k][0]], place[k][1], place[k][1] + 1)  6 us
    unnamed x21, local copies, waits for them, and re-layouts  3.7 us
  transfers between devices with their start and end apart: 15, of which 7 were waited for; matrix products, arithmetic and copies ran while one was open for 4% of the time, Pallas kernels for 8%

profile of v7, /device:TPU:10, one launch (start us, length us, event | category | flops | bytes accessed | tf_op | source)
XLA Modules:
  0.0 138.1 jit_solution(2582389525137123293)
XLA Ops:
  0.6 0.7 copy.14.refs_2_.refs_7_
  1.3 0.0 copy-start.2
  1.3 1.0 copy-done.2
  2.3 1.0 copy-done.4
  3.3 0.0 copy-start.8
  3.3 0.4 shard_map.110
  3.8 4.1 %collective-permute-start = (bf16[4,32,768]{2,1,0:T(8,128)(2,1)S(1)}, bf16[4,32,768]{2,1,0:T(8,128)(2,1)S(1)}, u32[]{:S(2)}, u32[]{:S(2)}) collective-permute-start(bf16[4,32,768]{2,1,0:T(8,128)(2,1)S(1)} %slice.133), channel_id=1, source_target_pairs={{0,32},{32,64},{64,96},{96,128},{128,160},{160,192},{192,224},{1,3... | collective-permute-start | bytes 589832 | tf_op jit(solution)/shard_map/ppermute | solution.py:53
  7.9 1.5 %collective-permute-start.3 = (bf16[4,32,768]{2,1,0:T(8,128)(2,1)S(1)}, bf16[4,32,768]{2,1,0:T(8,128)(2,1)S(1)}, u32[]{:S(2)}, u32[]{:S(2)}) collective-permute-start(bf16[4,32,768]{2,1,0:T(8,128)(2,1)S(1)} %pad_maximum_fusion.2), channel_id=1, source_target_pairs={{0,1},{1,2},{2,3},{3,4},{4,5},{5,6},{6,7},{8,9},{9,10},{10,11},{11... | collective-permute-start | bytes 589832 | tf_op jit(solution)/shard_map/ppermute | solution.py:53
  9.4 4.0 %collective-permute-done.refs_2_ = bf16[4,32,768]{2,1,0:T(8,128)(2,1)S(1)} collective-permute-done((bf16[4,32,768]{2,1,0:T(8,128)(2,1)S(1)}, bf16[4,32,768]{2,1,0:T(8,128)(2,1)S(1)}, u32[]{:S(2)}, u32[]{:S(2)}) %collective-permute-start) | collective-permute-done | bytes 196640 | tf_op jit(solution)/shard_map/ppermute | solution.py:53
  13.5 3.5 %collective-permute-start.1 = (bf16[4,32,768]{2,1,0:T(8,128)(2,1)S(1)}, bf16[4,32,768]{2,1,0:T(8,128)(2,1)S(1)}, u32[]{:S(2)}, u32[]{:S(2)}) collective-permute-start(bf16[4,32,768]{2,1,0:T(8,128)(2,1)S(1)} %pad_maximum_fusion), channel_id=1, source_target_pairs={{0,8},{8,16},{16,24},{1,9},{9,17},{17,25},{2,10},{10,18},{18,26},{... | collective-permute-start | bytes 589832 | tf_op jit(solution)/shard_map/ppermute | solution.py:53
  17.0 0.0 collective-permute-done.3.refs_5_
  17.1 2.9 %collective-permute-start.4 = (bf16[4,32,768]{2,1,0:T(8,128)(2,1)S(1)}, bf16[4,32,768]{2,1,0:T(8,128)(2,1)S(1)}, u32[]{:S(2)}, u32[]{:S(2)}) collective-permute-start(bf16[4,32,768]{2,1,0:T(8,128)(2,1)S(1)} %pad_maximum_fusion.3), channel_id=1, source_target_pairs={{0,32},{32,64},{64,96},{96,128},{128,160},{160,192},{192,224},{1,3... | collective-permute-start | bytes 589832 | tf_op jit(solution)/shard_map/ppermute | solution.py:53
  20.0 2.0 %collective-permute-done.1.refs_3_ = bf16[4,32,768]{2,1,0:T(8,128)(2,1)S(1)} collective-permute-done((bf16[4,32,768]{2,1,0:T(8,128)(2,1)S(1)}, bf16[4,32,768]{2,1,0:T(8,128)(2,1)S(1)}, u32[]{:S(2)}, u32[]{:S(2)}) %collective-permute-start.1) | collective-permute-done | bytes 196640 | tf_op jit(solution)/shard_map/ppermute | solution.py:53
  22.1 1.3 collective-permute-start.2
  23.4 2.8 %collective-permute-done.4.refs_6_ = bf16[4,32,768]{2,1,0:T(8,128)(2,1)S(1)} collective-permute-done((bf16[4,32,768]{2,1,0:T(8,128)(2,1)S(1)}, bf16[4,32,768]{2,1,0:T(8,128)(2,1)S(1)}, u32[]{:S(2)}, u32[]{:S(2)}) %collective-permute-start.4) | collective-permute-done | bytes 196640 | tf_op jit(solution)/shard_map/ppermute | solution.py:53
  26.2 3.3 %collective-permute-start.5 = (bf16[4,32,768]{2,1,0:T(8,128)(2,1)S(1)}, bf16[4,32,768]{2,1,0:T(8,128)(2,1)S(1)}, u32[]{:S(2)}, u32[]{:S(2)}) collective-permute-start(bf16[4,32,768]{2,1,0:T(8,128)(2,1)S(1)} %pad_maximum_fusion.4), channel_id=1, source_target_pairs={{0,8},{8,16},{16,24},{1,9},{9,17},{17,25},{2,10},{10,18},{18,26},{... | collective-permute-start | bytes 589832 | tf_op jit(solution)/shard_map/ppermute | solution.py:53
  29.5 0.0 copy-done.9
  29.6 0.0 collective-permute-done.2.refs_4_
  29.6 5.9 %collective-permute-done.5.refs_7_ = bf16[4,32,768]{2,1,0:T(8,128)(2,1)S(1)} collective-permute-done((bf16[4,32,768]{2,1,0:T(8,128)(2,1)S(1)}, bf16[4,32,768]{2,1,0:T(8,128)(2,1)S(1)}, u32[]{:S(2)}, u32[]{:S(2)}) %collective-permute-start.5) | collective-permute-done | bytes 196640 | tf_op jit(solution)/shard_map/ppermute | solution.py:53
  35.4 0.0 copy-done
  35.4 0.0 copy-done.1
  35.4 0.0 copy-done.3
  35.5 0.0 copy-done.8
  35.5 0.0 copy-start.5
  35.5 1.0 copy-done.5
  36.5 14.0 %shard_map.111 = (bf16[512,768]{1,0:T(8,128)(2,1)S(1)}, bf16[512,768]{1,0:T(8,128)(2,1)S(1)}, bf16[512,768]{1,0:T(8,128)(2,1)S(1)}, bf16[512,768]{1,0:T(8,128)(2...) custom-call(bf16[256,768]{1,0:T(8,128)(2,1)S(1)} %copy-done.3, ...), custom_call_target="tpu_custom_call" | custom-call | tf_op jit(solution)/shard_map/pallas_call | solution.py:304
  50.5 3.5 %shard_map.112 = bf16[512,2432]{1,0:T(8,128)(2,1)S(1)} custom-call(s32[1]{0:T(128)} %bitcast.refs_0_, bf16[512,768]{1,0:T(8,128)(2,1)S(1)} %get-tuple-element.43.refs_1_, bf16[512,768]{1,0:T(8,128)(2,1)S(1)} %get-tuple-element.44.refs_2_, bf16[512,768]{1,0:T(8,128)(2,1)S(1)} %get-tuple-element.45.refs_3_.refs_1_, ...), custom_call_target="tpu_custom_call" | custom-call | tf_op jit(solution)/shard_map/pallas_call | solution.py:304
  53.9 0.6 collective-permute-start.6
  54.5 2.5 %shard_map.113 = (bf16[7,32,768]{2,1,0:T(8,128)(2,1)S(1)}, bf16[7,32,768]{2,1,0:T(8,128)(2,1)S(1)}, bf16[256,1536]{1,0:T(8,128)(2,1)S(1)}) custom-call(bf16[512,768]{1,0:T(8,128)(2,1)S(1)} %get-tuple-element.49.refs_0_, bf16[512,768]{1,0:T(8,128)(2,1)S(1)} %get-tuple-element.45.refs_3_.refs_1_, bf16[512,768]{1,0:T(8,128)(2,1)S(1)} %get-tuple-element.44.refs_2_, ...), custom_call_target="tpu_custom_call" | custom-call | tf_op jit(solution)/shard_map/pallas_call | solution.py:304
  57.1 0.0 copy-start.7
  57.1 0.0 copy-start.6
  57.1 1.3 collective-permute-start.7
  58.5 0.0 copy-done.7
  58.5 3.4 %collective-permute-start.8 = (bf16[4,32,768]{2,1,0:T(8,128)(2,1)S(1)}, bf16[4,32,768]{2,1,0:T(8,128)(2,1)}, u32[]{:S(2)}, u32[]{:S(2)}) collective-permute-start(bf16[4,32,768]{2,1,0:T(8,128)(2,1)S(1)} %slice.155), channel_id=1, source_target_pairs={{32,0},{64,32},{96,64},{128,96},{160,128},{192,160},{224,192},{33,... | collective-permute-start | bytes 589832 | tf_op jit(solution)/shard_map/ppermute | solution.py:53
  61.9 0.0 collective-permute-done.6.refs_6_
  61.9 4.9 %shard_map.114 = bf16[512,2432]{1,0:T(8,128)(2,1)} custom-call(s32[1]{0:T(128)} %bitcast.refs_0_, bf16[512,768]{1,0:T(8,128)(2,1)S(1)} %get-tuple-element.43.refs_1_, bf16[512,768]{1,0:T(8,128)(2,1)S(1)} %get-tuple-element.44.refs_2_, bf16[512,768]{1,0:T(8,128)(2,1)S(1)} %get-tuple-element.45.refs_3_.refs_1_, ...), custom_call_target="tpu_custom_call" | custom-call | tf_op jit(solution)/shard_map/pallas_call | solution.py:304
  66.8 0.0 copy-done.6
  66.8 0.0 collective-permute-done.7.refs_1_
  66.8 3.4 %collective-permute-done.8.refs_4_ = bf16[4,32,768]{2,1,0:T(8,128)(2,1)} collective-permute-done((bf16[4,32,768]{2,1,0:T(8,128)(2,1)S(1)}, bf16[4,32,768]{2,1,0:T(8,128)(2,1)}, u32[]{:S(2)}, u32[]{:S(2)}) %collective-permute-start.8) | collective-permute-done | bytes 196640 | tf_op jit(solution)/shard_map/ppermute | solution.py:53
  70.2 7.3 %all-to-all-start = ((bf16[32,16,2432]{2,1,0:T(8,128)(2,1)}), bf16[32,16,2432]{2,1,0:T(8,128)(2,1)S(1)}, u32[]{:S(2)}, u32[]{:S(2)}) async-start(bf16[32,16,2432]{2,1,0:T(8,128)(2,1)} %bitcast.1), calls=%async_computation | async-start | bytes 4980736 | tf_op jit(solution)/shard_map/all_to_all | solution.py:357
  77.5 0.8 fusion.5
  78.4 0.9 fusion
  79.3 0.7 pad_maximum_fusion.6
  80.0 2.5 %collective-permute-start.9 = (bf16[4,32,768]{2,1,0:T(8,128)(2,1)}, bf16[4,32,768]{2,1,0:T(8,128)(2,1)}, u32[]{:S(2)}, u32[]{:S(2)}) collective-permute-start(bf16[4,32,768]{2,1,0:T(8,128)(2,1)} %pad_maximum_fusion.6), channel_id=1, source_target_pairs={{8,0},{16,8},{24,16},{9,1},{17,9},{25,17},{10,2},{18,10},{26,18},{... | collective-permute-start | bytes 589832 | tf_op jit(solution)/shard_map/ppermute | solution.py:53
  82.4 0.7 pad_maximum_fusion.7
  83.1 1.3 collective-permute-start.10
  84.4 27.4 %all-to-all-done.refs_1_ = bf16[32,16,2432]{2,1,0:T(8,128)(2,1)S(1)} async-done(((bf16[32,16,2432]{2,1,0:T(8,128)(2,1)}), bf16[32,16,2432]{2,1,0:T(8,128)(2,1)S(1)}, u32[]{:S(2)}, u32[]{:S(2)}) %all-to-all-start) | async-done | bytes 2490400 | tf_op jit(solution)/shard_map/all_to_all | solution.py:357
  111.8 1.0 shard_map.115
  112.8 0.0 collective-permute-done.9.refs_2_
  112.9 0.0 collective-permute-done.10.refs_5_
  112.9 0.9 slice.166
  113.8 0.8 slice.164
  114.6 1.9 %collective-permute-start.11 = (bf16[4,32,768]{2,1,0:T(8,128)(2,1)S(1)}, bf16[4,32,768]{2,1,0:T(8,128)(2,1)S(1)}, u32[]{:S(2)}, u32[]{:S(2)}) collective-permute-start(bf16[4,32,768]{2,1,0:T(8,128)(2,1)S(1)} %pad_maximum_fusion.8), channel_id=1, source_target_pairs={{32,0},{64,32},{96,64},{128,96},{160,128},{192,160},{224,192},{33,... | collective-permute-start | bytes 589832 | tf_op jit(solution)/shard_map/ppermute | solution.py:53
  116.5 0.8 fusion.4
  117.4 0.8 slice.169
  118.2 0.8 slice.167
  119.0 6.9 %all-to-all-start.1 = ((bf16[4,8,2432]{2,1,0:T(8,128)(2,1)}), bf16[4,8,2432]{2,1,0:T(8,128)(2,1)S(1)}, u32[]{:S(2)}, u32[]{:S(2)}) async-start(bf16[4,8,2432]{2,1,0:T(8,128)(2,1)} %shard_map.115), calls=%async_computation.1 | async-start | bytes 311296 | tf_op jit(solution)/shard_map/all_to_all | solution.py:362
  125.9 2.1 %collective-permute-start.12 = (bf16[4,32,768]{2,1,0:T(8,128)(2,1)S(1)}, bf16[4,32,768]{2,1,0:T(8,128)(2,1)S(1)}, u32[]{:S(2)}, u32[]{:S(2)}) collective-permute-start(bf16[4,32,768]{2,1,0:T(8,128)(2,1)S(1)} %pad_maximum_fusion.9), channel_id=1, source_target_pairs={{8,0},{16,8},{24,16},{9,1},{17,9},{25,17},{10,2},{18,10},{26,18},{... | collective-permute-start | bytes 589832 | tf_op jit(solution)/shard_map/ppermute | solution.py:53
  128.0 0.0 collective-permute-done.11.refs_3_
  128.1 6.4 %collective-permute-done.12.refs_6_ = bf16[4,32,768]{2,1,0:T(8,128)(2,1)S(1)} collective-permute-done((bf16[4,32,768]{2,1,0:T(8,128)(2,1)S(1)}, bf16[4,32,768]{2,1,0:T(8,128)(2,1)S(1)}, u32[]{:S(2)}, u32[]{:S(2)}) %collective-permute-start.12) | collective-permute-done | bytes 196640 | tf_op jit(solution)/shard_map/ppermute | solution.py:53
  134.5 2.3 %shard_map.116 = (bf16[256,768]{1,0:T(8,128)(2,1)}, bf16[256,768]{1,0:T(8,128)(2,1)}) custom-call(bf16[256,1536]{1,0:T(8,128)(2,1)S(1)} %get-tuple-element.51.refs_0_, bf16[4,32,768]{2,1,0:T(8,128)(2,1)S(1)} %collective-permute-done.7.refs_1_, bf16[4,32,768]{2,1,0:T(8,128)(2,1)} %collective-permute-done.9.refs_2_, ...), custom_call_target="tpu_custom_call" | custom-call | tf_op jit(solution)/shard_map/pallas_call | solution.py:304
  136.8 0.0 all-to-all-done.1.refs_0_
  136.9 0.6 shard_map.117
  137.5 0.6 slice_reduce_fusion
  (26 shorter events, 0.4 us)
Async XLA Ops:
  1.3 1.0 copy-start.2
  2.3 1.0 copy-start.4
  3.3 26.2 %copy-start.9 = (f32[768]{0:T(1024)S(1)}, f32[768]{0:T(1024)}, u32[]{:S(2)}) copy-start(f32[768]{0:T(1024)} %param.8) | copy-start | bytes 9220
  3.3 32.1 %copy-start = (bf16[768,768]{1,0:T(8,128)(2,1)S(1)}, bf16[768,768]{1,0:T(8,128)(2,1)}, u32[]{:S(2)}) copy-start(bf16[768,768]{1,0:T(8,128)(2,1)} %refs_6_.1) | copy-start | bytes 3538948
  3.3 32.1 %copy-start.1 = (bf16[768,2304]{1,0:T(8,128)(2,1)S(1)}, bf16[768,2304]{1,0:T(8,128)(2,1)}, u32[]{:S(2)}) copy-start(bf16[768,2304]{1,0:T(8,128)(2,1)} %refs_10_.1) | copy-start | bytes 10616836
  3.3 32.1 %copy-start.3 = (bf16[256,768]{1,0:T(8,128)(2,1)S(1)}, bf16[256,768]{1,0:T(8,128)(2,1)}, u32[]{:S(2)}) copy-start(bf16[256,768]{1,0:T(8,128)(2,1)} %refs_0_.1) | copy-start | bytes 1179652
  3.3 32.1 %copy-start.8 = (s32[1,512]{1,0:T(1,128)S(1)}, s32[1,512]{1,0:T(1,128)}, u32[]{:S(2)}) copy-start(s32[1,512]{1,0:T(1,128)} %refs_4_.1) | copy-start | bytes 6148
  3.8 9.7 %collective-permute-start = (bf16[4,32,768]{2,1,0:T(8,128)(2,1)S(1)}, bf16[4,32,768]{2,1,0:T(8,128)(2,1)S(1)}, u32[]{:S(2)}, u32[]{:S(2)}) collective-permute-start(bf16[4,32,768]{2,1,0:T(8,128)(2,1)S(1)} %slice.133), channel_id=1, source_target_pairs={{0,32},{32,64},{64,96},{96,128},{128,160},{160,192},{192,224},{1,3... | collective-permute-start | bytes 589832 | tf_op jit(solution)/shard_map/ppermute | solution.py:53
  7.9 9.1 %collective-permute-start.3 = (bf16[4,32,768]{2,1,0:T(8,128)(2,1)S(1)}, bf16[4,32,768]{2,1,0:T(8,128)(2,1)S(1)}, u32[]{:S(2)}, u32[]{:S(2)}) collective-permute-start(bf16[4,32,768]{2,1,0:T(8,128)(2,1)S(1)} %pad_maximum_fusion.2), channel_id=1, source_target_pairs={{0,1},{1,2},{2,3},{3,4},{4,5},{5,6},{6,7},{8,9},{9,10},{10,11},{11... | collective-permute-start | bytes 589832 | tf_op jit(solution)/shard_map/ppermute | solution.py:53
  13.5 8.5 %collective-permute-start.1 = (bf16[4,32,768]{2,1,0:T(8,128)(2,1)S(1)}, bf16[4,32,768]{2,1,0:T(8,128)(2,1)S(1)}, u32[]{:S(2)}, u32[]{:S(2)}) collective-permute-start(bf16[4,32,768]{2,1,0:T(8,128)(2,1)S(1)} %pad_maximum_fusion), channel_id=1, source_target_pairs={{0,8},{8,16},{16,24},{1,9},{9,17},{17,25},{2,10},{10,18},{18,26},{... | collective-permute-start | bytes 589832 | tf_op jit(solution)/shard_map/ppermute | solution.py:53
  17.1 9.1 %collective-permute-start.4 = (bf16[4,32,768]{2,1,0:T(8,128)(2,1)S(1)}, bf16[4,32,768]{2,1,0:T(8,128)(2,1)S(1)}, u32[]{:S(2)}, u32[]{:S(2)}) collective-permute-start(bf16[4,32,768]{2,1,0:T(8,128)(2,1)S(1)} %pad_maximum_fusion.3), channel_id=1, source_target_pairs={{0,32},{32,64},{64,96},{96,128},{128,160},{160,192},{192,224},{1,3... | collective-permute-start | bytes 589832 | tf_op jit(solution)/shard_map/ppermute | solution.py:53
  22.1 7.5 %collective-permute-start.2 = (bf16[4,32,768]{2,1,0:T(8,128)(2,1)S(1)}, bf16[4,32,768]{2,1,0:T(8,128)(2,1)S(1)}, u32[]{:S(2)}, u32[]{:S(2)}) collective-permute-start(bf16[4,32,768]{2,1,0:T(8,128)(2,1)S(1)} %pad_maximum_fusion.1), channel_id=1, source_target_pairs={{0,1},{1,2},{2,3},{3,4},{4,5},{5,6},{6,7},{8,9},{9,10},{10,11},{11... | collective-permute-start | bytes 589832 | tf_op jit(solution)/shard_map/ppermute | solution.py:53
  26.2 9.2 %collective-permute-start.5 = (bf16[4,32,768]{2,1,0:T(8,128)(2,1)S(1)}, bf16[4,32,768]{2,1,0:T(8,128)(2,1)S(1)}, u32[]{:S(2)}, u32[]{:S(2)}) collective-permute-start(bf16[4,32,768]{2,1,0:T(8,128)(2,1)S(1)} %pad_maximum_fusion.4), channel_id=1, source_target_pairs={{0,8},{8,16},{16,24},{1,9},{9,17},{17,25},{2,10},{10,18},{18,26},{... | collective-permute-start | bytes 589832 | tf_op jit(solution)/shard_map/ppermute | solution.py:53
  35.5 1.0 copy-start.5
  53.9 8.0 %collective-permute-start.6 = (bf16[512,2432]{1,0:T(8,128)(2,1)S(1)}, bf16[512,2432]{1,0:T(8,128)(2,1)S(1)}, u32[]{:S(2)}, u32[]{:S(2)}) collective-permute-start(bf16[512,2432]{1,0:T(8,128)(2,1)S(1)} %shard_map.112), channel_id=1, source_target_pairs={{0,1},{1,0},{2,3},{3,2},{4,5},{5,4},{6,7},{7,6},{8,9},{9,8},{10,11... | collective-permute-start | bytes 7471112 | tf_op jit(solution)/shard_map/ppermute | solution.py:87
  57.1 1.4 %copy-start.7 = (bf16[7,32,768]{2,1,0:T(8,128)(2,1)}, bf16[7,32,768]{2,1,0:T(8,128)(2,1)S(1)}, u32[]{:S(2)}) copy-start(bf16[7,32,768]{2,1,0:T(8,128)(2,1)S(1)} %get-tuple-element.61) | copy-start | bytes 1032196
  57.1 9.7 %copy-start.6 = (bf16[7,32,768]{2,1,0:T(8,128)(2,1)}, bf16[7,32,768]{2,1,0:T(8,128)(2,1)S(1)}, u32[]{:S(2)}) copy-start(bf16[7,32,768]{2,1,0:T(8,128)(2,1)S(1)} %get-tuple-element.64) | copy-start | bytes 1032196
  57.1 9.7 %collective-permute-start.7 = (bf16[4,32,768]{2,1,0:T(8,128)(2,1)S(1)}, bf16[4,32,768]{2,1,0:T(8,128)(2,1)S(1)}, u32[]{:S(2)}, u32[]{:S(2)}) collective-permute-start(bf16[4,32,768]{2,1,0:T(8,128)(2,1)S(1)} %pad_maximum_fusion.5), channel_id=1, source_target_pairs={{1,0},{2,1},{3,2},{4,3},{5,4},{6,5},{7,6},{9,8},{10,9},{11,10},{12... | collective-permute-start | bytes 589832 | tf_op jit(solution)/shard_map/ppermute | solution.py:53
  58.5 11.7 %collective-permute-start.8 = (bf16[4,32,768]{2,1,0:T(8,128)(2,1)S(1)}, bf16[4,32,768]{2,1,0:T(8,128)(2,1)}, u32[]{:S(2)}, u32[]{:S(2)}) collective-permute-start(bf16[4,32,768]{2,1,0:T(8,128)(2,1)S(1)} %slice.155), channel_id=1, source_target_pairs={{32,0},{64,32},{96,64},{128,96},{160,128},{192,160},{224,192},{33,... | collective-permute-start | bytes 589832 | tf_op jit(solution)/shard_map/ppermute | solution.py:53
  70.2 41.6 %all-to-all-start = ((bf16[32,16,2432]{2,1,0:T(8,128)(2,1)}), bf16[32,16,2432]{2,1,0:T(8,128)(2,1)S(1)}, u32[]{:S(2)}, u32[]{:S(2)}) async-start(bf16[32,16,2432]{2,1,0:T(8,128)(2,1)} %bitcast.1), calls=%async_computation | async-start | bytes 4980736 | tf_op jit(solution)/shard_map/all_to_all | solution.py:357
  80.0 32.9 %collective-permute-start.9 = (bf16[4,32,768]{2,1,0:T(8,128)(2,1)}, bf16[4,32,768]{2,1,0:T(8,128)(2,1)}, u32[]{:S(2)}, u32[]{:S(2)}) collective-permute-start(bf16[4,32,768]{2,1,0:T(8,128)(2,1)} %pad_maximum_fusion.6), channel_id=1, source_target_pairs={{8,0},{16,8},{24,16},{9,1},{17,9},{25,17},{10,2},{18,10},{26,18},{... | collective-permute-start | bytes 589832 | tf_op jit(solution)/shard_map/ppermute | solution.py:53
  83.1 29.7 %collective-permute-start.10 = (bf16[4,32,768]{2,1,0:T(8,128)(2,1)}, bf16[4,32,768]{2,1,0:T(8,128)(2,1)}, u32[]{:S(2)}, u32[]{:S(2)}) collective-permute-start(bf16[4,32,768]{2,1,0:T(8,128)(2,1)} %pad_maximum_fusion.7), channel_id=1, source_target_pairs={{1,0},{2,1},{3,2},{4,3},{5,4},{6,5},{7,6},{9,8},{10,9},{11,10},{12... | collective-permute-start | bytes 589832 | tf_op jit(solution)/shard_map/ppermute | solution.py:53
  114.6 13.4 %collective-permute-start.11 = (bf16[4,32,768]{2,1,0:T(8,128)(2,1)S(1)}, bf16[4,32,768]{2,1,0:T(8,128)(2,1)S(1)}, u32[]{:S(2)}, u32[]{:S(2)}) collective-permute-start(bf16[4,32,768]{2,1,0:T(8,128)(2,1)S(1)} %pad_maximum_fusion.8), channel_id=1, source_target_pairs={{32,0},{64,32},{96,64},{128,96},{160,128},{192,160},{224,192},{33,... | collective-permute-start | bytes 589832 | tf_op jit(solution)/shard_map/ppermute | solution.py:53
  119.0 17.9 %all-to-all-start.1 = ((bf16[4,8,2432]{2,1,0:T(8,128)(2,1)}), bf16[4,8,2432]{2,1,0:T(8,128)(2,1)S(1)}, u32[]{:S(2)}, u32[]{:S(2)}) async-start(bf16[4,8,2432]{2,1,0:T(8,128)(2,1)} %shard_map.115), calls=%async_computation.1 | async-start | bytes 311296 | tf_op jit(solution)/shard_map/all_to_all | solution.py:362
  125.9 8.6 %collective-permute-start.12 = (bf16[4,32,768]{2,1,0:T(8,128)(2,1)S(1)}, bf16[4,32,768]{2,1,0:T(8,128)(2,1)S(1)}, u32[]{:S(2)}, u32[]{:S(2)}) collective-permute-start(bf16[4,32,768]{2,1,0:T(8,128)(2,1)S(1)} %pad_maximum_fusion.9), channel_id=1, source_target_pairs={{8,0},{16,8},{24,16},{9,1},{17,9},{25,17},{10,2},{18,10},{26,18},{... | collective-permute-start | bytes 589832 | tf_op jit(solution)/shard_map/ppermute | solution.py:53

commit v8 on v7

--- a/solution.py
+++ b/solution.py
@@ -353,10 +353,10 @@
     down = step([[back_t], [back_g]], places, DOWN, 0, -1)
     (paired,) = call(functools.partial(half_sums, 0), [half], *operands, got, smem=(0,), mib=SUMS)
     paired, down = lax.optimization_barrier((paired, down))
-    down = step(down, places, DOWN, 1, -1)
     spread = lax.all_to_all(paired, ("gx", "gy"), split_axis=0, concat_axis=0, tiled=True)
     (part,) = call(sum2_body, [((4, 8, COLS), BF)], me, spread.reshape(32, 16, COLS), smem=(0,))
     part, down = lax.optimization_barrier((part, down))
+    down = step(down, places, DOWN, 1, -1)
     down = step(down, places, DOWN, 2, -1)
     groups = [[2 * i + core for i in range(4)] for core in range(2)]
     last = lax.all_to_all(

time: 139 us -> 137 us (0.986)
  blocking collectives: 0 us -> 38.5 us
  waiting for transfers between devices: 52 us -> 24.1 us
  local copies, waits for them, and re-layouts: 10.3 us -> 4.5 us
  starting transfers between devices: 43.9 us -> 40.2 us
  Pallas kernels: 29.3 us -> 27.5 us
    all_to_all x0 -> x1, blocking collectives: none -> 38.5 us  [on_device(): lax.all_to_all(paired, ('gx', 'gy'), split_axis=0, concat_axis=0, tiled=T...]
    all_to_all x1 -> x0, waiting for transfers between devices: 27.4 us -> none  [on_device(): lax.all_to_all(paired, ('gx', 'gy'), split_axis=0, concat_axis=0, tiled=T...]
    all_to_all x1 -> x0, starting transfers between devices: 7.31 us -> none  [on_device(): lax.all_to_all(paired, ('gx', 'gy'), split_axis=0, concat_axis=0, tiled=T...]
    slice x19 -> x15, local copies, waits for them, and re-layouts: 6 us -> 0.18 us  [stage(): lax.slice_in_dim(arrays[place[k][0]], place[k][1], place[k][1] + 1)]
    ppermute x12, waiting for transfers between devices: 24.6 us -> 21 us  [passed_along(): lax.ppermute(value, axis, [(source, source + steps) for source in range(i...]
    all_to_all x1, waiting for transfers between devices: 0.01 us -> 3.09 us  [on_device(): lax.all_to_all(part, 'gz', split_axis=0, concat_axis=0, tiled=True, axis_...]
    ppermute x12, starting transfers between devices: 29.1 us -> 31.7 us  [passed_along(): lax.ppermute(value, axis, [(source, source + steps) for source in range(i...]
    pallas_call x8, Pallas kernels: 29.3 us -> 27.5 us  [call(): pl.pallas_call(flat, out_shape=[jax.ShapeDtypeStruct(shape, dtype) for sh...]
  transfers between devices with their start and end apart: 15 -> 14, of which waited for: 7 -> 7; matrix products, arithmetic and copies ran while one was open for 4% -> 1% of each run, Pallas kernels for 8% -> 5%
where the time goes in v8:
time: 137 us; the launch traced here: 136 us
  starting transfers between devices  40.2 us (29%)
  blocking collectives  38.5 us (28%)
  Pallas kernels  27.5 us (20%)
  waiting for transfers between devices  24.1 us (18%)
  local copies, waits for them, and re-layouts  4.5 us (3%)
    all_to_all x1, blocking collectives, on_device(): lax.all_to_all(paired, ('gx', 'gy'), split_axis=0, concat_axis=0, tiled=T...  38.5 us
    ppermute x12, starting transfers between devices, passed_along(): lax.ppermute(value, axis, [(source, source + steps) for source in range(i...  31.7 us
    pallas_call x8, Pallas kernels, call(): pl.pallas_call(flat, out_shape=[jax.ShapeDtypeStruct(shape, dtype) for sh...  27.5 us
    ppermute x12, waiting for transfers between devices, passed_along(): lax.ppermute(value, axis, [(source, source + steps) for source in range(i...  21 us
    all_to_all x1, starting transfers between devices, on_device(): lax.all_to_all(part, 'gz', split_axis=0, concat_axis=0, tiled=True, axis_...  7.88 us
    unnamed x17, local copies, waits for them, and re-layouts  3.69 us
    all_to_all x1, waiting for transfers between devices, on_device(): lax.all_to_all(part, 'gz', split_axis=0, concat_axis=0, tiled=True, axis_...  3.09 us
  transfers between devices with their start and end apart: 14, of which 7 were waited for; matrix products, arithmetic and copies ran while one was open for 1% of the time, Pallas kernels for 5%

profile of v8, /device:TPU:10, one launch (start us, length us, event | category | flops | bytes accessed | tf_op | source)
XLA Modules:
  0.0 136.2 jit_solution(11241077993635011394)
XLA Ops:
  0.6 0.7 copy.14.refs_2_.refs_7_
  1.3 0.0 copy-start.2
  1.3 1.0 copy-done.2
  2.3 0.0 copy-start.4
  2.3 1.0 copy-done.4
  3.3 0.0 copy-start.7
  3.3 0.0 copy-start
  3.3 0.0 copy-start.1
  3.3 0.0 copy-start.3
  3.3 0.0 copy-start.6
  3.3 0.4 shard_map.110
  3.8 4.1 %collective-permute-start = (bf16[4,32,768]{2,1,0:T(8,128)(2,1)S(1)}, bf16[4,32,768]{2,1,0:T(8,128)(2,1)S(1)}, u32[]{:S(2)}, u32[]{:S(2)}) collective-permute-start(bf16[4,32,768]{2,1,0:T(8,128)(2,1)S(1)} %slice.133), channel_id=1, source_target_pairs={{0,32},{32,64},{64,96},{96,128},{128,160},{160,192},{192,224},{1,3... | collective-permute-start | bytes 589832 | tf_op jit(solution)/shard_map/ppermute | solution.py:53
  7.9 1.5 %collective-permute-start.3 = (bf16[4,32,768]{2,1,0:T(8,128)(2,1)S(1)}, bf16[4,32,768]{2,1,0:T(8,128)(2,1)S(1)}, u32[]{:S(2)}, u32[]{:S(2)}) collective-permute-start(bf16[4,32,768]{2,1,0:T(8,128)(2,1)S(1)} %pad_maximum_fusion.2), channel_id=1, source_target_pairs={{0,1},{1,2},{2,3},{3,4},{4,5},{5,6},{6,7},{8,9},{9,10},{10,11},{11... | collective-permute-start | bytes 589832 | tf_op jit(solution)/shard_map/ppermute | solution.py:53
  9.4 4.0 %collective-permute-done.refs_2_ = bf16[4,32,768]{2,1,0:T(8,128)(2,1)S(1)} collective-permute-done((bf16[4,32,768]{2,1,0:T(8,128)(2,1)S(1)}, bf16[4,32,768]{2,1,0:T(8,128)(2,1)S(1)}, u32[]{:S(2)}, u32[]{:S(2)}) %collective-permute-start) | collective-permute-done | bytes 196640 | tf_op jit(solution)/shard_map/ppermute | solution.py:53
  13.5 3.5 %collective-permute-start.1 = (bf16[4,32,768]{2,1,0:T(8,128)(2,1)S(1)}, bf16[4,32,768]{2,1,0:T(8,128)(2,1)S(1)}, u32[]{:S(2)}, u32[]{:S(2)}) collective-permute-start(bf16[4,32,768]{2,1,0:T(8,128)(2,1)S(1)} %pad_maximum_fusion), channel_id=1, source_target_pairs={{0,8},{8,16},{16,24},{1,9},{9,17},{17,25},{2,10},{10,18},{18,26},{... | collective-permute-start | bytes 589832 | tf_op jit(solution)/shard_map/ppermute | solution.py:53
  17.0 0.0 collective-permute-done.3.refs_5_
  17.1 2.9 %collective-permute-start.4 = (bf16[4,32,768]{2,1,0:T(8,128)(2,1)S(1)}, bf16[4,32,768]{2,1,0:T(8,128)(2,1)S(1)}, u32[]{:S(2)}, u32[]{:S(2)}) collective-permute-start(bf16[4,32,768]{2,1,0:T(8,128)(2,1)S(1)} %pad_maximum_fusion.3), channel_id=1, source_target_pairs={{0,32},{32,64},{64,96},{96,128},{128,160},{160,192},{192,224},{1,3... | collective-permute-start | bytes 589832 | tf_op jit(solution)/shard_map/ppermute | solution.py:53
  20.0 2.0 %collective-permute-done.1.refs_3_ = bf16[4,32,768]{2,1,0:T(8,128)(2,1)S(1)} collective-permute-done((bf16[4,32,768]{2,1,0:T(8,128)(2,1)S(1)}, bf16[4,32,768]{2,1,0:T(8,128)(2,1)S(1)}, u32[]{:S(2)}, u32[]{:S(2)}) %collective-permute-start.1) | collective-permute-done | bytes 196640 | tf_op jit(solution)/shard_map/ppermute | solution.py:53
  22.1 1.3 collective-permute-start.2
  23.4 2.8 %collective-permute-done.4.refs_6_ = bf16[4,32,768]{2,1,0:T(8,128)(2,1)S(1)} collective-permute-done((bf16[4,32,768]{2,1,0:T(8,128)(2,1)S(1)}, bf16[4,32,768]{2,1,0:T(8,128)(2,1)S(1)}, u32[]{:S(2)}, u32[]{:S(2)}) %collective-permute-start.4) | collective-permute-done | bytes 196640 | tf_op jit(solution)/shard_map/ppermute | solution.py:53
  26.2 3.3 %collective-permute-start.5 = (bf16[4,32,768]{2,1,0:T(8,128)(2,1)S(1)}, bf16[4,32,768]{2,1,0:T(8,128)(2,1)S(1)}, u32[]{:S(2)}, u32[]{:S(2)}) collective-permute-start(bf16[4,32,768]{2,1,0:T(8,128)(2,1)S(1)} %pad_maximum_fusion.4), channel_id=1, source_target_pairs={{0,8},{8,16},{16,24},{1,9},{9,17},{17,25},{2,10},{10,18},{18,26},{... | collective-permute-start | bytes 589832 | tf_op jit(solution)/shard_map/ppermute | solution.py:53
  29.5 0.0 copy-done.7
  29.6 0.0 collective-permute-done.2.refs_4_
  29.6 5.9 %collective-permute-done.5.refs_7_ = bf16[4,32,768]{2,1,0:T(8,128)(2,1)S(1)} collective-permute-done((bf16[4,32,768]{2,1,0:T(8,128)(2,1)S(1)}, bf16[4,32,768]{2,1,0:T(8,128)(2,1)S(1)}, u32[]{:S(2)}, u32[]{:S(2)}) %collective-permute-start.5) | collective-permute-done | bytes 196640 | tf_op jit(solution)/shard_map/ppermute | solution.py:53
  35.4 0.0 copy-done
  35.4 0.0 copy-done.1
  35.4 0.0 copy-done.3
  35.5 0.0 copy-done.6
  35.5 0.0 copy-start.5
  35.5 1.0 copy-done.5
  36.5 14.1 %shard_map.111 = (bf16[512,768]{1,0:T(8,128)(2,1)S(1)}, bf16[512,768]{1,0:T(8,128)(2,1)S(1)}, bf16[512,768]{1,0:T(8,128)(2,1)S(1)}, bf16[512,768]{1,0:T(8,128)(2...) custom-call(bf16[256,768]{1,0:T(8,128)(2,1)S(1)} %copy-done.3, ...), custom_call_target="tpu_custom_call" | custom-call | tf_op jit(solution)/shard_map/pallas_call | solution.py:304
  50.5 3.5 %shard_map.112 = bf16[512,2432]{1,0:T(8,128)(2,1)S(1)} custom-call(s32[1]{0:T(128)} %bitcast.refs_0_, bf16[512,768]{1,0:T(8,128)(2,1)S(1)} %get-tuple-element.41.refs_1_, bf16[512,768]{1,0:T(8,128)(2,1)S(1)} %get-tuple-element.42.refs_2_, bf16[512,768]{1,0:T(8,128)(2,1)S(1)} %get-tuple-element.43.refs_3_.refs_1_, ...), custom_call_target="tpu_custom_call" | custom-call | tf_op jit(solution)/shard_map/pallas_call | solution.py:304
  54.0 0.6 collective-permute-start.6
  54.6 2.6 %shard_map.113 = (bf16[7,32,768]{2,1,0:T(8,128)(2,1)S(1)}, bf16[7,32,768]{2,1,0:T(8,128)(2,1)S(1)}, bf16[256,1536]{1,0:T(8,128)(2,1)S(1)}) custom-call(bf16[512,768]{1,0:T(8,128)(2,1)S(1)} %get-tuple-element.47.refs_0_, bf16[512,768]{1,0:T(8,128)(2,1)S(1)} %get-tuple-element.43.refs_3_.refs_1_, bf16[512,768]{1,0:T(8,128)(2,1)S(1)} %get-tuple-element.42.refs_2_, ...), custom_call_target="tpu_custom_call" | custom-call | tf_op jit(solution)/shard_map/pallas_call | solution.py:304
  57.3 1.3 collective-permute-start.7
  58.6 3.4 %collective-permute-start.8 = (bf16[4,32,768]{2,1,0:T(8,128)(2,1)S(1)}, bf16[4,32,768]{2,1,0:T(8,128)(2,1)S(1)}, u32[]{:S(2)}, u32[]{:S(2)}) collective-permute-start(bf16[4,32,768]{2,1,0:T(8,128)(2,1)S(1)} %slice.155), channel_id=1, source_target_pairs={{32,0},{64,32},{96,64},{128,96},{160,128},{192,160},{224,192},{33,... | collective-permute-start | bytes 589832 | tf_op jit(solution)/shard_map/ppermute | solution.py:53
  62.0 0.0 collective-permute-done.6.refs_6_
  62.0 3.5 %shard_map.114 = bf16[512,2432]{1,0:T(8,128)(2,1)S(1)} custom-call(s32[1]{0:T(128)} %bitcast.refs_0_, bf16[512,768]{1,0:T(8,128)(2,1)S(1)} %get-tuple-element.41.refs_1_, bf16[512,768]{1,0:T(8,128)(2,1)S(1)} %get-tuple-element.42.refs_2_, bf16[512,768]{1,0:T(8,128)(2,1)S(1)} %get-tuple-element.43.refs_3_.refs_1_, ...), custom_call_target="tpu_custom_call" | custom-call | tf_op jit(solution)/shard_map/pallas_call | solution.py:304
  65.5 0.0 collective-permute-done.7.refs_1_
  65.5 4.7 %collective-permute-done.8.refs_4_ = bf16[4,32,768]{2,1,0:T(8,128)(2,1)S(1)} collective-permute-done((bf16[4,32,768]{2,1,0:T(8,128)(2,1)S(1)}, bf16[4,32,768]{2,1,0:T(8,128)(2,1)S(1)}, u32[]{:S(2)}, u32[]{:S(2)}) %collective-permute-start.8) | collective-permute-done | bytes 196640 | tf_op jit(solution)/shard_map/ppermute | solution.py:53
  70.2 38.5 %all_to_all.14.refs_1_ = bf16[32,16,2432]{2,1,0:T(8,128)(2,1)S(1)} all-to-all(bf16[32,16,2432]{2,1,0:T(8,128)(2,1)S(1)} %bitcast.2), channel_id=1, replica_groups=mesh['gx'=8,'gy'=4,'gz'=8] {'gx','gy'}, dimensions={0} | all-to-all | bytes 4980736 | tf_op jit(solution)/shard_map/all_to_all | solution.py:356
  108.7 1.0 shard_map.115
  109.8 3.1 %collective-permute-start.9 = (bf16[4,32,768]{2,1,0:T(8,128)(2,1)S(1)}, bf16[4,32,768]{2,1,0:T(8,128)(2,1)S(1)}, u32[]{:S(2)}, u32[]{:S(2)}) collective-permute-start(bf16[4,32,768]{2,1,0:T(8,128)(2,1)S(1)} %pad_maximum_fusion.6), channel_id=1, source_target_pairs={{8,0},{16,8},{24,16},{9,1},{17,9},{25,17},{10,2},{18,10},{26,18},{... | collective-permute-start | bytes 589832 | tf_op jit(solution)/shard_map/ppermute | solution.py:53
  112.9 1.3 collective-permute-start.11
  114.2 7.9 %all-to-all-start.1 = ((bf16[4,8,2432]{2,1,0:T(8,128)(2,1)}), bf16[4,8,2432]{2,1,0:T(8,128)(2,1)S(1)}, u32[]{:S(2)}, u32[]{:S(2)}) async-start(bf16[4,8,2432]{2,1,0:T(8,128)(2,1)} %shard_map.115), calls=%async_computation.1 | async-start | bytes 311296 | tf_op jit(solution)/shard_map/all_to_all | solution.py:362
  122.1 0.0 collective-permute-done.9.refs_2_
  122.2 4.1 %collective-permute-start.10 = (bf16[4,32,768]{2,1,0:T(8,128)(2,1)S(1)}, bf16[4,32,768]{2,1,0:T(8,128)(2,1)S(1)}, u32[]{:S(2)}, u32[]{:S(2)}) collective-permute-start(bf16[4,32,768]{2,1,0:T(8,128)(2,1)S(1)} %pad_maximum_fusion.7), channel_id=1, source_target_pairs={{32,0},{64,32},{96,64},{128,96},{160,128},{192,160},{224,192},{33,... | collective-permute-start | bytes 589832 | tf_op jit(solution)/shard_map/ppermute | solution.py:53
  126.3 0.0 collective-permute-done.11.refs_5_
  126.4 1.9 %collective-permute-start.12 = (bf16[4,32,768]{2,1,0:T(8,128)(2,1)S(1)}, bf16[4,32,768]{2,1,0:T(8,128)(2,1)S(1)}, u32[]{:S(2)}, u32[]{:S(2)}) collective-permute-start(bf16[4,32,768]{2,1,0:T(8,128)(2,1)S(1)} %pad_maximum_fusion.9), channel_id=1, source_target_pairs={{8,0},{16,8},{24,16},{9,1},{17,9},{25,17},{10,2},{18,10},{26,18},{... | collective-permute-start | bytes 589832 | tf_op jit(solution)/shard_map/ppermute | solution.py:53
  128.3 3.1 %all-to-all-done.1.refs_0_ = bf16[4,8,2432]{2,1,0:T(8,128)(2,1)S(1)} async-done(((bf16[4,8,2432]{2,1,0:T(8,128)(2,1)}), bf16[4,8,2432]{2,1,0:T(8,128)(2,1)S(1)}, u32[]{:S(2)}, u32[]{:S(2)}) %all-to-all-start.1) | async-done | bytes 155680 | tf_op jit(solution)/shard_map/all_to_all | solution.py:362
  131.4 0.6 shard_map.117
  132.0 0.6 slice_reduce_fusion
  132.7 0.0 collective-permute-done.10.refs_3_
  132.7 1.5 %collective-permute-done.12.refs_6_ = bf16[4,32,768]{2,1,0:T(8,128)(2,1)S(1)} collective-permute-done((bf16[4,32,768]{2,1,0:T(8,128)(2,1)S(1)}, bf16[4,32,768]{2,1,0:T(8,128)(2,1)S(1)}, u32[]{:S(2)}, u32[]{:S(2)}) %collective-permute-start.12) | collective-permute-done | bytes 196640 | tf_op jit(solution)/shard_map/ppermute | solution.py:53
  134.2 1.8 %shard_map.116 = (bf16[256,768]{1,0:T(8,128)(2,1)}, bf16[256,768]{1,0:T(8,128)(2,1)}) custom-call(bf16[256,1536]{1,0:T(8,128)(2,1)S(1)} %get-tuple-element.49.refs_0_, bf16[4,32,768]{2,1,0:T(8,128)(2,1)S(1)} %collective-permute-done.7.refs_1_, bf16[4,32,768]{2,1,0:T(8,128)(2,1)S(1)} %collective-permute-done.9.refs_2_, ...), custom_call_target="tpu_custom_call" | custom-call | tf_op jit(solution)/shard_map/pallas_call | solution.py:304
  (26 shorter events, 0.5 us)
Async XLA Ops:
  1.3 1.0 copy-start.2
  2.3 1.0 copy-start.4
  3.3 26.2 %copy-start.7 = (f32[768]{0:T(1024)S(1)}, f32[768]{0:T(1024)}, u32[]{:S(2)}) copy-start(f32[768]{0:T(1024)} %param.8) | copy-start | bytes 9220
  3.3 32.1 %copy-start = (bf16[768,768]{1,0:T(8,128)(2,1)S(1)}, bf16[768,768]{1,0:T(8,128)(2,1)}, u32[]{:S(2)}) copy-start(bf16[768,768]{1,0:T(8,128)(2,1)} %refs_6_.1) | copy-start | bytes 3538948
  3.3 32.1 %copy-start.1 = (bf16[768,2304]{1,0:T(8,128)(2,1)S(1)}, bf16[768,2304]{1,0:T(8,128)(2,1)}, u32[]{:S(2)}) copy-start(bf16[768,2304]{1,0:T(8,128)(2,1)} %refs_10_.1) | copy-start | bytes 10616836
  3.3 32.1 %copy-start.3 = (bf16[256,768]{1,0:T(8,128)(2,1)S(1)}, bf16[256,768]{1,0:T(8,128)(2,1)}, u32[]{:S(2)}) copy-start(bf16[256,768]{1,0:T(8,128)(2,1)} %refs_0_.1) | copy-start | bytes 1179652
  3.3 32.1 %copy-start.6 = (s32[1,512]{1,0:T(1,128)S(1)}, s32[1,512]{1,0:T(1,128)}, u32[]{:S(2)}) copy-start(s32[1,512]{1,0:T(1,128)} %refs_4_.1) | copy-start | bytes 6148
  3.8 9.7 %collective-permute-start = (bf16[4,32,768]{2,1,0:T(8,128)(2,1)S(1)}, bf16[4,32,768]{2,1,0:T(8,128)(2,1)S(1)}, u32[]{:S(2)}, u32[]{:S(2)}) collective-permute-start(bf16[4,32,768]{2,1,0:T(8,128)(2,1)S(1)} %slice.133), channel_id=1, source_target_pairs={{0,32},{32,64},{64,96},{96,128},{128,160},{160,192},{192,224},{1,3... | collective-permute-start | bytes 589832 | tf_op jit(solution)/shard_map/ppermute | solution.py:53
  7.9 9.1 %collective-permute-start.3 = (bf16[4,32,768]{2,1,0:T(8,128)(2,1)S(1)}, bf16[4,32,768]{2,1,0:T(8,128)(2,1)S(1)}, u32[]{:S(2)}, u32[]{:S(2)}) collective-permute-start(bf16[4,32,768]{2,1,0:T(8,128)(2,1)S(1)} %pad_maximum_fusion.2), channel_id=1, source_target_pairs={{0,1},{1,2},{2,3},{3,4},{4,5},{5,6},{6,7},{8,9},{9,10},{10,11},{11... | collective-permute-start | bytes 589832 | tf_op jit(solution)/shard_map/ppermute | solution.py:53
  13.5 8.5 %collective-permute-start.1 = (bf16[4,32,768]{2,1,0:T(8,128)(2,1)S(1)}, bf16[4,32,768]{2,1,0:T(8,128)(2,1)S(1)}, u32[]{:S(2)}, u32[]{:S(2)}) collective-permute-start(bf16[4,32,768]{2,1,0:T(8,128)(2,1)S(1)} %pad_maximum_fusion), channel_id=1, source_target_pairs={{0,8},{8,16},{16,24},{1,9},{9,17},{17,25},{2,10},{10,18},{18,26},{... | collective-permute-start | bytes 589832 | tf_op jit(solution)/shard_map/ppermute | solution.py:53
  17.1 9.1 %collective-permute-start.4 = (bf16[4,32,768]{2,1,0:T(8,128)(2,1)S(1)}, bf16[4,32,768]{2,1,0:T(8,128)(2,1)S(1)}, u32[]{:S(2)}, u32[]{:S(2)}) collective-permute-start(bf16[4,32,768]{2,1,0:T(8,128)(2,1)S(1)} %pad_maximum_fusion.3), channel_id=1, source_target_pairs={{0,32},{32,64},{64,96},{96,128},{128,160},{160,192},{192,224},{1,3... | collective-permute-start | bytes 589832 | tf_op jit(solution)/shard_map/ppermute | solution.py:53
  22.1 7.5 %collective-permute-start.2 = (bf16[4,32,768]{2,1,0:T(8,128)(2,1)S(1)}, bf16[4,32,768]{2,1,0:T(8,128)(2,1)S(1)}, u32[]{:S(2)}, u32[]{:S(2)}) collective-permute-start(bf16[4,32,768]{2,1,0:T(8,128)(2,1)S(1)} %pad_maximum_fusion.1), channel_id=1, source_target_pairs={{0,1},{1,2},{2,3},{3,4},{4,5},{5,6},{6,7},{8,9},{9,10},{10,11},{11... | collective-permute-start | bytes 589832 | tf_op jit(solution)/shard_map/ppermute | solution.py:53
  26.2 9.2 %collective-permute-start.5 = (bf16[4,32,768]{2,1,0:T(8,128)(2,1)S(1)}, bf16[4,32,768]{2,1,0:T(8,128)(2,1)S(1)}, u32[]{:S(2)}, u32[]{:S(2)}) collective-permute-start(bf16[4,32,768]{2,1,0:T(8,128)(2,1)S(1)} %pad_maximum_fusion.4), channel_id=1, source_target_pairs={{0,8},{8,16},{16,24},{1,9},{9,17},{17,25},{2,10},{10,18},{18,26},{... | collective-permute-start | bytes 589832 | tf_op jit(solution)/shard_map/ppermute | solution.py:53
  35.5 1.0 copy-start.5
  54.0 8.0 %collective-permute-start.6 = (bf16[512,2432]{1,0:T(8,128)(2,1)S(1)}, bf16[512,2432]{1,0:T(8,128)(2,1)S(1)}, u32[]{:S(2)}, u32[]{:S(2)}) collective-permute-start(bf16[512,2432]{1,0:T(8,128)(2,1)S(1)} %shard_map.112), channel_id=1, source_target_pairs={{0,1},{1,0},{2,3},{3,2},{4,5},{5,4},{6,7},{7,6},{8,9},{9,8},{10,11... | collective-permute-start | bytes 7471112 | tf_op jit(solution)/shard_map/ppermute | solution.py:87
  57.3 8.2 %collective-permute-start.7 = (bf16[4,32,768]{2,1,0:T(8,128)(2,1)S(1)}, bf16[4,32,768]{2,1,0:T(8,128)(2,1)S(1)}, u32[]{:S(2)}, u32[]{:S(2)}) collective-permute-start(bf16[4,32,768]{2,1,0:T(8,128)(2,1)S(1)} %pad_maximum_fusion.5), channel_id=1, source_target_pairs={{1,0},{2,1},{3,2},{4,3},{5,4},{6,5},{7,6},{9,8},{10,9},{11,10},{12... | collective-permute-start | bytes 589832 | tf_op jit(solution)/shard_map/ppermute | solution.py:53
  58.6 11.6 %collective-permute-start.8 = (bf16[4,32,768]{2,1,0:T(8,128)(2,1)S(1)}, bf16[4,32,768]{2,1,0:T(8,128)(2,1)S(1)}, u32[]{:S(2)}, u32[]{:S(2)}) collective-permute-start(bf16[4,32,768]{2,1,0:T(8,128)(2,1)S(1)} %slice.155), channel_id=1, source_target_pairs={{32,0},{64,32},{96,64},{128,96},{160,128},{192,160},{224,192},{33,... | collective-permute-start | bytes 589832 | tf_op jit(solution)/shard_map/ppermute | solution.py:53
  109.8 12.3 %collective-permute-start.9 = (bf16[4,32,768]{2,1,0:T(8,128)(2,1)S(1)}, bf16[4,32,768]{2,1,0:T(8,128)(2,1)S(1)}, u32[]{:S(2)}, u32[]{:S(2)}) collective-permute-start(bf16[4,32,768]{2,1,0:T(8,128)(2,1)S(1)} %pad_maximum_fusion.6), channel_id=1, source_target_pairs={{8,0},{16,8},{24,16},{9,1},{17,9},{25,17},{10,2},{18,10},{26,18},{... | collective-permute-start | bytes 589832 | tf_op jit(solution)/shard_map/ppermute | solution.py:53
  112.9 13.4 %collective-permute-start.11 = (bf16[4,32,768]{2,1,0:T(8,128)(2,1)S(1)}, bf16[4,32,768]{2,1,0:T(8,128)(2,1)S(1)}, u32[]{:S(2)}, u32[]{:S(2)}) collective-permute-start(bf16[4,32,768]{2,1,0:T(8,128)(2,1)S(1)} %pad_maximum_fusion.8), channel_id=1, source_target_pairs={{1,0},{2,1},{3,2},{4,3},{5,4},{6,5},{7,6},{9,8},{10,9},{11,10},{12... | collective-permute-start | bytes 589832 | tf_op jit(solution)/shard_map/ppermute | solution.py:53
  114.2 17.1 %all-to-all-start.1 = ((bf16[4,8,2432]{2,1,0:T(8,128)(2,1)}), bf16[4,8,2432]{2,1,0:T(8,128)(2,1)S(1)}, u32[]{:S(2)}, u32[]{:S(2)}) async-start(bf16[4,8,2432]{2,1,0:T(8,128)(2,1)} %shard_map.115), calls=%async_computation.1 | async-start | bytes 311296 | tf_op jit(solution)/shard_map/all_to_all | solution.py:362
  122.2 10.5 %collective-permute-start.10 = (bf16[4,32,768]{2,1,0:T(8,128)(2,1)S(1)}, bf16[4,32,768]{2,1,0:T(8,128)(2,1)S(1)}, u32[]{:S(2)}, u32[]{:S(2)}) collective-permute-start(bf16[4,32,768]{2,1,0:T(8,128)(2,1)S(1)} %pad_maximum_fusion.7), channel_id=1, source_target_pairs={{32,0},{64,32},{96,64},{128,96},{160,128},{192,160},{224,192},{33,... | collective-permute-start | bytes 589832 | tf_op jit(solution)/shard_map/ppermute | solution.py:53
  126.4 7.8 %collective-permute-start.12 = (bf16[4,32,768]{2,1,0:T(8,128)(2,1)S(1)}, bf16[4,32,768]{2,1,0:T(8,128)(2,1)S(1)}, u32[]{:S(2)}, u32[]{:S(2)}) collective-permute-start(bf16[4,32,768]{2,1,0:T(8,128)(2,1)S(1)} %pad_maximum_fusion.9), channel_id=1, source_target_pairs={{8,0},{16,8},{24,16},{9,1},{17,9},{25,17},{10,2},{18,10},{26,18},{... | collective-permute-start | bytes 589832 | tf_op jit(solution)/shard_map/ppermute | solution.py:53

commit v9 on v8

--- a/solution.py
+++ b/solution.py
@@ -352,7 +352,6 @@
     places = starts()
     down = step([[back_t], [back_g]], places, DOWN, 0, -1)
     (paired,) = call(functools.partial(half_sums, 0), [half], *operands, got, smem=(0,), mib=SUMS)
-    paired, down = lax.optimization_barrier((paired, down))
     spread = lax.all_to_all(paired, ("gx", "gy"), split_axis=0, concat_axis=0, tiled=True)
     (part,) = call(sum2_body, [((4, 8, COLS), BF)], me, spread.reshape(32, 16, COLS), smem=(0,))
     part, down = lax.optimization_barrier((part, down))

time: 137 us -> 140 us (1.022)
  blocking collectives: 38.5 us -> 0 us
  waiting for transfers between devices: 24.1 us -> 45.8 us
  starting transfers between devices: 40.2 us -> 49.2 us
  local copies, waits for them, and re-layouts: 4.5 us -> 13.1 us
    all_to_all x1 -> x0, blocking collectives: 38.5 us -> none  [on_device(): lax.all_to_all(paired, ('gx', 'gy'), split_axis=0, concat_axis=0, tiled=T...]
    all_to_all x0 -> x1, waiting for transfers between devices: none -> 21.5 us  [on_device(): lax.all_to_all(paired, ('gx', 'gy'), split_axis=0, concat_axis=0, tiled=T...]
    all_to_all x0 -> x1, starting transfers between devices: none -> 8.11 us  [on_device(): lax.all_to_all(paired, ('gx', 'gy'), split_axis=0, concat_axis=0, tiled=T...]
    unnamed x17 -> x41, local copies, waits for them, and re-layouts: 3.69 us -> 9.83 us
    ppermute x12, waiting for transfers between devices: 21 us -> 16 us  [passed_along(): lax.ppermute(value, axis, [(source, source + steps) for source in range(i...]
    ppermute x1, waiting for transfers between devices: 0.01 us -> 4.43 us  [crossed(): lax.ppermute(value, axis, [(source, source ^ mask) for source in range(co...]
    slice x15, local copies, waits for them, and re-layouts: 0.18 us -> 2.63 us  [stage(): lax.slice_in_dim(arrays[place[k][0]], place[k][1], place[k][1] + 1)]
  transfers between devices with their start and end apart: 14 -> 15, of which waited for: 7 -> 9; matrix products, arithmetic and copies ran while one was open for 1% -> 2% of each run, Pallas kernels for 5% -> 3%
where the time goes in v9:
time: 140 us; the launch traced here: 138 us
  starting transfers between devices  49.2 us (35%)
  waiting for transfers between devices  45.8 us (33%)
  Pallas kernels  27.8 us (20%)
  local copies, waits for them, and re-layouts  13.1 us (9%)
    ppermute x12, starting transfers between devices, passed_along(): lax.ppermute(value, axis, [(source, source + steps) for source in range(i...  31.8 us
    pallas_call x8, Pallas kernels, call(): pl.pallas_call(flat, out_shape=[jax.ShapeDtypeStruct(shape, dtype) for sh...  27.8 us
    all_to_all x1, waiting for transfers between devices, on_device(): lax.all_to_all(paired, ('gx', 'gy'), split_axis=0, concat_axis=0, tiled=T...  21.5 us
    ppermute x12, waiting for transfers between devices, passed_along(): lax.ppermute(value, axis, [(source, source + steps) for source in range(i...  16 us
    unnamed x41, local copies, waits for them, and re-layouts  9.83 us
    all_to_all x1, starting transfers between devices, on_device(): lax.all_to_all(part, 'gz', split_axis=0, concat_axis=0, tiled=True, axis_...  8.73 us
    all_to_all x1, starting transfers between devices, on_device(): lax.all_to_all(paired, ('gx', 'gy'), split_axis=0, concat_axis=0, tiled=T...  8.11 us
    ppermute x1, waiting for transfers between devices, crossed(): lax.ppermute(value, axis, [(source, source ^ mask) for source in range(co...  4.43 us
  transfers between devices with their start and end apart: 15, of which 9 were waited for; matrix products, arithmetic and copies ran while one was open for 2% of the time, Pallas kernels for 3%

profile of v9, /device:TPU:10, one launch (start us, length us, event | category | flops | bytes accessed | tf_op | source)
XLA Modules:
  0.0 138.3 jit_solution(14989546884256273174)
XLA Ops:
  0.6 0.7 copy.14.refs_2_.refs_7_
  1.3 1.0 copy-done.6
  2.3 1.0 copy-done.8
  3.3 0.0 copy-start.18
  3.3 0.4 shard_map.110
  3.8 4.1 %collective-permute-start = (bf16[4,32,768]{2,1,0:T(8,128)(2,1)S(1)}, bf16[4,32,768]{2,1,0:T(8,128)(2,1)S(1)}, u32[]{:S(2)}, u32[]{:S(2)}) collective-permute-start(bf16[4,32,768]{2,1,0:T(8,128)(2,1)S(1)} %slice.133), channel_id=1, source_target_pairs={{0,32},{32,64},{64,96},{96,128},{128,160},{160,192},{192,224},{1,3... | collective-permute-start | bytes 589832 | tf_op jit(solution)/shard_map/ppermute | solution.py:53
  7.9 1.5 %collective-permute-start.3 = (bf16[4,32,768]{2,1,0:T(8,128)(2,1)S(1)}, bf16[4,32,768]{2,1,0:T(8,128)(2,1)S(1)}, u32[]{:S(2)}, u32[]{:S(2)}) collective-permute-start(bf16[4,32,768]{2,1,0:T(8,128)(2,1)S(1)} %pad_maximum_fusion.2), channel_id=1, source_target_pairs={{0,1},{1,2},{2,3},{3,4},{4,5},{5,6},{6,7},{8,9},{9,10},{10,11},{11... | collective-permute-start | bytes 589832 | tf_op jit(solution)/shard_map/ppermute | solution.py:53
  9.4 4.0 %collective-permute-done.refs_2_ = bf16[4,32,768]{2,1,0:T(8,128)(2,1)S(1)} collective-permute-done((bf16[4,32,768]{2,1,0:T(8,128)(2,1)S(1)}, bf16[4,32,768]{2,1,0:T(8,128)(2,1)S(1)}, u32[]{:S(2)}, u32[]{:S(2)}) %collective-permute-start) | collective-permute-done | bytes 196640 | tf_op jit(solution)/shard_map/ppermute | solution.py:53
  13.5 3.5 %collective-permute-start.1 = (bf16[4,32,768]{2,1,0:T(8,128)(2,1)S(1)}, bf16[4,32,768]{2,1,0:T(8,128)(2,1)S(1)}, u32[]{:S(2)}, u32[]{:S(2)}) collective-permute-start(bf16[4,32,768]{2,1,0:T(8,128)(2,1)S(1)} %pad_maximum_fusion), channel_id=1, source_target_pairs={{0,8},{8,16},{16,24},{1,9},{9,17},{17,25},{2,10},{10,18},{18,26},{... | collective-permute-start | bytes 589832 | tf_op jit(solution)/shard_map/ppermute | solution.py:53
  17.0 0.0 collective-permute-done.3.refs_5_
  17.1 2.9 %collective-permute-start.4 = (bf16[4,32,768]{2,1,0:T(8,128)(2,1)S(1)}, bf16[4,32,768]{2,1,0:T(8,128)(2,1)S(1)}, u32[]{:S(2)}, u32[]{:S(2)}) collective-permute-start(bf16[4,32,768]{2,1,0:T(8,128)(2,1)S(1)} %pad_maximum_fusion.3), channel_id=1, source_target_pairs={{0,32},{32,64},{64,96},{96,128},{128,160},{160,192},{192,224},{1,3... | collective-permute-start | bytes 589832 | tf_op jit(solution)/shard_map/ppermute | solution.py:53
  20.0 2.0 %collective-permute-done.1.refs_3_ = bf16[4,32,768]{2,1,0:T(8,128)(2,1)S(1)} collective-permute-done((bf16[4,32,768]{2,1,0:T(8,128)(2,1)S(1)}, bf16[4,32,768]{2,1,0:T(8,128)(2,1)S(1)}, u32[]{:S(2)}, u32[]{:S(2)}) %collective-permute-start.1) | collective-permute-done | bytes 196640 | tf_op jit(solution)/shard_map/ppermute | solution.py:53
  22.1 1.3 collective-permute-start.2
  23.4 2.8 %collective-permute-done.4.refs_6_ = bf16[4,32,768]{2,1,0:T(8,128)(2,1)S(1)} collective-permute-done((bf16[4,32,768]{2,1,0:T(8,128)(2,1)S(1)}, bf16[4,32,768]{2,1,0:T(8,128)(2,1)S(1)}, u32[]{:S(2)}, u32[]{:S(2)}) %collective-permute-start.4) | collective-permute-done | bytes 196640 | tf_op jit(solution)/shard_map/ppermute | solution.py:53
  26.2 3.3 %collective-permute-start.5 = (bf16[4,32,768]{2,1,0:T(8,128)(2,1)S(1)}, bf16[4,32,768]{2,1,0:T(8,128)(2,1)S(1)}, u32[]{:S(2)}, u32[]{:S(2)}) collective-permute-start(bf16[4,32,768]{2,1,0:T(8,128)(2,1)S(1)} %pad_maximum_fusion.4), channel_id=1, source_target_pairs={{0,8},{8,16},{16,24},{1,9},{9,17},{17,25},{2,10},{10,18},{18,26},{... | collective-permute-start | bytes 589832 | tf_op jit(solution)/shard_map/ppermute | solution.py:53
  29.5 0.0 copy-done.19
  29.6 0.0 collective-permute-done.2.refs_4_
  29.6 5.9 %collective-permute-done.5.refs_7_ = bf16[4,32,768]{2,1,0:T(8,128)(2,1)S(1)} collective-permute-done((bf16[4,32,768]{2,1,0:T(8,128)(2,1)S(1)}, bf16[4,32,768]{2,1,0:T(8,128)(2,1)S(1)}, u32[]{:S(2)}, u32[]{:S(2)}) %collective-permute-start.5) | collective-permute-done | bytes 196640 | tf_op jit(solution)/shard_map/ppermute | solution.py:53
  35.4 0.0 copy-done.3
  35.4 0.0 copy-done.5
  35.4 0.0 copy-done.7
  35.5 0.0 copy-done.18
  35.5 0.0 copy-start.9
  35.5 1.0 copy-done.9
  36.5 14.0 %shard_map.111 = (bf16[512,768]{1,0:T(8,128)(2,1)S(1)}, bf16[512,768]{1,0:T(8,128)(2,1)S(1)}, bf16[512,768]{1,0:T(8,128)(2,1)S(1)}, bf16[512,768]{1,0:T(8,128)(2...) custom-call(bf16[256,768]{1,0:T(8,128)(2,1)S(1)} %copy-done.7, ...), custom_call_target="tpu_custom_call" | custom-call | tf_op jit(solution)/shard_map/pallas_call | solution.py:304
  50.5 0.0 copy-start.12
  50.5 0.0 copy-start.14
  50.5 3.5 %shard_map.112 = bf16[512,2432]{1,0:T(8,128)(2,1)S(1)} custom-call(s32[1]{0:T(128)} %bitcast.refs_0_, bf16[512,768]{1,0:T(8,128)(2,1)S(1)} %get-tuple-element.36.refs_1_, bf16[512,768]{1,0:T(8,128)(2,1)S(1)} %get-tuple-element.37.refs_2_, bf16[512,768]{1,0:T(8,128)(2,1)S(1)} %get-tuple-element.38.refs_3_.refs_1_, ...), custom_call_target="tpu_custom_call" | custom-call | tf_op jit(solution)/shard_map/pallas_call | solution.py:304
  54.0 0.6 collective-permute-start.6
  54.6 4.4 %collective-permute-done.6.refs_6_ = bf16[512,2432]{1,0:T(8,128)(2,1)S(1)} collective-permute-done((bf16[512,2432]{1,0:T(8,128)(2,1)S(1)}, bf16[512,2432]{1,0:T(8,128)(2,1)S(1)}, u32[]{:S(2)}, u32[]{:S(2)}) %collective-permute-start.6) | collective-permute-done | bytes 2490400 | tf_op jit(solution)/shard_map/ppermute | solution.py:87
  59.0 3.4 %shard_map.114 = bf16[512,2432]{1,0:T(8,128)(2,1)S(1)} custom-call(s32[1]{0:T(128)} %bitcast.refs_0_, bf16[512,768]{1,0:T(8,128)(2,1)S(1)} %get-tuple-element.36.refs_1_, bf16[512,768]{1,0:T(8,128)(2,1)S(1)} %get-tuple-element.37.refs_2_, bf16[512,768]{1,0:T(8,128)(2,1)S(1)} %get-tuple-element.38.refs_3_.refs_1_, ...), custom_call_target="tpu_custom_call" | custom-call | tf_op jit(solution)/shard_map/pallas_call | solution.py:304
  62.5 1.4 %copy-done = bf16[512,2432]{1,0:T(8,128)(2,1)} copy-done((bf16[512,2432]{1,0:T(8,128)(2,1)}, bf16[512,2432]{1,0:T(8,128)(2,1)S(1)}, u32[]{:S(2)}) %copy-start) | copy-done | bytes 2490392
  63.9 8.1 %all-to-all-start = ((bf16[32,16,2432]{2,1,0:T(8,128)(2,1)}), bf16[32,16,2432]{2,1,0:T(8,128)(2,1)S(1)}, u32[]{:S(2)}, u32[]{:S(2)}) async-start(bf16[32,16,2432]{2,1,0:T(8,128)(2,1)} %bitcast.2), calls=%async_computation | async-start | bytes 4980736 | tf_op jit(solution)/shard_map/all_to_all | solution.py:355
  72.0 1.1 copy-done.2
  73.2 1.3 copy-done.4
  74.4 1.1 copy-done.13
  75.6 1.1 copy-done.15
  76.7 2.5 %shard_map.113 = (bf16[7,32,768]{2,1,0:T(8,128)(2,1)S(1)}, bf16[7,32,768]{2,1,0:T(8,128)(2,1)S(1)}, bf16[256,1536]{1,0:T(8,128)(2,1)S(1)}) custom-call(bf16[512,768]{1,0:T(8,128)(2,1)S(1)} %copy-done.13, bf16[512,768]{1,0:T(8,128)(2,1)S(1)} %get-tuple-element.38.refs_3_.refs_1_, bf16[512,768]{1,0:T(8,128)(2,1)S(1)} %copy-done.2, ...), custom_call_target="tpu_custom_call" | custom-call | tf_op jit(solution)/shard_map/pallas_call | solution.py:304
  79.3 0.0 copy-start.16
  79.3 0.0 copy-start.17
  79.3 0.8 pad_maximum_fusion.5
  80.1 1.3 collective-permute-start.7
  81.4 0.7 slice.155
  82.1 0.0 copy-done.16
  82.1 3.4 %collective-permute-start.8 = (bf16[4,32,768]{2,1,0:T(8,128)(2,1)}, bf16[4,32,768]{2,1,0:T(8,128)(2,1)}, u32[]{:S(2)}, u32[]{:S(2)}) collective-permute-start(bf16[4,32,768]{2,1,0:T(8,128)(2,1)} %slice.155), channel_id=1, source_target_pairs={{32,0},{64,32},{96,64},{128,96},{160,128},{192,160},{224,192},{33,... | collective-permute-start | bytes 589832 | tf_op jit(solution)/shard_map/ppermute | solution.py:53
  85.5 21.5 %all-to-all-done.refs_1_ = bf16[32,16,2432]{2,1,0:T(8,128)(2,1)S(1)} async-done(((bf16[32,16,2432]{2,1,0:T(8,128)(2,1)}), bf16[32,16,2432]{2,1,0:T(8,128)(2,1)S(1)}, u32[]{:S(2)}, u32[]{:S(2)}) %all-to-all-start) | async-done | bytes 2490400 | tf_op jit(solution)/shard_map/all_to_all | solution.py:355
  107.0 1.0 shard_map.115
  108.0 0.0 collective-permute-done.7.refs_1_
  108.0 0.8 collective-permute-done.8.refs_4_
  108.8 0.9 fusion.5
  109.6 0.9 fusion
  110.6 3.5 %collective-permute-start.9 = (bf16[4,32,768]{2,1,0:T(8,128)(2,1)S(1)}, bf16[4,32,768]{2,1,0:T(8,128)(2,1)S(1)}, u32[]{:S(2)}, u32[]{:S(2)}) collective-permute-start(bf16[4,32,768]{2,1,0:T(8,128)(2,1)S(1)} %pad_maximum_fusion.6), channel_id=1, source_target_pairs={{8,0},{16,8},{24,16},{9,1},{17,9},{25,17},{10,2},{18,10},{26,18},{... | collective-permute-start | bytes 589832 | tf_op jit(solution)/shard_map/ppermute | solution.py:53
  114.1 1.3 collective-permute-start.11
  115.4 8.7 %all-to-all-start.1 = ((bf16[4,8,2432]{2,1,0:T(8,128)(2,1)}), bf16[4,8,2432]{2,1,0:T(8,128)(2,1)S(1)}, u32[]{:S(2)}, u32[]{:S(2)}) async-start(bf16[4,8,2432]{2,1,0:T(8,128)(2,1)} %shard_map.115), calls=%async_computation.1 | async-start | bytes 311296 | tf_op jit(solution)/shard_map/all_to_all | solution.py:361
  124.2 0.0 collective-permute-done.9.refs_2_
  124.2 3.9 %collective-permute-start.10 = (bf16[4,32,768]{2,1,0:T(8,128)(2,1)S(1)}, bf16[4,32,768]{2,1,0:T(8,128)(2,1)S(1)}, u32[]{:S(2)}, u32[]{:S(2)}) collective-permute-start(bf16[4,32,768]{2,1,0:T(8,128)(2,1)S(1)} %pad_maximum_fusion.7), channel_id=1, source_target_pairs={{32,0},{64,32},{96,64},{128,96},{160,128},{192,160},{224,192},{33,... | collective-permute-start | bytes 589832 | tf_op jit(solution)/shard_map/ppermute | solution.py:53
  128.1 0.0 collective-permute-done.11.refs_5_
  128.2 1.9 %collective-permute-start.12 = (bf16[4,32,768]{2,1,0:T(8,128)(2,1)S(1)}, bf16[4,32,768]{2,1,0:T(8,128)(2,1)S(1)}, u32[]{:S(2)}, u32[]{:S(2)}) collective-permute-start(bf16[4,32,768]{2,1,0:T(8,128)(2,1)S(1)} %pad_maximum_fusion.9), channel_id=1, source_target_pairs={{8,0},{16,8},{24,16},{9,1},{17,9},{25,17},{10,2},{18,10},{26,18},{... | collective-permute-start | bytes 589832 | tf_op jit(solution)/shard_map/ppermute | solution.py:53
  130.1 3.9 %all-to-all-done.1.refs_0_ = bf16[4,8,2432]{2,1,0:T(8,128)(2,1)S(1)} async-done(((bf16[4,8,2432]{2,1,0:T(8,128)(2,1)}), bf16[4,8,2432]{2,1,0:T(8,128)(2,1)S(1)}, u32[]{:S(2)}, u32[]{:S(2)}) %all-to-all-start.1) | async-done | bytes 155680 | tf_op jit(solution)/shard_map/all_to_all | solution.py:361
  134.0 0.6 shard_map.117
  134.7 0.6 slice_reduce_fusion
  135.3 0.0 collective-permute-done.10.refs_3_
  135.3 0.5 collective-permute-done.12.refs_6_
  135.8 2.4 %shard_map.116 = (bf16[256,768]{1,0:T(8,128)(2,1)}, bf16[256,768]{1,0:T(8,128)(2,1)}) custom-call(bf16[256,1536]{1,0:T(8,128)(2,1)S(1)} %copy-done.11, bf16[4,32,768]{2,1,0:T(8,128)(2,1)S(1)} %collective-permute-done.7.refs_1_, bf16[4,32,768]{2,1,0:T(8,128)(2,1)S(1)} %collective-permute-done.9.refs_2_, ...), custom_call_target="tpu_custom_call" | custom-call | tf_op jit(solution)/shard_map/pallas_call | solution.py:304
  (42 shorter events, 0.4 us)
Async XLA Ops:
  1.3 1.0 copy-start.6
  2.3 1.0 copy-start.8
  3.3 26.2 %copy-start.19 = (f32[768]{0:T(1024)S(1)}, f32[768]{0:T(1024)}, u32[]{:S(2)}) copy-start(f32[768]{0:T(1024)} %param.8) | copy-start | bytes 9220
  3.3 32.1 %copy-start.3 = (bf16[768,768]{1,0:T(8,128)(2,1)S(1)}, bf16[768,768]{1,0:T(8,128)(2,1)}, u32[]{:S(2)}) copy-start(bf16[768,768]{1,0:T(8,128)(2,1)} %refs_6_.1) | copy-start | bytes 3538948
  3.3 32.1 %copy-start.5 = (bf16[768,2304]{1,0:T(8,128)(2,1)S(1)}, bf16[768,2304]{1,0:T(8,128)(2,1)}, u32[]{:S(2)}) copy-start(bf16[768,2304]{1,0:T(8,128)(2,1)} %refs_10_.1) | copy-start | bytes 10616836
  3.3 32.1 %copy-start.7 = (bf16[256,768]{1,0:T(8,128)(2,1)S(1)}, bf16[256,768]{1,0:T(8,128)(2,1)}, u32[]{:S(2)}) copy-start(bf16[256,768]{1,0:T(8,128)(2,1)} %refs_0_.1) | copy-start | bytes 1179652
  3.3 32.1 %copy-start.18 = (s32[1,512]{1,0:T(1,128)S(1)}, s32[1,512]{1,0:T(1,128)}, u32[]{:S(2)}) copy-start(s32[1,512]{1,0:T(1,128)} %refs_4_.1) | copy-start | bytes 6148
  3.8 9.7 %collective-permute-start = (bf16[4,32,768]{2,1,0:T(8,128)(2,1)S(1)}, bf16[4,32,768]{2,1,0:T(8,128)(2,1)S(1)}, u32[]{:S(2)}, u32[]{:S(2)}) collective-permute-start(bf16[4,32,768]{2,1,0:T(8,128)(2,1)S(1)} %slice.133), channel_id=1, source_target_pairs={{0,32},{32,64},{64,96},{96,128},{128,160},{160,192},{192,224},{1,3... | collective-permute-start | bytes 589832 | tf_op jit(solution)/shard_map/ppermute | solution.py:53
  7.9 9.1 %collective-permute-start.3 = (bf16[4,32,768]{2,1,0:T(8,128)(2,1)S(1)}, bf16[4,32,768]{2,1,0:T(8,128)(2,1)S(1)}, u32[]{:S(2)}, u32[]{:S(2)}) collective-permute-start(bf16[4,32,768]{2,1,0:T(8,128)(2,1)S(1)} %pad_maximum_fusion.2), channel_id=1, source_target_pairs={{0,1},{1,2},{2,3},{3,4},{4,5},{5,6},{6,7},{8,9},{9,10},{10,11},{11... | collective-permute-start | bytes 589832 | tf_op jit(solution)/shard_map/ppermute | solution.py:53
  13.5 8.5 %collective-permute-start.1 = (bf16[4,32,768]{2,1,0:T(8,128)(2,1)S(1)}, bf16[4,32,768]{2,1,0:T(8,128)(2,1)S(1)}, u32[]{:S(2)}, u32[]{:S(2)}) collective-permute-start(bf16[4,32,768]{2,1,0:T(8,128)(2,1)S(1)} %pad_maximum_fusion), channel_id=1, source_target_pairs={{0,8},{8,16},{16,24},{1,9},{9,17},{17,25},{2,10},{10,18},{18,26},{... | collective-permute-start | bytes 589832 | tf_op jit(solution)/shard_map/ppermute | solution.py:53
  17.1 9.1 %collective-permute-start.4 = (bf16[4,32,768]{2,1,0:T(8,128)(2,1)S(1)}, bf16[4,32,768]{2,1,0:T(8,128)(2,1)S(1)}, u32[]{:S(2)}, u32[]{:S(2)}) collective-permute-start(bf16[4,32,768]{2,1,0:T(8,128)(2,1)S(1)} %pad_maximum_fusion.3), channel_id=1, source_target_pairs={{0,32},{32,64},{64,96},{96,128},{128,160},{160,192},{192,224},{1,3... | collective-permute-start | bytes 589832 | tf_op jit(solution)/shard_map/ppermute | solution.py:53
  22.1 7.5 %collective-permute-start.2 = (bf16[4,32,768]{2,1,0:T(8,128)(2,1)S(1)}, bf16[4,32,768]{2,1,0:T(8,128)(2,1)S(1)}, u32[]{:S(2)}, u32[]{:S(2)}) collective-permute-start(bf16[4,32,768]{2,1,0:T(8,128)(2,1)S(1)} %pad_maximum_fusion.1), channel_id=1, source_target_pairs={{0,1},{1,2},{2,3},{3,4},{4,5},{5,6},{6,7},{8,9},{9,10},{10,11},{11... | collective-permute-start | bytes 589832 | tf_op jit(solution)/shard_map/ppermute | solution.py:53
  26.2 9.2 %collective-permute-start.5 = (bf16[4,32,768]{2,1,0:T(8,128)(2,1)S(1)}, bf16[4,32,768]{2,1,0:T(8,128)(2,1)S(1)}, u32[]{:S(2)}, u32[]{:S(2)}) collective-permute-start(bf16[4,32,768]{2,1,0:T(8,128)(2,1)S(1)} %pad_maximum_fusion.4), channel_id=1, source_target_pairs={{0,8},{8,16},{16,24},{1,9},{9,17},{17,25},{2,10},{10,18},{18,26},{... | collective-permute-start | bytes 589832 | tf_op jit(solution)/shard_map/ppermute | solution.py:53
  35.5 1.0 copy-start.9
  50.5 3.5 %copy-start.12 = (bf16[512,768]{1,0:T(8,128)(2,1)}, bf16[512,768]{1,0:T(8,128)(2,1)S(1)}, u32[]{:S(2)}) copy-start(bf16[512,768]{1,0:T(8,128)(2,1)S(1)} %get-tuple-element.42.refs_0_) | copy-start | bytes 2359300
  50.5 3.5 %copy-start.14 = (bf16[512,768]{1,0:T(8,128)(2,1)}, bf16[512,768]{1,0:T(8,128)(2,1)S(1)}, u32[]{:S(2)}) copy-start(bf16[512,768]{1,0:T(8,128)(2,1)S(1)} %get-tuple-element.43.refs_3_) | copy-start | bytes 2359300
  50.5 8.5 %copy-start.1 = (bf16[512,768]{1,0:T(8,128)(2,1)}, bf16[512,768]{1,0:T(8,128)(2,1)S(1)}, u32[]{:S(2)}) copy-start(bf16[512,768]{1,0:T(8,128)(2,1)S(1)} %get-tuple-element.37.refs_2_) | copy-start | bytes 2359300
  54.0 5.0 %collective-permute-start.6 = (bf16[512,2432]{1,0:T(8,128)(2,1)S(1)}, bf16[512,2432]{1,0:T(8,128)(2,1)S(1)}, u32[]{:S(2)}, u32[]{:S(2)}) collective-permute-start(bf16[512,2432]{1,0:T(8,128)(2,1)S(1)} %shard_map.112), channel_id=1, source_target_pairs={{0,1},{1,0},{2,3},{3,2},{4,5},{5,4},{6,7},{7,6},{8,9},{9,8},{10,11... | collective-permute-start | bytes 7471112 | tf_op jit(solution)/shard_map/ppermute | solution.py:87
  62.4 1.5 %copy-start = (bf16[512,2432]{1,0:T(8,128)(2,1)}, bf16[512,2432]{1,0:T(8,128)(2,1)S(1)}, u32[]{:S(2)}) copy-start(bf16[512,2432]{1,0:T(8,128)(2,1)S(1)} %shard_map.114) | copy-start | bytes 7471108
  63.9 43.1 %all-to-all-start = ((bf16[32,16,2432]{2,1,0:T(8,128)(2,1)}), bf16[32,16,2432]{2,1,0:T(8,128)(2,1)S(1)}, u32[]{:S(2)}, u32[]{:S(2)}) async-start(bf16[32,16,2432]{2,1,0:T(8,128)(2,1)} %bitcast.2), calls=%async_computation | async-start | bytes 4980736 | tf_op jit(solution)/shard_map/all_to_all | solution.py:355
  72.0 1.1 copy-start.2
  73.2 1.3 copy-start.4
  74.4 1.1 copy-start.13
  75.6 1.1 copy-start.15
  79.2 2.8 %copy-start.10 = (bf16[256,1536]{1,0:T(8,128)(2,1)}, bf16[256,1536]{1,0:T(8,128)(2,1)S(1)}, u32[]{:S(2)}) copy-start(bf16[256,1536]{1,0:T(8,128)(2,1)S(1)} %get-tuple-element.44.refs_0_) | copy-start | bytes 2359300
  79.3 2.8 %copy-start.16 = (bf16[7,32,768]{2,1,0:T(8,128)(2,1)}, bf16[7,32,768]{2,1,0:T(8,128)(2,1)S(1)}, u32[]{:S(2)}) copy-start(bf16[7,32,768]{2,1,0:T(8,128)(2,1)S(1)} %get-tuple-element.48) | copy-start | bytes 1032196
  79.3 2.8 %copy-start.17 = (bf16[7,32,768]{2,1,0:T(8,128)(2,1)}, bf16[7,32,768]{2,1,0:T(8,128)(2,1)S(1)}, u32[]{:S(2)}) copy-start(bf16[7,32,768]{2,1,0:T(8,128)(2,1)S(1)} %get-tuple-element.50) | copy-start | bytes 1032196
  80.1 27.9 %collective-permute-start.7 = (bf16[4,32,768]{2,1,0:T(8,128)(2,1)}, bf16[4,32,768]{2,1,0:T(8,128)(2,1)S(1)}, u32[]{:S(2)}, u32[]{:S(2)}) collective-permute-start(bf16[4,32,768]{2,1,0:T(8,128)(2,1)} %pad_maximum_fusion.5), channel_id=1, source_target_pairs={{1,0},{2,1},{3,2},{4,3},{5,4},{6,5},{7,6},{9,8},{10,9},{11,10},{12... | collective-permute-start | bytes 589832 | tf_op jit(solution)/shard_map/ppermute | solution.py:53
  82.1 26.7 %collective-permute-start.8 = (bf16[4,32,768]{2,1,0:T(8,128)(2,1)}, bf16[4,32,768]{2,1,0:T(8,128)(2,1)}, u32[]{:S(2)}, u32[]{:S(2)}) collective-permute-start(bf16[4,32,768]{2,1,0:T(8,128)(2,1)} %slice.155), channel_id=1, source_target_pairs={{32,0},{64,32},{96,64},{128,96},{160,128},{192,160},{224,192},{33,... | collective-permute-start | bytes 589832 | tf_op jit(solution)/shard_map/ppermute | solution.py:53
  85.4 50.3 %copy-start.11 = (bf16[256,1536]{1,0:T(8,128)(2,1)S(1)}, bf16[256,1536]{1,0:T(8,128)(2,1)}, u32[]{:S(2)}) copy-start(bf16[256,1536]{1,0:T(8,128)(2,1)} %copy-done.10) | copy-start | bytes 2359300
  110.6 13.5 %collective-permute-start.9 = (bf16[4,32,768]{2,1,0:T(8,128)(2,1)S(1)}, bf16[4,32,768]{2,1,0:T(8,128)(2,1)S(1)}, u32[]{:S(2)}, u32[]{:S(2)}) collective-permute-start(bf16[4,32,768]{2,1,0:T(8,128)(2,1)S(1)} %pad_maximum_fusion.6), channel_id=1, source_target_pairs={{8,0},{16,8},{24,16},{9,1},{17,9},{25,17},{10,2},{18,10},{26,18},{... | collective-permute-start | bytes 589832 | tf_op jit(solution)/shard_map/ppermute | solution.py:53
  114.1 14.0 %collective-permute-start.11 = (bf16[4,32,768]{2,1,0:T(8,128)(2,1)S(1)}, bf16[4,32,768]{2,1,0:T(8,128)(2,1)S(1)}, u32[]{:S(2)}, u32[]{:S(2)}) collective-permute-start(bf16[4,32,768]{2,1,0:T(8,128)(2,1)S(1)} %pad_maximum_fusion.8), channel_id=1, source_target_pairs={{1,0},{2,1},{3,2},{4,3},{5,4},{6,5},{7,6},{9,8},{10,9},{11,10},{12... | collective-permute-start | bytes 589832 | tf_op jit(solution)/shard_map/ppermute | solution.py:53
  115.4 18.6 %all-to-all-start.1 = ((bf16[4,8,2432]{2,1,0:T(8,128)(2,1)}), bf16[4,8,2432]{2,1,0:T(8,128)(2,1)S(1)}, u32[]{:S(2)}, u32[]{:S(2)}) async-start(bf16[4,8,2432]{2,1,0:T(8,128)(2,1)} %shard_map.115), calls=%async_computation.1 | async-start | bytes 311296 | tf_op jit(solution)/shard_map/all_to_all | solution.py:361
  124.2 11.1 %collective-permute-start.10 = (bf16[4,32,768]{2,1,0:T(8,128)(2,1)S(1)}, bf16[4,32,768]{2,1,0:T(8,128)(2,1)S(1)}, u32[]{:S(2)}, u32[]{:S(2)}) collective-permute-start(bf16[4,32,768]{2,1,0:T(8,128)(2,1)S(1)} %pad_maximum_fusion.7), channel_id=1, source_target_pairs={{32,0},{64,32},{96,64},{128,96},{160,128},{192,160},{224,192},{33,... | collective-permute-start | bytes 589832 | tf_op jit(solution)/shard_map/ppermute | solution.py:53
  128.2 7.6 %collective-permute-start.12 = (bf16[4,32,768]{2,1,0:T(8,128)(2,1)S(1)}, bf16[4,32,768]{2,1,0:T(8,128)(2,1)S(1)}, u32[]{:S(2)}, u32[]{:S(2)}) collective-permute-start(bf16[4,32,768]{2,1,0:T(8,128)(2,1)S(1)} %pad_maximum_fusion.9), channel_id=1, source_target_pairs={{8,0},{16,8},{24,16},{9,1},{17,9},{25,17},{10,2},{18,10},{26,18},{... | collective-permute-start | bytes 589832 | tf_op jit(solution)/shard_map/ppermute | solution.py:53

commit v10 on v9

--- a/solution.py
+++ b/solution.py
@@ -352,6 +352,7 @@
     places = starts()
     down = step([[back_t], [back_g]], places, DOWN, 0, -1)
     (paired,) = call(functools.partial(half_sums, 0), [half], *operands, got, smem=(0,), mib=SUMS)
+    paired, down[0] = lax.optimization_barrier((paired, down[0]))
     spread = lax.all_to_all(paired, ("gx", "gy"), split_axis=0, concat_axis=0, tiled=True)
     (part,) = call(sum2_body, [((4, 8, COLS), BF)], me, spread.reshape(32, 16, COLS), smem=(0,))
     part, down = lax.optimization_barrier((part, down))

time: 140 us -> 142 us (1.014)
  starting transfers between devices: 49.2 us -> 56.1 us
  local copies, waits for them, and re-layouts: 13.1 us -> 8.53 us
  Pallas kernels: 27.8 us -> 29.3 us
    all_to_all x1, starting transfers between devices: 8.73 us -> 16 us  [on_device(): lax.all_to_all(part, 'gz', split_axis=0, concat_axis=0, tiled=True, axis_...]
    unnamed x41 -> x21, local copies, waits for them, and re-layouts: 9.83 us -> 4.35 us
    ppermute x1, waiting for transfers between devices: 4.43 us -> 0.01 us  [crossed(): lax.ppermute(value, axis, [(source, source ^ mask) for source in range(co...]
    all_to_all x1, waiting for transfers between devices: 21.5 us -> 23.7 us  [on_device(): lax.all_to_all(paired, ('gx', 'gy'), split_axis=0, concat_axis=0, tiled=T...]
    all_to_all x1, waiting for transfers between devices: 3.88 us -> 5.4 us  [on_device(): lax.all_to_all(part, 'gz', split_axis=0, concat_axis=0, tiled=True, axis_...]
    pallas_call x8, Pallas kernels: 27.8 us -> 29.3 us  [call(): pl.pallas_call(flat, out_shape=[jax.ShapeDtypeStruct(shape, dtype) for sh...]
  transfers between devices with their start and end apart: 15 -> 15, of which waited for: 9 -> 8; matrix products, arithmetic and copies ran while one was open for 2% -> 2% of each run, Pallas kernels for 3% -> 6%
where the time goes in v10:
time: 142 us; the launch traced here: 141 us
  starting transfers between devices  56.1 us (40%)
  waiting for transfers between devices  46 us (32%)
  Pallas kernels  29.3 us (21%)
  local copies, waits for them, and re-layouts  8.53 us (6%)
    ppermute x12, starting transfers between devices, passed_along(): lax.ppermute(value, axis, [(source, source + steps) for source in range(i...  31.3 us
    pallas_call x8, Pallas kernels, call(): pl.pallas_call(flat, out_shape=[jax.ShapeDtypeStruct(shape, dtype) for sh...  29.3 us
    all_to_all x1, waiting for transfers between devices, on_device(): lax.all_to_all(paired, ('gx', 'gy'), split_axis=0, concat_axis=0, tiled=T...  23.7 us
    ppermute x12, waiting for transfers between devices, passed_along(): lax.ppermute(value, axis, [(source, source + steps) for source in range(i...  16.9 us
    all_to_all x1, starting transfers between devices, on_device(): lax.all_to_all(part, 'gz', split_axis=0, concat_axis=0, tiled=True, axis_...  16 us
    all_to_all x1, starting transfers between devices, on_device(): lax.all_to_all(paired, ('gx', 'gy'), split_axis=0, concat_axis=0, tiled=T...  8.18 us
    all_to_all x1, waiting for transfers between devices, on_device(): lax.all_to_all(part, 'gz', split_axis=0, concat_axis=0, tiled=True, axis_...  5.4 us
    unnamed x21, local copies, waits for them, and re-layouts  4.35 us
  transfers between devices with their start and end apart: 15, of which 8 were waited for; matrix products, arithmetic and copies ran while one was open for 2% of the time, Pallas kernels for 6%

profile of v10, /device:TPU:10, one launch (start us, length us, event | category | flops | bytes accessed | tf_op | source)
XLA Modules:
  0.0 141.3 jit_solution(4907380468998986495)
XLA Ops:
  0.6 0.7 copy.14.refs_2_.refs_7_
  1.3 0.0 copy-start.2
  1.3 1.0 copy-done.2
  2.3 0.0 copy-start.4
  2.3 1.0 copy-done.4
  3.3 0.0 copy-start.9
  3.3 0.0 copy-start
  3.3 0.0 copy-start.1
  3.3 0.0 copy-start.3
  3.3 0.0 copy-start.8
  3.3 0.4 shard_map.110
  3.8 4.1 %collective-permute-start = (bf16[4,32,768]{2,1,0:T(8,128)(2,1)S(1)}, bf16[4,32,768]{2,1,0:T(8,128)(2,1)S(1)}, u32[]{:S(2)}, u32[]{:S(2)}) collective-permute-start(bf16[4,32,768]{2,1,0:T(8,128)(2,1)S(1)} %slice.133), channel_id=1, source_target_pairs={{0,32},{32,64},{64,96},{96,128},{128,160},{160,192},{192,224},{1,3... | collective-permute-start | bytes 589832 | tf_op jit(solution)/shard_map/ppermute | solution.py:53
  7.9 1.5 %collective-permute-start.3 = (bf16[4,32,768]{2,1,0:T(8,128)(2,1)S(1)}, bf16[4,32,768]{2,1,0:T(8,128)(2,1)S(1)}, u32[]{:S(2)}, u32[]{:S(2)}) collective-permute-start(bf16[4,32,768]{2,1,0:T(8,128)(2,1)S(1)} %pad_maximum_fusion.2), channel_id=1, source_target_pairs={{0,1},{1,2},{2,3},{3,4},{4,5},{5,6},{6,7},{8,9},{9,10},{10,11},{11... | collective-permute-start | bytes 589832 | tf_op jit(solution)/shard_map/ppermute | solution.py:53
  9.4 4.0 %collective-permute-done.refs_2_ = bf16[4,32,768]{2,1,0:T(8,128)(2,1)S(1)} collective-permute-done((bf16[4,32,768]{2,1,0:T(8,128)(2,1)S(1)}, bf16[4,32,768]{2,1,0:T(8,128)(2,1)S(1)}, u32[]{:S(2)}, u32[]{:S(2)}) %collective-permute-start) | collective-permute-done | bytes 196640 | tf_op jit(solution)/shard_map/ppermute | solution.py:53
  13.5 3.5 %collective-permute-start.1 = (bf16[4,32,768]{2,1,0:T(8,128)(2,1)S(1)}, bf16[4,32,768]{2,1,0:T(8,128)(2,1)S(1)}, u32[]{:S(2)}, u32[]{:S(2)}) collective-permute-start(bf16[4,32,768]{2,1,0:T(8,128)(2,1)S(1)} %pad_maximum_fusion), channel_id=1, source_target_pairs={{0,8},{8,16},{16,24},{1,9},{9,17},{17,25},{2,10},{10,18},{18,26},{... | collective-permute-start | bytes 589832 | tf_op jit(solution)/shard_map/ppermute | solution.py:53
  17.0 0.0 collective-permute-done.3.refs_5_
  17.1 2.9 %collective-permute-start.4 = (bf16[4,32,768]{2,1,0:T(8,128)(2,1)S(1)}, bf16[4,32,768]{2,1,0:T(8,128)(2,1)S(1)}, u32[]{:S(2)}, u32[]{:S(2)}) collective-permute-start(bf16[4,32,768]{2,1,0:T(8,128)(2,1)S(1)} %pad_maximum_fusion.3), channel_id=1, source_target_pairs={{0,32},{32,64},{64,96},{96,128},{128,160},{160,192},{192,224},{1,3... | collective-permute-start | bytes 589832 | tf_op jit(solution)/shard_map/ppermute | solution.py:53
  20.0 2.0 %collective-permute-done.1.refs_3_ = bf16[4,32,768]{2,1,0:T(8,128)(2,1)S(1)} collective-permute-done((bf16[4,32,768]{2,1,0:T(8,128)(2,1)S(1)}, bf16[4,32,768]{2,1,0:T(8,128)(2,1)S(1)}, u32[]{:S(2)}, u32[]{:S(2)}) %collective-permute-start.1) | collective-permute-done | bytes 196640 | tf_op jit(solution)/shard_map/ppermute | solution.py:53
  22.1 1.3 collective-permute-start.2
  23.4 2.8 %collective-permute-done.4.refs_6_ = bf16[4,32,768]{2,1,0:T(8,128)(2,1)S(1)} collective-permute-done((bf16[4,32,768]{2,1,0:T(8,128)(2,1)S(1)}, bf16[4,32,768]{2,1,0:T(8,128)(2,1)S(1)}, u32[]{:S(2)}, u32[]{:S(2)}) %collective-permute-start.4) | collective-permute-done | bytes 196640 | tf_op jit(solution)/shard_map/ppermute | solution.py:53
  26.2 3.3 %collective-permute-start.5 = (bf16[4,32,768]{2,1,0:T(8,128)(2,1)S(1)}, bf16[4,32,768]{2,1,0:T(8,128)(2,1)S(1)}, u32[]{:S(2)}, u32[]{:S(2)}) collective-permute-start(bf16[4,32,768]{2,1,0:T(8,128)(2,1)S(1)} %pad_maximum_fusion.4), channel_id=1, source_target_pairs={{0,8},{8,16},{16,24},{1,9},{9,17},{17,25},{2,10},{10,18},{18,26},{... | collective-permute-start | bytes 589832 | tf_op jit(solution)/shard_map/ppermute | solution.py:53
  29.5 0.0 copy-done.9
  29.6 0.0 collective-permute-done.2.refs_4_
  29.6 5.9 %collective-permute-done.5.refs_7_ = bf16[4,32,768]{2,1,0:T(8,128)(2,1)S(1)} collective-permute-done((bf16[4,32,768]{2,1,0:T(8,128)(2,1)S(1)}, bf16[4,32,768]{2,1,0:T(8,128)(2,1)S(1)}, u32[]{:S(2)}, u32[]{:S(2)}) %collective-permute-start.5) | collective-permute-done | bytes 196640 | tf_op jit(solution)/shard_map/ppermute | solution.py:53
  35.4 0.0 copy-done
  35.4 0.0 copy-done.1
  35.4 0.0 copy-done.3
  35.5 0.0 copy-done.8
  35.5 0.0 copy-start.5
  35.5 1.0 copy-done.5
  36.5 14.0 %shard_map.111 = (bf16[512,768]{1,0:T(8,128)(2,1)S(1)}, bf16[512,768]{1,0:T(8,128)(2,1)S(1)}, bf16[512,768]{1,0:T(8,128)(2,1)S(1)}, bf16[512,768]{1,0:T(8,128)(2...) custom-call(bf16[256,768]{1,0:T(8,128)(2,1)S(1)} %copy-done.3, ...), custom_call_target="tpu_custom_call" | custom-call | tf_op jit(solution)/shard_map/pallas_call | solution.py:304
  50.5 3.5 %shard_map.112 = bf16[512,2432]{1,0:T(8,128)(2,1)S(1)} custom-call(s32[1]{0:T(128)} %bitcast.refs_0_, bf16[512,768]{1,0:T(8,128)(2,1)S(1)} %get-tuple-element.39.refs_1_, bf16[512,768]{1,0:T(8,128)(2,1)S(1)} %get-tuple-element.40.refs_2_, bf16[512,768]{1,0:T(8,128)(2,1)S(1)} %get-tuple-element.41.refs_3_.refs_1_, ...), custom_call_target="tpu_custom_call" | custom-call | tf_op jit(solution)/shard_map/pallas_call | solution.py:304
  53.9 0.6 collective-permute-start.6
  54.5 2.5 %shard_map.113 = (bf16[7,32,768]{2,1,0:T(8,128)(2,1)S(1)}, bf16[7,32,768]{2,1,0:T(8,128)(2,1)S(1)}, bf16[256,1536]{1,0:T(8,128)(2,1)S(1)}) custom-call(bf16[512,768]{1,0:T(8,128)(2,1)S(1)} %get-tuple-element.45.refs_0_, bf16[512,768]{1,0:T(8,128)(2,1)S(1)} %get-tuple-element.41.refs_3_.refs_1_, bf16[512,768]{1,0:T(8,128)(2,1)S(1)} %get-tuple-element.40.refs_2_, ...), custom_call_target="tpu_custom_call" | custom-call | tf_op jit(solution)/shard_map/pallas_call | solution.py:304
  57.1 0.0 copy-start.6
  57.1 0.0 copy-start.7
  57.1 0.6 copy-done.6
  57.8 1.3 collective-permute-start.7
  59.1 0.0 collective-permute-done.6.refs_6_
  59.1 4.9 %shard_map.114 = bf16[512,2432]{1,0:T(8,128)(2,1)} custom-call(s32[1]{0:T(128)} %bitcast.refs_0_, bf16[512,768]{1,0:T(8,128)(2,1)S(1)} %get-tuple-element.39.refs_1_, bf16[512,768]{1,0:T(8,128)(2,1)S(1)} %get-tuple-element.40.refs_2_, bf16[512,768]{1,0:T(8,128)(2,1)S(1)} %get-tuple-element.41.refs_3_.refs_1_, ...), custom_call_target="tpu_custom_call" | custom-call | tf_op jit(solution)/shard_map/pallas_call | solution.py:304
  64.0 0.0 copy-done.7
  64.0 0.0 collective-permute-done.7.refs_1_
  64.0 8.2 %all-to-all-start = ((bf16[32,16,2432]{2,1,0:T(8,128)(2,1)}), bf16[32,16,2432]{2,1,0:T(8,128)(2,1)S(1)}, u32[]{:S(2)}, u32[]{:S(2)}) async-start(bf16[32,16,2432]{2,1,0:T(8,128)(2,1)} %bitcast.1), calls=%async_computation | async-start | bytes 4980736 | tf_op jit(solution)/shard_map/all_to_all | solution.py:356
  72.2 1.6 %slice.155 = bf16[4,32,768]{2,1,0:T(8,128)(2,1)} slice(bf16[7,32,768]{2,1,0:T(8,128)(2,1)} %copy-done.7), slice={[3:7], [0:32], [0:768]} | slice | bytes 393216 | tf_op jit(solution)/shard_map/slice | solution.py:62
  73.8 3.4 %collective-permute-start.8 = (bf16[4,32,768]{2,1,0:T(8,128)(2,1)}, bf16[4,32,768]{2,1,0:T(8,128)(2,1)}, u32[]{:S(2)}, u32[]{:S(2)}) collective-permute-start(bf16[4,32,768]{2,1,0:T(8,128)(2,1)} %slice.155), channel_id=1, source_target_pairs={{32,0},{64,32},{96,64},{128,96},{160,128},{192,160},{224,192},{33,... | collective-permute-start | bytes 589832 | tf_op jit(solution)/shard_map/ppermute | solution.py:53
  77.2 23.7 %all-to-all-done.refs_1_ = bf16[32,16,2432]{2,1,0:T(8,128)(2,1)S(1)} async-done(((bf16[32,16,2432]{2,1,0:T(8,128)(2,1)}), bf16[32,16,2432]{2,1,0:T(8,128)(2,1)S(1)}, u32[]{:S(2)}, u32[]{:S(2)}) %all-to-all-start) | async-done | bytes 2490400 | tf_op jit(solution)/shard_map/all_to_all | solution.py:356
  100.9 1.0 shard_map.115
  101.9 1.5 %collective-permute-done.8.refs_4_ = bf16[4,32,768]{2,1,0:T(8,128)(2,1)} collective-permute-done((bf16[4,32,768]{2,1,0:T(8,128)(2,1)}, bf16[4,32,768]{2,1,0:T(8,128)(2,1)}, u32[]{:S(2)}, u32[]{:S(2)}) %collective-permute-start.8) | collective-permute-done | bytes 196640 | tf_op jit(solution)/shard_map/ppermute | solution.py:53
  103.4 0.9 fusion.5
  104.3 0.9 fusion
  105.3 5.0 %collective-permute-start.9 = (bf16[4,32,768]{2,1,0:T(8,128)(2,1)S(1)}, bf16[4,32,768]{2,1,0:T(8,128)(2,1)S(1)}, u32[]{:S(2)}, u32[]{:S(2)}) collective-permute-start(bf16[4,32,768]{2,1,0:T(8,128)(2,1)S(1)} %pad_maximum_fusion.6), channel_id=1, source_target_pairs={{8,0},{16,8},{24,16},{9,1},{17,9},{25,17},{10,2},{18,10},{26,18},{... | collective-permute-start | bytes 589832 | tf_op jit(solution)/shard_map/ppermute | solution.py:53
  110.3 1.3 collective-permute-start.11
  111.6 16.0 %all-to-all-start.1 = ((bf16[4,8,2432]{2,1,0:T(8,128)(2,1)}), bf16[4,8,2432]{2,1,0:T(8,128)(2,1)S(1)}, u32[]{:S(2)}, u32[]{:S(2)}) async-start(bf16[4,8,2432]{2,1,0:T(8,128)(2,1)} %shard_map.115), calls=%async_computation.1 | async-start | bytes 311296 | tf_op jit(solution)/shard_map/all_to_all | solution.py:362
  127.6 0.0 collective-permute-done.9.refs_2_
  127.6 1.9 %collective-permute-start.10 = (bf16[4,32,768]{2,1,0:T(8,128)(2,1)S(1)}, bf16[4,32,768]{2,1,0:T(8,128)(2,1)S(1)}, u32[]{:S(2)}, u32[]{:S(2)}) collective-permute-start(bf16[4,32,768]{2,1,0:T(8,128)(2,1)S(1)} %pad_maximum_fusion.7), channel_id=1, source_target_pairs={{32,0},{64,32},{96,64},{128,96},{160,128},{192,160},{224,192},{33,... | collective-permute-start | bytes 589832 | tf_op jit(solution)/shard_map/ppermute | solution.py:53
  129.5 0.0 collective-permute-done.11.refs_5_
  129.6 1.9 %collective-permute-start.12 = (bf16[4,32,768]{2,1,0:T(8,128)(2,1)S(1)}, bf16[4,32,768]{2,1,0:T(8,128)(2,1)S(1)}, u32[]{:S(2)}, u32[]{:S(2)}) collective-permute-start(bf16[4,32,768]{2,1,0:T(8,128)(2,1)S(1)} %pad_maximum_fusion.9), channel_id=1, source_target_pairs={{8,0},{16,8},{24,16},{9,1},{17,9},{25,17},{10,2},{18,10},{26,18},{... | collective-permute-start | bytes 589832 | tf_op jit(solution)/shard_map/ppermute | solution.py:53
  131.5 5.4 %all-to-all-done.1.refs_0_ = bf16[4,8,2432]{2,1,0:T(8,128)(2,1)S(1)} async-done(((bf16[4,8,2432]{2,1,0:T(8,128)(2,1)}), bf16[4,8,2432]{2,1,0:T(8,128)(2,1)S(1)}, u32[]{:S(2)}, u32[]{:S(2)}) %all-to-all-start.1) | async-done | bytes 155680 | tf_op jit(solution)/shard_map/all_to_all | solution.py:362
  136.9 0.6 shard_map.117
  137.6 0.6 slice_reduce_fusion
  138.2 0.0 collective-permute-done.10.refs_3_
  138.2 0.6 collective-permute-done.12.refs_6_
  138.8 2.4 %shard_map.116 = (bf16[256,768]{1,0:T(8,128)(2,1)}, bf16[256,768]{1,0:T(8,128)(2,1)}) custom-call(bf16[256,1536]{1,0:T(8,128)(2,1)S(1)} %get-tuple-element.47.refs_0_, bf16[4,32,768]{2,1,0:T(8,128)(2,1)S(1)} %collective-permute-done.7.refs_1_, bf16[4,32,768]{2,1,0:T(8,128)(2,1)S(1)} %collective-permute-done.9.refs_2_, ...), custom_call_target="tpu_custom_call" | custom-call | tf_op jit(solution)/shard_map/pallas_call | solution.py:304
  (23 shorter events, 0.4 us)
Async XLA Ops:
  1.3 1.0 copy-start.2
  2.3 1.0 copy-start.4
  3.3 26.2 %copy-start.9 = (f32[768]{0:T(1024)S(1)}, f32[768]{0:T(1024)}, u32[]{:S(2)}) copy-start(f32[768]{0:T(1024)} %param.8) | copy-start | bytes 9220
  3.3 32.1 %copy-start = (bf16[768,768]{1,0:T(8,128)(2,1)S(1)}, bf16[768,768]{1,0:T(8,128)(2,1)}, u32[]{:S(2)}) copy-start(bf16[768,768]{1,0:T(8,128)(2,1)} %refs_6_.1) | copy-start | bytes 3538948
  3.3 32.1 %copy-start.1 = (bf16[768,2304]{1,0:T(8,128)(2,1)S(1)}, bf16[768,2304]{1,0:T(8,128)(2,1)}, u32[]{:S(2)}) copy-start(bf16[768,2304]{1,0:T(8,128)(2,1)} %refs_10_.1) | copy-start | bytes 10616836
  3.3 32.1 %copy-start.3 = (bf16[256,768]{1,0:T(8,128)(2,1)S(1)}, bf16[256,768]{1,0:T(8,128)(2,1)}, u32[]{:S(2)}) copy-start(bf16[256,768]{1,0:T(8,128)(2,1)} %refs_0_.1) | copy-start | bytes 1179652
  3.3 32.1 %copy-start.8 = (s32[1,512]{1,0:T(1,128)S(1)}, s32[1,512]{1,0:T(1,128)}, u32[]{:S(2)}) copy-start(s32[1,512]{1,0:T(1,128)} %refs_4_.1) | copy-start | bytes 6148
  3.8 9.7 %collective-permute-start = (bf16[4,32,768]{2,1,0:T(8,128)(2,1)S(1)}, bf16[4,32,768]{2,1,0:T(8,128)(2,1)S(1)}, u32[]{:S(2)}, u32[]{:S(2)}) collective-permute-start(bf16[4,32,768]{2,1,0:T(8,128)(2,1)S(1)} %slice.133), channel_id=1, source_target_pairs={{0,32},{32,64},{64,96},{96,128},{128,160},{160,192},{192,224},{1,3... | collective-permute-start | bytes 589832 | tf_op jit(solution)/shard_map/ppermute | solution.py:53
  7.9 9.1 %collective-permute-start.3 = (bf16[4,32,768]{2,1,0:T(8,128)(2,1)S(1)}, bf16[4,32,768]{2,1,0:T(8,128)(2,1)S(1)}, u32[]{:S(2)}, u32[]{:S(2)}) collective-permute-start(bf16[4,32,768]{2,1,0:T(8,128)(2,1)S(1)} %pad_maximum_fusion.2), channel_id=1, source_target_pairs={{0,1},{1,2},{2,3},{3,4},{4,5},{5,6},{6,7},{8,9},{9,10},{10,11},{11... | collective-permute-start | bytes 589832 | tf_op jit(solution)/shard_map/ppermute | solution.py:53
  13.5 8.5 %collective-permute-start.1 = (bf16[4,32,768]{2,1,0:T(8,128)(2,1)S(1)}, bf16[4,32,768]{2,1,0:T(8,128)(2,1)S(1)}, u32[]{:S(2)}, u32[]{:S(2)}) collective-permute-start(bf16[4,32,768]{2,1,0:T(8,128)(2,1)S(1)} %pad_maximum_fusion), channel_id=1, source_target_pairs={{0,8},{8,16},{16,24},{1,9},{9,17},{17,25},{2,10},{10,18},{18,26},{... | collective-permute-start | bytes 589832 | tf_op jit(solution)/shard_map/ppermute | solution.py:53
  17.1 9.1 %collective-permute-start.4 = (bf16[4,32,768]{2,1,0:T(8,128)(2,1)S(1)}, bf16[4,32,768]{2,1,0:T(8,128)(2,1)S(1)}, u32[]{:S(2)}, u32[]{:S(2)}) collective-permute-start(bf16[4,32,768]{2,1,0:T(8,128)(2,1)S(1)} %pad_maximum_fusion.3), channel_id=1, source_target_pairs={{0,32},{32,64},{64,96},{96,128},{128,160},{160,192},{192,224},{1,3... | collective-permute-start | bytes 589832 | tf_op jit(solution)/shard_map/ppermute | solution.py:53
  22.1 7.5 %collective-permute-start.2 = (bf16[4,32,768]{2,1,0:T(8,128)(2,1)S(1)}, bf16[4,32,768]{2,1,0:T(8,128)(2,1)S(1)}, u32[]{:S(2)}, u32[]{:S(2)}) collective-permute-start(bf16[4,32,768]{2,1,0:T(8,128)(2,1)S(1)} %pad_maximum_fusion.1), channel_id=1, source_target_pairs={{0,1},{1,2},{2,3},{3,4},{4,5},{5,6},{6,7},{8,9},{9,10},{10,11},{11... | collective-permute-start | bytes 589832 | tf_op jit(solution)/shard_map/ppermute | solution.py:53
  26.2 9.2 %collective-permute-start.5 = (bf16[4,32,768]{2,1,0:T(8,128)(2,1)S(1)}, bf16[4,32,768]{2,1,0:T(8,128)(2,1)S(1)}, u32[]{:S(2)}, u32[]{:S(2)}) collective-permute-start(bf16[4,32,768]{2,1,0:T(8,128)(2,1)S(1)} %pad_maximum_fusion.4), channel_id=1, source_target_pairs={{0,8},{8,16},{16,24},{1,9},{9,17},{17,25},{2,10},{10,18},{18,26},{... | collective-permute-start | bytes 589832 | tf_op jit(solution)/shard_map/ppermute | solution.py:53
  35.5 1.0 copy-start.5
  53.9 5.2 %collective-permute-start.6 = (bf16[512,2432]{1,0:T(8,128)(2,1)S(1)}, bf16[512,2432]{1,0:T(8,128)(2,1)S(1)}, u32[]{:S(2)}, u32[]{:S(2)}) collective-permute-start(bf16[512,2432]{1,0:T(8,128)(2,1)S(1)} %shard_map.112), channel_id=1, source_target_pairs={{0,1},{1,0},{2,3},{3,2},{4,5},{5,4},{6,7},{7,6},{8,9},{9,8},{10,11... | collective-permute-start | bytes 7471112 | tf_op jit(solution)/shard_map/ppermute | solution.py:87
  57.1 0.7 copy-start.6
  57.1 6.9 %copy-start.7 = (bf16[7,32,768]{2,1,0:T(8,128)(2,1)}, bf16[7,32,768]{2,1,0:T(8,128)(2,1)S(1)}, u32[]{:S(2)}) copy-start(bf16[7,32,768]{2,1,0:T(8,128)(2,1)S(1)} %get-tuple-element.56) | copy-start | bytes 1032196
  57.8 6.2 %collective-permute-start.7 = (bf16[4,32,768]{2,1,0:T(8,128)(2,1)S(1)}, bf16[4,32,768]{2,1,0:T(8,128)(2,1)S(1)}, u32[]{:S(2)}, u32[]{:S(2)}) collective-permute-start(bf16[4,32,768]{2,1,0:T(8,128)(2,1)S(1)} %pad_maximum_fusion.5), channel_id=1, source_target_pairs={{1,0},{2,1},{3,2},{4,3},{5,4},{6,5},{7,6},{9,8},{10,9},{11,10},{12... | collective-permute-start | bytes 589832 | tf_op jit(solution)/shard_map/ppermute | solution.py:53
  64.0 36.9 %all-to-all-start = ((bf16[32,16,2432]{2,1,0:T(8,128)(2,1)}), bf16[32,16,2432]{2,1,0:T(8,128)(2,1)S(1)}, u32[]{:S(2)}, u32[]{:S(2)}) async-start(bf16[32,16,2432]{2,1,0:T(8,128)(2,1)} %bitcast.1), calls=%async_computation | async-start | bytes 4980736 | tf_op jit(solution)/shard_map/all_to_all | solution.py:356
  73.8 29.6 %collective-permute-start.8 = (bf16[4,32,768]{2,1,0:T(8,128)(2,1)}, bf16[4,32,768]{2,1,0:T(8,128)(2,1)}, u32[]{:S(2)}, u32[]{:S(2)}) collective-permute-start(bf16[4,32,768]{2,1,0:T(8,128)(2,1)} %slice.155), channel_id=1, source_target_pairs={{32,0},{64,32},{96,64},{128,96},{160,128},{192,160},{224,192},{33,... | collective-permute-start | bytes 589832 | tf_op jit(solution)/shard_map/ppermute | solution.py:53
  105.3 22.3 %collective-permute-start.9 = (bf16[4,32,768]{2,1,0:T(8,128)(2,1)S(1)}, bf16[4,32,768]{2,1,0:T(8,128)(2,1)S(1)}, u32[]{:S(2)}, u32[]{:S(2)}) collective-permute-start(bf16[4,32,768]{2,1,0:T(8,128)(2,1)S(1)} %pad_maximum_fusion.6), channel_id=1, source_target_pairs={{8,0},{16,8},{24,16},{9,1},{17,9},{25,17},{10,2},{18,10},{26,18},{... | collective-permute-start | bytes 589832 | tf_op jit(solution)/shard_map/ppermute | solution.py:53
  110.3 19.3 %collective-permute-start.11 = (bf16[4,32,768]{2,1,0:T(8,128)(2,1)S(1)}, bf16[4,32,768]{2,1,0:T(8,128)(2,1)S(1)}, u32[]{:S(2)}, u32[]{:S(2)}) collective-permute-start(bf16[4,32,768]{2,1,0:T(8,128)(2,1)S(1)} %pad_maximum_fusion.8), channel_id=1, source_target_pairs={{1,0},{2,1},{3,2},{4,3},{5,4},{6,5},{7,6},{9,8},{10,9},{11,10},{12... | collective-permute-start | bytes 589832 | tf_op jit(solution)/shard_map/ppermute | solution.py:53
  111.6 25.3 %all-to-all-start.1 = ((bf16[4,8,2432]{2,1,0:T(8,128)(2,1)}), bf16[4,8,2432]{2,1,0:T(8,128)(2,1)S(1)}, u32[]{:S(2)}, u32[]{:S(2)}) async-start(bf16[4,8,2432]{2,1,0:T(8,128)(2,1)} %shard_map.115), calls=%async_computation.1 | async-start | bytes 311296 | tf_op jit(solution)/shard_map/all_to_all | solution.py:362
  127.6 10.6 %collective-permute-start.10 = (bf16[4,32,768]{2,1,0:T(8,128)(2,1)S(1)}, bf16[4,32,768]{2,1,0:T(8,128)(2,1)S(1)}, u32[]{:S(2)}, u32[]{:S(2)}) collective-permute-start(bf16[4,32,768]{2,1,0:T(8,128)(2,1)S(1)} %pad_maximum_fusion.7), channel_id=1, source_target_pairs={{32,0},{64,32},{96,64},{128,96},{160,128},{192,160},{224,192},{33,... | collective-permute-start | bytes 589832 | tf_op jit(solution)/shard_map/ppermute | solution.py:53
  129.6 9.2 %collective-permute-start.12 = (bf16[4,32,768]{2,1,0:T(8,128)(2,1)S(1)}, bf16[4,32,768]{2,1,0:T(8,128)(2,1)S(1)}, u32[]{:S(2)}, u32[]{:S(2)}) collective-permute-start(bf16[4,32,768]{2,1,0:T(8,128)(2,1)S(1)} %pad_maximum_fusion.9), channel_id=1, source_target_pairs={{8,0},{16,8},{24,16},{9,1},{17,9},{25,17},{10,2},{18,10},{26,18},{... | collective-permute-start | bytes 589832 | tf_op jit(solution)/shard_map/ppermute | solution.py:53
